TPU v7x, 512 devices: a whole 4x8x8 slice. The times are simulated.
512 devices in a mesh: dp: 64 (over y_lo, z, core), mp: 8 (over y_hi, x).
Axes of the slice: x: 4, y: 8 (y_hi: 2, y_lo: 4; y = y_hi * 4 + y_lo), z: 8, core: 2. Of those that a mesh axis runs over, the one named last changes fastest.
Arguments:
- tokens: bfloat16 [1024, 6144], P('dp', 'mp'), may hold values from -6 to 6
- norm_gain: float32 [6144], P('mp'), may hold values from 0.25 to 1.75
- w_up: bfloat16 [6144, 24576], P('mp', 'dp'), may hold values from -0.078125 to 0.078125
- cotangent: bfloat16 [1024, 24576], P('mp', 'dp'), may hold values from -32 to 32
Outputs:
- sharp_grad: float32 [6144, 24576], P('mp', 'dp')
All inputs are finite; a program needn't handle non-finite values.
Results may differ from a plain program's by a relative error of at most 0.0048.
Values may be sent and summed in bfloat16 or wider, within the bound.
No kernel may reach another device: no remote copies, remote signals or barrier semaphores. Data moves between devices by JAX's collectives and lax.ppermute only.
A program may use at most 64 MiB of HBM per device.

v0:
```python
import math

import jax
import jax.numpy as jnp
from jax import lax
from jax.sharding import PartitionSpec as P

FF = 24576


def gelu_slope(value):
    cdf = 0.5 * (1.0 + lax.erf(value * (1.0 / math.sqrt(2.0))))
    dens = jnp.exp(-0.5 * value * value) * (1.0 / math.sqrt(2.0 * math.pi))
    return cdf + value * dens


def per_device(tokens, norm_gain, w_up, cotangent):
    values = tokens.astype(jnp.float32)
    width = values.shape[1] * lax.axis_size("mp")
    total, squares = lax.psum((jnp.sum(values, axis=1), jnp.sum(values * values, axis=1)), "mp")
    mean = total / width
    var = squares / width - mean * mean
    normed = (
        (values - mean[:, None]) * lax.rsqrt(var[:, None] + 1e-06) * norm_gain[None, :]
    ).astype(jnp.bfloat16)
    token_count = tokens.shape[0] * lax.axis_size("dp")
    scale = 1.0 / math.sqrt(token_count)

    def project(weights):
        return jnp.dot(
            lax.all_gather(normed, "dp", axis=0, tiled=True),
            weights,
            preferred_element_type=jnp.float32,
        )

    def backproject(slope_all):
        return lax.dot_general(
            lax.all_gather(normed, "dp", axis=0, tiled=True),
            slope_all,
            (((0,), (0,)), ((), ())),
            preferred_element_type=jnp.float32,
        )

    def weight_grad(weights):
        partial_pre = project(weights)
        pre = lax.psum_scatter(partial_pre, "mp", scatter_dimension=0, tiled=True)
        slope = (cotangent.astype(jnp.float32) * gelu_slope(pre) * scale).astype(jnp.bfloat16)
        slope_all = lax.all_gather(slope, "mp", axis=0, tiled=True)
        return backproject(slope_all)

    ascent = weight_grad(w_up)
    squared = lax.psum(jnp.sum(ascent * ascent), ("dp", "mp"))
    size = jnp.sqrt(squared) + 1e-12
    radius = 0.5 * math.sqrt(FF)
    perturbed = (w_up.astype(jnp.float32) + radius * ascent / size).astype(jnp.bfloat16)
    return weight_grad(perturbed)


def solution(mesh):
    placed = (P("dp", "mp"), P("mp"), P("mp", "dp"), P("mp", "dp"))
    return jax.shard_map(
        per_device, mesh=mesh, in_specs=placed, out_specs=P("mp", "dp"), check_vma=False
    )
```

profile of v0, /device:TPU:1, one launch (start us, length us, event | category | flops | bytes accessed | tf_op | source)
XLA Modules:
  0.0 538.4 jit_solution(538916531870151645)
XLA Ops:
  6.5 0.0 all-gather.2.cloned.1.call-start
  6.5 0.9 convert_reduce_fusion
  7.4 28.8 %all-reduce = (f32[16]{0:T(128)S(1)}, f32[16]{0:T(128)S(1)}) all-reduce(f32[16]{0:T(128)S(1)} %get-tuple-element.6, f32[16]{0:T(128)S(1)} %get-tuple-element.5), channel_id=1, replica_groups=mesh['dp'=64,'mp'=8] {'mp'}, use_global_device_ids=true, to_apply=%region_3.0 | all-reduce | flops 32 | bytes 256 | tf_op jit(solution)/shard_map/psum | solution.py:20
  36.3 1.4 fusion.17
  37.7 0.0 all-gather.2.cloned.1.call-update
  37.7 0.0 reduce-scatter.3.cloned.1.call-start
  37.8 118.3 %all-gather.2.cloned.1.call-done = bf16[1024,768]{1,0:T(8,128)(2,1)} async-done(((bf16[16,768]{1,0:T(8,128)(2,1)}), bf16[1024,768]{1,0:T(8,128)(2,1)}) %all-gather.2.cloned.1.call-update) | async-done | bytes 1572880 | tf_op jit(solution)/shard_map/all_gather | solution.py:38
  156.1 3.7 fusion.20
  159.8 0.0 copy-start
  159.8 0.0 copy-start.1
  159.8 0.0 reduce-scatter.3.cloned.1.call-update
  159.8 0.0 reduce-scatter.5.cloned.1.call-start
  159.8 92.5 %reduce-scatter.3.cloned.1.call-done = f32[128,384]{1,0:T(8,128)} async-done(((f32[1024,384]{1,0:T(8,128)}), f32[128,384]{1,0:T(8,128)}) %reduce-scatter.3.cloned.1.call-update) | async-done | bytes 196624 | tf_op jit(solution)/shard_map/reduce_scatter | solution.py:46
  252.3 0.0 copy-done
  252.3 1.0 fusion.4
  253.3 38.8 %all_gather.13 = bf16[1024,384]{1,0:T(8,128)(2,1)S(1)} all-gather(bf16[128,384]{1,0:T(8,128)(2,1)S(1)} %fusion.4), channel_id=1, replica_groups=mesh['dp'=64,'mp'=8] {'mp'}, dimensions={0}, use_global_device_ids=true | all-gather | bytes 884736 | tf_op jit(solution)/shard_map/all_gather | solution.py:48
  292.2 0.0 copy-done.1
  292.2 0.0 copy-start.2
  292.2 1.7 multiply_reduce_fusion
  293.9 104.6 %psum.23 = f32[]{:T(128)} all-reduce(f32[]{:T(128)} %get-tuple-element.11), channel_id=1, replica_groups=mesh['dp'=64,'mp'=8] {'dp','mp'}, use_global_device_ids=true, to_apply=%region_6.0 | all-reduce | flops 1 | bytes 8 | tf_op jit(solution)/shard_map/psum | solution.py:52
  399.2 0.0 copy-done.2
  399.2 2.2 fusion
  401.4 0.0 reduce-scatter.5.cloned.1.call-update
  401.4 88.6 %reduce-scatter.5.cloned.1.call-done = f32[128,384]{1,0:T(8,128)} async-done(((f32[1024,384]{1,0:T(8,128)}), f32[128,384]{1,0:T(8,128)}) %reduce-scatter.5.cloned.1.call-update) | async-done | bytes 196624 | tf_op jit(solution)/shard_map/reduce_scatter | solution.py:46
  490.0 1.0 fusion.6
  491.1 38.8 %all_gather.14 = bf16[1024,384]{1,0:T(8,128)(2,1)S(1)} all-gather(bf16[128,384]{1,0:T(8,128)(2,1)S(1)} %fusion.6), channel_id=1, replica_groups=mesh['dp'=64,'mp'=8] {'mp'}, dimensions={0}, use_global_device_ids=true | all-gather | bytes 884736 | tf_op jit(solution)/shard_map/all_gather | solution.py:48
  529.9 2.0 fusion.21
  (1 shorter events, 0.0 us)
Async XLA Ops:
  6.5 149.6 %all-gather.2.cloned.1.call-start = ((), (), s32[]{:S(2)}) async-start(), calls=%async_computation.2 | async-start | bytes 1597440 | tf_op jit(solution)/shard_map/all_gather | solution.py:38
  37.7 214.6 %reduce-scatter.3.cloned.1.call-start = ((), (), s32[]{:S(2)}) async-start(), calls=%async_computation.3 | async-start | bytes 1769472 | tf_op jit(solution)/shard_map/reduce_scatter | solution.py:46
  159.8 92.5 %copy-start = (bf16[128,384]{1,0:T(8,128)(2,1)S(1)}, bf16[128,384]{1,0:T(8,128)(2,1)}, u32[]{:S(2)}) copy-start(bf16[128,384]{1,0:T(8,128)(2,1)} %param.7) | copy-start | bytes 294916
  159.8 132.4 %copy-start.1 = (bf16[1024,768]{1,0:T(8,128)(2,1)S(1)}, bf16[1024,768]{1,0:T(8,128)(2,1)}, u32[]{:S(2)}) copy-start(bf16[1024,768]{1,0:T(8,128)(2,1)} %all-gather.2.cloned.1.call-done) | copy-start | bytes 4718596
  159.8 330.2 %reduce-scatter.5.cloned.1.call-start = ((), (), s32[]{:S(2)}) async-start(), calls=%async_computation.4 | async-start | bytes 1769472 | tf_op jit(solution)/shard_map/reduce_scatter | solution.py:46
  292.2 107.0 %copy-start.2 = (bf16[768,384]{1,0:T(8,128)(2,1)S(1)}, bf16[768,384]{1,0:T(8,128)(2,1)}, u32[]{:S(2)}) copy-start(bf16[768,384]{1,0:T(8,128)(2,1)} %param.6) | copy-start | bytes 1769476
Sparse Core Ops, SparseCore 0:
  37.8 118.2 all-gather.1
  160.7 91.5 reduce-scatter.2
  401.5 88.4 reduce-scatter.4
where the time goes:
time: 546 us; the launch traced here: 538 us
  waiting for transfers between devices  299 us (55%)
  blocking collectives  211 us (39%)
  between operations  13.8 us (3%)
  matrix products  9.55 us (2%)
    reduce_scatter x2, waiting for transfers between devices, weight_grad(): pre = lax.psum_scatter(partial_pre, 'mp', scatter_dimension=0, tiled=True)  181 us
    all_gather x1, waiting for transfers between devices, backproject(): lax.all_gather(normed, 'dp', axis=0, tiled=True)  118 us
    psum x1, blocking collectives, per_device(): squared = lax.psum(jnp.sum(ascent * ascent), ('dp', 'mp'))  105 us
    all_gather x2, blocking collectives, weight_grad(): slope_all = lax.all_gather(slope, 'mp', axis=0, tiled=True)  77.6 us
    psum x1, blocking collectives, per_device(): lax.psum((jnp.sum(values, axis=1), jnp.sum(values * values, axis=1)), 'mp')  28.8 us
  transfers between devices with their start and end apart: 3, of which 3 were waited for; matrix products, arithmetic and copies ran while one was open for 0% of the time, Pallas kernels for 0%

commit v1 on v0

v1 whole, which is shorter than its diff:
```python
import math

import jax
import jax.numpy as jnp
from jax import lax
from jax.sharding import Mesh
from jax.sharding import PartitionSpec as P

FF = 24576
D = 6144
TOKENS = 1024
DP = ("yl", "z", "c")
MP = ("yh", "x")
BF = jnp.bfloat16
F32 = jnp.float32


def gelu_slope(value):
    cdf = 0.5 * (1.0 + lax.erf(value * (1.0 / math.sqrt(2.0))))
    dens = jnp.exp(-0.5 * value * value) * (1.0 / math.sqrt(2.0 * math.pi))
    return cdf + value * dens


def swap(value, axis, bit):
    size = lax.axis_size(axis)
    return lax.ppermute(value, axis, [(i, i ^ bit) for i in range(size)])


def butterfly(value, steps):
    for axis, bit in steps:
        value = value + swap(value, axis, bit)
    return value


OVER_MP = (("x", 1), ("x", 2), ("yh", 1))
OVER_DP = (("c", 1), ("z", 1), ("z", 2), ("z", 4), ("yl", 1), ("yl", 2))


def spread(value, axes, count):
    copies = jnp.broadcast_to(value[None], (count,) + value.shape)
    return lax.all_to_all(copies, axes, 0, 0, tiled=True)


def spread_dp(value):
    mine = spread(value, ("yl", "z"), 32)
    other = swap(mine, "c", 1)
    core = lax.axis_index("c")
    first = jnp.where(core == 0, mine, other)
    second = jnp.where(core == 0, other, mine)
    return jnp.stack([first, second], axis=1)


def per_device(tokens, norm_gain, w_up, cotangent):
    scale = 1.0 / math.sqrt(TOKENS)
    with jax.named_scope("token_gather"):
        raw = spread_dp(tokens).reshape(TOKENS, -1)
    with jax.named_scope("stats"):
        values = tokens.astype(F32)
        sums = jnp.stack([jnp.sum(values, axis=1), jnp.sum(values * values, axis=1)])
        sums = butterfly(sums, OVER_MP)
        place = lax.axis_index(DP)
        mine = (jnp.arange(64) == place)[None, :, None]
        sums = jnp.where(mine, sums[:, None, :], 0.0).reshape(16, 128)
        sums = butterfly(sums, OVER_DP).reshape(2, TOKENS)
        mean = sums[0] / D
        var = sums[1] / D - mean * mean
        inv = lax.rsqrt(var + 1e-06)
    with jax.named_scope("cot_gather"):
        cot = spread(cotangent, MP, 8).reshape(TOKENS, -1)
    with jax.named_scope("normalize"):
        normed = ((raw.astype(F32) - mean[:, None]) * inv[:, None] * norm_gain[None, :]).astype(BF)
    with jax.named_scope("gram"):
        rows = lax.dynamic_slice_in_dim(normed, place * 16, 16, 0)
        gram = lax.dot_general(rows, normed, (((1,), (1,)), ((), ())), preferred_element_type=F32)
        gram = spread(gram.astype(BF), MP, 8)
        gram = jnp.sum(gram.astype(F32), axis=0).astype(BF)
        gram = spread_dp(gram).reshape(TOKENS, TOKENS)
    with jax.named_scope("project"):
        part = jnp.dot(normed, w_up, preferred_element_type=F32).astype(BF)
        part = lax.all_to_all(part.reshape(8, 128, -1), MP, 0, 0, tiled=True)
        own = jnp.sum(part.astype(F32), axis=0).astype(BF)
        pre = spread(own, MP, 8).reshape(TOKENS, -1).astype(F32)

    def slope_at(value):
        return (cot.astype(F32) * gelu_slope(value) * scale).astype(BF)

    with jax.named_scope("ascent"):
        slope = slope_at(pre)
        along = jnp.dot(gram, slope, preferred_element_type=F32)
        squared = jnp.sum(slope.astype(F32) * along)
        squared = butterfly(squared.reshape(1, 1), OVER_DP)
        size = jnp.sqrt(jnp.maximum(squared, 0.0)) + 1e-12
        radius = 0.5 * math.sqrt(FF)
    with jax.named_scope("sharp"):
        sharp = slope_at(pre + along * (radius / size))
        return lax.dot_general(normed, sharp, (((0,), (0,)), ((), ())), preferred_element_type=F32)


def solution(mesh):
    fine = Mesh(mesh.devices.reshape(4, 8, 2, 2, 4), DP + MP)
    placed = (P(DP, MP), P(MP), P(MP, DP), P(MP, DP))
    return jax.shard_map(
        per_device, mesh=fine, in_specs=placed, out_specs=P(MP, DP), check_vma=False
    )
```

time: 546 us -> 241 us (0.44)
  the two profiles are of different devices: /device:TPU:1 before, /device:TPU:8 now
where the time goes in v1:
time: 241 us; the launch traced here: 239 us
  waiting for transfers between devices  112 us (46%)
  starting transfers between devices  105 us (44%)
  matrix products  6.9 us (3%)
  local copies, waits for them, and re-layouts  6.58 us (3%)
  between operations  4.84 us (2%)
  other arithmetic  4.51 us (2%)
    all_to_all x5, waiting for transfers between devices, spread(): return lax.all_to_all(copies, axes, 0, 0, tiled=True)  69.1 us
    ppermute x17, starting transfers between devices, swap(): return lax.ppermute(value, axis, [(i, i ^ bit) for i in range(size)])  63.5 us
    all_to_all x5, starting transfers between devices, spread(): return lax.all_to_all(copies, axes, 0, 0, tiled=True)  37.6 us
    ppermute x17, waiting for transfers between devices, swap(): return lax.ppermute(value, axis, [(i, i ^ bit) for i in range(size)])  28.5 us
    all_to_all x1, waiting for transfers between devices, per_device(): part = lax.all_to_all(part.reshape(8, 128, -1), MP, 0, 0, tiled=True)  14.3 us
    broadcast_in_dim x5, local copies, waits for them, and re-layouts, spread(): copies = jnp.broadcast_to(value[None], (count,) + value.shape)  5.47 us
  transfers between devices with their start and end apart: 23, of which 19 were waited for; matrix products, arithmetic and copies ran while one was open for 2% of the time, Pallas kernels for 0%

profile of v1, /device:TPU:8, one launch (start us, length us, event | category | flops | bytes accessed | tf_op | source)
XLA Modules:
  0.0 239.4 jit_solution(12669356215296026796)
XLA Ops:
  0.0 1.7 broadcast_in_dim.30
  1.7 14.0 %all-to-all-start = ((bf16[32,16,768]{2,1,0:T(8,128)(2,1)}), bf16[32,16,768]{2,1,0:T(8,128)(2,1)S(1)}, u32[]{:S(2)}, u32[]{:S(2)}) async-start(bf16[32,16,768]{2,1,0:T(8,128)(2,1)} %broadcast_in_dim.30), calls=%async_computation | async-start | bytes 1572864 | tf_op jit(solution)/shard_map/token_gather/all_to_all | solution.py:41
  15.7 0.1 convert_reduce_fusion
  15.9 3.4 %collective-permute-start.1 = (f32[2,16]{1,0:T(2,128)S(1)}, f32[2,16]{1,0:T(2,128)S(1)}, u32[]{:S(2)}, u32[]{:S(2)}) collective-permute-start(f32[2,16]{1,0:T(2,128)S(1)} %pad_maximum_fusion.2), channel_id=1, source_target_pairs={{0,1},{1,0},{2,3},{3,2},{4,5},{5,4},{6,7},{7,6},{8,9},{9,8},{10,11... | collective-permute-start | bytes 392 | tf_op jit(solution)/shard_map/stats/ppermute | solution.py:26
  19.3 2.0 collective-permute-done.1
  21.3 4.9 %collective-permute-start.2 = (f32[2,16]{1,0:T(2,128)S(1)}, f32[2,16]{1,0:T(2,128)S(1)}, u32[]{:S(2)}, u32[]{:S(2)}) collective-permute-start(f32[2,16]{1,0:T(2,128)S(1)} %fusion.38), channel_id=1, source_target_pairs={{0,2},{1,3},{2,0},{3,1},{4,6},{5,7},{6,4},{7,5},{8,10},{9,11},{10,... | collective-permute-start | bytes 392 | tf_op jit(solution)/shard_map/stats/ppermute | solution.py:26
  26.3 2.0 collective-permute-done.2
  28.3 5.0 %collective-permute-start.3 = (f32[2,16]{1,0:T(2,128)S(1)}, f32[2,16]{1,0:T(2,128)S(1)}, u32[]{:S(2)}, u32[]{:S(2)}) collective-permute-start(f32[2,16]{1,0:T(2,128)S(1)} %fusion.47), channel_id=1, source_target_pairs={{0,4},{4,0},{1,5},{5,1},{2,6},{6,2},{3,7},{7,3},{8,12},{12,8},{9,1... | collective-permute-start | bytes 392 | tf_op jit(solution)/shard_map/stats/ppermute | solution.py:26
  33.4 4.0 %all-to-all-done = bf16[32,16,768]{2,1,0:T(8,128)(2,1)S(1)} async-done(((bf16[32,16,768]{2,1,0:T(8,128)(2,1)}), bf16[32,16,768]{2,1,0:T(8,128)(2,1)S(1)}, u32[]{:S(2)}, u32[]{:S(2)}) %all-to-all-start) | async-done | bytes 786464 | tf_op jit(solution)/shard_map/token_gather/all_to_all | solution.py:41
  37.3 1.9 collective-permute-start
  39.3 0.1 broadcast_select_fusion
  39.4 0.1 select_n.39
  39.4 2.4 %collective-permute-start.4 = (f32[16,128]{1,0:T(8,128)S(1)}, f32[16,128]{1,0:T(8,128)S(1)}, u32[]{:S(2)}, u32[]{:S(2)}) collective-permute-start(f32[16,128]{1,0:T(8,128)S(1)} %select_n.39), channel_id=1, source_target_pairs={{0,8},{8,0},{1,9},{9,1},{2,10},{10,2},{3,11},{11,3},{4,12},{12,4},... | collective-permute-start | bytes 24584 | tf_op jit(solution)/shard_map/stats/ppermute | solution.py:26
  41.8 0.8 collective-permute-done.4
  42.7 4.6 %collective-permute-start.5 = (f32[16,128]{1,0:T(8,128)S(1)}, f32[16,128]{1,0:T(8,128)S(1)}, u32[]{:S(2)}, u32[]{:S(2)}) collective-permute-start(f32[16,128]{1,0:T(8,128)S(1)} %add.93), channel_id=1, source_target_pairs={{0,16},{16,0},{32,48},{48,32},{64,80},{80,64},{96,112},{112,96},{1... | collective-permute-start | bytes 24584 | tf_op jit(solution)/shard_map/stats/ppermute | solution.py:26
  47.3 1.6 collective-permute-done.5
  48.9 3.6 %collective-permute-start.6 = (f32[16,128]{1,0:T(8,128)S(1)}, f32[16,128]{1,0:T(8,128)S(1)}, u32[]{:S(2)}, u32[]{:S(2)}) collective-permute-start(f32[16,128]{1,0:T(8,128)S(1)} %add.94), channel_id=1, source_target_pairs={{0,32},{16,48},{32,0},{48,16},{64,96},{80,112},{96,64},{112,80},{1... | collective-permute-start | bytes 24584 | tf_op jit(solution)/shard_map/stats/ppermute | solution.py:26
  52.5 2.9 %collective-permute-done.6 = f32[16,128]{1,0:T(8,128)S(1)} collective-permute-done((f32[16,128]{1,0:T(8,128)S(1)}, f32[16,128]{1,0:T(8,128)S(1)}, u32[]{:S(2)}, u32[]{:S(2)}) %collective-permute-start.6) | collective-permute-done | bytes 8224 | tf_op jit(solution)/shard_map/stats/ppermute | solution.py:26
  55.3 4.8 %collective-permute-start.7 = (f32[16,128]{1,0:T(8,128)S(1)}, f32[16,128]{1,0:T(8,128)S(1)}, u32[]{:S(2)}, u32[]{:S(2)}) collective-permute-start(f32[16,128]{1,0:T(8,128)S(1)} %add.95), channel_id=1, source_target_pairs={{0,64},{16,80},{32,96},{48,112},{64,0},{80,16},{96,32},{112,48},{1... | collective-permute-start | bytes 24584 | tf_op jit(solution)/shard_map/stats/ppermute | solution.py:26
  60.2 4.6 %collective-permute-done.7 = f32[16,128]{1,0:T(8,128)S(1)} collective-permute-done((f32[16,128]{1,0:T(8,128)S(1)}, f32[16,128]{1,0:T(8,128)S(1)}, u32[]{:S(2)}, u32[]{:S(2)}) %collective-permute-start.7) | collective-permute-done | bytes 8224 | tf_op jit(solution)/shard_map/stats/ppermute | solution.py:26
  64.8 2.8 %collective-permute-start.8 = (f32[16,128]{1,0:T(8,128)S(1)}, f32[16,128]{1,0:T(8,128)S(1)}, u32[]{:S(2)}, u32[]{:S(2)}) collective-permute-start(f32[16,128]{1,0:T(8,128)S(1)} %add.96), channel_id=1, source_target_pairs={{0,128},{128,0},{256,384},{384,256},{1,129},{129,1},{257,385},{385... | collective-permute-start | bytes 24584 | tf_op jit(solution)/shard_map/stats/ppermute | solution.py:26
  67.6 2.7 %collective-permute-done.8 = f32[16,128]{1,0:T(8,128)S(1)} collective-permute-done((f32[16,128]{1,0:T(8,128)S(1)}, f32[16,128]{1,0:T(8,128)S(1)}, u32[]{:S(2)}, u32[]{:S(2)}) %collective-permute-start.8) | collective-permute-done | bytes 8224 | tf_op jit(solution)/shard_map/stats/ppermute | solution.py:26
  70.3 3.0 %collective-permute-start.9 = (f32[16,128]{1,0:T(8,128)S(1)}, f32[16,128]{1,0:T(8,128)S(1)}, u32[]{:S(2)}, u32[]{:S(2)}) collective-permute-start(f32[16,128]{1,0:T(8,128)S(1)} %add.97), channel_id=1, source_target_pairs={{0,256},{128,384},{256,0},{384,128},{1,257},{129,385},{257,1},{385... | collective-permute-start | bytes 24584 | tf_op jit(solution)/shard_map/stats/ppermute | solution.py:26
  73.4 1.0 broadcast_in_dim.34
  74.3 6.9 %all-to-all-start.1 = ((bf16[8,128,384]{2,1,0:T(8,128)(2,1)}), bf16[8,128,384]{2,1,0:T(8,128)(2,1)S(1)}, u32[]{:S(2)}, u32[]{:S(2)}) async-start(bf16[8,128,384]{2,1,0:T(8,128)(2,1)} %broadcast_in_dim.34), calls=%async_computation.1 | async-start | bytes 1572864 | tf_op jit(solution)/shard_map/cot_gather/all_to_all | solution.py:41
  81.2 0.1 select_bitcast_fusion.3
  81.4 0.1 pad_maximum_fusion.1
  81.5 0.5 copy-done.5
  82.0 0.5 fusion.2
  82.6 0.5 convolution_convert_fusion.1
  83.1 18.0 %all-to-all-done.1 = bf16[8,128,384]{2,1,0:T(8,128)(2,1)S(1)} async-done(((bf16[8,128,384]{2,1,0:T(8,128)(2,1)}), bf16[8,128,384]{2,1,0:T(8,128)(2,1)S(1)}, u32[]{:S(2)}, u32[]{:S(2)}) %all-to-all-start.1) | async-done | bytes 786464 | tf_op jit(solution)/shard_map/cot_gather/all_to_all | solution.py:41
  101.1 0.7 broadcast_in_dim.36
  101.8 3.4 %all-to-all-start.4 = ((bf16[8,16,1024]{2,1,0:T(8,128)(2,1)}), bf16[8,16,1024]{2,1,0:T(8,128)(2,1)S(1)}, u32[]{:S(2)}, u32[]{:S(2)}) async-start(bf16[8,16,1024]{2,1,0:T(8,128)(2,1)} %broadcast_in_dim.36), calls=%async_computation.4 | async-start | bytes 524288 | tf_op jit(solution)/shard_map/gram/all_to_all | solution.py:41
  105.3 1.9 convolution_convert_fusion
  107.1 9.5 %all-to-all-done.4 = bf16[8,16,1024]{2,1,0:T(8,128)(2,1)S(1)} async-done(((bf16[8,16,1024]{2,1,0:T(8,128)(2,1)}), bf16[8,16,1024]{2,1,0:T(8,128)(2,1)S(1)}, u32[]{:S(2)}, u32[]{:S(2)}) %all-to-all-start.4) | async-done | bytes 262176 | tf_op jit(solution)/shard_map/gram/all_to_all | solution.py:41
  116.7 3.5 %all-to-all-start.2 = ((bf16[8,128,384]{2,1,0:T(8,128)(2,1)}), bf16[8,128,384]{2,1,0:T(8,128)(2,1)S(1)}, u32[]{:S(2)}, u32[]{:S(2)}) async-start(bf16[8,128,384]{2,1,0:T(8,128)(2,1)} %bitcast.63), calls=%async_computation.2 | async-start | bytes 1572864 | tf_op jit(solution)/shard_map/project/all_to_all | solution.py:80
  120.3 14.3 %all-to-all-done.2 = bf16[8,128,384]{2,1,0:T(8,128)(2,1)S(1)} async-done(((bf16[8,128,384]{2,1,0:T(8,128)(2,1)}), bf16[8,128,384]{2,1,0:T(8,128)(2,1)S(1)}, u32[]{:S(2)}, u32[]{:S(2)}) %all-to-all-start.2) | async-done | bytes 786464 | tf_op jit(solution)/shard_map/project/all_to_all | solution.py:80
  134.6 1.1 broadcast_in_dim.37
  135.7 9.4 %all-to-all-start.5 = ((bf16[32,16,1024]{2,1,0:T(8,128)(2,1)}), bf16[32,16,1024]{2,1,0:T(8,128)(2,1)S(1)}, u32[]{:S(2)}, u32[]{:S(2)}) async-start(bf16[32,16,1024]{2,1,0:T(8,128)(2,1)} %broadcast_in_dim.37), calls=%async_computation.5 | async-start | bytes 2097152 | tf_op jit(solution)/shard_map/gram/all_to_all | solution.py:41
  145.1 0.1 reduce_sum.53
  145.2 19.5 %all-to-all-done.5 = bf16[32,16,1024]{2,1,0:T(8,128)(2,1)S(1)} async-done(((bf16[32,16,1024]{2,1,0:T(8,128)(2,1)}), bf16[32,16,1024]{2,1,0:T(8,128)(2,1)S(1)}, u32[]{:S(2)}, u32[]{:S(2)}) %all-to-all-start.5) | async-done | bytes 1048608 | tf_op jit(solution)/shard_map/gram/all_to_all | solution.py:41
  164.7 0.9 broadcast_in_dim.35
  165.7 3.9 %all-to-all-start.3 = ((bf16[8,128,384]{2,1,0:T(8,128)(2,1)}), bf16[8,128,384]{2,1,0:T(8,128)(2,1)S(1)}, u32[]{:S(2)}, u32[]{:S(2)}) async-start(bf16[8,128,384]{2,1,0:T(8,128)(2,1)} %broadcast_in_dim.35), calls=%async_computation.3 | async-start | bytes 1572864 | tf_op jit(solution)/shard_map/project/all_to_all | solution.py:41
  169.6 1.9 collective-permute-start.10
  171.5 18.1 %all-to-all-done.3 = bf16[8,128,384]{2,1,0:T(8,128)(2,1)S(1)} async-done(((bf16[8,128,384]{2,1,0:T(8,128)(2,1)}), bf16[8,128,384]{2,1,0:T(8,128)(2,1)S(1)}, u32[]{:S(2)}, u32[]{:S(2)}) %all-to-all-start.3) | async-done | bytes 786464 | tf_op jit(solution)/shard_map/project/all_to_all | solution.py:41
  189.6 0.8 fusion.9
  190.4 1.4 select_bitcast_fusion.1
  191.8 0.2 pad_maximum_fusion
  192.0 2.5 %multiply_reduce_fusion = (f32[]{:T(128)}, f32[1024,384]{1,0:T(8,128)S(1)}) fusion(bf16[8,128,384]{2,1,0:T(8,128)(2,1)S(1)} %all-to-all-done.3, bf16[8,128,384]{2,1,0:T(8,128)(2,1)S(1)} %all-to-all-done.1, bf16[1024,1024]{1,0:T(8,128)(2,1)S(1)} %bitcast.62, bf16[1024,384]{1,0:T(8,128)(2,1)S(1)} %bitcast.64), kind=kOutput, calls=%fused_computation.39 | convolution fusion | flops 811597824 | bytes 6029316 | tf_op jit(solution)/shard_map/ascent/dot_general | solution.py:89
  194.5 1.9 collective-permute-start.11
  196.4 1.2 collective-permute-done.11
  198.9 6.4 %collective-permute-start.12 = (f32[1,1]{1,0:T(1,128)}, f32[1,1]{1,0:T(1,128)}, u32[]{:S(2)}, u32[]{:S(2)}) collective-permute-start(f32[1,1]{1,0:T(1,128)} %add.106), channel_id=1, source_target_pairs={{0,16},{16,0},{32,48},{48,32},{64,80},{80,64},{96,112},{112,96},{1... | collective-permute-start | bytes 20 | tf_op jit(solution)/shard_map/ascent/ppermute | solution.py:26
  205.3 0.2 collective-permute-done.12
  206.1 4.7 %collective-permute-start.13 = (f32[1,1]{1,0:T(1,128)}, f32[1,1]{1,0:T(1,128)}, u32[]{:S(2)}, u32[]{:S(2)}) collective-permute-start(f32[1,1]{1,0:T(1,128)} %add.107), channel_id=1, source_target_pairs={{0,32},{16,48},{32,0},{48,16},{64,96},{80,112},{96,64},{112,80},{1... | collective-permute-start | bytes 20 | tf_op jit(solution)/shard_map/ascent/ppermute | solution.py:26
  210.8 1.6 collective-permute-done.13
  213.0 5.7 %collective-permute-start.14 = (f32[1,1]{1,0:T(1,128)}, f32[1,1]{1,0:T(1,128)}, u32[]{:S(2)}, u32[]{:S(2)}) collective-permute-start(f32[1,1]{1,0:T(1,128)} %add.108), channel_id=1, source_target_pairs={{0,64},{16,80},{32,96},{48,112},{64,0},{80,16},{96,32},{112,48},{1... | collective-permute-start | bytes 20 | tf_op jit(solution)/shard_map/ascent/ppermute | solution.py:26
  218.8 3.6 %collective-permute-done.14 = f32[1,1]{1,0:T(1,128)} collective-permute-done((f32[1,1]{1,0:T(1,128)}, f32[1,1]{1,0:T(1,128)}, u32[]{:S(2)}, u32[]{:S(2)}) %collective-permute-start.14) | collective-permute-done | bytes 36 | tf_op jit(solution)/shard_map/ascent/ppermute | solution.py:26
  222.9 3.2 %collective-permute-start.15 = (f32[1,1]{1,0:T(1,128)}, f32[1,1]{1,0:T(1,128)}, u32[]{:S(2)}, u32[]{:S(2)}) collective-permute-start(f32[1,1]{1,0:T(1,128)} %add.109), channel_id=1, source_target_pairs={{0,128},{128,0},{256,384},{384,256},{1,129},{129,1},{257,385},{385... | collective-permute-start | bytes 20 | tf_op jit(solution)/shard_map/ascent/ppermute | solution.py:26
  226.1 2.2 collective-permute-done.15
  229.0 3.2 %collective-permute-start.16 = (f32[1,1]{1,0:T(1,128)}, f32[1,1]{1,0:T(1,128)}, u32[]{:S(2)}, u32[]{:S(2)}) collective-permute-start(f32[1,1]{1,0:T(1,128)} %add.110), channel_id=1, source_target_pairs={{0,256},{128,384},{256,0},{384,128},{1,257},{129,385},{257,1},{385... | collective-permute-start | bytes 20 | tf_op jit(solution)/shard_map/ascent/ppermute | solution.py:26
  232.2 3.1 %collective-permute-done.16 = f32[1,1]{1,0:T(1,128)} collective-permute-done((f32[1,1]{1,0:T(1,128)}, f32[1,1]{1,0:T(1,128)}, u32[]{:S(2)}, u32[]{:S(2)}) %collective-permute-start.16) | collective-permute-done | bytes 36 | tf_op jit(solution)/shard_map/ascent/ppermute | solution.py:26
  236.0 0.9 fusion.23
  236.9 0.5 copy-done.2
  237.4 2.0 fusion.39
  (28 shorter events, 0.1 us)
Async XLA Ops:
  0.0 105.3 %copy-start = (bf16[768,384]{1,0:T(8,128)(2,1)S(1)}, bf16[768,384]{1,0:T(8,128)(2,1)}, u32[]{:S(2)}) copy-start(bf16[768,384]{1,0:T(8,128)(2,1)} %param.6) | copy-start | bytes 1769476
  0.0 15.7 %copy-start.3 = (bf16[16,768]{1,0:T(8,128)(2,1)S(1)}, bf16[16,768]{1,0:T(8,128)(2,1)}, u32[]{:S(2)}) copy-start(bf16[16,768]{1,0:T(8,128)(2,1)} %param.4) | copy-start | bytes 73732
  0.0 73.3 %copy-start.4 = (bf16[128,384]{1,0:T(8,128)(2,1)S(1)}, bf16[128,384]{1,0:T(8,128)(2,1)}, u32[]{:S(2)}) copy-start(bf16[128,384]{1,0:T(8,128)(2,1)} %param.7) | copy-start | bytes 294916
  1.7 35.6 %all-to-all-start = ((bf16[32,16,768]{2,1,0:T(8,128)(2,1)}), bf16[32,16,768]{2,1,0:T(8,128)(2,1)S(1)}, u32[]{:S(2)}, u32[]{:S(2)}) async-start(bf16[32,16,768]{2,1,0:T(8,128)(2,1)} %broadcast_in_dim.30), calls=%async_computation | async-start | bytes 1572864 | tf_op jit(solution)/shard_map/token_gather/all_to_all | solution.py:41
  15.9 5.5 %collective-permute-start.1 = (f32[2,16]{1,0:T(2,128)S(1)}, f32[2,16]{1,0:T(2,128)S(1)}, u32[]{:S(2)}, u32[]{:S(2)}) collective-permute-start(f32[2,16]{1,0:T(2,128)S(1)} %pad_maximum_fusion.2), channel_id=1, source_target_pairs={{0,1},{1,0},{2,3},{3,2},{4,5},{5,4},{6,7},{7,6},{8,9},{9,8},{10,11... | collective-permute-start | bytes 392 | tf_op jit(solution)/shard_map/stats/ppermute | solution.py:26
  21.3 7.0 %collective-permute-start.2 = (f32[2,16]{1,0:T(2,128)S(1)}, f32[2,16]{1,0:T(2,128)S(1)}, u32[]{:S(2)}, u32[]{:S(2)}) collective-permute-start(f32[2,16]{1,0:T(2,128)S(1)} %fusion.38), channel_id=1, source_target_pairs={{0,2},{1,3},{2,0},{3,1},{4,6},{5,7},{6,4},{7,5},{8,10},{9,11},{10,... | collective-permute-start | bytes 392 | tf_op jit(solution)/shard_map/stats/ppermute | solution.py:26
  28.3 10.9 %collective-permute-start.3 = (f32[2,16]{1,0:T(2,128)S(1)}, f32[2,16]{1,0:T(2,128)S(1)}, u32[]{:S(2)}, u32[]{:S(2)}) collective-permute-start(f32[2,16]{1,0:T(2,128)S(1)} %fusion.47), channel_id=1, source_target_pairs={{0,4},{4,0},{1,5},{5,1},{2,6},{6,2},{3,7},{7,3},{8,12},{12,8},{9,1... | collective-permute-start | bytes 392 | tf_op jit(solution)/shard_map/stats/ppermute | solution.py:26
  37.3 43.9 %collective-permute-start = (bf16[32,16,768]{2,1,0:T(8,128)(2,1)S(1)}, bf16[32,16,768]{2,1,0:T(8,128)(2,1)S(1)}, u32[]{:S(2)}, u32[]{:S(2)}) collective-permute-start(bf16[32,16,768]{2,1,0:T(8,128)(2,1)S(1)} %all-to-all-done), channel_id=1, source_target_pairs={{0,8},{8,0},{1,9},{9,1},{2,10},{10,2},{3,11},{11,3},{4,12},{12,4},... | collective-permute-start | bytes 2359304 | tf_op jit(solution)/shard_map/token_gather/ppermute | solution.py:26
  39.4 3.2 %collective-permute-start.4 = (f32[16,128]{1,0:T(8,128)S(1)}, f32[16,128]{1,0:T(8,128)S(1)}, u32[]{:S(2)}, u32[]{:S(2)}) collective-permute-start(f32[16,128]{1,0:T(8,128)S(1)} %select_n.39), channel_id=1, source_target_pairs={{0,8},{8,0},{1,9},{9,1},{2,10},{10,2},{3,11},{11,3},{4,12},{12,4},... | collective-permute-start | bytes 24584 | tf_op jit(solution)/shard_map/stats/ppermute | solution.py:26
  42.7 6.2 %collective-permute-start.5 = (f32[16,128]{1,0:T(8,128)S(1)}, f32[16,128]{1,0:T(8,128)S(1)}, u32[]{:S(2)}, u32[]{:S(2)}) collective-permute-start(f32[16,128]{1,0:T(8,128)S(1)} %add.93), channel_id=1, source_target_pairs={{0,16},{16,0},{32,48},{48,32},{64,80},{80,64},{96,112},{112,96},{1... | collective-permute-start | bytes 24584 | tf_op jit(solution)/shard_map/stats/ppermute | solution.py:26
  48.9 6.4 %collective-permute-start.6 = (f32[16,128]{1,0:T(8,128)S(1)}, f32[16,128]{1,0:T(8,128)S(1)}, u32[]{:S(2)}, u32[]{:S(2)}) collective-permute-start(f32[16,128]{1,0:T(8,128)S(1)} %add.94), channel_id=1, source_target_pairs={{0,32},{16,48},{32,0},{48,16},{64,96},{80,112},{96,64},{112,80},{1... | collective-permute-start | bytes 24584 | tf_op jit(solution)/shard_map/stats/ppermute | solution.py:26
  55.3 9.4 %collective-permute-start.7 = (f32[16,128]{1,0:T(8,128)S(1)}, f32[16,128]{1,0:T(8,128)S(1)}, u32[]{:S(2)}, u32[]{:S(2)}) collective-permute-start(f32[16,128]{1,0:T(8,128)S(1)} %add.95), channel_id=1, source_target_pairs={{0,64},{16,80},{32,96},{48,112},{64,0},{80,16},{96,32},{112,48},{1... | collective-permute-start | bytes 24584 | tf_op jit(solution)/shard_map/stats/ppermute | solution.py:26
  64.8 5.5 %collective-permute-start.8 = (f32[16,128]{1,0:T(8,128)S(1)}, f32[16,128]{1,0:T(8,128)S(1)}, u32[]{:S(2)}, u32[]{:S(2)}) collective-permute-start(f32[16,128]{1,0:T(8,128)S(1)} %add.96), channel_id=1, source_target_pairs={{0,128},{128,0},{256,384},{384,256},{1,129},{129,1},{257,385},{385... | collective-permute-start | bytes 24584 | tf_op jit(solution)/shard_map/stats/ppermute | solution.py:26
  70.3 10.9 %collective-permute-start.9 = (f32[16,128]{1,0:T(8,128)S(1)}, f32[16,128]{1,0:T(8,128)S(1)}, u32[]{:S(2)}, u32[]{:S(2)}) collective-permute-start(f32[16,128]{1,0:T(8,128)S(1)} %add.97), channel_id=1, source_target_pairs={{0,256},{128,384},{256,0},{384,128},{1,257},{129,385},{257,1},{385... | collective-permute-start | bytes 24584 | tf_op jit(solution)/shard_map/stats/ppermute | solution.py:26
  74.3 26.8 %all-to-all-start.1 = ((bf16[8,128,384]{2,1,0:T(8,128)(2,1)}), bf16[8,128,384]{2,1,0:T(8,128)(2,1)S(1)}, u32[]{:S(2)}, u32[]{:S(2)}) async-start(bf16[8,128,384]{2,1,0:T(8,128)(2,1)} %broadcast_in_dim.34), calls=%async_computation.1 | async-start | bytes 1572864 | tf_op jit(solution)/shard_map/cot_gather/all_to_all | solution.py:41
  81.4 0.7 copy-start.5
  82.6 24.5 %copy-start.1 = (bf16[1024,768]{1,0:T(8,128)(2,1)}, bf16[1024,768]{1,0:T(8,128)(2,1)S(1)}, u32[]{:S(2)}) copy-start(bf16[1024,768]{1,0:T(8,128)(2,1)S(1)} %fusion.2) | copy-start | bytes 4718596
  101.8 14.8 %all-to-all-start.4 = ((bf16[8,16,1024]{2,1,0:T(8,128)(2,1)}), bf16[8,16,1024]{2,1,0:T(8,128)(2,1)S(1)}, u32[]{:S(2)}, u32[]{:S(2)}) async-start(bf16[8,16,1024]{2,1,0:T(8,128)(2,1)} %broadcast_in_dim.36), calls=%async_computation.4 | async-start | bytes 524288 | tf_op jit(solution)/shard_map/gram/all_to_all | solution.py:41
  116.7 17.9 %all-to-all-start.2 = ((bf16[8,128,384]{2,1,0:T(8,128)(2,1)}), bf16[8,128,384]{2,1,0:T(8,128)(2,1)S(1)}, u32[]{:S(2)}, u32[]{:S(2)}) async-start(bf16[8,128,384]{2,1,0:T(8,128)(2,1)} %bitcast.63), calls=%async_computation.2 | async-start | bytes 1572864 | tf_op jit(solution)/shard_map/project/all_to_all | solution.py:80
  135.7 29.0 %all-to-all-start.5 = ((bf16[32,16,1024]{2,1,0:T(8,128)(2,1)}), bf16[32,16,1024]{2,1,0:T(8,128)(2,1)S(1)}, u32[]{:S(2)}, u32[]{:S(2)}) async-start(bf16[32,16,1024]{2,1,0:T(8,128)(2,1)} %broadcast_in_dim.37), calls=%async_computation.5 | async-start | bytes 2097152 | tf_op jit(solution)/shard_map/gram/all_to_all | solution.py:41
  165.7 23.9 %all-to-all-start.3 = ((bf16[8,128,384]{2,1,0:T(8,128)(2,1)}), bf16[8,128,384]{2,1,0:T(8,128)(2,1)S(1)}, u32[]{:S(2)}, u32[]{:S(2)}) async-start(bf16[8,128,384]{2,1,0:T(8,128)(2,1)} %broadcast_in_dim.35), calls=%async_computation.3 | async-start | bytes 1572864 | tf_op jit(solution)/shard_map/project/all_to_all | solution.py:41
  169.6 20.8 %collective-permute-start.10 = (bf16[32,16,1024]{2,1,0:T(8,128)(2,1)S(1)}, bf16[32,16,1024]{2,1,0:T(8,128)(2,1)}, u32[]{:S(2)}, u32[]{:S(2)}) collective-permute-start(bf16[32,16,1024]{2,1,0:T(8,128)(2,1)S(1)} %all-to-all-done.5), channel_id=1, source_target_pairs={{0,8},{8,0},{1,9},{9,1},{2,10},{10,2},{3,11},{11,3},{4,12},{12,4},... | collective-permute-start | bytes 3145736 | tf_op jit(solution)/shard_map/gram/ppermute | solution.py:26
  194.5 3.1 %collective-permute-start.11 = (f32[1,1]{1,0:T(1,128)}, f32[1,1]{1,0:T(1,128)}, u32[]{:S(2)}, u32[]{:S(2)}) collective-permute-start(f32[1,1]{1,0:T(1,128)} %bitcast.16), channel_id=1, source_target_pairs={{0,8},{8,0},{1,9},{9,1},{2,10},{10,2},{3,11},{11,3},{4,12},{12,4},... | collective-permute-start | bytes 20 | tf_op jit(solution)/shard_map/ascent/ppermute | solution.py:26
  198.9 6.6 %collective-permute-start.12 = (f32[1,1]{1,0:T(1,128)}, f32[1,1]{1,0:T(1,128)}, u32[]{:S(2)}, u32[]{:S(2)}) collective-permute-start(f32[1,1]{1,0:T(1,128)} %add.106), channel_id=1, source_target_pairs={{0,16},{16,0},{32,48},{48,32},{64,80},{80,64},{96,112},{112,96},{1... | collective-permute-start | bytes 20 | tf_op jit(solution)/shard_map/ascent/ppermute | solution.py:26
  206.1 6.3 %collective-permute-start.13 = (f32[1,1]{1,0:T(1,128)}, f32[1,1]{1,0:T(1,128)}, u32[]{:S(2)}, u32[]{:S(2)}) collective-permute-start(f32[1,1]{1,0:T(1,128)} %add.107), channel_id=1, source_target_pairs={{0,32},{16,48},{32,0},{48,16},{64,96},{80,112},{96,64},{112,80},{1... | collective-permute-start | bytes 20 | tf_op jit(solution)/shard_map/ascent/ppermute | solution.py:26
  213.0 9.3 %collective-permute-start.14 = (f32[1,1]{1,0:T(1,128)}, f32[1,1]{1,0:T(1,128)}, u32[]{:S(2)}, u32[]{:S(2)}) collective-permute-start(f32[1,1]{1,0:T(1,128)} %add.108), channel_id=1, source_target_pairs={{0,64},{16,80},{32,96},{48,112},{64,0},{80,16},{96,32},{112,48},{1... | collective-permute-start | bytes 20 | tf_op jit(solution)/shard_map/ascent/ppermute | solution.py:26
  222.9 5.4 %collective-permute-start.15 = (f32[1,1]{1,0:T(1,128)}, f32[1,1]{1,0:T(1,128)}, u32[]{:S(2)}, u32[]{:S(2)}) collective-permute-start(f32[1,1]{1,0:T(1,128)} %add.109), channel_id=1, source_target_pairs={{0,128},{128,0},{256,384},{384,256},{1,129},{129,1},{257,385},{385... | collective-permute-start | bytes 20 | tf_op jit(solution)/shard_map/ascent/ppermute | solution.py:26
  229.0 6.3 %collective-permute-start.16 = (f32[1,1]{1,0:T(1,128)}, f32[1,1]{1,0:T(1,128)}, u32[]{:S(2)}, u32[]{:S(2)}) collective-permute-start(f32[1,1]{1,0:T(1,128)} %add.110), channel_id=1, source_target_pairs={{0,256},{128,384},{256,0},{384,128},{1,257},{129,385},{257,1},{385... | collective-permute-start | bytes 20 | tf_op jit(solution)/shard_map/ascent/ppermute | solution.py:26
  236.0 1.4 copy-start.2

commit v2 on v1

v2 whole, which is shorter than its diff:
```python
import math

import jax
import jax.numpy as jnp
from jax import lax
from jax.sharding import Mesh
from jax.sharding import PartitionSpec as P

FF = 24576
D = 6144
TOKENS = 1024
DP = ("yl", "z", "c")
MP = ("yh", "x")
BF = jnp.bfloat16
F32 = jnp.float32


def gelu_slope(value):
    cdf = 0.5 * (1.0 + lax.erf(value * (1.0 / math.sqrt(2.0))))
    dens = jnp.exp(-0.5 * value * value) * (1.0 / math.sqrt(2.0 * math.pi))
    return cdf + value * dens


def swap(value, axis, bit):
    size = lax.axis_size(axis)
    return lax.ppermute(value, axis, [(i, i ^ bit) for i in range(size)])


def spread(value, axes, count):
    copies = jnp.broadcast_to(value[None], (count,) + value.shape)
    return lax.all_to_all(copies, axes, 0, 0, tiled=True)


def spread_dp(value):
    mine = spread(value, ("yl", "z"), 32)
    other = swap(mine, "c", 1)
    core = lax.axis_index("c")
    first = jnp.where(core == 0, mine, other)
    second = jnp.where(core == 0, other, mine)
    return jnp.stack([first, second], axis=1)


def ordered(blocks, index):
    odd, high = (index & 1) == 1, (index & 2) == 2
    near = [jnp.where(odd, blocks[q ^ 1], blocks[q]) for q in range(4)]
    return [jnp.where(high, near[q ^ 2], near[q]) for q in range(4)]


def gather_x(value):
    x = lax.axis_index("x")
    blocks = [value] + [swap(value, "x", b) for b in (1, 2, 3)]
    return ordered(blocks, x)


def pair_y(value):
    other = swap(value, "yh", 1)
    low = lax.axis_index("yh") == 0
    return jnp.stack([jnp.where(low, value, other), jnp.where(low, other, value)])


def per_device(tokens, norm_gain, w_up, cotangent):
    scale = 1.0 / math.sqrt(TOKENS)
    columns = w_up.shape[1]
    x = lax.axis_index("x")
    with jax.named_scope("stats"):
        values = tokens.astype(F32)
        sums = jnp.stack([jnp.sum(values, axis=1), jnp.sum(values * values, axis=1)])
        for axis, bit in (("x", 1), ("x", 2), ("yh", 1)):
            sums = sums + swap(sums, axis, bit)
        mean = sums[0] / D
        var = sums[1] / D - mean * mean
        inv = lax.rsqrt(var + 1e-06)
        rows = ((values - mean[:, None]) * inv[:, None] * norm_gain[None, :]).astype(BF)
    with jax.named_scope("token_gather"):
        normed = spread_dp(rows).reshape(TOKENS, -1)
    with jax.named_scope("cot_gather"):
        cot = jnp.stack(gather_x(pair_y(cotangent)), axis=1).reshape(TOKENS, columns)
    with jax.named_scope("gram"):
        gram = lax.dot_general(rows, normed, (((1,), (1,)), ((), ())), preferred_element_type=F32)
        gram = spread(gram.astype(BF), MP, 8)
        gram = jnp.sum(gram.astype(F32), axis=0).astype(BF)
        gram = spread_dp(gram).reshape(TOKENS, TOKENS)
    with jax.named_scope("project"):
        part = jnp.dot(normed, w_up, preferred_element_type=F32).astype(BF)
        part = part.reshape(4, 256, columns)

        def block(b):
            return lax.dynamic_index_in_dim(part, x ^ b, 0, keepdims=False)

        total = block(0).astype(F32)
        for b in (1, 2, 3):
            total = total + swap(block(b), "x", b).astype(F32)
        half = total.astype(BF)
        both = (half.astype(F32) + swap(half, "yh", 1).astype(F32)).astype(BF)
        pre = jnp.concatenate(gather_x(both), axis=0).astype(F32)

    def slope_at(value):
        return (cot.astype(F32) * gelu_slope(value) * scale).astype(BF)

    with jax.named_scope("ascent"):
        slope = slope_at(pre)
        along = jnp.dot(gram, slope, preferred_element_type=F32)
        squared = jnp.sum(slope.astype(F32) * along)
        squared = jnp.sum(spread(jnp.full((1, 128), squared), DP, 64)[:, 0, 0])
        size = jnp.sqrt(jnp.maximum(squared, 0.0)) + 1e-12
        radius = 0.5 * math.sqrt(FF)
    with jax.named_scope("sharp"):
        sharp = slope_at(pre + along * (radius / size))
        return lax.dot_general(normed, sharp, (((0,), (0,)), ((), ())), preferred_element_type=F32)


def solution(mesh):
    fine = Mesh(mesh.devices.reshape(4, 8, 2, 2, 4), DP + MP)
    placed = (P(DP, MP), P(MP), P(MP, DP), P(MP, DP))
    return jax.shard_map(
        per_device, mesh=fine, in_specs=placed, out_specs=P(MP, DP), check_vma=False
    )
```

time: 241 us -> 180 us (0.75)
  the two profiles are of different devices: /device:TPU:8 before, /device:TPU:1 now
where the time goes in v2:
time: 180 us; the launch traced here: 179 us
  starting transfers between devices  70.9 us (39%)
  blocking collectives  65 us (36%)
  waiting for transfers between devices  17.7 us (10%)
  other arithmetic  12.4 us (7%)
  matrix products  7.77 us (4%)
  local copies, waits for them, and re-layouts  3.63 us (2%)
    all_to_all x3, blocking collectives, spread(): return lax.all_to_all(copies, axes, 0, 0, tiled=True)  65 us
    ppermute x16, starting transfers between devices, swap(): return lax.ppermute(value, axis, [(i, i ^ bit) for i in range(size)])  63 us
    ppermute x16, waiting for transfers between devices, swap(): return lax.ppermute(value, axis, [(i, i ^ bit) for i in range(size)])  14.1 us
    all_to_all x1, starting transfers between devices, spread(): return lax.all_to_all(copies, axes, 0, 0, tiled=True)  7.87 us
    dot_general x1, matrix products, per_device(): along = jnp.dot(gram, slope, preferred_element_type=F32)  4.26 us
    convert_element_type x2, other arithmetic, slope_at(): return (cot.astype(F32) * gelu_slope(value) * scale).astype(BF)  3.75 us
  transfers between devices with their start and end apart: 17, of which 8 were waited for; matrix products, arithmetic and copies ran while one was open for 5% of the time, Pallas kernels for 0%

profile of v2, /device:TPU:1, one launch (start us, length us, event | category | flops | bytes accessed | tf_op | source)
XLA Modules:
  0.0 178.7 jit_solution(2468462385212155374)
XLA Ops:
  0.0 0.9 convert_reduce_fusion
  0.9 3.9 %collective-permute-start = (f32[2,16]{1,0:T(2,128)S(1)}, f32[2,16]{1,0:T(2,128)S(1)}, u32[]{:S(2)}, u32[]{:S(2)}) collective-permute-start(f32[2,16]{1,0:T(2,128)S(1)} %pad_maximum_fusion.4), channel_id=1, source_target_pairs={{0,1},{1,0},{2,3},{3,2},{4,5},{5,4},{6,7},{7,6},{8,9},{9,8},{10,11... | collective-permute-start | bytes 392 | tf_op jit(solution)/shard_map/stats/ppermute | solution.py:26
  4.9 0.9 collective-permute-done
  5.8 4.9 %collective-permute-start.1 = (f32[2,16]{1,0:T(2,128)S(1)}, f32[2,16]{1,0:T(2,128)S(1)}, u32[]{:S(2)}, u32[]{:S(2)}) collective-permute-start(f32[2,16]{1,0:T(2,128)S(1)} %fusion.30), channel_id=1, source_target_pairs={{0,2},{1,3},{2,0},{3,1},{4,6},{5,7},{6,4},{7,5},{8,10},{9,11},{10,... | collective-permute-start | bytes 392 | tf_op jit(solution)/shard_map/stats/ppermute | solution.py:26
  10.7 0.9 collective-permute-done.1
  11.7 7.7 %collective-permute-start.2 = (f32[2,16]{1,0:T(2,128)S(1)}, f32[2,16]{1,0:T(2,128)S(1)}, u32[]{:S(2)}, u32[]{:S(2)}) collective-permute-start(f32[2,16]{1,0:T(2,128)S(1)} %fusion.40), channel_id=1, source_target_pairs={{0,4},{4,0},{1,5},{5,1},{2,6},{6,2},{3,7},{7,3},{8,12},{12,8},{9,1... | collective-permute-start | bytes 392 | tf_op jit(solution)/shard_map/stats/ppermute | solution.py:26
  19.4 0.9 collective-permute-done.2
  20.3 0.8 fusion.27
  21.2 0.1 broadcast_in_dim.8
  21.2 32.0 %all_to_all.20 = bf16[32,16,768]{2,1,0:T(8,128)(2,1)S(1)} all-to-all(bf16[32,16,768]{2,1,0:T(8,128)(2,1)S(1)} %broadcast_in_dim.8), channel_id=1, replica_groups=mesh['yl'=4,'z'=8,'c'=2,'yh'=2,'x'=4] {'yl','z'}, dimensions={0} | all-to-all | bytes 1572864 | tf_op jit(solution)/shard_map/token_gather/all_to_all | solution.py:31
  53.2 6.1 %collective-permute-start.3 = (bf16[32,16,768]{2,1,0:T(8,128)(2,1)S(1)}, bf16[32,16,768]{2,1,0:T(8,128)(2,1)S(1)}, u32[]{:S(2)}, u32[]{:S(2)}) collective-permute-start(bf16[32,16,768]{2,1,0:T(8,128)(2,1)S(1)} %all_to_all.20), channel_id=1, source_target_pairs={{0,8},{8,0},{1,9},{9,1},{2,10},{10,2},{3,11},{11,3},{4,12},{12,4},... | collective-permute-start | bytes 2359304 | tf_op jit(solution)/shard_map/token_gather/ppermute | solution.py:26
  59.3 1.9 %collective-permute-done.3 = bf16[32,16,768]{2,1,0:T(8,128)(2,1)S(1)} collective-permute-done((bf16[32,16,768]{2,1,0:T(8,128)(2,1)S(1)}, bf16[32,16,768]{2,1,0:T(8,128)(2,1)S(1)}, u32[]{:S(2)}, u32[]{:S(2)}) %collective-permute-start.3) | collective-permute-done | bytes 786464 | tf_op jit(solution)/shard_map/token_gather/ppermute | solution.py:26
  61.2 0.1 select_bitcast_fusion.3
  61.3 0.2 pad_maximum_fusion.1
  61.5 0.5 convolution_convert_fusion.1
  62.0 16.4 %all_to_all.21 = bf16[8,16,1024]{2,1,0:T(8,128)(2,1)S(1)} all-to-all(bf16[8,16,1024]{2,1,0:T(8,128)(2,1)S(1)} %broadcast_in_dim.9), channel_id=1, replica_groups=mesh['yl'=4,'z'=8,'c'=2,'yh'=2,'x'=4] {'yh','x'}, dimensions={0} | all-to-all | bytes 524288 | tf_op jit(solution)/shard_map/gram/all_to_all | solution.py:31
  78.5 1.1 broadcast_in_dim.10
  79.6 7.9 %all-to-all-start.2 = ((bf16[32,16,1024]{2,1,0:T(8,128)(2,1)}), bf16[32,16,1024]{2,1,0:T(8,128)(2,1)S(1)}, u32[]{:S(2)}, u32[]{:S(2)}) async-start(bf16[32,16,1024]{2,1,0:T(8,128)(2,1)} %broadcast_in_dim.10), calls=%async_computation.2 | async-start | bytes 2097152 | tf_op jit(solution)/shard_map/gram/all_to_all | solution.py:31
  87.5 0.0 copy-start.10
  87.5 1.0 convolution_convert_fusion
  88.5 0.9 copy-done.9
  89.4 0.8 dynamic-slice_bitcast_fusion.2
  90.2 1.9 %collective-permute-start.8 = (bf16[256,384]{1,0:T(8,128)(2,1)}, bf16[256,384]{1,0:T(8,128)(2,1)}, u32[]{:S(2)}, u32[]{:S(2)}) collective-permute-start(bf16[256,384]{1,0:T(8,128)(2,1)} %get-tuple-element.19), channel_id=1, source_target_pairs={{0,1},{1,0},{2,3},{3,2},{4,5},{5,4},{6,7},{7,6},{8,9},{9,8},{10,11... | collective-permute-start | bytes 589832 | tf_op jit(solution)/shard_map/project/ppermute | solution.py:26
  92.1 3.5 %collective-permute-start.10 = (bf16[256,384]{1,0:T(8,128)(2,1)}, bf16[256,384]{1,0:T(8,128)(2,1)}, u32[]{:S(2)}, u32[]{:S(2)}) collective-permute-start(bf16[256,384]{1,0:T(8,128)(2,1)} %get-tuple-element.20), channel_id=1, source_target_pairs={{0,3},{1,2},{2,1},{3,0},{4,7},{5,6},{6,5},{7,4},{8,11},{9,10},{10,... | collective-permute-start | bytes 589832 | tf_op jit(solution)/shard_map/project/ppermute | solution.py:26
  95.6 3.6 %collective-permute-start.9 = (bf16[256,384]{1,0:T(8,128)(2,1)S(1)}, bf16[256,384]{1,0:T(8,128)(2,1)}, u32[]{:S(2)}, u32[]{:S(2)}) collective-permute-start(bf16[256,384]{1,0:T(8,128)(2,1)S(1)} %get-tuple-element.21), channel_id=1, source_target_pairs={{0,2},{1,3},{2,0},{3,1},{4,6},{5,7},{6,4},{7,5},{8,10},{9,11},{10,... | collective-permute-start | bytes 589832 | tf_op jit(solution)/shard_map/project/ppermute | solution.py:26
  99.2 2.2 %collective-permute-start.4 = (bf16[128,384]{1,0:T(8,128)(2,1)S(1)}, bf16[128,384]{1,0:T(8,128)(2,1)}, u32[]{:S(2)}, u32[]{:S(2)}) collective-permute-start(bf16[128,384]{1,0:T(8,128)(2,1)S(1)} %copy-done.10), channel_id=1, source_target_pairs={{0,4},{4,0},{1,5},{5,1},{2,6},{6,2},{3,7},{7,3},{8,12},{12,8},{9,1... | collective-permute-start | bytes 294920 | tf_op jit(solution)/shard_map/cot_gather/ppermute | solution.py:26
  101.4 0.0 collective-permute-done.8
  101.4 0.0 collective-permute-done.10
  101.4 2.4 %collective-permute-done.9 = bf16[256,384]{1,0:T(8,128)(2,1)} collective-permute-done((bf16[256,384]{1,0:T(8,128)(2,1)S(1)}, bf16[256,384]{1,0:T(8,128)(2,1)}, u32[]{:S(2)}, u32[]{:S(2)}) %collective-permute-start.9) | collective-permute-done | bytes 196640 | tf_op jit(solution)/shard_map/project/ppermute | solution.py:26
  103.8 1.3 fusion.23
  105.2 4.6 %collective-permute-start.11 = (bf16[256,384]{1,0:T(8,128)(2,1)S(1)}, bf16[256,384]{1,0:T(8,128)(2,1)}, u32[]{:S(2)}, u32[]{:S(2)}) collective-permute-start(bf16[256,384]{1,0:T(8,128)(2,1)S(1)} %fusion.23), channel_id=1, source_target_pairs={{0,4},{4,0},{1,5},{5,1},{2,6},{6,2},{3,7},{7,3},{8,12},{12,8},{9,1... | collective-permute-start | bytes 589832 | tf_op jit(solution)/shard_map/project/ppermute | solution.py:26
  109.8 0.0 collective-permute-done.4
  109.8 1.0 select_bitcast_fusion.9
  110.8 0.7 pad_maximum_fusion.3
  111.5 1.9 %collective-permute-start.7 = (bf16[2,128,384]{2,1,0:T(8,128)(2,1)}, bf16[2,128,384]{2,1,0:T(8,128)(2,1)}, u32[]{:S(2)}, u32[]{:S(2)}) collective-permute-start(bf16[2,128,384]{2,1,0:T(8,128)(2,1)} %pad_maximum_fusion.3), channel_id=1, source_target_pairs={{0,1},{1,0},{2,3},{3,2},{4,5},{5,4},{6,7},{7,6},{8,9},{9,8},{10,11... | collective-permute-start | bytes 589832 | tf_op jit(solution)/shard_map/cot_gather/ppermute | solution.py:26
  113.4 4.1 %collective-permute-start.6 = (bf16[2,128,384]{2,1,0:T(8,128)(2,1)}, bf16[2,128,384]{2,1,0:T(8,128)(2,1)}, u32[]{:S(2)}, u32[]{:S(2)}) collective-permute-start(bf16[2,128,384]{2,1,0:T(8,128)(2,1)} %pad_maximum_fusion.3), channel_id=1, source_target_pairs={{0,2},{1,3},{2,0},{3,1},{4,6},{5,7},{6,4},{7,5},{8,10},{9,11},{10,... | collective-permute-start | bytes 589832 | tf_op jit(solution)/shard_map/cot_gather/ppermute | solution.py:26
  117.5 3.6 %collective-permute-start.5 = (bf16[2,128,384]{2,1,0:T(8,128)(2,1)}, bf16[2,128,384]{2,1,0:T(8,128)(2,1)}, u32[]{:S(2)}, u32[]{:S(2)}) collective-permute-start(bf16[2,128,384]{2,1,0:T(8,128)(2,1)} %pad_maximum_fusion.3), channel_id=1, source_target_pairs={{0,3},{1,2},{2,1},{3,0},{4,7},{5,6},{6,5},{7,4},{8,11},{9,10},{10,... | collective-permute-start | bytes 589832 | tf_op jit(solution)/shard_map/cot_gather/ppermute | solution.py:26
  121.1 3.6 %all-to-all-done.2 = bf16[32,16,1024]{2,1,0:T(8,128)(2,1)S(1)} async-done(((bf16[32,16,1024]{2,1,0:T(8,128)(2,1)}), bf16[32,16,1024]{2,1,0:T(8,128)(2,1)S(1)}, u32[]{:S(2)}, u32[]{:S(2)}) %all-to-all-start.2) | async-done | bytes 1048608 | tf_op jit(solution)/shard_map/gram/all_to_all | solution.py:31
  124.7 5.5 %collective-permute-start.15 = (bf16[32,16,1024]{2,1,0:T(8,128)(2,1)S(1)}, bf16[32,16,1024]{2,1,0:T(8,128)(2,1)S(1)}, u32[]{:S(2)}, u32[]{:S(2)}) collective-permute-start(bf16[32,16,1024]{2,1,0:T(8,128)(2,1)S(1)} %all-to-all-done.2), channel_id=1, source_target_pairs={{0,8},{8,0},{1,9},{9,1},{2,10},{10,2},{3,11},{11,3},{4,12},{12,4},... | collective-permute-start | bytes 3145736 | tf_op jit(solution)/shard_map/gram/ppermute | solution.py:26
  130.2 0.0 collective-permute-done.11
  130.2 1.0 add_convert_fusion
  131.2 1.9 %collective-permute-start.14 = (bf16[256,384]{1,0:T(8,128)(2,1)S(1)}, bf16[256,384]{1,0:T(8,128)(2,1)S(1)}, u32[]{:S(2)}, u32[]{:S(2)}) collective-permute-start(bf16[256,384]{1,0:T(8,128)(2,1)S(1)} %add_convert_fusion), channel_id=1, source_target_pairs={{0,1},{1,0},{2,3},{3,2},{4,5},{5,4},{6,7},{7,6},{8,9},{9,8},{10,11... | collective-permute-start | bytes 589832 | tf_op jit(solution)/shard_map/project/ppermute | solution.py:26
  133.1 0.0 collective-permute-done.7
  133.1 4.2 %collective-permute-start.13 = (bf16[256,384]{1,0:T(8,128)(2,1)S(1)}, bf16[256,384]{1,0:T(8,128)(2,1)S(1)}, u32[]{:S(2)}, u32[]{:S(2)}) collective-permute-start(bf16[256,384]{1,0:T(8,128)(2,1)S(1)} %add_convert_fusion), channel_id=1, source_target_pairs={{0,2},{1,3},{2,0},{3,1},{4,6},{5,7},{6,4},{7,5},{8,10},{9,11},{10,... | collective-permute-start | bytes 589832 | tf_op jit(solution)/shard_map/project/ppermute | solution.py:26
  137.3 0.0 collective-permute-done.6
  137.3 3.5 %collective-permute-start.12 = (bf16[256,384]{1,0:T(8,128)(2,1)S(1)}, bf16[256,384]{1,0:T(8,128)(2,1)S(1)}, u32[]{:S(2)}, u32[]{:S(2)}) collective-permute-start(bf16[256,384]{1,0:T(8,128)(2,1)S(1)} %add_convert_fusion), channel_id=1, source_target_pairs={{0,3},{1,2},{2,1},{3,0},{4,7},{5,6},{6,5},{7,4},{8,11},{9,10},{10,... | collective-permute-start | bytes 589832 | tf_op jit(solution)/shard_map/project/ppermute | solution.py:26
  140.8 0.0 collective-permute-done.5
  140.8 1.3 select_bitcast_fusion.7
  142.2 0.0 collective-permute-done.14
  142.2 2.4 %collective-permute-done.13 = bf16[256,384]{1,0:T(8,128)(2,1)S(1)} collective-permute-done((bf16[256,384]{1,0:T(8,128)(2,1)S(1)}, bf16[256,384]{1,0:T(8,128)(2,1)S(1)}, u32[]{:S(2)}, u32[]{:S(2)}) %collective-permute-start.13) | collective-permute-done | bytes 196640 | tf_op jit(solution)/shard_map/project/ppermute | solution.py:26
  144.6 4.5 %collective-permute-done.12 = bf16[256,384]{1,0:T(8,128)(2,1)S(1)} collective-permute-done((bf16[256,384]{1,0:T(8,128)(2,1)S(1)}, bf16[256,384]{1,0:T(8,128)(2,1)S(1)}, u32[]{:S(2)}, u32[]{:S(2)}) %collective-permute-start.12) | collective-permute-done | bytes 196640 | tf_op jit(solution)/shard_map/project/ppermute | solution.py:26
  149.1 0.1 broadcast_select_fusion.7
  149.3 0.0 copy-start.7
  149.3 0.1 maximum_convert_fusion
  149.4 0.8 fusion.6
  150.2 0.0 collective-permute-done.15
  150.2 0.1 select_bitcast_fusion.1
  150.4 0.2 pad_maximum_fusion
  150.7 4.3 %multiply_reduce_fusion = (f32[]{:T(128)}, f32[1024,384]{1,0:T(8,128)}) fusion(bf16[256,384]{1,0:T(8,128)(2,1)S(1)} %get-tuple-element.18, bf16[256,384]{1,0:T(8,128)(2,1)S(1)} %get-tuple-element.17, bf16[256,384]{1,0:T(8,128)(2,1)S(1)} %get-tuple-element.16, bf16[256,384]{1,0:T(8,128)(2,1)S(1)} %get-tuple-element.15, ...), kind=kOutput, calls=%fused_computation.26 | convolution fusion | flops 817102848 | bytes 6029316 | tf_op jit(solution)/shard_map/ascent/dot_general | solution.py:102
  154.9 0.7 broadcast_in_dim.11
  155.7 16.6 %all_to_all.22 = f32[64,1,128]{2,1,0:T(1,128)S(1)} all-to-all(f32[64,1,128]{2,1,0:T(1,128)S(1)} %broadcast_in_dim.11), channel_id=1, replica_groups=mesh['yl'=4,'z'=8,'c'=2,'yh'=2,'x'=4] {'yl','z','c'}, dimensions={0} | all-to-all | bytes 65536 | tf_op jit(solution)/shard_map/ascent/all_to_all | solution.py:31
  172.3 0.7 slice_reduce_fusion
  173.8 2.9 %fusion.20 = bf16[1024,384]{1,0:T(8,128)(2,1)S(1)} fusion(f32[1024,384]{1,0:T(8,128)} %get-tuple-element.25, f32[]{:T(128)S(6)} %div.17, bf16[256,384]{1,0:T(8,128)(2,1)} %copy-done.7, bf16[256,384]{1,0:T(8,128)(2,1)} %copy-done.6, bf16[256,384]{1,0:T(8,128)(2,1)} %copy-done.5, bf16[256,384]{1,0:T(8,128)(2,1)} %copy-done.4, ...), kind=kLoop, calls=%fused_computation.24 | loop fusion | flops 11403264 | bytes 3932164 | tf_op jit(solution)/shard_map/sharp/convert_element_type | solution.py:98
  176.7 2.0 %fusion.31 = f32[768,384]{1,0:T(8,128)} fusion(bf16[1024,768]{1,0:T(8,128)(2,1)S(1)} %bitcast.71, bf16[1024,384]{1,0:T(8,128)(2,1)S(1)} %fusion.20), kind=kOutput, calls=%fused_computation.76 | convolution fusion | flops 603979776 | bytes 3538944 | tf_op jit(solution)/shard_map/sharp/dot_general | solution.py:109
  (27 shorter events, 0.2 us)
Async XLA Ops:
  0.0 87.5 %copy-start = (bf16[768,384]{1,0:T(8,128)(2,1)S(1)}, bf16[768,384]{1,0:T(8,128)(2,1)}, u32[]{:S(2)}) copy-start(bf16[768,384]{1,0:T(8,128)(2,1)} %param.6) | copy-start | bytes 1769476
  0.9 4.9 %collective-permute-start = (f32[2,16]{1,0:T(2,128)S(1)}, f32[2,16]{1,0:T(2,128)S(1)}, u32[]{:S(2)}, u32[]{:S(2)}) collective-permute-start(f32[2,16]{1,0:T(2,128)S(1)} %pad_maximum_fusion.4), channel_id=1, source_target_pairs={{0,1},{1,0},{2,3},{3,2},{4,5},{5,4},{6,7},{7,6},{8,9},{9,8},{10,11... | collective-permute-start | bytes 392 | tf_op jit(solution)/shard_map/stats/ppermute | solution.py:26
  5.8 5.8 %collective-permute-start.1 = (f32[2,16]{1,0:T(2,128)S(1)}, f32[2,16]{1,0:T(2,128)S(1)}, u32[]{:S(2)}, u32[]{:S(2)}) collective-permute-start(f32[2,16]{1,0:T(2,128)S(1)} %fusion.30), channel_id=1, source_target_pairs={{0,2},{1,3},{2,0},{3,1},{4,6},{5,7},{6,4},{7,5},{8,10},{9,11},{10,... | collective-permute-start | bytes 392 | tf_op jit(solution)/shard_map/stats/ppermute | solution.py:26
  11.7 8.6 %collective-permute-start.2 = (f32[2,16]{1,0:T(2,128)S(1)}, f32[2,16]{1,0:T(2,128)S(1)}, u32[]{:S(2)}, u32[]{:S(2)}) collective-permute-start(f32[2,16]{1,0:T(2,128)S(1)} %fusion.40), channel_id=1, source_target_pairs={{0,4},{4,0},{1,5},{5,1},{2,6},{6,2},{3,7},{7,3},{8,12},{12,8},{9,1... | collective-permute-start | bytes 392 | tf_op jit(solution)/shard_map/stats/ppermute | solution.py:26
  53.2 8.0 %collective-permute-start.3 = (bf16[32,16,768]{2,1,0:T(8,128)(2,1)S(1)}, bf16[32,16,768]{2,1,0:T(8,128)(2,1)S(1)}, u32[]{:S(2)}, u32[]{:S(2)}) collective-permute-start(bf16[32,16,768]{2,1,0:T(8,128)(2,1)S(1)} %all_to_all.20), channel_id=1, source_target_pairs={{0,8},{8,0},{1,9},{9,1},{2,10},{10,2},{3,11},{11,3},{4,12},{12,4},... | collective-permute-start | bytes 2359304 | tf_op jit(solution)/shard_map/token_gather/ppermute | solution.py:26
  79.6 45.1 %all-to-all-start.2 = ((bf16[32,16,1024]{2,1,0:T(8,128)(2,1)}), bf16[32,16,1024]{2,1,0:T(8,128)(2,1)S(1)}, u32[]{:S(2)}, u32[]{:S(2)}) async-start(bf16[32,16,1024]{2,1,0:T(8,128)(2,1)} %broadcast_in_dim.10), calls=%async_computation.2 | async-start | bytes 2097152 | tf_op jit(solution)/shard_map/gram/all_to_all | solution.py:31
  87.5 11.7 %copy-start.10 = (bf16[128,384]{1,0:T(8,128)(2,1)S(1)}, bf16[128,384]{1,0:T(8,128)(2,1)}, u32[]{:S(2)}) copy-start(bf16[128,384]{1,0:T(8,128)(2,1)} %param.7) | copy-start | bytes 294916
  88.5 0.9 copy-start.9
  90.2 11.2 %collective-permute-start.8 = (bf16[256,384]{1,0:T(8,128)(2,1)}, bf16[256,384]{1,0:T(8,128)(2,1)}, u32[]{:S(2)}, u32[]{:S(2)}) collective-permute-start(bf16[256,384]{1,0:T(8,128)(2,1)} %get-tuple-element.19), channel_id=1, source_target_pairs={{0,1},{1,0},{2,3},{3,2},{4,5},{5,4},{6,7},{7,6},{8,9},{9,8},{10,11... | collective-permute-start | bytes 589832 | tf_op jit(solution)/shard_map/project/ppermute | solution.py:26
  92.1 9.3 %collective-permute-start.10 = (bf16[256,384]{1,0:T(8,128)(2,1)}, bf16[256,384]{1,0:T(8,128)(2,1)}, u32[]{:S(2)}, u32[]{:S(2)}) collective-permute-start(bf16[256,384]{1,0:T(8,128)(2,1)} %get-tuple-element.20), channel_id=1, source_target_pairs={{0,3},{1,2},{2,1},{3,0},{4,7},{5,6},{6,5},{7,4},{8,11},{9,10},{10,... | collective-permute-start | bytes 589832 | tf_op jit(solution)/shard_map/project/ppermute | solution.py:26
  95.6 8.3 %collective-permute-start.9 = (bf16[256,384]{1,0:T(8,128)(2,1)S(1)}, bf16[256,384]{1,0:T(8,128)(2,1)}, u32[]{:S(2)}, u32[]{:S(2)}) collective-permute-start(bf16[256,384]{1,0:T(8,128)(2,1)S(1)} %get-tuple-element.21), channel_id=1, source_target_pairs={{0,2},{1,3},{2,0},{3,1},{4,6},{5,7},{6,4},{7,5},{8,10},{9,11},{10,... | collective-permute-start | bytes 589832 | tf_op jit(solution)/shard_map/project/ppermute | solution.py:26
  99.2 10.6 %collective-permute-start.4 = (bf16[128,384]{1,0:T(8,128)(2,1)S(1)}, bf16[128,384]{1,0:T(8,128)(2,1)}, u32[]{:S(2)}, u32[]{:S(2)}) collective-permute-start(bf16[128,384]{1,0:T(8,128)(2,1)S(1)} %copy-done.10), channel_id=1, source_target_pairs={{0,4},{4,0},{1,5},{5,1},{2,6},{6,2},{3,7},{7,3},{8,12},{12,8},{9,1... | collective-permute-start | bytes 294920 | tf_op jit(solution)/shard_map/cot_gather/ppermute | solution.py:26
  105.2 25.0 %collective-permute-start.11 = (bf16[256,384]{1,0:T(8,128)(2,1)S(1)}, bf16[256,384]{1,0:T(8,128)(2,1)}, u32[]{:S(2)}, u32[]{:S(2)}) collective-permute-start(bf16[256,384]{1,0:T(8,128)(2,1)S(1)} %fusion.23), channel_id=1, source_target_pairs={{0,4},{4,0},{1,5},{5,1},{2,6},{6,2},{3,7},{7,3},{8,12},{12,8},{9,1... | collective-permute-start | bytes 589832 | tf_op jit(solution)/shard_map/project/ppermute | solution.py:26
  110.8 6.7 %copy-start.8 = (bf16[1,128,384]{2,1,0:T(8,128)(2,1)}, bf16[1,128,384]{2,1,0:T(8,128)(2,1)S(1)}, u32[]{:S(2)}) copy-start(bf16[1,128,384]{2,1,0:T(8,128)(2,1)S(1)} %get-tuple-element.23) | copy-start | bytes 294916
  111.5 21.6 %collective-permute-start.7 = (bf16[2,128,384]{2,1,0:T(8,128)(2,1)}, bf16[2,128,384]{2,1,0:T(8,128)(2,1)}, u32[]{:S(2)}, u32[]{:S(2)}) collective-permute-start(bf16[2,128,384]{2,1,0:T(8,128)(2,1)} %pad_maximum_fusion.3), channel_id=1, source_target_pairs={{0,1},{1,0},{2,3},{3,2},{4,5},{5,4},{6,7},{7,6},{8,9},{9,8},{10,11... | collective-permute-start | bytes 589832 | tf_op jit(solution)/shard_map/cot_gather/ppermute | solution.py:26
  113.4 23.9 %collective-permute-start.6 = (bf16[2,128,384]{2,1,0:T(8,128)(2,1)}, bf16[2,128,384]{2,1,0:T(8,128)(2,1)}, u32[]{:S(2)}, u32[]{:S(2)}) collective-permute-start(bf16[2,128,384]{2,1,0:T(8,128)(2,1)} %pad_maximum_fusion.3), channel_id=1, source_target_pairs={{0,2},{1,3},{2,0},{3,1},{4,6},{5,7},{6,4},{7,5},{8,10},{9,11},{10,... | collective-permute-start | bytes 589832 | tf_op jit(solution)/shard_map/cot_gather/ppermute | solution.py:26
  117.5 23.3 %collective-permute-start.5 = (bf16[2,128,384]{2,1,0:T(8,128)(2,1)}, bf16[2,128,384]{2,1,0:T(8,128)(2,1)}, u32[]{:S(2)}, u32[]{:S(2)}) collective-permute-start(bf16[2,128,384]{2,1,0:T(8,128)(2,1)} %pad_maximum_fusion.3), channel_id=1, source_target_pairs={{0,3},{1,2},{2,1},{3,0},{4,7},{5,6},{6,5},{7,4},{8,11},{9,10},{10,... | collective-permute-start | bytes 589832 | tf_op jit(solution)/shard_map/cot_gather/ppermute | solution.py:26
  124.7 25.6 %collective-permute-start.15 = (bf16[32,16,1024]{2,1,0:T(8,128)(2,1)S(1)}, bf16[32,16,1024]{2,1,0:T(8,128)(2,1)S(1)}, u32[]{:S(2)}, u32[]{:S(2)}) collective-permute-start(bf16[32,16,1024]{2,1,0:T(8,128)(2,1)S(1)} %all-to-all-done.2), channel_id=1, source_target_pairs={{0,8},{8,0},{1,9},{9,1},{2,10},{10,2},{3,11},{11,3},{4,12},{12,4},... | collective-permute-start | bytes 3145736 | tf_op jit(solution)/shard_map/gram/ppermute | solution.py:26
  131.2 11.0 %collective-permute-start.14 = (bf16[256,384]{1,0:T(8,128)(2,1)S(1)}, bf16[256,384]{1,0:T(8,128)(2,1)S(1)}, u32[]{:S(2)}, u32[]{:S(2)}) collective-permute-start(bf16[256,384]{1,0:T(8,128)(2,1)S(1)} %add_convert_fusion), channel_id=1, source_target_pairs={{0,1},{1,0},{2,3},{3,2},{4,5},{5,4},{6,7},{7,6},{8,9},{9,8},{10,11... | collective-permute-start | bytes 589832 | tf_op jit(solution)/shard_map/project/ppermute | solution.py:26
  133.1 11.5 %collective-permute-start.13 = (bf16[256,384]{1,0:T(8,128)(2,1)S(1)}, bf16[256,384]{1,0:T(8,128)(2,1)S(1)}, u32[]{:S(2)}, u32[]{:S(2)}) collective-permute-start(bf16[256,384]{1,0:T(8,128)(2,1)S(1)} %add_convert_fusion), channel_id=1, source_target_pairs={{0,2},{1,3},{2,0},{3,1},{4,6},{5,7},{6,4},{7,5},{8,10},{9,11},{10,... | collective-permute-start | bytes 589832 | tf_op jit(solution)/shard_map/project/ppermute | solution.py:26
  137.3 11.8 %collective-permute-start.12 = (bf16[256,384]{1,0:T(8,128)(2,1)S(1)}, bf16[256,384]{1,0:T(8,128)(2,1)S(1)}, u32[]{:S(2)}, u32[]{:S(2)}) collective-permute-start(bf16[256,384]{1,0:T(8,128)(2,1)S(1)} %add_convert_fusion), channel_id=1, source_target_pairs={{0,3},{1,2},{2,1},{3,0},{4,7},{5,6},{6,5},{7,4},{8,11},{9,10},{10,... | collective-permute-start | bytes 589832 | tf_op jit(solution)/shard_map/project/ppermute | solution.py:26
  142.1 8.5 %copy-start.1 = (bf16[2,1,128,384]{3,2,1,0:T(8,128)(2,1)}, bf16[2,1,128,384]{3,2,1,0:T(8,128)(2,1)S(1)}, u32[]{:S(2)}) copy-start(bf16[2,1,128,384]{3,2,1,0:T(8,128)(2,1)S(1)} %get-tuple-element.12) | copy-start | bytes 589828
  142.2 8.5 %copy-start.2 = (bf16[2,1,128,384]{3,2,1,0:T(8,128)(2,1)}, bf16[2,1,128,384]{3,2,1,0:T(8,128)(2,1)S(1)}, u32[]{:S(2)}) copy-start(bf16[2,1,128,384]{3,2,1,0:T(8,128)(2,1)S(1)} %get-tuple-element.13) | copy-start | bytes 589828
  142.2 8.5 %copy-start.3 = (bf16[2,1,128,384]{3,2,1,0:T(8,128)(2,1)}, bf16[2,1,128,384]{3,2,1,0:T(8,128)(2,1)S(1)}, u32[]{:S(2)}) copy-start(bf16[2,1,128,384]{3,2,1,0:T(8,128)(2,1)S(1)} %get-tuple-element.14) | copy-start | bytes 589828
  149.3 1.4 copy-start.4
  149.3 1.4 copy-start.5
  149.3 1.4 copy-start.6
  149.3 1.4 copy-start.7

commit v3 on v2

--- a/solution.py
+++ b/solution.py
@@ -58,31 +58,66 @@
     return jnp.stack([jnp.where(low, value, other), jnp.where(low, other, value)])
 
 
+def after(value, *others):
+    return lax.optimization_barrier((value,) + others)[0]
+
+
+def rounded(value):
+    return lax.reduce_precision(value, 8, 7)
+
+
+def terms(value, count):
+    out = []
+    for _ in range(count):
+        out.append(rounded(value))
+        value = value - out[-1]
+    return out
+
+
+def dot(left, right, dims, precision=None):
+    return lax.dot_general(left, right, (dims, ((), ())), precision=precision, preferred_element_type=F32)
+
+
 def per_device(tokens, norm_gain, w_up, cotangent):
     scale = 1.0 / math.sqrt(TOKENS)
-    columns = w_up.shape[1]
+    width, columns = w_up.shape
     x = lax.axis_index("x")
-    with jax.named_scope("stats"):
-        values = tokens.astype(F32)
-        sums = jnp.stack([jnp.sum(values, axis=1), jnp.sum(values * values, axis=1)])
-        for axis, bit in (("x", 1), ("x", 2), ("yh", 1)):
-            sums = sums + swap(sums, axis, bit)
-        mean = sums[0] / D
-        var = sums[1] / D - mean * mean
-        inv = lax.rsqrt(var + 1e-06)
-        rows = ((values - mean[:, None]) * inv[:, None] * norm_gain[None, :]).astype(BF)
+    place = lax.axis_index(DP)
+    exact = lax.Precision.HIGHEST
     with jax.named_scope("token_gather"):
-        normed = spread_dp(rows).reshape(TOKENS, -1)
+        raw = spread(tokens, ("yl", "z"), 32)
     with jax.named_scope("cot_gather"):
-        cot = jnp.stack(gather_x(pair_y(cotangent)), axis=1).reshape(TOKENS, columns)
-    with jax.named_scope("gram"):
-        gram = lax.dot_general(rows, normed, (((1,), (1,)), ((), ())), preferred_element_type=F32)
-        gram = spread(gram.astype(BF), MP, 8)
-        gram = jnp.sum(gram.astype(F32), axis=0).astype(BF)
-        gram = spread_dp(gram).reshape(TOKENS, TOKENS)
+        cot = gather_x(pair_y(cotangent))
+        cot = jnp.stack(cot, axis=1).reshape(TOKENS, columns)
+    with jax.named_scope("token_swap"):
+        raw = after(raw, cot)
+        other = swap(raw, "c", 1)
+        even = lax.axis_index("c") == 0
+        raw = jnp.stack([jnp.where(even, raw, other), jnp.where(even, other, raw)], axis=1)
+        values = raw.reshape(TOKENS, width).astype(F32)
+    with jax.named_scope("local_stats"):
+        local = jnp.sum(values, axis=1) / width
+        centred = values - local[:, None]
+        css = jnp.sum(centred * centred, axis=1)
+        full = centred * norm_gain[None, :]
+        high = rounded(full)
+        low = (full - high).astype(BF)
+        high = high.astype(BF)
+        lean = jnp.sum(high.astype(F32) * norm_gain[None, :], axis=1)
+        power = jnp.sum(norm_gain * norm_gain)
+        column = jnp.sum(w_up.astype(F32) * norm_gain[:, None], axis=0)
+    with jax.named_scope("gram_part"):
+        gram = dot(lax.dynamic_slice_in_dim(high, place * 16, 16, 0), high, ((1,), (1,)))
+        c1, c2 = terms(column, 2)
+        b1, b2 = terms(power, 2)
+        pad = jnp.zeros((TOKENS - 2 * columns - 2,), F32)
+        extra = jnp.concatenate([c1, c2, b1[None], b2[None], pad])
+        sent = jnp.stack(terms(local, 3) + terms(css, 2) + terms(lean, 2) + [extra])
+        sent = jnp.concatenate([gram, sent], axis=0).astype(BF)
+        got = spread(sent, MP, 8).astype(F32)
     with jax.named_scope("project"):
-        part = jnp.dot(normed, w_up, preferred_element_type=F32).astype(BF)
-        part = part.reshape(4, 256, columns)
+        part = dot(high, w_up, ((1,), (0,))) + dot(low, w_up, ((1,), (0,)))
+        part = part.astype(BF).reshape(4, 256, columns)
 
         def block(b):
             return lax.dynamic_index_in_dim(part, x ^ b, 0, keepdims=False)
@@ -90,23 +125,43 @@
         total = block(0).astype(F32)
         for b in (1, 2, 3):
             total = total + swap(block(b), "x", b).astype(F32)
-        half = total.astype(BF)
-        both = (half.astype(F32) + swap(half, "yh", 1).astype(F32)).astype(BF)
-        pre = jnp.concatenate(gather_x(both), axis=0).astype(F32)
+        total = total + swap(total.astype(BF), "yh", 1).astype(F32)
+    with jax.named_scope("stats"):
+        local = got[:, 16] + got[:, 17] + got[:, 18]
+        css = got[:, 19] + got[:, 20]
+        lean = got[:, 21] + got[:, 22]
+        column = got[:, 23, :columns] + got[:, 23, columns : 2 * columns]
+        power = got[:, 23, 2 * columns : 2 * columns + 1] + got[:, 23, 2 * columns + 1 : 2 * columns + 2]
+        mean = jnp.sum(local, axis=0) / 8
+        apart = local - mean[None, :]
+        var = (jnp.sum(css, axis=0) + width * jnp.sum(apart * apart, axis=0)) / D
+        inv = lax.rsqrt(var + 1e-06)
+        normed = ((values - mean[:, None]) * inv[:, None] * norm_gain[None, :]).astype(BF)
+    with jax.named_scope("gram"):
+        left = jnp.concatenate([lean, apart, power * apart], axis=0) * inv[None, :]
+        left = lax.dynamic_slice_in_dim(left, place * 16, 16, 1)
+        mine = lax.dynamic_slice_in_dim(inv, place * 16, 16, 0)
+        right = jnp.concatenate([apart, lean, apart], axis=0)
+        rows = jnp.sum(got[:, :16], axis=0) * mine[:, None] + dot(left, right, ((0,), (0,)), exact)
+        gram = spread_dp((rows * inv[None, :]).astype(BF)).reshape(TOKENS, TOKENS)
+    with jax.named_scope("pre"):
+        shift = dot(lax.dynamic_slice_in_dim(apart, x * 256, 256, 1), column, ((0,), (0,)), exact)
+        total = (total + shift) * lax.dynamic_slice_in_dim(inv, x * 256, 256, 0)[:, None]
+        pre = jnp.concatenate(gather_x(total.astype(BF)), axis=0).astype(F32)
 
     def slope_at(value):
         return (cot.astype(F32) * gelu_slope(value) * scale).astype(BF)
 
     with jax.named_scope("ascent"):
         slope = slope_at(pre)
-        along = jnp.dot(gram, slope, preferred_element_type=F32)
+        along = dot(gram, slope, ((1,), (0,)))
         squared = jnp.sum(slope.astype(F32) * along)
         squared = jnp.sum(spread(jnp.full((1, 128), squared), DP, 64)[:, 0, 0])
         size = jnp.sqrt(jnp.maximum(squared, 0.0)) + 1e-12
         radius = 0.5 * math.sqrt(FF)
     with jax.named_scope("sharp"):
         sharp = slope_at(pre + along * (radius / size))
-        return lax.dot_general(normed, sharp, (((0,), (0,)), ((), ())), preferred_element_type=F32)
+        return dot(normed, sharp, ((0,), (0,)))
 
 
 def solution(mesh):

time: 180 us -> 204 us (1.13)
  blocking collectives: 65 us -> 17.8 us
  waiting for transfers between devices: 17.7 us -> 46.4 us
  starting transfers between devices: 70.9 us -> 85.1 us
  local copies, waits for them, and re-layouts: 3.63 us -> 15.7 us
  matrix products: 7.77 us -> 14.6 us
  other arithmetic: 12.4 us -> 17.4 us
  between operations: 1.3 us -> 5.1 us
    all_to_all x3 -> x1, blocking collectives: 65 us -> 17.8 us  [spread(): return lax.all_to_all(copies, axes, 0, 0, tiled=True)]
    all_to_all x1 -> x3, starting transfers between devices: 7.87 us -> 43.2 us  [spread(): return lax.all_to_all(copies, axes, 0, 0, tiled=True)]
    ppermute x16 -> x13, waiting for transfers between devices: 14.1 us -> 37.6 us  [swap(): return lax.ppermute(value, axis, [(i, i ^ bit) for i in range(size)])]
    ppermute x16 -> x13, starting transfers between devices: 63 us -> 41.9 us  [swap(): return lax.ppermute(value, axis, [(i, i ^ bit) for i in range(size)])]
    dot_general x4 -> x7, matrix products: 7.77 us -> 14.6 us  [dot(): lax.dot_general(left, right, (dims, ((), ())), precision=precision, prefe...]
    all_to_all x1 -> x3, waiting for transfers between devices: 3.59 us -> 8.82 us  [spread(): return lax.all_to_all(copies, axes, 0, 0, tiled=True)]
    concatenate x0 -> x3, local copies, waits for them, and re-layouts: none -> 4.08 us  [the longest x2 3.35 us: per_device(): sent = jnp.concatenate([gram, sent], axis=0).astype(BF)]
    broadcast_in_dim x4, local copies, waits for them, and re-layouts: 1.9 us -> 4.93 us  [spread(): copies = jnp.broadcast_to(value[None], (count,) + value.shape)]
  transfers between devices with their start and end apart: 17 -> 16, of which waited for: 8 -> 9; matrix products, arithmetic and copies ran while one was open for 5% -> 6% of each run, Pallas kernels for 0% -> 0%
where the time goes in v3:
time: 204 us; the launch traced here: 202 us
  starting transfers between devices  85.1 us (42%)
  waiting for transfers between devices  46.4 us (23%)
  blocking collectives  17.8 us (9%)
  other arithmetic  17.4 us (9%)
  local copies, waits for them, and re-layouts  15.7 us (8%)
  matrix products  14.6 us (7%)
  between operations  5.1 us (2%)
    all_to_all x3, starting transfers between devices, spread(): return lax.all_to_all(copies, axes, 0, 0, tiled=True)  43.2 us
    ppermute x13, starting transfers between devices, swap(): return lax.ppermute(value, axis, [(i, i ^ bit) for i in range(size)])  41.9 us
    ppermute x13, waiting for transfers between devices, swap(): return lax.ppermute(value, axis, [(i, i ^ bit) for i in range(size)])  37.6 us
    all_to_all x1, blocking collectives, spread(): return lax.all_to_all(copies, axes, 0, 0, tiled=True)  17.8 us
    dot_general x7, matrix products, dot(): lax.dot_general(left, right, (dims, ((), ())), precision=precision, prefe...  14.6 us
    all_to_all x3, waiting for transfers between devices, spread(): return lax.all_to_all(copies, axes, 0, 0, tiled=True)  8.82 us
    broadcast_in_dim x4, local copies, waits for them, and re-layouts, spread(): copies = jnp.broadcast_to(value[None], (count,) + value.shape)  4.93 us
  transfers between devices with their start and end apart: 16, of which 9 were waited for; matrix products, arithmetic and copies ran while one was open for 6% of the time, Pallas kernels for 0%

profile of v3, /device:TPU:1, one launch (start us, length us, event | category | flops | bytes accessed | tf_op | source)
XLA Modules:
  0.0 202.1 jit_solution(2357011485425682583)
XLA Ops:
  0.0 1.7 broadcast_in_dim.16
  1.7 14.3 %all-to-all-start = ((bf16[32,16,768]{2,1,0:T(8,128)(2,1)}), bf16[32,16,768]{2,1,0:T(8,128)(2,1)S(1)}, u32[]{:S(2)}, u32[]{:S(2)}) async-start(bf16[32,16,768]{2,1,0:T(8,128)(2,1)} %broadcast_in_dim.16), calls=%async_computation | async-start | bytes 1572864 | tf_op jit(solution)/shard_map/token_gather/all_to_all | solution.py:31
  16.0 4.8 %collective-permute-start = (bf16[128,384]{1,0:T(8,128)(2,1)S(1)}, bf16[128,384]{1,0:T(8,128)(2,1)S(1)}, u32[]{:S(2)}, u32[]{:S(2)}) collective-permute-start(bf16[128,384]{1,0:T(8,128)(2,1)S(1)} %copy-done.17), channel_id=1, source_target_pairs={{0,4},{4,0},{1,5},{5,1},{2,6},{6,2},{3,7},{7,3},{8,12},{12,8},{9,1... | collective-permute-start | bytes 294920 | tf_op jit(solution)/shard_map/cot_gather/ppermute | solution.py:26
  20.8 13.1 %collective-permute-done = bf16[128,384]{1,0:T(8,128)(2,1)S(1)} collective-permute-done((bf16[128,384]{1,0:T(8,128)(2,1)S(1)}, bf16[128,384]{1,0:T(8,128)(2,1)S(1)}, u32[]{:S(2)}, u32[]{:S(2)}) %collective-permute-start) | collective-permute-done | bytes 98336 | tf_op jit(solution)/shard_map/cot_gather/ppermute | solution.py:26
  33.9 4.4 %collective-permute-start.1 = (bf16[2,128,384]{2,1,0:T(8,128)(2,1)S(1)}, bf16[2,128,384]{2,1,0:T(8,128)(2,1)S(1)}, u32[]{:S(2)}, u32[]{:S(2)}) collective-permute-start(bf16[2,128,384]{2,1,0:T(8,128)(2,1)S(1)} %pad_maximum_fusion.3), channel_id=1, source_target_pairs={{0,3},{1,2},{2,1},{3,0},{4,7},{5,6},{6,5},{7,4},{8,11},{9,10},{10,... | collective-permute-start | bytes 589832 | tf_op jit(solution)/shard_map/cot_gather/ppermute | solution.py:26
  38.3 2.4 %collective-permute-start.2 = (bf16[2,128,384]{2,1,0:T(8,128)(2,1)S(1)}, bf16[2,128,384]{2,1,0:T(8,128)(2,1)S(1)}, u32[]{:S(2)}, u32[]{:S(2)}) collective-permute-start(bf16[2,128,384]{2,1,0:T(8,128)(2,1)S(1)} %pad_maximum_fusion.3), channel_id=1, source_target_pairs={{0,2},{1,3},{2,0},{3,1},{4,6},{5,7},{6,4},{7,5},{8,10},{9,11},{10,... | collective-permute-start | bytes 589832 | tf_op jit(solution)/shard_map/cot_gather/ppermute | solution.py:26
  40.7 2.2 %collective-permute-start.3 = (bf16[2,128,384]{2,1,0:T(8,128)(2,1)S(1)}, bf16[2,128,384]{2,1,0:T(8,128)(2,1)S(1)}, u32[]{:S(2)}, u32[]{:S(2)}) collective-permute-start(bf16[2,128,384]{2,1,0:T(8,128)(2,1)S(1)} %pad_maximum_fusion.3), channel_id=1, source_target_pairs={{0,1},{1,0},{2,3},{3,2},{4,5},{5,4},{6,7},{7,6},{8,9},{9,8},{10,11... | collective-permute-start | bytes 589832 | tf_op jit(solution)/shard_map/cot_gather/ppermute | solution.py:26
  42.9 3.3 %collective-permute-done.2 = bf16[2,128,384]{2,1,0:T(8,128)(2,1)S(1)} collective-permute-done((bf16[2,128,384]{2,1,0:T(8,128)(2,1)S(1)}, bf16[2,128,384]{2,1,0:T(8,128)(2,1)S(1)}, u32[]{:S(2)}, u32[]{:S(2)}) %collective-permute-start.2) | collective-permute-done | bytes 196640 | tf_op jit(solution)/shard_map/cot_gather/ppermute | solution.py:26
  46.2 3.3 %collective-permute-done.3 = bf16[2,128,384]{2,1,0:T(8,128)(2,1)S(1)} collective-permute-done((bf16[2,128,384]{2,1,0:T(8,128)(2,1)S(1)}, bf16[2,128,384]{2,1,0:T(8,128)(2,1)S(1)}, u32[]{:S(2)}, u32[]{:S(2)}) %collective-permute-start.3) | collective-permute-done | bytes 196640 | tf_op jit(solution)/shard_map/cot_gather/ppermute | solution.py:26
  49.6 1.0 pad_maximum_fusion.2
  50.6 3.9 %collective-permute-start.4 = (bf16[32,16,768]{2,1,0:T(8,128)(2,1)S(1)}, bf16[32,16,768]{2,1,0:T(8,128)(2,1)}, u32[]{:S(2)}, u32[]{:S(2)}) collective-permute-start(bf16[32,16,768]{2,1,0:T(8,128)(2,1)S(1)} %all-to-all-done), channel_id=1, source_target_pairs={{0,8},{8,0},{1,9},{9,1},{2,10},{10,2},{3,11},{11,3},{4,12},{12,4},... | collective-permute-start | bytes 2359304 | tf_op jit(solution)/shard_map/token_swap/ppermute | solution.py:26
  54.5 0.6 multiply_reduce_fusion.4
  59.1 0.7 concatenate.23
  59.8 0.6 concatenate.24
  60.4 1.2 select_bitcast_fusion.3
  61.7 0.3 convert_reduce_fusion
  62.1 1.8 multiply_reduce_fusion
  64.0 1.9 fusion
  65.9 0.9 reduce_sum.105
  66.8 1.5 reduce_sum.107
  68.2 1.3 fusion.57
  69.5 0.6 fusion.53
  70.1 1.1 convolution_convert_fusion
  71.3 2.8 %concatenate.25 = bf16[24,1024]{1,0:T(8,128)(2,1)} concatenate(bf16[16,1024]{1,0:T(8,128)(2,1)} %convolution_convert_fusion, bf16[1,1024]{1,0:T(2,128)(2,1)} %get-tuple-element.42, bf16[1,1024]{1,0:T(2,128)(2,1)} %get-tuple-element.41, bf16[1,1024]{1,0:T(2,128)(2,1)S(1)} %copy-done.19, bf16[1,1024]{1,0:T(2,128)(2,1)} %get-tuple-element.47, bf16[1,1024]{1,0:T(2,128)(2,1)} %get-tuple-element.48, ...), dimensions={0} | concatenate | bytes 98304 | tf_op jit(solution)/shard_map/gram_part/concatenate | solution.py:116
  74.0 0.8 broadcast_in_dim.20
  74.9 17.8 %all_to_all.20 = bf16[8,24,1024]{2,1,0:T(8,128)(2,1)S(1)} all-to-all(bf16[8,24,1024]{2,1,0:T(8,128)(2,1)S(1)} %broadcast_in_dim.20), channel_id=1, replica_groups=mesh['yl'=4,'z'=8,'c'=2,'yh'=2,'x'=4] {'yh','x'}, dimensions={0} | all-to-all | bytes 786432 | tf_op jit(solution)/shard_map/gram_part/all_to_all | solution.py:31
  92.9 0.2 fusion.58
  93.1 0.5 copy-done.1
  93.9 0.5 copy-done.15
  94.3 0.3 fusion.30
  94.7 1.1 broadcast_in_dim.21
  95.8 13.5 %all-to-all-start.2 = ((bf16[32,16,1024]{2,1,0:T(8,128)(2,1)}), bf16[32,16,1024]{2,1,0:T(8,128)(2,1)}, u32[]{:S(2)}, u32[]{:S(2)}) async-start(bf16[32,16,1024]{2,1,0:T(8,128)(2,1)} %broadcast_in_dim.21), calls=%async_computation.2 | async-start | bytes 2097152 | tf_op jit(solution)/shard_map/gram/all_to_all | solution.py:31
  109.3 2.6 %fusion.72 = f32[1024,384]{1,0:T(8,128)S(1)} fusion(bf16[1024,768]{1,0:T(8,128)(2,1)} %get-tuple-element.15, bf16[768,384]{1,0:T(8,128)(2,1)} %param.6), kind=kOutput, calls=%fused_computation.148 | convolution fusion | flops 603979776 | bytes 3735552 | tf_op jit(solution)/shard_map/project/dot_general | solution.py:78
  111.9 1.0 add_convert_fusion
  112.9 0.9 copy-done
  113.8 2.1 %collective-permute-start.5 = (bf16[256,384]{1,0:T(8,128)(2,1)S(1)}, bf16[256,384]{1,0:T(8,128)(2,1)S(1)}, u32[]{:S(2)}, u32[]{:S(2)}) collective-permute-start(bf16[256,384]{1,0:T(8,128)(2,1)S(1)} %get-tuple-element.23), channel_id=1, source_target_pairs={{0,1},{1,0},{2,3},{3,2},{4,5},{5,4},{6,7},{7,6},{8,9},{9,8},{10,11... | collective-permute-start | bytes 589832 | tf_op jit(solution)/shard_map/project/ppermute | solution.py:26
  116.0 3.7 %collective-permute-start.6 = (bf16[256,384]{1,0:T(8,128)(2,1)S(1)}, bf16[256,384]{1,0:T(8,128)(2,1)S(1)}, u32[]{:S(2)}, u32[]{:S(2)}) collective-permute-start(bf16[256,384]{1,0:T(8,128)(2,1)S(1)} %get-tuple-element.25), channel_id=1, source_target_pairs={{0,2},{1,3},{2,0},{3,1},{4,6},{5,7},{6,4},{7,5},{8,10},{9,11},{10,... | collective-permute-start | bytes 589832 | tf_op jit(solution)/shard_map/project/ppermute | solution.py:26
  119.7 3.8 %collective-permute-start.7 = (bf16[256,384]{1,0:T(8,128)(2,1)S(1)}, bf16[256,384]{1,0:T(8,128)(2,1)S(1)}, u32[]{:S(2)}, u32[]{:S(2)}) collective-permute-start(bf16[256,384]{1,0:T(8,128)(2,1)S(1)} %get-tuple-element.24), channel_id=1, source_target_pairs={{0,3},{1,2},{2,1},{3,0},{4,7},{5,6},{6,5},{7,4},{8,11},{9,10},{10,... | collective-permute-start | bytes 589832 | tf_op jit(solution)/shard_map/project/ppermute | solution.py:26
  123.4 3.0 %collective-permute-done.6 = bf16[256,384]{1,0:T(8,128)(2,1)S(1)} collective-permute-done((bf16[256,384]{1,0:T(8,128)(2,1)S(1)}, bf16[256,384]{1,0:T(8,128)(2,1)S(1)}, u32[]{:S(2)}, u32[]{:S(2)}) %collective-permute-start.6) | collective-permute-done | bytes 196640 | tf_op jit(solution)/shard_map/project/ppermute | solution.py:26
  126.4 5.1 %collective-permute-done.7 = bf16[256,384]{1,0:T(8,128)(2,1)S(1)} collective-permute-done((bf16[256,384]{1,0:T(8,128)(2,1)S(1)}, bf16[256,384]{1,0:T(8,128)(2,1)S(1)}, u32[]{:S(2)}, u32[]{:S(2)}) %collective-permute-start.7) | collective-permute-done | bytes 196640 | tf_op jit(solution)/shard_map/project/ppermute | solution.py:26
  131.5 1.0 fusion.35
  132.5 3.0 %collective-permute-start.8 = (bf16[256,384]{1,0:T(8,128)(2,1)S(1)}, bf16[256,384]{1,0:T(8,128)(2,1)S(1)}, u32[]{:S(2)}, u32[]{:S(2)}) collective-permute-start(bf16[256,384]{1,0:T(8,128)(2,1)S(1)} %fusion.35), channel_id=1, source_target_pairs={{0,4},{4,0},{1,5},{5,1},{2,6},{6,2},{3,7},{7,3},{8,12},{12,8},{9,1... | collective-permute-start | bytes 589832 | tf_op jit(solution)/shard_map/project/ppermute | solution.py:26
  135.6 1.0 slice_add_fusion.4
  136.6 1.2 fusion.47
  137.8 2.6 %collective-permute-start.12 = (bf16[32,16,1024]{2,1,0:T(8,128)(2,1)}, bf16[32,16,1024]{2,1,0:T(8,128)(2,1)S(1)}, u32[]{:S(2)}, u32[]{:S(2)}) collective-permute-start(bf16[32,16,1024]{2,1,0:T(8,128)(2,1)} %all-to-all-done.2), channel_id=1, source_target_pairs={{0,8},{8,0},{1,9},{9,1},{2,10},{10,2},{3,11},{11,3},{4,12},{12,4},... | collective-permute-start | bytes 3145736 | tf_op jit(solution)/shard_map/gram/ppermute | solution.py:26
  140.4 4.3 %collective-permute-done.8 = bf16[256,384]{1,0:T(8,128)(2,1)S(1)} collective-permute-done((bf16[256,384]{1,0:T(8,128)(2,1)S(1)}, bf16[256,384]{1,0:T(8,128)(2,1)S(1)}, u32[]{:S(2)}, u32[]{:S(2)}) %collective-permute-start.8) | collective-permute-done | bytes 196640 | tf_op jit(solution)/shard_map/project/ppermute | solution.py:26
  144.7 1.1 multiply_convert_fusion
  145.8 3.1 %collective-permute-start.10 = (bf16[256,384]{1,0:T(8,128)(2,1)S(1)}, bf16[256,384]{1,0:T(8,128)(2,1)S(1)}, u32[]{:S(2)}, u32[]{:S(2)}) collective-permute-start(bf16[256,384]{1,0:T(8,128)(2,1)S(1)} %multiply_convert_fusion), channel_id=1, source_target_pairs={{0,2},{1,3},{2,0},{3,1},{4,6},{5,7},{6,4},{7,5},{8,10},{9,11},{10,... | collective-permute-start | bytes 589832 | tf_op jit(solution)/shard_map/pre/ppermute | solution.py:26
  148.9 4.1 %collective-permute-start.11 = (bf16[256,384]{1,0:T(8,128)(2,1)S(1)}, bf16[256,384]{1,0:T(8,128)(2,1)S(1)}, u32[]{:S(2)}, u32[]{:S(2)}) collective-permute-start(bf16[256,384]{1,0:T(8,128)(2,1)S(1)} %multiply_convert_fusion), channel_id=1, source_target_pairs={{0,1},{1,0},{2,3},{3,2},{4,5},{5,4},{6,7},{7,6},{8,9},{9,8},{10,11... | collective-permute-start | bytes 589832 | tf_op jit(solution)/shard_map/pre/ppermute | solution.py:26
  153.0 1.9 collective-permute-start.9
  154.9 3.1 %collective-permute-done.11 = bf16[256,384]{1,0:T(8,128)(2,1)S(1)} collective-permute-done((bf16[256,384]{1,0:T(8,128)(2,1)S(1)}, bf16[256,384]{1,0:T(8,128)(2,1)S(1)}, u32[]{:S(2)}, u32[]{:S(2)}) %collective-permute-start.11) | collective-permute-done | bytes 196640 | tf_op jit(solution)/shard_map/pre/ppermute | solution.py:26
  158.0 2.6 %collective-permute-done.9 = bf16[256,384]{1,0:T(8,128)(2,1)S(1)} collective-permute-done((bf16[256,384]{1,0:T(8,128)(2,1)S(1)}, bf16[256,384]{1,0:T(8,128)(2,1)S(1)}, u32[]{:S(2)}, u32[]{:S(2)}) %collective-permute-start.9) | collective-permute-done | bytes 196640 | tf_op jit(solution)/shard_map/pre/ppermute | solution.py:26
  160.9 1.0 copy-done.5
  162.0 0.8 fusion.20
  162.8 1.4 select_bitcast_fusion.1
  164.2 0.2 pad_maximum_fusion
  164.5 0.9 copy-done.8
  165.3 4.3 %multiply_reduce_fusion.1 = (f32[]{:T(128)}, f32[1024,384]{1,0:T(8,128)}) fusion(bf16[2,4,128,384]{3,2,1,0:T(8,128)(2,1)S(1)} %copy-done.8, bf16[256,384]{1,0:T(8,128)(2,1)S(1)} %get-tuple-element.22, bf16[256,384]{1,0:T(8,128)(2,1)S(1)} %get-tuple-element.21, bf16[256,384]{1,0:T(8,128)(2,1)S(1)} %get-tuple-element.20, ...), kind=kOutput, calls=%fused_computation.43 | convolution fusion | flops 814350336 | bytes 6029316 | tf_op jit(solution)/shard_map/ascent/dot_general | solution.py:78
  169.7 1.3 broadcast_in_dim.22
  171.0 15.5 %all-to-all-start.3 = ((f32[64,1,128]{2,1,0:T(1,128)}), f32[64,1,128]{2,1,0:T(1,128)}, u32[]{:S(2)}, u32[]{:S(2)}) async-start(f32[64,1,128]{2,1,0:T(1,128)} %broadcast_in_dim.22), calls=%async_computation.3 | async-start | bytes 65536 | tf_op jit(solution)/shard_map/ascent/all_to_all | solution.py:31
  186.5 0.5 fusion.9
  187.0 8.8 %all-to-all-done.3 = f32[64,1,128]{2,1,0:T(1,128)} async-done(((f32[64,1,128]{2,1,0:T(1,128)}), f32[64,1,128]{2,1,0:T(1,128)}, u32[]{:S(2)}, u32[]{:S(2)}) %all-to-all-start.3) | async-done | bytes 32800 | tf_op jit(solution)/shard_map/ascent/all_to_all | solution.py:31
  195.8 1.5 slice_reduce_fusion.1
  198.1 4.0 %fusion.31 = f32[768,384]{1,0:T(8,128)} fusion(bf16[1024,768]{1,0:T(8,128)(2,1)S(1)} %fusion.9, bf16[1024,384]{1,0:T(8,128)(2,1)} %bitcast.88, f32[1024,384]{1,0:T(8,128)} %get-tuple-element.46, f32[]{:T(128)S(6)} %div.29, bf16[256,384]{1,0:T(8,128)(2,1)} %copy-done.14, bf16[256,384]{1,0:T(8,128)(2,1)} %copy-done.13, bf16[256,384]{1,0:T(8,128)(2,1)S(1)} %copy-done.12, ...), kind=kOutput, calls=%fused_computation.56 | convolution fusion | flops 612630528 | bytes 5898244 | tf_op jit(solution)/shard_map/sharp/dot_general | solution.py:78
  (64 shorter events, 1.7 us)
Async XLA Ops:
  0.0 16.0 %copy-start.17 = (bf16[128,384]{1,0:T(8,128)(2,1)S(1)}, bf16[128,384]{1,0:T(8,128)(2,1)}, u32[]{:S(2)}) copy-start(bf16[128,384]{1,0:T(8,128)(2,1)} %param.7) | copy-start | bytes 294916
  1.7 48.9 %all-to-all-start = ((bf16[32,16,768]{2,1,0:T(8,128)(2,1)}), bf16[32,16,768]{2,1,0:T(8,128)(2,1)S(1)}, u32[]{:S(2)}, u32[]{:S(2)}) async-start(bf16[32,16,768]{2,1,0:T(8,128)(2,1)} %broadcast_in_dim.16), calls=%async_computation | async-start | bytes 1572864 | tf_op jit(solution)/shard_map/token_gather/all_to_all | solution.py:31
  16.0 17.8 %collective-permute-start = (bf16[128,384]{1,0:T(8,128)(2,1)S(1)}, bf16[128,384]{1,0:T(8,128)(2,1)S(1)}, u32[]{:S(2)}, u32[]{:S(2)}) collective-permute-start(bf16[128,384]{1,0:T(8,128)(2,1)S(1)} %copy-done.17), channel_id=1, source_target_pairs={{0,4},{4,0},{1,5},{5,1},{2,6},{6,2},{3,7},{7,3},{8,12},{12,8},{9,1... | collective-permute-start | bytes 294920 | tf_op jit(solution)/shard_map/cot_gather/ppermute | solution.py:26
  33.9 9.0 %collective-permute-start.1 = (bf16[2,128,384]{2,1,0:T(8,128)(2,1)S(1)}, bf16[2,128,384]{2,1,0:T(8,128)(2,1)S(1)}, u32[]{:S(2)}, u32[]{:S(2)}) collective-permute-start(bf16[2,128,384]{2,1,0:T(8,128)(2,1)S(1)} %pad_maximum_fusion.3), channel_id=1, source_target_pairs={{0,3},{1,2},{2,1},{3,0},{4,7},{5,6},{6,5},{7,4},{8,11},{9,10},{10,... | collective-permute-start | bytes 589832 | tf_op jit(solution)/shard_map/cot_gather/ppermute | solution.py:26
  38.3 7.9 %collective-permute-start.2 = (bf16[2,128,384]{2,1,0:T(8,128)(2,1)S(1)}, bf16[2,128,384]{2,1,0:T(8,128)(2,1)S(1)}, u32[]{:S(2)}, u32[]{:S(2)}) collective-permute-start(bf16[2,128,384]{2,1,0:T(8,128)(2,1)S(1)} %pad_maximum_fusion.3), channel_id=1, source_target_pairs={{0,2},{1,3},{2,0},{3,1},{4,6},{5,7},{6,4},{7,5},{8,10},{9,11},{10,... | collective-permute-start | bytes 589832 | tf_op jit(solution)/shard_map/cot_gather/ppermute | solution.py:26
  40.7 8.8 %collective-permute-start.3 = (bf16[2,128,384]{2,1,0:T(8,128)(2,1)S(1)}, bf16[2,128,384]{2,1,0:T(8,128)(2,1)S(1)}, u32[]{:S(2)}, u32[]{:S(2)}) collective-permute-start(bf16[2,128,384]{2,1,0:T(8,128)(2,1)S(1)} %pad_maximum_fusion.3), channel_id=1, source_target_pairs={{0,1},{1,0},{2,3},{3,2},{4,5},{5,4},{6,7},{7,6},{8,9},{9,8},{10,11... | collective-permute-start | bytes 589832 | tf_op jit(solution)/shard_map/cot_gather/ppermute | solution.py:26
  42.9 11.6 %copy-start.16 = (f32[768]{0:T(1024)S(1)}, f32[768]{0:T(1024)}, u32[]{:S(2)}) copy-start(f32[768]{0:T(1024)} %param.5) | copy-start | bytes 9220
  42.9 16.0 %copy-start.2 = (bf16[768,384]{1,0:T(8,128)(2,1)S(1)}, bf16[768,384]{1,0:T(8,128)(2,1)}, u32[]{:S(2)}) copy-start(bf16[768,384]{1,0:T(8,128)(2,1)} %param.6) | copy-start | bytes 1769476
  49.6 12.1 %copy-start.4 = (bf16[2,1,128,384]{3,2,1,0:T(8,128)(2,1)}, bf16[2,1,128,384]{3,2,1,0:T(8,128)(2,1)S(1)}, u32[]{:S(2)}) copy-start(bf16[2,1,128,384]{3,2,1,0:T(8,128)(2,1)S(1)} %get-tuple-element.32) | copy-start | bytes 589828
  49.6 12.1 %copy-start.6 = (bf16[2,1,128,384]{3,2,1,0:T(8,128)(2,1)}, bf16[2,1,128,384]{3,2,1,0:T(8,128)(2,1)S(1)}, u32[]{:S(2)}) copy-start(bf16[2,1,128,384]{3,2,1,0:T(8,128)(2,1)S(1)} %get-tuple-element.33) | copy-start | bytes 589828
  50.6 9.8 %collective-permute-start.4 = (bf16[32,16,768]{2,1,0:T(8,128)(2,1)S(1)}, bf16[32,16,768]{2,1,0:T(8,128)(2,1)}, u32[]{:S(2)}, u32[]{:S(2)}) collective-permute-start(bf16[32,16,768]{2,1,0:T(8,128)(2,1)S(1)} %all-to-all-done), channel_id=1, source_target_pairs={{0,8},{8,0},{1,9},{9,1},{2,10},{10,2},{3,11},{11,3},{4,12},{12,4},... | collective-permute-start | bytes 2359304 | tf_op jit(solution)/shard_map/token_swap/ppermute | solution.py:26
  70.1 1.1 copy-start.18
  70.1 1.1 copy-start.19
  92.7 0.9 copy-start.1
  93.7 0.6 copy-start.15
  95.8 42.1 %all-to-all-start.2 = ((bf16[32,16,1024]{2,1,0:T(8,128)(2,1)}), bf16[32,16,1024]{2,1,0:T(8,128)(2,1)}, u32[]{:S(2)}, u32[]{:S(2)}) async-start(bf16[32,16,1024]{2,1,0:T(8,128)(2,1)} %broadcast_in_dim.21), calls=%async_computation.2 | async-start | bytes 2097152 | tf_op jit(solution)/shard_map/gram/all_to_all | solution.py:31
  109.3 2.6 %copy-start.3 = (bf16[768,384]{1,0:T(8,128)(2,1)S(1)}, bf16[768,384]{1,0:T(8,128)(2,1)}, u32[]{:S(2)}) copy-start(bf16[768,384]{1,0:T(8,128)(2,1)} %param.6) | copy-start | bytes 1769476
  112.9 0.9 copy-start
  113.8 9.6 %collective-permute-start.5 = (bf16[256,384]{1,0:T(8,128)(2,1)S(1)}, bf16[256,384]{1,0:T(8,128)(2,1)S(1)}, u32[]{:S(2)}, u32[]{:S(2)}) collective-permute-start(bf16[256,384]{1,0:T(8,128)(2,1)S(1)} %get-tuple-element.23), channel_id=1, source_target_pairs={{0,1},{1,0},{2,3},{3,2},{4,5},{5,4},{6,7},{7,6},{8,9},{9,8},{10,11... | collective-permute-start | bytes 589832 | tf_op jit(solution)/shard_map/project/ppermute | solution.py:26
  116.0 10.5 %collective-permute-start.6 = (bf16[256,384]{1,0:T(8,128)(2,1)S(1)}, bf16[256,384]{1,0:T(8,128)(2,1)S(1)}, u32[]{:S(2)}, u32[]{:S(2)}) collective-permute-start(bf16[256,384]{1,0:T(8,128)(2,1)S(1)} %get-tuple-element.25), channel_id=1, source_target_pairs={{0,2},{1,3},{2,0},{3,1},{4,6},{5,7},{6,4},{7,5},{8,10},{9,11},{10,... | collective-permute-start | bytes 589832 | tf_op jit(solution)/shard_map/project/ppermute | solution.py:26
  119.7 11.8 %collective-permute-start.7 = (bf16[256,384]{1,0:T(8,128)(2,1)S(1)}, bf16[256,384]{1,0:T(8,128)(2,1)S(1)}, u32[]{:S(2)}, u32[]{:S(2)}) collective-permute-start(bf16[256,384]{1,0:T(8,128)(2,1)S(1)} %get-tuple-element.24), channel_id=1, source_target_pairs={{0,3},{1,2},{2,1},{3,0},{4,7},{5,6},{6,5},{7,4},{8,11},{9,10},{10,... | collective-permute-start | bytes 589832 | tf_op jit(solution)/shard_map/project/ppermute | solution.py:26
  132.5 12.2 %collective-permute-start.8 = (bf16[256,384]{1,0:T(8,128)(2,1)S(1)}, bf16[256,384]{1,0:T(8,128)(2,1)S(1)}, u32[]{:S(2)}, u32[]{:S(2)}) collective-permute-start(bf16[256,384]{1,0:T(8,128)(2,1)S(1)} %fusion.35), channel_id=1, source_target_pairs={{0,4},{4,0},{1,5},{5,1},{2,6},{6,2},{3,7},{7,3},{8,12},{12,8},{9,1... | collective-permute-start | bytes 589832 | tf_op jit(solution)/shard_map/project/ppermute | solution.py:26
  137.8 25.0 %collective-permute-start.12 = (bf16[32,16,1024]{2,1,0:T(8,128)(2,1)}, bf16[32,16,1024]{2,1,0:T(8,128)(2,1)S(1)}, u32[]{:S(2)}, u32[]{:S(2)}) collective-permute-start(bf16[32,16,1024]{2,1,0:T(8,128)(2,1)} %all-to-all-done.2), channel_id=1, source_target_pairs={{0,8},{8,0},{1,9},{9,1},{2,10},{10,2},{3,11},{11,3},{4,12},{12,4},... | collective-permute-start | bytes 3145736 | tf_op jit(solution)/shard_map/gram/ppermute | solution.py:26
  145.8 9.1 %collective-permute-start.10 = (bf16[256,384]{1,0:T(8,128)(2,1)S(1)}, bf16[256,384]{1,0:T(8,128)(2,1)S(1)}, u32[]{:S(2)}, u32[]{:S(2)}) collective-permute-start(bf16[256,384]{1,0:T(8,128)(2,1)S(1)} %multiply_convert_fusion), channel_id=1, source_target_pairs={{0,2},{1,3},{2,0},{3,1},{4,6},{5,7},{6,4},{7,5},{8,10},{9,11},{10,... | collective-permute-start | bytes 589832 | tf_op jit(solution)/shard_map/pre/ppermute | solution.py:26
  148.9 9.1 %collective-permute-start.11 = (bf16[256,384]{1,0:T(8,128)(2,1)S(1)}, bf16[256,384]{1,0:T(8,128)(2,1)S(1)}, u32[]{:S(2)}, u32[]{:S(2)}) collective-permute-start(bf16[256,384]{1,0:T(8,128)(2,1)S(1)} %multiply_convert_fusion), channel_id=1, source_target_pairs={{0,1},{1,0},{2,3},{3,2},{4,5},{5,4},{6,7},{7,6},{8,9},{9,8},{10,11... | collective-permute-start | bytes 589832 | tf_op jit(solution)/shard_map/pre/ppermute | solution.py:26
  153.0 7.6 %collective-permute-start.9 = (bf16[256,384]{1,0:T(8,128)(2,1)S(1)}, bf16[256,384]{1,0:T(8,128)(2,1)S(1)}, u32[]{:S(2)}, u32[]{:S(2)}) collective-permute-start(bf16[256,384]{1,0:T(8,128)(2,1)S(1)} %multiply_convert_fusion), channel_id=1, source_target_pairs={{0,3},{1,2},{2,1},{3,0},{4,7},{5,6},{6,5},{7,4},{8,11},{9,10},{10,... | collective-permute-start | bytes 589832 | tf_op jit(solution)/shard_map/pre/ppermute | solution.py:26
  160.7 3.7 %copy-start.9 = (bf16[256,384]{1,0:T(8,128)(2,1)}, bf16[256,384]{1,0:T(8,128)(2,1)S(1)}, u32[]{:S(2)}) copy-start(bf16[256,384]{1,0:T(8,128)(2,1)S(1)} %get-tuple-element.19) | copy-start | bytes 589828
  160.7 3.7 %copy-start.11 = (bf16[256,384]{1,0:T(8,128)(2,1)}, bf16[256,384]{1,0:T(8,128)(2,1)S(1)}, u32[]{:S(2)}) copy-start(bf16[256,384]{1,0:T(8,128)(2,1)S(1)} %get-tuple-element.20) | copy-start | bytes 589828
  160.7 3.7 %copy-start.13 = (bf16[256,384]{1,0:T(8,128)(2,1)}, bf16[256,384]{1,0:T(8,128)(2,1)S(1)}, u32[]{:S(2)}) copy-start(bf16[256,384]{1,0:T(8,128)(2,1)S(1)} %get-tuple-element.21) | copy-start | bytes 589828
  160.7 3.7 %copy-start.14 = (bf16[256,384]{1,0:T(8,128)(2,1)}, bf16[256,384]{1,0:T(8,128)(2,1)S(1)}, u32[]{:S(2)}) copy-start(bf16[256,384]{1,0:T(8,128)(2,1)S(1)} %get-tuple-element.22) | copy-start | bytes 589828
  160.7 1.1 copy-start.5
  160.8 1.3 copy-start.7
  164.2 1.1 copy-start.8
  171.0 24.8 %all-to-all-start.3 = ((f32[64,1,128]{2,1,0:T(1,128)}), f32[64,1,128]{2,1,0:T(1,128)}, u32[]{:S(2)}, u32[]{:S(2)}) async-start(f32[64,1,128]{2,1,0:T(1,128)} %broadcast_in_dim.22), calls=%async_computation.3 | async-start | bytes 65536 | tf_op jit(solution)/shard_map/ascent/all_to_all | solution.py:31
  186.4 11.6 %copy-start.10 = (bf16[256,384]{1,0:T(8,128)(2,1)S(1)}, bf16[256,384]{1,0:T(8,128)(2,1)}, u32[]{:S(2)}) copy-start(bf16[256,384]{1,0:T(8,128)(2,1)} %copy-done.9) | copy-start | bytes 589828
  186.5 11.6 %copy-start.12 = (bf16[256,384]{1,0:T(8,128)(2,1)S(1)}, bf16[256,384]{1,0:T(8,128)(2,1)}, u32[]{:S(2)}) copy-start(bf16[256,384]{1,0:T(8,128)(2,1)} %copy-done.11) | copy-start | bytes 589828

commit v4 on v2

v4 whole, which is shorter than its diff:
```python
import math

import jax
import jax.numpy as jnp
from jax import lax
from jax.sharding import Mesh
from jax.sharding import PartitionSpec as P

FF = 24576
D = 6144
TOKENS = 1024
DP = ("yl", "z", "c")
MP = ("yh", "x")
BF = jnp.bfloat16
F32 = jnp.float32


def gelu_slope(value):
    cdf = 0.5 * (1.0 + lax.erf(value * (1.0 / math.sqrt(2.0))))
    dens = jnp.exp(-0.5 * value * value) * (1.0 / math.sqrt(2.0 * math.pi))
    return cdf + value * dens


def swap(value, axis, bit):
    size = lax.axis_size(axis)
    return lax.ppermute(value, axis, [(i, i ^ bit) for i in range(size)])


def spread(value, axes, count):
    copies = jnp.broadcast_to(value[None], (count,) + value.shape)
    return lax.all_to_all(copies, axes, 0, 0, tiled=True)


def after(value, *others):
    return lax.optimization_barrier((value,) + others)[0]


def join_cores(mine):
    other = swap(mine, "c", 1)
    even = lax.axis_index("c") == 0
    return jnp.stack([jnp.where(even, mine, other), jnp.where(even, other, mine)], axis=1)


def ordered(blocks, index):
    odd, high = (index & 1) == 1, (index & 2) == 2
    near = [jnp.where(odd, blocks[q ^ 1], blocks[q]) for q in range(4)]
    return [jnp.where(high, near[q ^ 2], near[q]) for q in range(4)]


def gather_x(value):
    return [value] + [swap(value, "x", b) for b in (1, 2, 3)]


def pair_y(value):
    other = swap(value, "yh", 1)
    low = lax.axis_index("yh") == 0
    return jnp.stack([jnp.where(low, value, other), jnp.where(low, other, value)])


def dot(left, right, dims):
    return lax.dot_general(left, right, (dims, ((), ())), preferred_element_type=F32)


def per_device(tokens, norm_gain, w_up, cotangent):
    scale = 1.0 / math.sqrt(TOKENS)
    columns = w_up.shape[1]
    x = lax.axis_index("x")
    with jax.named_scope("stats"):
        values = tokens.astype(F32)
        sums = jnp.concatenate([jnp.sum(values, axis=1), jnp.sum(values * values, axis=1)])
        sums = spread(sums[None], MP, 8)
        pair = pair_y(cotangent)
        sums = jnp.sum(after(sums, pair), axis=(0, 1))
        mean = sums[:16] / D
        var = sums[16:] / D - mean * mean
        inv = lax.rsqrt(var + 1e-06)
        rows = ((values - mean[:, None]) * inv[:, None] * norm_gain[None, :]).astype(BF)
    with jax.named_scope("token_gather"):
        mine = spread(rows, ("yl", "z"), 32)
        cot = gather_x(after(pair, rows))
        normed = join_cores(after(mine, *cot)).reshape(TOKENS, -1)
        cot = jnp.stack(ordered(cot, x), axis=1).reshape(TOKENS, columns)
    with jax.named_scope("gram_part"):
        gram = dot(rows, normed, ((1,), (1,)))
        gram = spread(gram.astype(BF), MP, 8)
    with jax.named_scope("project"):
        part = dot(normed, w_up, ((1,), (0,))).astype(BF).reshape(4, 256, columns)

        def block(b):
            return lax.dynamic_index_in_dim(part, x ^ b, 0, keepdims=False)

        moved = [swap(block(b), "x", b) for b in (1, 2, 3)]
        gram = after(gram, *moved)
        total = block(0).astype(F32) + sum(m.astype(F32) for m in moved)
    with jax.named_scope("gram_gather"):
        gram = jnp.sum(gram.astype(F32), axis=0).astype(BF)
        gram = spread(gram, ("yl", "z"), 32)
    with jax.named_scope("pre"):
        total = total + swap(total.astype(BF), "yh", 1).astype(F32)
        moved = gather_x(total.astype(BF))
        gram = join_cores(after(gram, *moved)).reshape(TOKENS, TOKENS)
        pre = jnp.concatenate(ordered(moved, x), axis=0).astype(F32)

    def slope_at(value):
        return (cot.astype(F32) * gelu_slope(value) * scale).astype(BF)

    with jax.named_scope("ascent"):
        slope = slope_at(pre)
        along = dot(gram, slope, ((1,), (0,)))
        squared = jnp.sum(slope.astype(F32) * along)
        squared = jnp.sum(spread(jnp.full((1, 128), squared), DP, 64)[:, 0, 0])
        size = jnp.sqrt(jnp.maximum(squared, 0.0)) + 1e-12
        radius = 0.5 * math.sqrt(FF)
    with jax.named_scope("sharp"):
        sharp = slope_at(pre + along * (radius / size))
        return dot(normed, sharp, ((0,), (0,)))


def solution(mesh):
    fine = Mesh(mesh.devices.reshape(4, 8, 2, 2, 4), DP + MP)
    placed = (P(DP, MP), P(MP), P(MP, DP), P(MP, DP))
    return jax.shard_map(
        per_device, mesh=fine, in_specs=placed, out_specs=P(MP, DP), check_vma=False
    )
```

time: 180 us -> 183 us (1.017)
  blocking collectives: 65 us -> 22.2 us
  waiting for transfers between devices: 17.7 us -> 50.9 us
  starting transfers between devices: 70.9 us -> 78.9 us
  local copies, waits for them, and re-layouts: 3.63 us -> 6.44 us
  other arithmetic: 12.4 us -> 14.3 us
    all_to_all x3 -> x1, blocking collectives: 65 us -> 22.2 us  [spread(): return lax.all_to_all(copies, axes, 0, 0, tiled=True)]
    ppermute x16 -> x13, waiting for transfers between devices: 14.1 us -> 38.1 us  [swap(): return lax.ppermute(value, axis, [(i, i ^ bit) for i in range(size)])]
    all_to_all x1 -> x4, starting transfers between devices: 7.87 us -> 26.6 us  [spread(): return lax.all_to_all(copies, axes, 0, 0, tiled=True)]
    ppermute x16 -> x13, starting transfers between devices: 63 us -> 52.3 us  [swap(): return lax.ppermute(value, axis, [(i, i ^ bit) for i in range(size)])]
    all_to_all x1 -> x4, waiting for transfers between devices: 3.59 us -> 12.8 us  [spread(): return lax.all_to_all(copies, axes, 0, 0, tiled=True)]
    broadcast_in_dim x4 -> x5, local copies, waits for them, and re-layouts: 1.9 us -> 4.03 us  [spread(): copies = jnp.broadcast_to(value[None], (count,) + value.shape)]
  transfers between devices with their start and end apart: 17 -> 17, of which waited for: 8 -> 10; matrix products, arithmetic and copies ran while one was open for 5% -> 5% of each run, Pallas kernels for 0% -> 0%
where the time goes in v4:
time: 183 us; the launch traced here: 182 us
  starting transfers between devices  78.9 us (43%)
  waiting for transfers between devices  50.9 us (28%)
  blocking collectives  22.2 us (12%)
  other arithmetic  14.3 us (8%)
  matrix products  7.73 us (4%)
  local copies, waits for them, and re-layouts  6.44 us (4%)
    ppermute x13, starting transfers between devices, swap(): return lax.ppermute(value, axis, [(i, i ^ bit) for i in range(size)])  52.3 us
    ppermute x13, waiting for transfers between devices, swap(): return lax.ppermute(value, axis, [(i, i ^ bit) for i in range(size)])  38.1 us
    all_to_all x4, starting transfers between devices, spread(): return lax.all_to_all(copies, axes, 0, 0, tiled=True)  26.6 us
    all_to_all x1, blocking collectives, spread(): return lax.all_to_all(copies, axes, 0, 0, tiled=True)  22.2 us
    all_to_all x4, waiting for transfers between devices, spread(): return lax.all_to_all(copies, axes, 0, 0, tiled=True)  12.8 us
    dot_general x4, matrix products, dot(): lax.dot_general(left, right, (dims, ((), ())), preferred_element_type=F32)  7.73 us
    broadcast_in_dim x5, local copies, waits for them, and re-layouts, spread(): copies = jnp.broadcast_to(value[None], (count,) + value.shape)  4.03 us
    convert_element_type x2, other arithmetic, slope_at(): return (cot.astype(F32) * gelu_slope(value) * scale).astype(BF)  3.75 us
  transfers between devices with their start and end apart: 17, of which 10 were waited for; matrix products, arithmetic and copies ran while one was open for 5% of the time, Pallas kernels for 0%

profile of v4, /device:TPU:1, one launch (start us, length us, event | category | flops | bytes accessed | tf_op | source)
XLA Modules:
  0.0 181.8 jit_solution(2425623472782673500)
XLA Ops:
  0.0 8.4 %collective-permute-start = (bf16[128,384]{1,0:T(8,128)(2,1)}, bf16[128,384]{1,0:T(8,128)(2,1)S(1)}, u32[]{:S(2)}, u32[]{:S(2)}) collective-permute-start(bf16[128,384]{1,0:T(8,128)(2,1)} %param.7), channel_id=1, source_target_pairs={{0,4},{4,0},{1,5},{5,1},{2,6},{6,2},{3,7},{7,3},{8,12},{12,8},{9,1... | collective-permute-start | bytes 294920 | tf_op jit(solution)/shard_map/stats/ppermute | solution.py:26
  8.4 0.9 convert_reduce_fusion
  9.3 0.1 pad_maximum_fusion.4
  9.4 0.6 broadcast_in_dim.10
  10.0 4.0 %all-to-all-start = ((f32[8,1,32]{2,1,0:T(1,128)}), f32[8,1,32]{2,1,0:T(1,128)S(1)}, u32[]{:S(2)}, u32[]{:S(2)}) async-start(f32[8,1,32]{2,1,0:T(1,128)} %broadcast_in_dim.10), calls=%async_computation | async-start | bytes 8192 | tf_op jit(solution)/shard_map/stats/all_to_all | solution.py:31
  14.0 0.0 collective-permute-done
  14.0 0.9 select_bitcast_fusion.9
  14.9 7.9 %all-to-all-done = f32[8,1,32]{2,1,0:T(1,128)S(1)} async-done(((f32[8,1,32]{2,1,0:T(1,128)}), f32[8,1,32]{2,1,0:T(1,128)S(1)}, u32[]{:S(2)}, u32[]{:S(2)}) %all-to-all-start) | async-done | bytes 1056 | tf_op jit(solution)/shard_map/stats/all_to_all | solution.py:31
  22.8 0.1 slice_multiply_fusion
  22.9 0.8 fusion.25
  23.7 0.9 broadcast_in_dim.11
  24.7 13.0 %all-to-all-start.1 = ((bf16[32,16,768]{2,1,0:T(8,128)(2,1)}), bf16[32,16,768]{2,1,0:T(8,128)(2,1)S(1)}, u32[]{:S(2)}, u32[]{:S(2)}) async-start(bf16[32,16,768]{2,1,0:T(8,128)(2,1)} %broadcast_in_dim.11), calls=%async_computation.1 | async-start | bytes 1572864 | tf_op jit(solution)/shard_map/token_gather/all_to_all | solution.py:31
  37.7 2.8 %collective-permute-start.3 = (bf16[2,128,384]{2,1,0:T(8,128)(2,1)S(1)}, bf16[2,128,384]{2,1,0:T(8,128)(2,1)S(1)}, u32[]{:S(2)}, u32[]{:S(2)}) collective-permute-start(bf16[2,128,384]{2,1,0:T(8,128)(2,1)S(1)} %pad_maximum_fusion.3), channel_id=1, source_target_pairs={{0,3},{1,2},{2,1},{3,0},{4,7},{5,6},{6,5},{7,4},{8,11},{9,10},{10,... | collective-permute-start | bytes 589832 | tf_op jit(solution)/shard_map/token_gather/ppermute | solution.py:26
  40.5 3.1 %collective-permute-start.2 = (bf16[2,128,384]{2,1,0:T(8,128)(2,1)S(1)}, bf16[2,128,384]{2,1,0:T(8,128)(2,1)S(1)}, u32[]{:S(2)}, u32[]{:S(2)}) collective-permute-start(bf16[2,128,384]{2,1,0:T(8,128)(2,1)S(1)} %pad_maximum_fusion.3), channel_id=1, source_target_pairs={{0,2},{1,3},{2,0},{3,1},{4,6},{5,7},{6,4},{7,5},{8,10},{9,11},{10,... | collective-permute-start | bytes 589832 | tf_op jit(solution)/shard_map/token_gather/ppermute | solution.py:26
  43.6 3.1 %collective-permute-start.1 = (bf16[2,128,384]{2,1,0:T(8,128)(2,1)S(1)}, bf16[2,128,384]{2,1,0:T(8,128)(2,1)S(1)}, u32[]{:S(2)}, u32[]{:S(2)}) collective-permute-start(bf16[2,128,384]{2,1,0:T(8,128)(2,1)S(1)} %pad_maximum_fusion.3), channel_id=1, source_target_pairs={{0,1},{1,0},{2,3},{3,2},{4,5},{5,4},{6,7},{7,6},{8,9},{9,8},{10,11... | collective-permute-start | bytes 589832 | tf_op jit(solution)/shard_map/token_gather/ppermute | solution.py:26
  46.7 2.0 %collective-permute-done.2 = bf16[2,128,384]{2,1,0:T(8,128)(2,1)S(1)} collective-permute-done((bf16[2,128,384]{2,1,0:T(8,128)(2,1)S(1)}, bf16[2,128,384]{2,1,0:T(8,128)(2,1)S(1)}, u32[]{:S(2)}, u32[]{:S(2)}) %collective-permute-start.2) | collective-permute-done | bytes 196640 | tf_op jit(solution)/shard_map/token_gather/ppermute | solution.py:26
  48.8 2.4 %collective-permute-done.1 = bf16[2,128,384]{2,1,0:T(8,128)(2,1)S(1)} collective-permute-done((bf16[2,128,384]{2,1,0:T(8,128)(2,1)S(1)}, bf16[2,128,384]{2,1,0:T(8,128)(2,1)S(1)}, u32[]{:S(2)}, u32[]{:S(2)}) %collective-permute-start.1) | collective-permute-done | bytes 196640 | tf_op jit(solution)/shard_map/token_gather/ppermute | solution.py:26
  51.2 0.7 copy-done.16
  51.9 5.0 %all-to-all-done.1 = bf16[32,16,768]{2,1,0:T(8,128)(2,1)S(1)} async-done(((bf16[32,16,768]{2,1,0:T(8,128)(2,1)}), bf16[32,16,768]{2,1,0:T(8,128)(2,1)S(1)}, u32[]{:S(2)}, u32[]{:S(2)}) %all-to-all-start.1) | async-done | bytes 786464 | tf_op jit(solution)/shard_map/token_gather/all_to_all | solution.py:31
  56.8 5.5 %collective-permute-start.4 = (bf16[32,16,768]{2,1,0:T(8,128)(2,1)S(1)}, bf16[32,16,768]{2,1,0:T(8,128)(2,1)S(1)}, u32[]{:S(2)}, u32[]{:S(2)}) collective-permute-start(bf16[32,16,768]{2,1,0:T(8,128)(2,1)S(1)} %all-to-all-done.1), channel_id=1, source_target_pairs={{0,8},{8,0},{1,9},{9,1},{2,10},{10,2},{3,11},{11,3},{4,12},{12,4},... | collective-permute-start | bytes 2359304 | tf_op jit(solution)/shard_map/token_gather/ppermute | solution.py:26
  62.4 1.9 %collective-permute-done.4 = bf16[32,16,768]{2,1,0:T(8,128)(2,1)S(1)} collective-permute-done((bf16[32,16,768]{2,1,0:T(8,128)(2,1)S(1)}, bf16[32,16,768]{2,1,0:T(8,128)(2,1)S(1)}, u32[]{:S(2)}, u32[]{:S(2)}) %collective-permute-start.4) | collective-permute-done | bytes 786464 | tf_op jit(solution)/shard_map/token_gather/ppermute | solution.py:26
  64.2 0.1 select_bitcast_fusion.3
  64.3 0.1 pad_maximum_fusion.1
  64.5 0.5 convolution_convert_fusion.1
  65.0 0.8 broadcast_in_dim.12
  65.7 3.4 %all-to-all-start.2 = ((bf16[8,16,1024]{2,1,0:T(8,128)(2,1)}), bf16[8,16,1024]{2,1,0:T(8,128)(2,1)S(1)}, u32[]{:S(2)}, u32[]{:S(2)}) async-start(bf16[8,16,1024]{2,1,0:T(8,128)(2,1)} %broadcast_in_dim.12), calls=%async_computation.2 | async-start | bytes 524288 | tf_op jit(solution)/shard_map/gram_part/all_to_all | solution.py:31
  69.2 1.0 convolution_convert_fusion
  70.2 0.9 copy-done.8
  71.1 0.1 dynamic-slice_bitcast_fusion
  71.1 4.5 %collective-permute-start.7 = (bf16[256,384]{1,0:T(8,128)(2,1)S(1)}, bf16[256,384]{1,0:T(8,128)(2,1)S(1)}, u32[]{:S(2)}, u32[]{:S(2)}) collective-permute-start(bf16[256,384]{1,0:T(8,128)(2,1)S(1)} %get-tuple-element.29), channel_id=1, source_target_pairs={{0,3},{1,2},{2,1},{3,0},{4,7},{5,6},{6,5},{7,4},{8,11},{9,10},{10,... | collective-permute-start | bytes 589832 | tf_op jit(solution)/shard_map/project/ppermute | solution.py:26
  75.6 2.5 %collective-permute-start.6 = (bf16[256,384]{1,0:T(8,128)(2,1)S(1)}, bf16[256,384]{1,0:T(8,128)(2,1)S(1)}, u32[]{:S(2)}, u32[]{:S(2)}) collective-permute-start(bf16[256,384]{1,0:T(8,128)(2,1)S(1)} %get-tuple-element.30), channel_id=1, source_target_pairs={{0,2},{1,3},{2,0},{3,1},{4,6},{5,7},{6,4},{7,5},{8,10},{9,11},{10,... | collective-permute-start | bytes 589832 | tf_op jit(solution)/shard_map/project/ppermute | solution.py:26
  78.1 2.0 %collective-permute-start.5 = (bf16[256,384]{1,0:T(8,128)(2,1)S(1)}, bf16[256,384]{1,0:T(8,128)(2,1)S(1)}, u32[]{:S(2)}, u32[]{:S(2)}) collective-permute-start(bf16[256,384]{1,0:T(8,128)(2,1)S(1)} %get-tuple-element.31), channel_id=1, source_target_pairs={{0,1},{1,0},{2,3},{3,2},{4,5},{5,4},{6,7},{7,6},{8,9},{9,8},{10,11... | collective-permute-start | bytes 589832 | tf_op jit(solution)/shard_map/project/ppermute | solution.py:26
  80.1 4.5 %collective-permute-done.7 = bf16[256,384]{1,0:T(8,128)(2,1)S(1)} collective-permute-done((bf16[256,384]{1,0:T(8,128)(2,1)S(1)}, bf16[256,384]{1,0:T(8,128)(2,1)S(1)}, u32[]{:S(2)}, u32[]{:S(2)}) %collective-permute-start.7) | collective-permute-done | bytes 196640 | tf_op jit(solution)/shard_map/project/ppermute | solution.py:26
  84.6 0.0 collective-permute-done.6
  84.6 2.3 %collective-permute-done.5 = bf16[256,384]{1,0:T(8,128)(2,1)S(1)} collective-permute-done((bf16[256,384]{1,0:T(8,128)(2,1)S(1)}, bf16[256,384]{1,0:T(8,128)(2,1)S(1)}, u32[]{:S(2)}, u32[]{:S(2)}) %collective-permute-start.5) | collective-permute-done | bytes 196640 | tf_op jit(solution)/shard_map/project/ppermute | solution.py:26
  87.0 0.0 all-to-all-done.2
  87.0 1.1 broadcast_in_dim.13
  88.1 6.1 %all-to-all-start.3 = ((bf16[32,16,1024]{2,1,0:T(8,128)(2,1)}), bf16[32,16,1024]{2,1,0:T(8,128)(2,1)S(1)}, u32[]{:S(2)}, u32[]{:S(2)}) async-start(bf16[32,16,1024]{2,1,0:T(8,128)(2,1)} %broadcast_in_dim.13), calls=%async_computation.3 | async-start | bytes 2097152 | tf_op jit(solution)/shard_map/gram_gather/all_to_all | solution.py:31
  94.3 1.2 fusion.21
  95.5 6.6 %collective-permute-start.8 = (bf16[256,384]{1,0:T(8,128)(2,1)S(1)}, bf16[256,384]{1,0:T(8,128)(2,1)S(1)}, u32[]{:S(2)}, u32[]{:S(2)}) collective-permute-start(bf16[256,384]{1,0:T(8,128)(2,1)S(1)} %fusion.21), channel_id=1, source_target_pairs={{0,4},{4,0},{1,5},{5,1},{2,6},{6,2},{3,7},{7,3},{8,12},{12,8},{9,1... | collective-permute-start | bytes 589832 | tf_op jit(solution)/shard_map/pre/ppermute | solution.py:26
  102.1 17.6 %collective-permute-done.8 = bf16[256,384]{1,0:T(8,128)(2,1)S(1)} collective-permute-done((bf16[256,384]{1,0:T(8,128)(2,1)S(1)}, bf16[256,384]{1,0:T(8,128)(2,1)S(1)}, u32[]{:S(2)}, u32[]{:S(2)}) %collective-permute-start.8) | collective-permute-done | bytes 196640 | tf_op jit(solution)/shard_map/pre/ppermute | solution.py:26
  119.7 1.2 add_convert_fusion
  120.9 3.1 %collective-permute-start.11 = (bf16[256,384]{1,0:T(8,128)(2,1)S(1)}, bf16[256,384]{1,0:T(8,128)(2,1)S(1)}, u32[]{:S(2)}, u32[]{:S(2)}) collective-permute-start(bf16[256,384]{1,0:T(8,128)(2,1)S(1)} %add_convert_fusion), channel_id=1, source_target_pairs={{0,1},{1,0},{2,3},{3,2},{4,5},{5,4},{6,7},{7,6},{8,9},{9,8},{10,11... | collective-permute-start | bytes 589832 | tf_op jit(solution)/shard_map/pre/ppermute | solution.py:26
  124.0 4.3 %collective-permute-start.10 = (bf16[256,384]{1,0:T(8,128)(2,1)S(1)}, bf16[256,384]{1,0:T(8,128)(2,1)S(1)}, u32[]{:S(2)}, u32[]{:S(2)}) collective-permute-start(bf16[256,384]{1,0:T(8,128)(2,1)S(1)} %add_convert_fusion), channel_id=1, source_target_pairs={{0,2},{1,3},{2,0},{3,1},{4,6},{5,7},{6,4},{7,5},{8,10},{9,11},{10,... | collective-permute-start | bytes 589832 | tf_op jit(solution)/shard_map/pre/ppermute | solution.py:26
  128.3 2.2 %collective-permute-start.9 = (bf16[256,384]{1,0:T(8,128)(2,1)S(1)}, bf16[256,384]{1,0:T(8,128)(2,1)}, u32[]{:S(2)}, u32[]{:S(2)}) collective-permute-start(bf16[256,384]{1,0:T(8,128)(2,1)S(1)} %add_convert_fusion), channel_id=1, source_target_pairs={{0,3},{1,2},{2,1},{3,0},{4,7},{5,6},{6,5},{7,4},{8,11},{9,10},{10,... | collective-permute-start | bytes 589832 | tf_op jit(solution)/shard_map/pre/ppermute | solution.py:26
  130.5 0.0 collective-permute-done.11
  130.6 2.5 %collective-permute-done.10 = bf16[256,384]{1,0:T(8,128)(2,1)S(1)} collective-permute-done((bf16[256,384]{1,0:T(8,128)(2,1)S(1)}, bf16[256,384]{1,0:T(8,128)(2,1)S(1)}, u32[]{:S(2)}, u32[]{:S(2)}) %collective-permute-start.10) | collective-permute-done | bytes 196640 | tf_op jit(solution)/shard_map/pre/ppermute | solution.py:26
  133.0 0.7 copy-done.19
  133.7 4.8 %collective-permute-done.9 = bf16[256,384]{1,0:T(8,128)(2,1)} collective-permute-done((bf16[256,384]{1,0:T(8,128)(2,1)S(1)}, bf16[256,384]{1,0:T(8,128)(2,1)}, u32[]{:S(2)}, u32[]{:S(2)}) %collective-permute-start.9) | collective-permute-done | bytes 196640 | tf_op jit(solution)/shard_map/pre/ppermute | solution.py:26
  138.5 4.3 %collective-permute-start.12 = (bf16[32,16,1024]{2,1,0:T(8,128)(2,1)S(1)}, bf16[32,16,1024]{2,1,0:T(8,128)(2,1)}, u32[]{:S(2)}, u32[]{:S(2)}) collective-permute-start(bf16[32,16,1024]{2,1,0:T(8,128)(2,1)S(1)} %all-to-all-done.3), channel_id=1, source_target_pairs={{0,8},{8,0},{1,9},{9,1},{2,10},{10,2},{3,11},{11,3},{4,12},{12,4},... | collective-permute-start | bytes 3145736 | tf_op jit(solution)/shard_map/pre/ppermute | solution.py:26
  142.9 1.4 select_bitcast_fusion.7
  144.3 0.0 copy-done.20
  144.3 1.2 broadcast_select_fusion.7
  145.6 0.0 copy-start.7
  145.6 0.1 maximum_convert_fusion
  145.8 0.8 fusion.6
  146.6 1.4 select_bitcast_fusion.1
  148.0 0.2 pad_maximum_fusion
  148.2 4.2 %multiply_reduce_fusion = (f32[]{:T(128)}, f32[1024,384]{1,0:T(8,128)}) fusion(bf16[256,384]{1,0:T(8,128)(2,1)S(1)} %get-tuple-element.28, bf16[256,384]{1,0:T(8,128)(2,1)S(1)} %get-tuple-element.27, bf16[256,384]{1,0:T(8,128)(2,1)S(1)} %get-tuple-element.26, bf16[256,384]{1,0:T(8,128)(2,1)S(1)} %get-tuple-element.25, ...), kind=kOutput, calls=%fused_computation.26 | convolution fusion | flops 817102848 | bytes 6029316 | tf_op jit(solution)/shard_map/ascent/dot_general | solution.py:61
  152.5 0.6 broadcast_in_dim.14
  153.1 22.2 %all_to_all.25 = f32[64,1,128]{2,1,0:T(1,128)S(1)} all-to-all(f32[64,1,128]{2,1,0:T(1,128)S(1)} %broadcast_in_dim.14), channel_id=1, replica_groups=mesh['yl'=4,'z'=8,'c'=2,'yh'=2,'x'=4] {'yl','z','c'}, dimensions={0} | all-to-all | bytes 65536 | tf_op jit(solution)/shard_map/ascent/all_to_all | solution.py:31
  175.4 0.7 slice_reduce_fusion
  176.8 2.9 %fusion.20 = bf16[1024,384]{1,0:T(8,128)(2,1)S(1)} fusion(f32[1024,384]{1,0:T(8,128)} %get-tuple-element.37, f32[]{:T(128)S(6)} %div.11, bf16[256,384]{1,0:T(8,128)(2,1)} %copy-done.7, bf16[256,384]{1,0:T(8,128)(2,1)} %copy-done.6, bf16[256,384]{1,0:T(8,128)(2,1)} %copy-done.5, bf16[256,384]{1,0:T(8,128)(2,1)} %copy-done.4, ...), kind=kLoop, calls=%fused_computation.24 | loop fusion | flops 11403264 | bytes 3932164 | tf_op jit(solution)/shard_map/sharp/convert_element_type | solution.py:105
  179.7 2.0 %fusion.26 = f32[768,384]{1,0:T(8,128)} fusion(bf16[1024,768]{1,0:T(8,128)(2,1)S(1)} %bitcast.63, bf16[1024,384]{1,0:T(8,128)(2,1)S(1)} %fusion.20), kind=kOutput, calls=%fused_computation.71 | convolution fusion | flops 603979776 | bytes 3538944 | tf_op jit(solution)/shard_map/sharp/dot_general | solution.py:61
  (43 shorter events, 0.2 us)
Async XLA Ops:
  0.0 69.2 %copy-start = (bf16[768,384]{1,0:T(8,128)(2,1)S(1)}, bf16[768,384]{1,0:T(8,128)(2,1)}, u32[]{:S(2)}) copy-start(bf16[768,384]{1,0:T(8,128)(2,1)} %param.6) | copy-start | bytes 1769476
  0.0 14.0 %collective-permute-start = (bf16[128,384]{1,0:T(8,128)(2,1)}, bf16[128,384]{1,0:T(8,128)(2,1)S(1)}, u32[]{:S(2)}, u32[]{:S(2)}) collective-permute-start(bf16[128,384]{1,0:T(8,128)(2,1)} %param.7), channel_id=1, source_target_pairs={{0,4},{4,0},{1,5},{5,1},{2,6},{6,2},{3,7},{7,3},{8,12},{12,8},{9,1... | collective-permute-start | bytes 294920 | tf_op jit(solution)/shard_map/stats/ppermute | solution.py:26
  10.0 12.9 %all-to-all-start = ((f32[8,1,32]{2,1,0:T(1,128)}), f32[8,1,32]{2,1,0:T(1,128)S(1)}, u32[]{:S(2)}, u32[]{:S(2)}) async-start(f32[8,1,32]{2,1,0:T(1,128)} %broadcast_in_dim.10), calls=%async_computation | async-start | bytes 8192 | tf_op jit(solution)/shard_map/stats/all_to_all | solution.py:31
  14.9 49.4 %copy-start.11 = (bf16[2,128,384]{2,1,0:T(8,128)(2,1)}, bf16[2,128,384]{2,1,0:T(8,128)(2,1)S(1)}, u32[]{:S(2)}) copy-start(bf16[2,128,384]{2,1,0:T(8,128)(2,1)S(1)} %pad_maximum_fusion.3) | copy-start | bytes 589828
  24.7 32.2 %all-to-all-start.1 = ((bf16[32,16,768]{2,1,0:T(8,128)(2,1)}), bf16[32,16,768]{2,1,0:T(8,128)(2,1)S(1)}, u32[]{:S(2)}, u32[]{:S(2)}) async-start(bf16[32,16,768]{2,1,0:T(8,128)(2,1)} %broadcast_in_dim.11), calls=%async_computation.1 | async-start | bytes 1572864 | tf_op jit(solution)/shard_map/token_gather/all_to_all | solution.py:31
  37.7 9.0 %collective-permute-start.3 = (bf16[2,128,384]{2,1,0:T(8,128)(2,1)S(1)}, bf16[2,128,384]{2,1,0:T(8,128)(2,1)S(1)}, u32[]{:S(2)}, u32[]{:S(2)}) collective-permute-start(bf16[2,128,384]{2,1,0:T(8,128)(2,1)S(1)} %pad_maximum_fusion.3), channel_id=1, source_target_pairs={{0,3},{1,2},{2,1},{3,0},{4,7},{5,6},{6,5},{7,4},{8,11},{9,10},{10,... | collective-permute-start | bytes 589832 | tf_op jit(solution)/shard_map/token_gather/ppermute | solution.py:26
  40.5 8.3 %collective-permute-start.2 = (bf16[2,128,384]{2,1,0:T(8,128)(2,1)S(1)}, bf16[2,128,384]{2,1,0:T(8,128)(2,1)S(1)}, u32[]{:S(2)}, u32[]{:S(2)}) collective-permute-start(bf16[2,128,384]{2,1,0:T(8,128)(2,1)S(1)} %pad_maximum_fusion.3), channel_id=1, source_target_pairs={{0,2},{1,3},{2,0},{3,1},{4,6},{5,7},{6,4},{7,5},{8,10},{9,11},{10,... | collective-permute-start | bytes 589832 | tf_op jit(solution)/shard_map/token_gather/ppermute | solution.py:26
  43.6 7.6 %collective-permute-start.1 = (bf16[2,128,384]{2,1,0:T(8,128)(2,1)S(1)}, bf16[2,128,384]{2,1,0:T(8,128)(2,1)S(1)}, u32[]{:S(2)}, u32[]{:S(2)}) collective-permute-start(bf16[2,128,384]{2,1,0:T(8,128)(2,1)S(1)} %pad_maximum_fusion.3), channel_id=1, source_target_pairs={{0,1},{1,0},{2,3},{3,2},{4,5},{5,4},{6,7},{7,6},{8,9},{9,8},{10,11... | collective-permute-start | bytes 589832 | tf_op jit(solution)/shard_map/token_gather/ppermute | solution.py:26
  46.7 4.5 %copy-start.14 = (bf16[2,128,384]{2,1,0:T(8,128)(2,1)}, bf16[2,128,384]{2,1,0:T(8,128)(2,1)S(1)}, u32[]{:S(2)}) copy-start(bf16[2,128,384]{2,1,0:T(8,128)(2,1)S(1)} %collective-permute-done.3) | copy-start | bytes 589828
  48.7 2.4 %copy-start.15 = (bf16[2,128,384]{2,1,0:T(8,128)(2,1)}, bf16[2,128,384]{2,1,0:T(8,128)(2,1)S(1)}, u32[]{:S(2)}) copy-start(bf16[2,128,384]{2,1,0:T(8,128)(2,1)S(1)} %collective-permute-done.2) | copy-start | bytes 589828
  51.2 0.7 copy-start.16
  56.8 7.4 %collective-permute-start.4 = (bf16[32,16,768]{2,1,0:T(8,128)(2,1)S(1)}, bf16[32,16,768]{2,1,0:T(8,128)(2,1)S(1)}, u32[]{:S(2)}, u32[]{:S(2)}) collective-permute-start(bf16[32,16,768]{2,1,0:T(8,128)(2,1)S(1)} %all-to-all-done.1), channel_id=1, source_target_pairs={{0,8},{8,0},{1,9},{9,1},{2,10},{10,2},{3,11},{11,3},{4,12},{12,4},... | collective-permute-start | bytes 2359304 | tf_op jit(solution)/shard_map/token_gather/ppermute | solution.py:26
  65.7 21.2 %all-to-all-start.2 = ((bf16[8,16,1024]{2,1,0:T(8,128)(2,1)}), bf16[8,16,1024]{2,1,0:T(8,128)(2,1)S(1)}, u32[]{:S(2)}, u32[]{:S(2)}) async-start(bf16[8,16,1024]{2,1,0:T(8,128)(2,1)} %broadcast_in_dim.12), calls=%async_computation.2 | async-start | bytes 524288 | tf_op jit(solution)/shard_map/gram_part/all_to_all | solution.py:31
  70.2 0.9 copy-start.8
  71.1 13.5 %collective-permute-start.7 = (bf16[256,384]{1,0:T(8,128)(2,1)S(1)}, bf16[256,384]{1,0:T(8,128)(2,1)S(1)}, u32[]{:S(2)}, u32[]{:S(2)}) collective-permute-start(bf16[256,384]{1,0:T(8,128)(2,1)S(1)} %get-tuple-element.29), channel_id=1, source_target_pairs={{0,3},{1,2},{2,1},{3,0},{4,7},{5,6},{6,5},{7,4},{8,11},{9,10},{10,... | collective-permute-start | bytes 589832 | tf_op jit(solution)/shard_map/project/ppermute | solution.py:26
  75.6 9.0 %collective-permute-start.6 = (bf16[256,384]{1,0:T(8,128)(2,1)S(1)}, bf16[256,384]{1,0:T(8,128)(2,1)S(1)}, u32[]{:S(2)}, u32[]{:S(2)}) collective-permute-start(bf16[256,384]{1,0:T(8,128)(2,1)S(1)} %get-tuple-element.30), channel_id=1, source_target_pairs={{0,2},{1,3},{2,0},{3,1},{4,6},{5,7},{6,4},{7,5},{8,10},{9,11},{10,... | collective-permute-start | bytes 589832 | tf_op jit(solution)/shard_map/project/ppermute | solution.py:26
  78.1 8.9 %collective-permute-start.5 = (bf16[256,384]{1,0:T(8,128)(2,1)S(1)}, bf16[256,384]{1,0:T(8,128)(2,1)S(1)}, u32[]{:S(2)}, u32[]{:S(2)}) collective-permute-start(bf16[256,384]{1,0:T(8,128)(2,1)S(1)} %get-tuple-element.31), channel_id=1, source_target_pairs={{0,1},{1,0},{2,3},{3,2},{4,5},{5,4},{6,7},{7,6},{8,9},{9,8},{10,11... | collective-permute-start | bytes 589832 | tf_op jit(solution)/shard_map/project/ppermute | solution.py:26
  84.6 3.5 %copy-start.9 = (bf16[256,384]{1,0:T(8,128)(2,1)}, bf16[256,384]{1,0:T(8,128)(2,1)S(1)}, u32[]{:S(2)}) copy-start(bf16[256,384]{1,0:T(8,128)(2,1)S(1)} %collective-permute-done.6) | copy-start | bytes 589828
  87.0 1.2 copy-start.10
  88.1 50.4 %all-to-all-start.3 = ((bf16[32,16,1024]{2,1,0:T(8,128)(2,1)}), bf16[32,16,1024]{2,1,0:T(8,128)(2,1)S(1)}, u32[]{:S(2)}, u32[]{:S(2)}) async-start(bf16[32,16,1024]{2,1,0:T(8,128)(2,1)} %broadcast_in_dim.13), calls=%async_computation.3 | async-start | bytes 2097152 | tf_op jit(solution)/shard_map/gram_gather/all_to_all | solution.py:31
  95.5 24.2 %collective-permute-start.8 = (bf16[256,384]{1,0:T(8,128)(2,1)S(1)}, bf16[256,384]{1,0:T(8,128)(2,1)S(1)}, u32[]{:S(2)}, u32[]{:S(2)}) collective-permute-start(bf16[256,384]{1,0:T(8,128)(2,1)S(1)} %fusion.21), channel_id=1, source_target_pairs={{0,4},{4,0},{1,5},{5,1},{2,6},{6,2},{3,7},{7,3},{8,12},{12,8},{9,1... | collective-permute-start | bytes 589832 | tf_op jit(solution)/shard_map/pre/ppermute | solution.py:26
  120.9 12.1 %copy-start.12 = (bf16[256,384]{1,0:T(8,128)(2,1)}, bf16[256,384]{1,0:T(8,128)(2,1)S(1)}, u32[]{:S(2)}) copy-start(bf16[256,384]{1,0:T(8,128)(2,1)S(1)} %add_convert_fusion) | copy-start | bytes 589828
  120.9 9.6 %collective-permute-start.11 = (bf16[256,384]{1,0:T(8,128)(2,1)S(1)}, bf16[256,384]{1,0:T(8,128)(2,1)S(1)}, u32[]{:S(2)}, u32[]{:S(2)}) collective-permute-start(bf16[256,384]{1,0:T(8,128)(2,1)S(1)} %add_convert_fusion), channel_id=1, source_target_pairs={{0,1},{1,0},{2,3},{3,2},{4,5},{5,4},{6,7},{7,6},{8,9},{9,8},{10,11... | collective-permute-start | bytes 589832 | tf_op jit(solution)/shard_map/pre/ppermute | solution.py:26
  124.0 9.0 %collective-permute-start.10 = (bf16[256,384]{1,0:T(8,128)(2,1)S(1)}, bf16[256,384]{1,0:T(8,128)(2,1)S(1)}, u32[]{:S(2)}, u32[]{:S(2)}) collective-permute-start(bf16[256,384]{1,0:T(8,128)(2,1)S(1)} %add_convert_fusion), channel_id=1, source_target_pairs={{0,2},{1,3},{2,0},{3,1},{4,6},{5,7},{6,4},{7,5},{8,10},{9,11},{10,... | collective-permute-start | bytes 589832 | tf_op jit(solution)/shard_map/pre/ppermute | solution.py:26
  128.3 10.2 %collective-permute-start.9 = (bf16[256,384]{1,0:T(8,128)(2,1)S(1)}, bf16[256,384]{1,0:T(8,128)(2,1)}, u32[]{:S(2)}, u32[]{:S(2)}) collective-permute-start(bf16[256,384]{1,0:T(8,128)(2,1)S(1)} %add_convert_fusion), channel_id=1, source_target_pairs={{0,3},{1,2},{2,1},{3,0},{4,7},{5,6},{6,5},{7,4},{8,11},{9,10},{10,... | collective-permute-start | bytes 589832 | tf_op jit(solution)/shard_map/pre/ppermute | solution.py:26
  130.5 2.5 %copy-start.17 = (bf16[256,384]{1,0:T(8,128)(2,1)}, bf16[256,384]{1,0:T(8,128)(2,1)S(1)}, u32[]{:S(2)}) copy-start(bf16[256,384]{1,0:T(8,128)(2,1)S(1)} %collective-permute-done.11) | copy-start | bytes 589828
  133.0 0.7 copy-start.19
  138.5 8.0 %collective-permute-start.12 = (bf16[32,16,1024]{2,1,0:T(8,128)(2,1)S(1)}, bf16[32,16,1024]{2,1,0:T(8,128)(2,1)}, u32[]{:S(2)}, u32[]{:S(2)}) collective-permute-start(bf16[32,16,1024]{2,1,0:T(8,128)(2,1)S(1)} %all-to-all-done.3), channel_id=1, source_target_pairs={{0,8},{8,0},{1,9},{9,1},{2,10},{10,2},{3,11},{11,3},{4,12},{12,4},... | collective-permute-start | bytes 3145736 | tf_op jit(solution)/shard_map/pre/ppermute | solution.py:26
  142.9 1.4 copy-start.13
  142.9 1.4 copy-start.18
  142.9 1.4 copy-start.20
  144.3 3.8 %copy-start.1 = (bf16[2,1,128,384]{3,2,1,0:T(8,128)(2,1)}, bf16[2,1,128,384]{3,2,1,0:T(8,128)(2,1)S(1)}, u32[]{:S(2)}) copy-start(bf16[2,1,128,384]{3,2,1,0:T(8,128)(2,1)S(1)} %get-tuple-element.22) | copy-start | bytes 589828
  144.3 3.9 %copy-start.2 = (bf16[2,1,128,384]{3,2,1,0:T(8,128)(2,1)}, bf16[2,1,128,384]{3,2,1,0:T(8,128)(2,1)S(1)}, u32[]{:S(2)}) copy-start(bf16[2,1,128,384]{3,2,1,0:T(8,128)(2,1)S(1)} %get-tuple-element.23) | copy-start | bytes 589828
  144.3 3.9 %copy-start.3 = (bf16[2,1,128,384]{3,2,1,0:T(8,128)(2,1)}, bf16[2,1,128,384]{3,2,1,0:T(8,128)(2,1)S(1)}, u32[]{:S(2)}) copy-start(bf16[2,1,128,384]{3,2,1,0:T(8,128)(2,1)S(1)} %get-tuple-element.24) | copy-start | bytes 589828
  145.6 2.6 %copy-start.4 = (bf16[256,384]{1,0:T(8,128)(2,1)}, bf16[256,384]{1,0:T(8,128)(2,1)S(1)}, u32[]{:S(2)}) copy-start(bf16[256,384]{1,0:T(8,128)(2,1)S(1)} %get-tuple-element.25) | copy-start | bytes 589828
  145.6 2.6 %copy-start.5 = (bf16[256,384]{1,0:T(8,128)(2,1)}, bf16[256,384]{1,0:T(8,128)(2,1)S(1)}, u32[]{:S(2)}) copy-start(bf16[256,384]{1,0:T(8,128)(2,1)S(1)} %get-tuple-element.26) | copy-start | bytes 589828
  145.6 2.6 %copy-start.6 = (bf16[256,384]{1,0:T(8,128)(2,1)}, bf16[256,384]{1,0:T(8,128)(2,1)S(1)}, u32[]{:S(2)}) copy-start(bf16[256,384]{1,0:T(8,128)(2,1)S(1)} %get-tuple-element.27) | copy-start | bytes 589828
  145.6 2.6 %copy-start.7 = (bf16[256,384]{1,0:T(8,128)(2,1)}, bf16[256,384]{1,0:T(8,128)(2,1)S(1)}, u32[]{:S(2)}) copy-start(bf16[256,384]{1,0:T(8,128)(2,1)S(1)} %get-tuple-element.28) | copy-start | bytes 589828

commit v5 on v4

--- a/solution.py
+++ b/solution.py
@@ -3,6 +3,8 @@
 import jax
 import jax.numpy as jnp
 from jax import lax
+from jax.experimental import pallas as pl
+from jax.experimental.pallas import tpu as pltpu
 from jax.sharding import Mesh
 from jax.sharding import PartitionSpec as P
 
@@ -57,48 +59,128 @@
     return jnp.stack([jnp.where(low, value, other), jnp.where(low, other, value)])
 
 
-def dot(left, right, dims):
-    return lax.dot_general(left, right, (dims, ((), ())), preferred_element_type=F32)
+def dot(left, right, dims, precision=None):
+    return lax.dot_general(left, right, (dims, ((), ())), precision=precision, preferred_element_type=F32)
+
+
+def split(value, count):
+    out = []
+    for _ in range(count):
+        out.append(value.astype(BF).astype(F32))
+        value = value - out[-1]
+    return out
+
+
+def local_kernel(at, mine, other, gain, w, joined, own, near, opposite, far, sent, high, part):
+    place, core, x = at[0], at[1], at[2]
+    g = gain[...]
+    width = g.shape[1]
+    ones = jnp.ones((8, width), BF)
+    gains = jnp.concatenate(split(g, 3) + [jnp.zeros((5, width), F32)], axis=0).astype(BF)
+    local, css, lean = [], [], []
+    for i in range(8):
+        chips = pl.ds(4 * i, 4)
+        joined[chips, core] = mine[chips]
+        joined[chips, 1 - core] = other[chips]
+        raw = joined[chips].reshape(128, width)
+        value = raw.astype(F32)
+        centred = value - jnp.sum(value, axis=1, keepdims=True) * (1.0 / width)
+        full = centred * g
+        first = full.astype(BF)
+        second = (full - first.astype(F32)).astype(BF)
+        high[pl.ds(128 * i, 128)] = first
+        rows = dot(first, w[...], ((1,), (0,))) + dot(second, w[...], ((1,), (0,)))
+        part[i // 2, pl.ds(128 * (i % 2), 128)] = rows
+        square = centred * centred
+        top = square.astype(BF)
+        rest = (square - top.astype(F32)).astype(BF)
+        across = ((1,), (1,))
+        local.append(dot(ones, raw, across)[:1] * (1.0 / width))
+        css.append((dot(ones, top, across) + dot(ones, rest, across))[:1])
+        lean.append(jnp.sum(dot(gains, first, across), axis=0, keepdims=True))
+    own[...] = part[x]
+    near[...] = part[x ^ 1].astype(BF)
+    opposite[...] = part[x ^ 2].astype(BF)
+    far[...] = part[x ^ 3].astype(BF)
+    gram = dot(high[pl.ds(pl.multiple_of(place * 16, 16), 16)], high[...], ((1,), (1,)))
+    local, css, lean = (jnp.concatenate(v, axis=1) for v in (local, css, lean))
+    column = jnp.sum(dot(gains, w[...], ((1,), (0,))), axis=0, keepdims=True)
+    power = jnp.broadcast_to(jnp.sum(g * g, axis=1, keepdims=True), (1, 128))
+    extra = jnp.concatenate(split(column, 2) + split(power, 2), axis=1)
+    rows = [gram] + split(local, 3) + split(css, 2) + split(lean, 2) + [extra, jnp.zeros((8, TOKENS), F32)]
+    sent[...] = jnp.concatenate(rows, axis=0).astype(BF)
+
+
+def local_work(at, mine, other, gain, w):
+    width, columns = w.shape
+    block = jax.ShapeDtypeStruct((256, columns), BF)
+    vmem = pl.BlockSpec(memory_space=pltpu.VMEM)
+    return pl.pallas_call(
+        local_kernel,
+        out_shape=[
+            jax.ShapeDtypeStruct((32, 2, 16, width), BF),
+            jax.ShapeDtypeStruct((256, columns), F32),
+            block,
+            block,
+            block,
+            jax.ShapeDtypeStruct((32, TOKENS), BF),
+        ],
+        in_specs=[pl.BlockSpec(memory_space=pltpu.SMEM)] + [vmem] * 4,
+        out_specs=[vmem] * 6,
+        scratch_shapes=[pltpu.VMEM((TOKENS, width), BF), pltpu.VMEM((4, 256, columns), F32)],
+        compiler_params=pltpu.CompilerParams(vmem_limit_bytes=40 << 20),
+        cost_estimate=pl.CostEstimate(flops=2 * TOKENS * width * columns * 2, bytes_accessed=8 << 20, transcendentals=0),
+        name="local_work",
+    )(at, mine, other, gain, w)
 
 
 def per_device(tokens, norm_gain, w_up, cotangent):
     scale = 1.0 / math.sqrt(TOKENS)
-    columns = w_up.shape[1]
+    width, columns = w_up.shape
     x = lax.axis_index("x")
+    place = lax.axis_index(DP)
+    exact = lax.Precision.HIGHEST
+    with jax.named_scope("token_gather"):
+        mine = spread(tokens, ("yl", "z"), 32)
+        other = swap(mine, "c", 1)
+    with jax.named_scope("local_work"):
+        at = jnp.stack([place, lax.axis_index("c"), x]).astype(jnp.int32)
+        joined, total, near, opposite, far, sent = local_work(at, mine, other, norm_gain[None], w_up)
+    with jax.named_scope("sums_x"):
+        got = spread(sent, MP, 8)
+        moved = [swap(v, "x", b) for b, v in ((1, near), (2, opposite), (3, far))]
+        pair = pair_y(after(cotangent, near))
+        got = after(got, pair, *moved).astype(F32)
+        total = total + sum(m.astype(F32) for m in moved)
     with jax.named_scope("stats"):
-        values = tokens.astype(F32)
-        sums = jnp.concatenate([jnp.sum(values, axis=1), jnp.sum(values * values, axis=1)])
-        sums = spread(sums[None], MP, 8)
-        pair = pair_y(cotangent)
-        sums = jnp.sum(after(sums, pair), axis=(0, 1))
-        mean = sums[:16] / D
-        var = sums[16:] / D - mean * mean
+        local = got[:, 16] + got[:, 17] + got[:, 18]
+        css = got[:, 19] + got[:, 20]
+        lean = got[:, 21] + got[:, 22]
+        column = got[:, 23, :columns] + got[:, 23, columns : 2 * columns]
+        power = got[:, 23, 2 * columns : 2 * columns + 1] + got[:, 23, 2 * columns + 128 : 2 * columns + 129]
+        mean = jnp.sum(local, axis=0) / 8
+        apart = local - mean[None, :]
+        var = (jnp.sum(css, axis=0) + width * jnp.sum(apart * apart, axis=0)) / D
         inv = lax.rsqrt(var + 1e-06)
-        rows = ((values - mean[:, None]) * inv[:, None] * norm_gain[None, :]).astype(BF)
-    with jax.named_scope("token_gather"):
-        mine = spread(rows, ("yl", "z"), 32)
-        cot = gather_x(after(pair, rows))
-        normed = join_cores(after(mine, *cot)).reshape(TOKENS, -1)
+    with jax.named_scope("gram"):
+        left = jnp.concatenate([lean, apart, power * apart], axis=0) * inv[None, :]
+        left = lax.dynamic_slice_in_dim(left, place * 16, 16, 1)
+        own = lax.dynamic_slice_in_dim(inv, place * 16, 16, 0)
+        right = jnp.concatenate([apart, lean, apart], axis=0)
+        rows = jnp.sum(got[:, :16], axis=0) * own[:, None] + dot(left, right, ((0,), (0,)), exact)
+        gram = spread((rows * inv[None, :]).astype(BF), ("yl", "z"), 32)
+    with jax.named_scope("pre"):
+        half = total.astype(BF)
+        moved = swap(half, "yh", 1)
+        cot = gather_x(after(pair, half))
+        normed = joined.reshape(TOKENS, width).astype(F32) - mean[:, None]
+        normed = (normed * inv[:, None] * norm_gain[None, :]).astype(BF)
+        shift = dot(lax.dynamic_slice_in_dim(apart, x * 256, 256, 1), column, ((0,), (0,)), exact)
+        total = total + shift
+        total = (total + after(moved, normed, *cot).astype(F32)) * lax.dynamic_slice_in_dim(inv, x * 256, 256, 0)[:, None]
+        moved = gather_x(total.astype(BF))
         cot = jnp.stack(ordered(cot, x), axis=1).reshape(TOKENS, columns)
-    with jax.named_scope("gram_part"):
-        gram = dot(rows, normed, ((1,), (1,)))
-        gram = spread(gram.astype(BF), MP, 8)
-    with jax.named_scope("project"):
-        part = dot(normed, w_up, ((1,), (0,))).astype(BF).reshape(4, 256, columns)
-
-        def block(b):
-            return lax.dynamic_index_in_dim(part, x ^ b, 0, keepdims=False)
-
-        moved = [swap(block(b), "x", b) for b in (1, 2, 3)]
-        gram = after(gram, *moved)
-        total = block(0).astype(F32) + sum(m.astype(F32) for m in moved)
-    with jax.named_scope("gram_gather"):
-        gram = jnp.sum(gram.astype(F32), axis=0).astype(BF)
-        gram = spread(gram, ("yl", "z"), 32)
-    with jax.named_scope("pre"):
-        total = total + swap(total.astype(BF), "yh", 1).astype(F32)
-        moved = gather_x(total.astype(BF))
-        gram = join_cores(after(gram, *moved)).reshape(TOKENS, TOKENS)
+        gram = join_cores(after(gram, cot, *moved)).reshape(TOKENS, TOKENS)
         pre = jnp.concatenate(ordered(moved, x), axis=0).astype(F32)
 
     def slope_at(value):

time: 183 us -> 175 us (0.956)
  blocking collectives: 22.2 us -> 58.6 us
  waiting for transfers between devices: 50.9 us -> 21.4 us
  starting transfers between devices: 78.9 us -> 58.3 us
  Pallas kernels: 0 us -> 5.22 us
  other arithmetic: 14.3 us -> 10.4 us
  local copies, waits for them, and re-layouts: 6.44 us -> 8.9 us
  matrix products: 7.73 us -> 9.85 us
    all_to_all x1 -> x2, blocking collectives: 22.2 us -> 58.6 us  [spread(): return lax.all_to_all(copies, axes, 0, 0, tiled=True)]
    ppermute x13, waiting for transfers between devices: 38.1 us -> 21.3 us  [swap(): return lax.ppermute(value, axis, [(i, i ^ bit) for i in range(size)])]
    all_to_all x4 -> x2, starting transfers between devices: 26.6 us -> 12.8 us  [spread(): return lax.all_to_all(copies, axes, 0, 0, tiled=True)]
    all_to_all x4 -> x2, waiting for transfers between devices: 12.8 us -> 0.01 us  [spread(): return lax.all_to_all(copies, axes, 0, 0, tiled=True)]
    ppermute x13, starting transfers between devices: 52.3 us -> 45.5 us  [swap(): return lax.ppermute(value, axis, [(i, i ^ bit) for i in range(size)])]
    pallas_call x0 -> x1, Pallas kernels: none -> 5.22 us  [local_work(): pl.pallas_call(local_kernel, out_shape=[jax.ShapeDtypeStruct((32, 2, 16,...]
    unnamed x42 -> x37, local copies, waits for them, and re-layouts: 2.34 us -> 5.32 us
    convert_element_type x2 -> x1, other arithmetic: 3.75 us -> 0.82 us  [slope_at(): return (cot.astype(F32) * gelu_slope(value) * scale).astype(BF)]
  transfers between devices with their start and end apart: 17 -> 15, of which waited for: 10 -> 7; matrix products, arithmetic and copies ran while one was open for 5% -> 6% of each run, Pallas kernels for 0% -> 0%
where the time goes in v5:
time: 175 us; the launch traced here: 174 us
  blocking collectives  58.6 us (33%)
  starting transfers between devices  58.3 us (33%)
  waiting for transfers between devices  21.4 us (12%)
  other arithmetic  10.4 us (6%)
  matrix products  9.85 us (6%)
  local copies, waits for them, and re-layouts  8.9 us (5%)
  Pallas kernels  5.22 us (3%)
    all_to_all x2, blocking collectives, spread(): return lax.all_to_all(copies, axes, 0, 0, tiled=True)  58.6 us
    ppermute x13, starting transfers between devices, swap(): return lax.ppermute(value, axis, [(i, i ^ bit) for i in range(size)])  45.5 us
    ppermute x13, waiting for transfers between devices, swap(): return lax.ppermute(value, axis, [(i, i ^ bit) for i in range(size)])  21.3 us
    all_to_all x2, starting transfers between devices, spread(): return lax.all_to_all(copies, axes, 0, 0, tiled=True)  12.8 us
    dot_general x4, matrix products, dot(): lax.dot_general(left, right, (dims, ((), ())), precision=precision, prefe...  9.85 us
    unnamed x37, local copies, waits for them, and re-layouts  5.32 us
    pallas_call x1, Pallas kernels, local_work(): pl.pallas_call(local_kernel, out_shape=[jax.ShapeDtypeStruct((32, 2, 16,...  5.22 us
  transfers between devices with their start and end apart: 15, of which 7 were waited for; matrix products, arithmetic and copies ran while one was open for 6% of the time, Pallas kernels for 0%

profile of v5, /device:TPU:1, one launch (start us, length us, event | category | flops | bytes accessed | tf_op | source)
XLA Modules:
  0.0 173.8 jit_solution(12170345154772647246)
XLA Ops:
  0.0 0.8 broadcast_in_dim.10
  0.8 34.5 %all_to_all.20.mine = bf16[32,16,768]{2,1,0:T(8,128)(2,1)S(1)} all-to-all(bf16[32,16,768]{2,1,0:T(8,128)(2,1)S(1)} %broadcast_in_dim.10), channel_id=1, replica_groups=mesh['yl'=4,'z'=8,'c'=2,'yh'=2,'x'=4] {'yl','z'}, dimensions={0} | all-to-all | bytes 1572864 | tf_op jit(solution)/shard_map/token_gather/all_to_all | solution.py:33
  35.3 4.2 %collective-permute-start = (bf16[32,16,768]{2,1,0:T(8,128)(2,1)S(1)}, bf16[32,16,768]{2,1,0:T(8,128)(2,1)S(1)}, u32[]{:S(2)}, u32[]{:S(2)}) collective-permute-start(bf16[32,16,768]{2,1,0:T(8,128)(2,1)S(1)} %all_to_all.20.mine), channel_id=1, source_target_pairs={{0,8},{8,0},{1,9},{9,1},{2,10},{10,2},{3,11},{11,3},{4,12},{12,4},... | collective-permute-start | bytes 2359304 | tf_op jit(solution)/shard_map/token_gather/ppermute | solution.py:28
  39.6 0.1 pad_add_fusion.at
  39.7 1.8 %collective-permute-done.other = bf16[32,16,768]{2,1,0:T(8,128)(2,1)S(1)} collective-permute-done((bf16[32,16,768]{2,1,0:T(8,128)(2,1)S(1)}, bf16[32,16,768]{2,1,0:T(8,128)(2,1)S(1)}, u32[]{:S(2)}, u32[]{:S(2)}) %collective-permute-start) | collective-permute-done | bytes 786464 | tf_op jit(solution)/shard_map/token_gather/ppermute | solution.py:28
  41.5 1.1 copy-done
  42.5 5.2 %local_work.1 = (bf16[32,2,16,768]{3,2,1,0:T(8,128)(2,1)S(1)}, f32[256,384]{1,0:T(8,128)S(1)}, bf16[256,384]{1,0:T(8,128)(2,1)S(1)}, bf16[256,384]{1,0:T(8,128)(...) custom-call(s32[3]{0:T(128)S(1)} %pad_add_fusion.at, bf16[32,16,768]{2,1,0:T(8,128)(2,1)S(1)} %all_to_all.20.mine, ...), custom_call_target="tpu_custom_call" | custom-call | flops 1207959552 | bytes 8388608 | tf_op jit(solution)/shard_map/local_work/local_work/pallas_call | solution.py:118
  47.8 0.7 copy-done.1
  48.4 0.7 copy-done.3
  49.1 0.7 copy-done.5
  49.8 0.9 broadcast_in_dim.12
  50.6 6.7 %all-to-all-start.1 = ((bf16[8,32,1024]{2,1,0:T(8,128)(2,1)}), bf16[8,32,1024]{2,1,0:T(8,128)(2,1)S(1)}, u32[]{:S(2)}, u32[]{:S(2)}) async-start(bf16[8,32,1024]{2,1,0:T(8,128)(2,1)} %broadcast_in_dim.12), calls=%async_computation.1 | async-start | bytes 1048576 | tf_op jit(solution)/shard_map/sums_x/all_to_all | solution.py:33
  57.3 7.3 %collective-permute-start.1 = (bf16[128,384]{1,0:T(8,128)(2,1)}, bf16[128,384]{1,0:T(8,128)(2,1)}, u32[]{:S(2)}, u32[]{:S(2)}) collective-permute-start(bf16[128,384]{1,0:T(8,128)(2,1)} %param.7), channel_id=1, source_target_pairs={{0,4},{4,0},{1,5},{5,1},{2,6},{6,2},{3,7},{7,3},{8,12},{12,8},{9,1... | collective-permute-start | bytes 294920 | tf_op jit(solution)/shard_map/sums_x/ppermute | solution.py:28
  64.6 3.1 %collective-permute-start.2 = (bf16[256,384]{1,0:T(8,128)(2,1)S(1)}, bf16[256,384]{1,0:T(8,128)(2,1)S(1)}, u32[]{:S(2)}, u32[]{:S(2)}) collective-permute-start(bf16[256,384]{1,0:T(8,128)(2,1)S(1)} %copy-done.6), channel_id=1, source_target_pairs={{0,1},{1,0},{2,3},{3,2},{4,5},{5,4},{6,7},{7,6},{8,9},{9,8},{10,11... | collective-permute-start | bytes 589832 | tf_op jit(solution)/shard_map/sums_x/ppermute | solution.py:28
  67.7 4.3 %collective-permute-start.3 = (bf16[256,384]{1,0:T(8,128)(2,1)S(1)}, bf16[256,384]{1,0:T(8,128)(2,1)S(1)}, u32[]{:S(2)}, u32[]{:S(2)}) collective-permute-start(bf16[256,384]{1,0:T(8,128)(2,1)S(1)} %copy-done.4), channel_id=1, source_target_pairs={{0,2},{1,3},{2,0},{3,1},{4,6},{5,7},{6,4},{7,5},{8,10},{9,11},{10,... | collective-permute-start | bytes 589832 | tf_op jit(solution)/shard_map/sums_x/ppermute | solution.py:28
  72.0 2.2 %collective-permute-start.4 = (bf16[256,384]{1,0:T(8,128)(2,1)S(1)}, bf16[256,384]{1,0:T(8,128)(2,1)}, u32[]{:S(2)}, u32[]{:S(2)}) collective-permute-start(bf16[256,384]{1,0:T(8,128)(2,1)S(1)} %copy-done.2), channel_id=1, source_target_pairs={{0,3},{1,2},{2,1},{3,0},{4,7},{5,6},{6,5},{7,4},{8,11},{9,10},{10,... | collective-permute-start | bytes 589832 | tf_op jit(solution)/shard_map/sums_x/ppermute | solution.py:28
  74.2 1.0 select_bitcast_fusion.7
  75.2 0.7 pad_maximum_fusion.2
  75.9 2.8 %collective-permute-done.3 = bf16[256,384]{1,0:T(8,128)(2,1)S(1)} collective-permute-done((bf16[256,384]{1,0:T(8,128)(2,1)S(1)}, bf16[256,384]{1,0:T(8,128)(2,1)S(1)}, u32[]{:S(2)}, u32[]{:S(2)}) %collective-permute-start.3) | collective-permute-done | bytes 196640 | tf_op jit(solution)/shard_map/sums_x/ppermute | solution.py:28
  78.7 5.6 %collective-permute-done.4 = bf16[256,384]{1,0:T(8,128)(2,1)} collective-permute-done((bf16[256,384]{1,0:T(8,128)(2,1)S(1)}, bf16[256,384]{1,0:T(8,128)(2,1)}, u32[]{:S(2)}, u32[]{:S(2)}) %collective-permute-start.4) | collective-permute-done | bytes 196640 | tf_op jit(solution)/shard_map/sums_x/ppermute | solution.py:28
  84.3 0.1 convert_element_type.83
  84.4 0.0 copy-start.7
  84.4 0.2 slice_add_fusion
  84.6 0.1 fusion.44
  84.7 0.6 copy-done.7
  85.4 0.1 broadcast_multiply_fusion
  85.5 0.1 dynamic_slice.14
  85.6 0.3 fusion.26
  85.9 1.1 broadcast_in_dim.13
  87.0 6.1 %all-to-all-start.2 = ((bf16[32,16,1024]{2,1,0:T(8,128)(2,1)}), bf16[32,16,1024]{2,1,0:T(8,128)(2,1)S(1)}, u32[]{:S(2)}, u32[]{:S(2)}) async-start(bf16[32,16,1024]{2,1,0:T(8,128)(2,1)} %broadcast_in_dim.13), calls=%async_computation.2 | async-start | bytes 2097152 | tf_op jit(solution)/shard_map/gram/all_to_all | solution.py:33
  93.2 1.0 fusion.35
  94.2 2.2 %collective-permute-start.5 = (bf16[2,128,384]{2,1,0:T(8,128)(2,1)}, bf16[2,128,384]{2,1,0:T(8,128)(2,1)S(1)}, u32[]{:S(2)}, u32[]{:S(2)}) collective-permute-start(bf16[2,128,384]{2,1,0:T(8,128)(2,1)} %pad_maximum_fusion.2), channel_id=1, source_target_pairs={{0,3},{1,2},{2,1},{3,0},{4,7},{5,6},{6,5},{7,4},{8,11},{9,10},{10,... | collective-permute-start | bytes 589832 | tf_op jit(solution)/shard_map/pre/ppermute | solution.py:28
  96.4 2.7 %collective-permute-start.6 = (bf16[2,128,384]{2,1,0:T(8,128)(2,1)}, bf16[2,128,384]{2,1,0:T(8,128)(2,1)S(1)}, u32[]{:S(2)}, u32[]{:S(2)}) collective-permute-start(bf16[2,128,384]{2,1,0:T(8,128)(2,1)} %pad_maximum_fusion.2), channel_id=1, source_target_pairs={{0,2},{1,3},{2,0},{3,1},{4,6},{5,7},{6,4},{7,5},{8,10},{9,11},{10,... | collective-permute-start | bytes 589832 | tf_op jit(solution)/shard_map/pre/ppermute | solution.py:28
  99.1 4.1 %collective-permute-start.7 = (bf16[2,128,384]{2,1,0:T(8,128)(2,1)}, bf16[2,128,384]{2,1,0:T(8,128)(2,1)S(1)}, u32[]{:S(2)}, u32[]{:S(2)}) collective-permute-start(bf16[2,128,384]{2,1,0:T(8,128)(2,1)} %pad_maximum_fusion.2), channel_id=1, source_target_pairs={{0,1},{1,0},{2,3},{3,2},{4,5},{5,4},{6,7},{7,6},{8,9},{9,8},{10,11... | collective-permute-start | bytes 589832 | tf_op jit(solution)/shard_map/pre/ppermute | solution.py:28
  103.2 2.2 %collective-permute-start.8 = (bf16[256,384]{1,0:T(8,128)(2,1)S(1)}, bf16[256,384]{1,0:T(8,128)(2,1)S(1)}, u32[]{:S(2)}, u32[]{:S(2)}) collective-permute-start(bf16[256,384]{1,0:T(8,128)(2,1)S(1)} %fusion.35), channel_id=1, source_target_pairs={{0,4},{4,0},{1,5},{5,1},{2,6},{6,2},{3,7},{7,3},{8,12},{12,8},{9,1... | collective-permute-start | bytes 589832 | tf_op jit(solution)/shard_map/pre/ppermute | solution.py:28
  105.4 1.7 fusion.2
  107.1 0.0 collective-permute-done.5
  107.1 1.8 %collective-permute-done.7 = bf16[2,128,384]{2,1,0:T(8,128)(2,1)S(1)} collective-permute-done((bf16[2,128,384]{2,1,0:T(8,128)(2,1)}, bf16[2,128,384]{2,1,0:T(8,128)(2,1)S(1)}, u32[]{:S(2)}, u32[]{:S(2)}) %collective-permute-start.7) | collective-permute-done | bytes 196640 | tf_op jit(solution)/shard_map/pre/ppermute | solution.py:28
  109.0 4.8 %collective-permute-done.8 = bf16[256,384]{1,0:T(8,128)(2,1)S(1)} collective-permute-done((bf16[256,384]{1,0:T(8,128)(2,1)S(1)}, bf16[256,384]{1,0:T(8,128)(2,1)S(1)}, u32[]{:S(2)}, u32[]{:S(2)}) %collective-permute-start.8) | collective-permute-done | bytes 196640 | tf_op jit(solution)/shard_map/pre/ppermute | solution.py:28
  113.7 0.1 dynamic_slice.13
  113.8 1.0 slice_add_fusion.4
  114.8 1.5 fusion.24
  116.3 3.1 %collective-permute-start.10 = (bf16[256,384]{1,0:T(8,128)(2,1)S(1)}, bf16[256,384]{1,0:T(8,128)(2,1)S(1)}, u32[]{:S(2)}, u32[]{:S(2)}) collective-permute-start(bf16[256,384]{1,0:T(8,128)(2,1)S(1)} %fusion.24), channel_id=1, source_target_pairs={{0,2},{1,3},{2,0},{3,1},{4,6},{5,7},{6,4},{7,5},{8,10},{9,11},{10,... | collective-permute-start | bytes 589832 | tf_op jit(solution)/shard_map/pre/ppermute | solution.py:28
  119.4 2.2 %collective-permute-start.11 = (bf16[256,384]{1,0:T(8,128)(2,1)S(1)}, bf16[256,384]{1,0:T(8,128)(2,1)S(1)}, u32[]{:S(2)}, u32[]{:S(2)}) collective-permute-start(bf16[256,384]{1,0:T(8,128)(2,1)S(1)} %fusion.24), channel_id=1, source_target_pairs={{0,1},{1,0},{2,3},{3,2},{4,5},{5,4},{6,7},{7,6},{8,9},{9,8},{10,11... | collective-permute-start | bytes 589832 | tf_op jit(solution)/shard_map/pre/ppermute | solution.py:28
  121.6 3.7 %collective-permute-start.9 = (bf16[256,384]{1,0:T(8,128)(2,1)S(1)}, bf16[256,384]{1,0:T(8,128)(2,1)S(1)}, u32[]{:S(2)}, u32[]{:S(2)}) collective-permute-start(bf16[256,384]{1,0:T(8,128)(2,1)S(1)} %fusion.24), channel_id=1, source_target_pairs={{0,3},{1,2},{2,1},{3,0},{4,7},{5,6},{6,5},{7,4},{8,11},{9,10},{10,... | collective-permute-start | bytes 589832 | tf_op jit(solution)/shard_map/pre/ppermute | solution.py:28
  125.3 0.1 select_bitcast_fusion.5
  125.4 1.0 pad_maximum_fusion.1
  126.4 0.0 collective-permute-done.10
  126.4 1.8 %collective-permute-done.11 = bf16[256,384]{1,0:T(8,128)(2,1)S(1)} collective-permute-done((bf16[256,384]{1,0:T(8,128)(2,1)S(1)}, bf16[256,384]{1,0:T(8,128)(2,1)S(1)}, u32[]{:S(2)}, u32[]{:S(2)}) %collective-permute-start.11) | collective-permute-done | bytes 196640 | tf_op jit(solution)/shard_map/pre/ppermute | solution.py:28
  128.2 2.8 %collective-permute-done.9 = bf16[256,384]{1,0:T(8,128)(2,1)S(1)} collective-permute-done((bf16[256,384]{1,0:T(8,128)(2,1)S(1)}, bf16[256,384]{1,0:T(8,128)(2,1)S(1)}, u32[]{:S(2)}, u32[]{:S(2)}) %collective-permute-start.9) | collective-permute-done | bytes 196640 | tf_op jit(solution)/shard_map/pre/ppermute | solution.py:28
  131.1 0.7 copy-done.16
  131.8 4.3 %collective-permute-start.12 = (bf16[32,16,1024]{2,1,0:T(8,128)(2,1)S(1)}, bf16[32,16,1024]{2,1,0:T(8,128)(2,1)S(1)}, u32[]{:S(2)}, u32[]{:S(2)}) collective-permute-start(bf16[32,16,1024]{2,1,0:T(8,128)(2,1)S(1)} %all-to-all-done.2), channel_id=1, source_target_pairs={{0,8},{8,0},{1,9},{9,1},{2,10},{10,2},{3,11},{11,3},{4,12},{12,4},... | collective-permute-start | bytes 3145736 | tf_op jit(solution)/shard_map/pre/ppermute | solution.py:28
  136.1 1.3 broadcast_select_fusion.7
  137.4 0.1 maximum_convert_fusion
  137.5 0.8 fusion.13
  138.4 0.1 select_bitcast_fusion.1
  138.5 0.0 copy-start.9
  138.5 0.2 pad_maximum_fusion
  138.8 0.9 copy-done.9
  139.7 4.2 %multiply_reduce_fusion = (f32[]{:T(128)}, f32[1024,384]{1,0:T(8,128)}) fusion(bf16[2,4,128,384]{3,2,1,0:T(8,128)(2,1)S(1)} %copy-done.9, bf16[256,384]{1,0:T(8,128)(2,1)S(1)} %get-tuple-element.40, bf16[256,384]{1,0:T(8,128)(2,1)S(1)} %get-tuple-element.39, bf16[256,384]{1,0:T(8,128)(2,1)S(1)} %get-tuple-element.38, ...), kind=kOutput, calls=%fused_computation.29 | convolution fusion | flops 814350336 | bytes 6029316 | tf_op jit(solution)/shard_map/ascent/dot_general | solution.py:63
  143.9 0.7 broadcast_in_dim.14
  144.6 24.1 %all_to_all.21 = f32[64,1,128]{2,1,0:T(1,128)S(1)} all-to-all(f32[64,1,128]{2,1,0:T(1,128)S(1)} %broadcast_in_dim.14), channel_id=1, replica_groups=mesh['yl'=4,'z'=8,'c'=2,'yh'=2,'x'=4] {'yl','z','c'}, dimensions={0} | all-to-all | bytes 65536 | tf_op jit(solution)/shard_map/ascent/all_to_all | solution.py:33
  168.6 0.7 slice_reduce_fusion.1
  170.0 3.8 %fusion.27 = f32[768,384]{1,0:T(8,128)} fusion(bf16[1024,768]{1,0:T(8,128)(2,1)S(1)} %copy-done.8, bf16[1024,384]{1,0:T(8,128)(2,1)S(1)} %bitcast.49, f32[1024,384]{1,0:T(8,128)} %get-tuple-element.48, f32[]{:T(128)S(6)} %div.19, bf16[256,384]{1,0:T(8,128)(2,1)} %copy-done.11, bf16[256,384]{1,0:T(8,128)(2,1)} %copy-done.10, ...), kind=kOutput, calls=%fused_computation.41 | convolution fusion | flops 612630528 | bytes 5898244 | tf_op jit(solution)/shard_map/sharp/dot_general | solution.py:63
  (39 shorter events, 0.1 us)
Async XLA Ops:
  0.0 39.6 %copy-start.17 = (f32[768]{0:T(1024)S(1)}, f32[768]{0:T(1024)}, u32[]{:S(2)}) copy-start(f32[768]{0:T(1024)} %param.5) | copy-start | bytes 9220
  35.3 6.1 %collective-permute-start = (bf16[32,16,768]{2,1,0:T(8,128)(2,1)S(1)}, bf16[32,16,768]{2,1,0:T(8,128)(2,1)S(1)}, u32[]{:S(2)}, u32[]{:S(2)}) collective-permute-start(bf16[32,16,768]{2,1,0:T(8,128)(2,1)S(1)} %all_to_all.20.mine), channel_id=1, source_target_pairs={{0,8},{8,0},{1,9},{9,1},{2,10},{10,2},{3,11},{11,3},{4,12},{12,4},... | collective-permute-start | bytes 2359304 | tf_op jit(solution)/shard_map/token_gather/ppermute | solution.py:28
  41.5 1.1 copy-start
  47.8 0.7 copy-start.1
  48.4 0.7 copy-start.3
  49.1 0.7 copy-start.5
  49.8 14.8 %copy-start.6 = (bf16[256,384]{1,0:T(8,128)(2,1)S(1)}, bf16[256,384]{1,0:T(8,128)(2,1)}, u32[]{:S(2)}) copy-start(bf16[256,384]{1,0:T(8,128)(2,1)} %copy-done.5) | copy-start | bytes 589828
  49.8 17.9 %copy-start.4 = (bf16[256,384]{1,0:T(8,128)(2,1)S(1)}, bf16[256,384]{1,0:T(8,128)(2,1)}, u32[]{:S(2)}) copy-start(bf16[256,384]{1,0:T(8,128)(2,1)} %copy-done.3) | copy-start | bytes 589828
  49.8 22.2 %copy-start.2 = (bf16[256,384]{1,0:T(8,128)(2,1)S(1)}, bf16[256,384]{1,0:T(8,128)(2,1)}, u32[]{:S(2)}) copy-start(bf16[256,384]{1,0:T(8,128)(2,1)} %copy-done.1) | copy-start | bytes 589828
  50.6 33.6 %all-to-all-start.1 = ((bf16[8,32,1024]{2,1,0:T(8,128)(2,1)}), bf16[8,32,1024]{2,1,0:T(8,128)(2,1)S(1)}, u32[]{:S(2)}, u32[]{:S(2)}) async-start(bf16[8,32,1024]{2,1,0:T(8,128)(2,1)} %broadcast_in_dim.12), calls=%async_computation.1 | async-start | bytes 1048576 | tf_op jit(solution)/shard_map/sums_x/all_to_all | solution.py:33
  57.3 16.9 %collective-permute-start.1 = (bf16[128,384]{1,0:T(8,128)(2,1)}, bf16[128,384]{1,0:T(8,128)(2,1)}, u32[]{:S(2)}, u32[]{:S(2)}) collective-permute-start(bf16[128,384]{1,0:T(8,128)(2,1)} %param.7), channel_id=1, source_target_pairs={{0,4},{4,0},{1,5},{5,1},{2,6},{6,2},{3,7},{7,3},{8,12},{12,8},{9,1... | collective-permute-start | bytes 294920 | tf_op jit(solution)/shard_map/sums_x/ppermute | solution.py:28
  64.6 11.3 %collective-permute-start.2 = (bf16[256,384]{1,0:T(8,128)(2,1)S(1)}, bf16[256,384]{1,0:T(8,128)(2,1)S(1)}, u32[]{:S(2)}, u32[]{:S(2)}) collective-permute-start(bf16[256,384]{1,0:T(8,128)(2,1)S(1)} %copy-done.6), channel_id=1, source_target_pairs={{0,1},{1,0},{2,3},{3,2},{4,5},{5,4},{6,7},{7,6},{8,9},{9,8},{10,11... | collective-permute-start | bytes 589832 | tf_op jit(solution)/shard_map/sums_x/ppermute | solution.py:28
  67.7 11.0 %collective-permute-start.3 = (bf16[256,384]{1,0:T(8,128)(2,1)S(1)}, bf16[256,384]{1,0:T(8,128)(2,1)S(1)}, u32[]{:S(2)}, u32[]{:S(2)}) collective-permute-start(bf16[256,384]{1,0:T(8,128)(2,1)S(1)} %copy-done.4), channel_id=1, source_target_pairs={{0,2},{1,3},{2,0},{3,1},{4,6},{5,7},{6,4},{7,5},{8,10},{9,11},{10,... | collective-permute-start | bytes 589832 | tf_op jit(solution)/shard_map/sums_x/ppermute | solution.py:28
  72.0 12.2 %collective-permute-start.4 = (bf16[256,384]{1,0:T(8,128)(2,1)S(1)}, bf16[256,384]{1,0:T(8,128)(2,1)}, u32[]{:S(2)}, u32[]{:S(2)}) collective-permute-start(bf16[256,384]{1,0:T(8,128)(2,1)S(1)} %copy-done.2), channel_id=1, source_target_pairs={{0,3},{1,2},{2,1},{3,0},{4,7},{5,6},{6,5},{7,4},{8,11},{9,10},{10,... | collective-permute-start | bytes 589832 | tf_op jit(solution)/shard_map/sums_x/ppermute | solution.py:28
  84.4 1.0 copy-start.7
  87.0 44.1 %all-to-all-start.2 = ((bf16[32,16,1024]{2,1,0:T(8,128)(2,1)}), bf16[32,16,1024]{2,1,0:T(8,128)(2,1)S(1)}, u32[]{:S(2)}, u32[]{:S(2)}) async-start(bf16[32,16,1024]{2,1,0:T(8,128)(2,1)} %broadcast_in_dim.13), calls=%async_computation.2 | async-start | bytes 2097152 | tf_op jit(solution)/shard_map/gram/all_to_all | solution.py:33
  94.2 12.9 %collective-permute-start.5 = (bf16[2,128,384]{2,1,0:T(8,128)(2,1)}, bf16[2,128,384]{2,1,0:T(8,128)(2,1)S(1)}, u32[]{:S(2)}, u32[]{:S(2)}) collective-permute-start(bf16[2,128,384]{2,1,0:T(8,128)(2,1)} %pad_maximum_fusion.2), channel_id=1, source_target_pairs={{0,3},{1,2},{2,1},{3,0},{4,7},{5,6},{6,5},{7,4},{8,11},{9,10},{10,... | collective-permute-start | bytes 589832 | tf_op jit(solution)/shard_map/pre/ppermute | solution.py:28
  96.4 10.7 %collective-permute-start.6 = (bf16[2,128,384]{2,1,0:T(8,128)(2,1)}, bf16[2,128,384]{2,1,0:T(8,128)(2,1)S(1)}, u32[]{:S(2)}, u32[]{:S(2)}) collective-permute-start(bf16[2,128,384]{2,1,0:T(8,128)(2,1)} %pad_maximum_fusion.2), channel_id=1, source_target_pairs={{0,2},{1,3},{2,0},{3,1},{4,6},{5,7},{6,4},{7,5},{8,10},{9,11},{10,... | collective-permute-start | bytes 589832 | tf_op jit(solution)/shard_map/pre/ppermute | solution.py:28
  99.1 9.9 %collective-permute-start.7 = (bf16[2,128,384]{2,1,0:T(8,128)(2,1)}, bf16[2,128,384]{2,1,0:T(8,128)(2,1)S(1)}, u32[]{:S(2)}, u32[]{:S(2)}) collective-permute-start(bf16[2,128,384]{2,1,0:T(8,128)(2,1)} %pad_maximum_fusion.2), channel_id=1, source_target_pairs={{0,1},{1,0},{2,3},{3,2},{4,5},{5,4},{6,7},{7,6},{8,9},{9,8},{10,11... | collective-permute-start | bytes 589832 | tf_op jit(solution)/shard_map/pre/ppermute | solution.py:28
  103.2 10.5 %collective-permute-start.8 = (bf16[256,384]{1,0:T(8,128)(2,1)S(1)}, bf16[256,384]{1,0:T(8,128)(2,1)S(1)}, u32[]{:S(2)}, u32[]{:S(2)}) collective-permute-start(bf16[256,384]{1,0:T(8,128)(2,1)S(1)} %fusion.35), channel_id=1, source_target_pairs={{0,4},{4,0},{1,5},{5,1},{2,6},{6,2},{3,7},{7,3},{8,12},{12,8},{9,1... | collective-permute-start | bytes 589832 | tf_op jit(solution)/shard_map/pre/ppermute | solution.py:28
  105.4 19.9 %copy-start.12 = (bf16[2,128,384]{2,1,0:T(8,128)(2,1)S(1)}, bf16[2,128,384]{2,1,0:T(8,128)(2,1)}, u32[]{:S(2)}) copy-start(bf16[2,128,384]{2,1,0:T(8,128)(2,1)} %pad_maximum_fusion.2) | copy-start | bytes 589828
  116.3 10.2 %copy-start.13 = (bf16[256,384]{1,0:T(8,128)(2,1)}, bf16[256,384]{1,0:T(8,128)(2,1)S(1)}, u32[]{:S(2)}) copy-start(bf16[256,384]{1,0:T(8,128)(2,1)S(1)} %fusion.24) | copy-start | bytes 589828
  116.3 10.1 %collective-permute-start.10 = (bf16[256,384]{1,0:T(8,128)(2,1)S(1)}, bf16[256,384]{1,0:T(8,128)(2,1)S(1)}, u32[]{:S(2)}, u32[]{:S(2)}) collective-permute-start(bf16[256,384]{1,0:T(8,128)(2,1)S(1)} %fusion.24), channel_id=1, source_target_pairs={{0,2},{1,3},{2,0},{3,1},{4,6},{5,7},{6,4},{7,5},{8,10},{9,11},{10,... | collective-permute-start | bytes 589832 | tf_op jit(solution)/shard_map/pre/ppermute | solution.py:28
  119.4 8.8 %collective-permute-start.11 = (bf16[256,384]{1,0:T(8,128)(2,1)S(1)}, bf16[256,384]{1,0:T(8,128)(2,1)S(1)}, u32[]{:S(2)}, u32[]{:S(2)}) collective-permute-start(bf16[256,384]{1,0:T(8,128)(2,1)S(1)} %fusion.24), channel_id=1, source_target_pairs={{0,1},{1,0},{2,3},{3,2},{4,5},{5,4},{6,7},{7,6},{8,9},{9,8},{10,11... | collective-permute-start | bytes 589832 | tf_op jit(solution)/shard_map/pre/ppermute | solution.py:28
  121.6 9.5 %collective-permute-start.9 = (bf16[256,384]{1,0:T(8,128)(2,1)S(1)}, bf16[256,384]{1,0:T(8,128)(2,1)S(1)}, u32[]{:S(2)}, u32[]{:S(2)}) collective-permute-start(bf16[256,384]{1,0:T(8,128)(2,1)S(1)} %fusion.24), channel_id=1, source_target_pairs={{0,3},{1,2},{2,1},{3,0},{4,7},{5,6},{6,5},{7,4},{8,11},{9,10},{10,... | collective-permute-start | bytes 589832 | tf_op jit(solution)/shard_map/pre/ppermute | solution.py:28
  126.4 1.8 %copy-start.14 = (bf16[256,384]{1,0:T(8,128)(2,1)}, bf16[256,384]{1,0:T(8,128)(2,1)S(1)}, u32[]{:S(2)}) copy-start(bf16[256,384]{1,0:T(8,128)(2,1)S(1)} %collective-permute-done.10) | copy-start | bytes 589828
  128.2 2.9 %copy-start.15 = (bf16[256,384]{1,0:T(8,128)(2,1)}, bf16[256,384]{1,0:T(8,128)(2,1)S(1)}, u32[]{:S(2)}) copy-start(bf16[256,384]{1,0:T(8,128)(2,1)S(1)} %collective-permute-done.11) | copy-start | bytes 589828
  131.1 0.7 copy-start.16
  131.8 6.6 %collective-permute-start.12 = (bf16[32,16,1024]{2,1,0:T(8,128)(2,1)S(1)}, bf16[32,16,1024]{2,1,0:T(8,128)(2,1)S(1)}, u32[]{:S(2)}, u32[]{:S(2)}) collective-permute-start(bf16[32,16,1024]{2,1,0:T(8,128)(2,1)S(1)} %all-to-all-done.2), channel_id=1, source_target_pairs={{0,8},{8,0},{1,9},{9,1},{2,10},{10,2},{3,11},{11,3},{4,12},{12,4},... | collective-permute-start | bytes 3145736 | tf_op jit(solution)/shard_map/pre/ppermute | solution.py:28
  137.4 1.3 copy-start.10
  137.4 1.3 copy-start.11
  138.5 1.1 copy-start.9
  139.7 30.4 %copy-start.8 = (bf16[1024,768]{1,0:T(8,128)(2,1)S(1)}, bf16[1024,768]{1,0:T(8,128)(2,1)}, u32[]{:S(2)}) copy-start(bf16[1024,768]{1,0:T(8,128)(2,1)} %fusion.2) | copy-start | bytes 4718596

commit v6 on v5

--- a/solution.py
+++ b/solution.py
@@ -107,7 +107,7 @@
     column = jnp.sum(dot(gains, w[...], ((1,), (0,))), axis=0, keepdims=True)
     power = jnp.broadcast_to(jnp.sum(g * g, axis=1, keepdims=True), (1, 128))
     extra = jnp.concatenate(split(column, 2) + split(power, 2), axis=1)
-    rows = [gram] + split(local, 3) + split(css, 2) + split(lean, 2) + [extra, jnp.zeros((8, TOKENS), F32)]
+    rows = [gram] + split(local, 3) + split(css, 2) + split(lean, 2) + [extra]
     sent[...] = jnp.concatenate(rows, axis=0).astype(BF)
 
 
@@ -123,10 +123,10 @@
             block,
             block,
             block,
-            jax.ShapeDtypeStruct((32, TOKENS), BF),
+            jax.ShapeDtypeStruct((24, TOKENS), BF),
         ],
         in_specs=[pl.BlockSpec(memory_space=pltpu.SMEM)] + [vmem] * 4,
-        out_specs=[vmem] * 6,
+        out_specs=[vmem] * 2 + [pl.BlockSpec()] * 4,
         scratch_shapes=[pltpu.VMEM((TOKENS, width), BF), pltpu.VMEM((4, 256, columns), F32)],
         compiler_params=pltpu.CompilerParams(vmem_limit_bytes=40 << 20),
         cost_estimate=pl.CostEstimate(flops=2 * TOKENS * width * columns * 2, bytes_accessed=8 << 20, transcendentals=0),
@@ -141,7 +141,10 @@
     place = lax.axis_index(DP)
     exact = lax.Precision.HIGHEST
     with jax.named_scope("token_gather"):
+        pair = pair_y(cotangent)
         mine = spread(tokens, ("yl", "z"), 32)
+        cot = gather_x(pair)
+        mine = after(mine, *cot)
         other = swap(mine, "c", 1)
     with jax.named_scope("local_work"):
         at = jnp.stack([place, lax.axis_index("c"), x]).astype(jnp.int32)
@@ -149,8 +152,7 @@
     with jax.named_scope("sums_x"):
         got = spread(sent, MP, 8)
         moved = [swap(v, "x", b) for b, v in ((1, near), (2, opposite), (3, far))]
-        pair = pair_y(after(cotangent, near))
-        got = after(got, pair, *moved).astype(F32)
+        got = after(got, *moved).astype(F32)
         total = total + sum(m.astype(F32) for m in moved)
     with jax.named_scope("stats"):
         local = got[:, 16] + got[:, 17] + got[:, 18]
@@ -168,19 +170,21 @@
         own = lax.dynamic_slice_in_dim(inv, place * 16, 16, 0)
         right = jnp.concatenate([apart, lean, apart], axis=0)
         rows = jnp.sum(got[:, :16], axis=0) * own[:, None] + dot(left, right, ((0,), (0,)), exact)
-        gram = spread((rows * inv[None, :]).astype(BF), ("yl", "z"), 32)
-    with jax.named_scope("pre"):
+        rows = (rows * inv[None, :]).astype(BF)
         half = total.astype(BF)
         moved = swap(half, "yh", 1)
-        cot = gather_x(after(pair, half))
+        gram = jnp.stack(ordered([rows] + [swap(rows, "yl", b) for b in (1, 2, 3)], lax.axis_index("yl")))
+        gram = spread(gram, ("z",), 8)
+    with jax.named_scope("pre"):
         normed = joined.reshape(TOKENS, width).astype(F32) - mean[:, None]
         normed = (normed * inv[:, None] * norm_gain[None, :]).astype(BF)
         shift = dot(lax.dynamic_slice_in_dim(apart, x * 256, 256, 1), column, ((0,), (0,)), exact)
         total = total + shift
-        total = (total + after(moved, normed, *cot).astype(F32)) * lax.dynamic_slice_in_dim(inv, x * 256, 256, 0)[:, None]
+        total = (total + after(moved, normed).astype(F32)) * lax.dynamic_slice_in_dim(inv, x * 256, 256, 0)[:, None]
         moved = gather_x(total.astype(BF))
         cot = jnp.stack(ordered(cot, x), axis=1).reshape(TOKENS, columns)
-        gram = join_cores(after(gram, cot, *moved)).reshape(TOKENS, TOKENS)
+        gram = join_cores(after(gram, *moved).reshape(32, 16, TOKENS)).reshape(8, 4, 32, TOKENS)
+        gram = jnp.swapaxes(gram, 0, 1).reshape(TOKENS, TOKENS)
         pre = jnp.concatenate(ordered(moved, x), axis=0).astype(F32)
 
     def slope_at(value):

time: 175 us -> 187 us (1.069)
  blocking collectives: 58.6 us -> 16.8 us
  starting transfers between devices: 58.3 us -> 87.8 us
  waiting for transfers between devices: 21.4 us -> 47.1 us
  matrix products: 9.85 us -> 5.46 us
  other arithmetic: 10.4 us -> 12.5 us
    all_to_all x2 -> x1, blocking collectives: 58.6 us -> 16.8 us  [spread(): return lax.all_to_all(copies, axes, 0, 0, tiled=True)]
    ppermute x13 -> x16, waiting for transfers between devices: 21.3 us -> 47.1 us  [swap(): return lax.ppermute(value, axis, [(i, i ^ bit) for i in range(size)])]
    ppermute x13 -> x16, starting transfers between devices: 45.5 us -> 61.3 us  [swap(): return lax.ppermute(value, axis, [(i, i ^ bit) for i in range(size)])]
    all_to_all x2 -> x3, starting transfers between devices: 12.8 us -> 26.6 us  [spread(): return lax.all_to_all(copies, axes, 0, 0, tiled=True)]
    dot_general x4, matrix products: 9.85 us -> 5.46 us  [dot(): lax.dot_general(left, right, (dims, ((), ())), precision=precision, prefe...]
    convert_element_type x1 -> x2, other arithmetic: 0.82 us -> 3.71 us  [slope_at(): return (cot.astype(F32) * gelu_slope(value) * scale).astype(BF)]
    unnamed x37 -> x43, local copies, waits for them, and re-layouts: 5.32 us -> 4.53 us
  transfers between devices with their start and end apart: 15 -> 19, of which waited for: 7 -> 11; matrix products, arithmetic and copies ran while one was open for 6% -> 4% of each run, Pallas kernels for 0% -> 0%
where the time goes in v6:
time: 187 us; the launch traced here: 186 us
  starting transfers between devices  87.8 us (47%)
  waiting for transfers between devices  47.1 us (25%)
  blocking collectives  16.8 us (9%)
  other arithmetic  12.5 us (7%)
  local copies, waits for them, and re-layouts  9.21 us (5%)
  matrix products  5.46 us (3%)
  Pallas kernels  5.23 us (3%)
    ppermute x16, starting transfers between devices, swap(): return lax.ppermute(value, axis, [(i, i ^ bit) for i in range(size)])  61.3 us
    ppermute x16, waiting for transfers between devices, swap(): return lax.ppermute(value, axis, [(i, i ^ bit) for i in range(size)])  47.1 us
    all_to_all x3, starting transfers between devices, spread(): return lax.all_to_all(copies, axes, 0, 0, tiled=True)  26.6 us
    all_to_all x1, blocking collectives, spread(): return lax.all_to_all(copies, axes, 0, 0, tiled=True)  16.8 us
    dot_general x4, matrix products, dot(): lax.dot_general(left, right, (dims, ((), ())), precision=precision, prefe...  5.46 us
    pallas_call x1, Pallas kernels, local_work(): pl.pallas_call(local_kernel, out_shape=[jax.ShapeDtypeStruct((32, 2, 16,...  5.23 us
    unnamed x43, local copies, waits for them, and re-layouts  4.53 us
    broadcast_in_dim x4, local copies, waits for them, and re-layouts, spread(): copies = jnp.broadcast_to(value[None], (count,) + value.shape)  4.25 us
  transfers between devices with their start and end apart: 19, of which 11 were waited for; matrix products, arithmetic and copies ran while one was open for 4% of the time, Pallas kernels for 0%

profile of v6, /device:TPU:1, one launch (start us, length us, event | category | flops | bytes accessed | tf_op | source)
XLA Modules:
  0.0 185.5 jit_solution(9385440209775269742)
XLA Ops:
  0.0 1.7 broadcast_in_dim.10
  1.7 14.3 %all-to-all-start = ((bf16[32,16,768]{2,1,0:T(8,128)(2,1)}), bf16[32,16,768]{2,1,0:T(8,128)(2,1)S(1)}, u32[]{:S(2)}, u32[]{:S(2)}) async-start(bf16[32,16,768]{2,1,0:T(8,128)(2,1)} %broadcast_in_dim.10), calls=%async_computation | async-start | bytes 1572864 | tf_op jit(solution)/shard_map/token_gather/all_to_all | solution.py:33
  16.0 4.8 %collective-permute-start = (bf16[128,384]{1,0:T(8,128)(2,1)S(1)}, bf16[128,384]{1,0:T(8,128)(2,1)S(1)}, u32[]{:S(2)}, u32[]{:S(2)}) collective-permute-start(bf16[128,384]{1,0:T(8,128)(2,1)S(1)} %copy-done.19), channel_id=1, source_target_pairs={{0,4},{4,0},{1,5},{5,1},{2,6},{6,2},{3,7},{7,3},{8,12},{12,8},{9,1... | collective-permute-start | bytes 294920 | tf_op jit(solution)/shard_map/token_gather/ppermute | solution.py:28
  20.8 13.1 %collective-permute-done = bf16[128,384]{1,0:T(8,128)(2,1)S(1)} collective-permute-done((bf16[128,384]{1,0:T(8,128)(2,1)S(1)}, bf16[128,384]{1,0:T(8,128)(2,1)S(1)}, u32[]{:S(2)}, u32[]{:S(2)}) %collective-permute-start) | collective-permute-done | bytes 98336 | tf_op jit(solution)/shard_map/token_gather/ppermute | solution.py:28
  33.9 4.4 %collective-permute-start.3 = (bf16[2,128,384]{2,1,0:T(8,128)(2,1)S(1)}, bf16[2,128,384]{2,1,0:T(8,128)(2,1)S(1)}, u32[]{:S(2)}, u32[]{:S(2)}) collective-permute-start(bf16[2,128,384]{2,1,0:T(8,128)(2,1)S(1)} %pad_maximum_fusion.2), channel_id=1, source_target_pairs={{0,3},{1,2},{2,1},{3,0},{4,7},{5,6},{6,5},{7,4},{8,11},{9,10},{10,... | collective-permute-start | bytes 589832 | tf_op jit(solution)/shard_map/token_gather/ppermute | solution.py:28
  38.3 2.4 %collective-permute-start.2 = (bf16[2,128,384]{2,1,0:T(8,128)(2,1)S(1)}, bf16[2,128,384]{2,1,0:T(8,128)(2,1)S(1)}, u32[]{:S(2)}, u32[]{:S(2)}) collective-permute-start(bf16[2,128,384]{2,1,0:T(8,128)(2,1)S(1)} %pad_maximum_fusion.2), channel_id=1, source_target_pairs={{0,2},{1,3},{2,0},{3,1},{4,6},{5,7},{6,4},{7,5},{8,10},{9,11},{10,... | collective-permute-start | bytes 589832 | tf_op jit(solution)/shard_map/token_gather/ppermute | solution.py:28
  40.8 2.2 %collective-permute-start.1 = (bf16[2,128,384]{2,1,0:T(8,128)(2,1)S(1)}, bf16[2,128,384]{2,1,0:T(8,128)(2,1)}, u32[]{:S(2)}, u32[]{:S(2)}) collective-permute-start(bf16[2,128,384]{2,1,0:T(8,128)(2,1)S(1)} %pad_maximum_fusion.2), channel_id=1, source_target_pairs={{0,1},{1,0},{2,3},{3,2},{4,5},{5,4},{6,7},{7,6},{8,9},{9,8},{10,11... | collective-permute-start | bytes 589832 | tf_op jit(solution)/shard_map/token_gather/ppermute | solution.py:28
  43.0 3.3 %collective-permute-done.2 = bf16[2,128,384]{2,1,0:T(8,128)(2,1)S(1)} collective-permute-done((bf16[2,128,384]{2,1,0:T(8,128)(2,1)S(1)}, bf16[2,128,384]{2,1,0:T(8,128)(2,1)S(1)}, u32[]{:S(2)}, u32[]{:S(2)}) %collective-permute-start.2) | collective-permute-done | bytes 196640 | tf_op jit(solution)/shard_map/token_gather/ppermute | solution.py:28
  46.3 0.7 copy-done.16
  46.9 2.7 %collective-permute-done.1 = bf16[2,128,384]{2,1,0:T(8,128)(2,1)} collective-permute-done((bf16[2,128,384]{2,1,0:T(8,128)(2,1)S(1)}, bf16[2,128,384]{2,1,0:T(8,128)(2,1)}, u32[]{:S(2)}, u32[]{:S(2)}) %collective-permute-start.1) | collective-permute-done | bytes 196640 | tf_op jit(solution)/shard_map/token_gather/ppermute | solution.py:28
  49.6 4.5 %collective-permute-start.4 = (bf16[32,16,768]{2,1,0:T(8,128)(2,1)S(1)}, bf16[32,16,768]{2,1,0:T(8,128)(2,1)S(1)}, u32[]{:S(2)}, u32[]{:S(2)}) collective-permute-start(bf16[32,16,768]{2,1,0:T(8,128)(2,1)S(1)} %all-to-all-done.mine), channel_id=1, source_target_pairs={{0,8},{8,0},{1,9},{9,1},{2,10},{10,2},{3,11},{11,3},{4,12},{12,4},... | collective-permute-start | bytes 2359304 | tf_op jit(solution)/shard_map/token_gather/ppermute | solution.py:28
  54.1 0.1 pad_add_fusion.at
  54.2 1.8 collective-permute-done.4.other
  56.0 1.1 copy-done
  57.1 5.2 %local_work.1 = (bf16[32,2,16,768]{3,2,1,0:T(8,128)(2,1)S(1)}, f32[256,384]{1,0:T(8,128)S(1)}, bf16[256,384]{1,0:T(8,128)(2,1)S(1)}, bf16[256,384]{1,0:T(8,128)(...) custom-call(s32[3]{0:T(128)S(1)} %pad_add_fusion.at, bf16[32,16,768]{2,1,0:T(8,128)(2,1)S(1)} %all-to-all-done.mine, ...), custom_call_target="tpu_custom_call" | custom-call | flops 1207959552 | bytes 8388608 | tf_op jit(solution)/shard_map/local_work/local_work/pallas_call | solution.py:118
  62.3 0.7 copy-done.1
  63.0 0.7 copy-done.2
  63.6 0.7 copy-done.3
  64.3 0.8 broadcast_in_dim.12
  65.1 5.5 %all-to-all-start.1 = ((bf16[8,24,1024]{2,1,0:T(8,128)(2,1)}), bf16[8,24,1024]{2,1,0:T(8,128)(2,1)S(1)}, u32[]{:S(2)}, u32[]{:S(2)}) async-start(bf16[8,24,1024]{2,1,0:T(8,128)(2,1)} %broadcast_in_dim.12), calls=%async_computation.1 | async-start | bytes 786432 | tf_op jit(solution)/shard_map/sums_x/all_to_all | solution.py:33
  70.6 3.4 %collective-permute-start.5 = (bf16[256,384]{1,0:T(8,128)(2,1)}, bf16[256,384]{1,0:T(8,128)(2,1)S(1)}, u32[]{:S(2)}, u32[]{:S(2)}) collective-permute-start(bf16[256,384]{1,0:T(8,128)(2,1)} %copy-done.3), channel_id=1, source_target_pairs={{0,1},{1,0},{2,3},{3,2},{4,5},{5,4},{6,7},{7,6},{8,9},{9,8},{10,11... | collective-permute-start | bytes 589832 | tf_op jit(solution)/shard_map/sums_x/ppermute | solution.py:28
  74.0 4.3 %collective-permute-start.6 = (bf16[256,384]{1,0:T(8,128)(2,1)}, bf16[256,384]{1,0:T(8,128)(2,1)S(1)}, u32[]{:S(2)}, u32[]{:S(2)}) collective-permute-start(bf16[256,384]{1,0:T(8,128)(2,1)} %copy-done.2), channel_id=1, source_target_pairs={{0,2},{1,3},{2,0},{3,1},{4,6},{5,7},{6,4},{7,5},{8,10},{9,11},{10,... | collective-permute-start | bytes 589832 | tf_op jit(solution)/shard_map/sums_x/ppermute | solution.py:28
  78.3 1.9 %collective-permute-start.7 = (bf16[256,384]{1,0:T(8,128)(2,1)}, bf16[256,384]{1,0:T(8,128)(2,1)S(1)}, u32[]{:S(2)}, u32[]{:S(2)}) collective-permute-start(bf16[256,384]{1,0:T(8,128)(2,1)} %copy-done.1), channel_id=1, source_target_pairs={{0,3},{1,2},{2,1},{3,0},{4,7},{5,6},{6,5},{7,4},{8,11},{9,10},{10,... | collective-permute-start | bytes 589832 | tf_op jit(solution)/shard_map/sums_x/ppermute | solution.py:28
  80.2 0.5 collective-permute-done.5
  80.7 6.2 %collective-permute-done.6 = bf16[256,384]{1,0:T(8,128)(2,1)S(1)} collective-permute-done((bf16[256,384]{1,0:T(8,128)(2,1)}, bf16[256,384]{1,0:T(8,128)(2,1)S(1)}, u32[]{:S(2)}, u32[]{:S(2)}) %collective-permute-start.6) | collective-permute-done | bytes 196640 | tf_op jit(solution)/shard_map/sums_x/ppermute | solution.py:28
  86.9 4.2 %collective-permute-done.7 = bf16[256,384]{1,0:T(8,128)(2,1)S(1)} collective-permute-done((bf16[256,384]{1,0:T(8,128)(2,1)}, bf16[256,384]{1,0:T(8,128)(2,1)S(1)}, u32[]{:S(2)}, u32[]{:S(2)}) %collective-permute-start.7) | collective-permute-done | bytes 196640 | tf_op jit(solution)/shard_map/sums_x/ppermute | solution.py:28
  91.1 0.1 convert_element_type.86
  91.2 0.1 fusion.44
  91.4 0.7 copy-done.4
  92.1 0.2 slice_add_fusion
  92.4 0.1 broadcast_multiply_fusion
  92.5 0.1 dynamic_slice.14
  92.5 0.3 fusion.28
  92.9 1.9 %collective-permute-start.14 = (bf16[16,1024]{1,0:T(8,128)(2,1)S(1)}, bf16[16,1024]{1,0:T(8,128)(2,1)S(1)}, u32[]{:S(2)}, u32[]{:S(2)}) collective-permute-start(bf16[16,1024]{1,0:T(8,128)(2,1)S(1)} %fusion.28), channel_id=1, source_target_pairs={{0,128},{128,0},{256,384},{384,256},{1,129},{129,1},{257,385},{385... | collective-permute-start | bytes 98312 | tf_op jit(solution)/shard_map/gram/ppermute | solution.py:28
  94.8 7.2 %collective-permute-start.13 = (bf16[16,1024]{1,0:T(8,128)(2,1)S(1)}, bf16[16,1024]{1,0:T(8,128)(2,1)S(1)}, u32[]{:S(2)}, u32[]{:S(2)}) collective-permute-start(bf16[16,1024]{1,0:T(8,128)(2,1)S(1)} %fusion.28), channel_id=1, source_target_pairs={{0,256},{128,384},{256,0},{384,128},{1,257},{129,385},{257,1},{385... | collective-permute-start | bytes 98312 | tf_op jit(solution)/shard_map/gram/ppermute | solution.py:28
  102.0 3.0 %collective-permute-start.12 = (bf16[16,1024]{1,0:T(8,128)(2,1)S(1)}, bf16[16,1024]{1,0:T(8,128)(2,1)S(1)}, u32[]{:S(2)}, u32[]{:S(2)}) collective-permute-start(bf16[16,1024]{1,0:T(8,128)(2,1)S(1)} %fusion.28), channel_id=1, source_target_pairs={{0,384},{128,256},{256,128},{384,0},{1,385},{129,257},{257,129},{3... | collective-permute-start | bytes 98312 | tf_op jit(solution)/shard_map/gram/ppermute | solution.py:28
  105.1 3.4 %collective-permute-done.12 = bf16[16,1024]{1,0:T(8,128)(2,1)S(1)} collective-permute-done((bf16[16,1024]{1,0:T(8,128)(2,1)S(1)}, bf16[16,1024]{1,0:T(8,128)(2,1)S(1)}, u32[]{:S(2)}, u32[]{:S(2)}) %collective-permute-start.12) | collective-permute-done | bytes 32800 | tf_op jit(solution)/shard_map/gram/ppermute | solution.py:28
  108.5 1.1 broadcast_in_dim.13
  109.6 6.7 %all-to-all-start.2 = ((bf16[8,4,16,1024]{3,2,1,0:T(8,128)(2,1)}), bf16[8,4,16,1024]{3,2,1,0:T(8,128)(2,1)S(1)}, u32[]{:S(2)}, u32[]{:S(2)}) async-start(bf16[8,4,16,1024]{3,2,1,0:T(8,128)(2,1)} %broadcast_in_dim.13), calls=%async_computation.2 | async-start | bytes 2097152 | tf_op jit(solution)/shard_map/gram/all_to_all | solution.py:33
  116.4 1.0 fusion.35
  117.4 8.0 %collective-permute-start.8 = (bf16[256,384]{1,0:T(8,128)(2,1)S(1)}, bf16[256,384]{1,0:T(8,128)(2,1)S(1)}, u32[]{:S(2)}, u32[]{:S(2)}) collective-permute-start(bf16[256,384]{1,0:T(8,128)(2,1)S(1)} %fusion.35), channel_id=1, source_target_pairs={{0,4},{4,0},{1,5},{5,1},{2,6},{6,2},{3,7},{7,3},{8,12},{12,8},{9,1... | collective-permute-start | bytes 589832 | tf_op jit(solution)/shard_map/gram/ppermute | solution.py:28
  125.4 1.7 fusion.2
  127.1 5.2 %collective-permute-done.8 = bf16[256,384]{1,0:T(8,128)(2,1)S(1)} collective-permute-done((bf16[256,384]{1,0:T(8,128)(2,1)S(1)}, bf16[256,384]{1,0:T(8,128)(2,1)S(1)}, u32[]{:S(2)}, u32[]{:S(2)}) %collective-permute-start.8) | collective-permute-done | bytes 196640 | tf_op jit(solution)/shard_map/gram/ppermute | solution.py:28
  132.4 1.0 slice_add_fusion.4
  133.4 0.6 fusion.26
  134.0 1.9 %collective-permute-start.11 = (bf16[256,384]{1,0:T(8,128)(2,1)S(1)}, bf16[256,384]{1,0:T(8,128)(2,1)S(1)}, u32[]{:S(2)}, u32[]{:S(2)}) collective-permute-start(bf16[256,384]{1,0:T(8,128)(2,1)S(1)} %fusion.26), channel_id=1, source_target_pairs={{0,1},{1,0},{2,3},{3,2},{4,5},{5,4},{6,7},{7,6},{8,9},{9,8},{10,11... | collective-permute-start | bytes 589832 | tf_op jit(solution)/shard_map/pre/ppermute | solution.py:28
  135.9 3.4 %collective-permute-start.10 = (bf16[256,384]{1,0:T(8,128)(2,1)S(1)}, bf16[256,384]{1,0:T(8,128)(2,1)S(1)}, u32[]{:S(2)}, u32[]{:S(2)}) collective-permute-start(bf16[256,384]{1,0:T(8,128)(2,1)S(1)} %fusion.26), channel_id=1, source_target_pairs={{0,2},{1,3},{2,0},{3,1},{4,6},{5,7},{6,4},{7,5},{8,10},{9,11},{10,... | collective-permute-start | bytes 589832 | tf_op jit(solution)/shard_map/pre/ppermute | solution.py:28
  139.3 4.3 %collective-permute-start.9 = (bf16[256,384]{1,0:T(8,128)(2,1)S(1)}, bf16[256,384]{1,0:T(8,128)(2,1)S(1)}, u32[]{:S(2)}, u32[]{:S(2)}) collective-permute-start(bf16[256,384]{1,0:T(8,128)(2,1)S(1)} %fusion.26), channel_id=1, source_target_pairs={{0,3},{1,2},{2,1},{3,0},{4,7},{5,6},{6,5},{7,4},{8,11},{9,10},{10,... | collective-permute-start | bytes 589832 | tf_op jit(solution)/shard_map/pre/ppermute | solution.py:28
  143.6 2.2 %collective-permute-done.10 = bf16[256,384]{1,0:T(8,128)(2,1)S(1)} collective-permute-done((bf16[256,384]{1,0:T(8,128)(2,1)S(1)}, bf16[256,384]{1,0:T(8,128)(2,1)S(1)}, u32[]{:S(2)}, u32[]{:S(2)}) %collective-permute-start.10) | collective-permute-done | bytes 196640 | tf_op jit(solution)/shard_map/pre/ppermute | solution.py:28
  145.8 4.6 %collective-permute-done.9 = bf16[256,384]{1,0:T(8,128)(2,1)S(1)} collective-permute-done((bf16[256,384]{1,0:T(8,128)(2,1)S(1)}, bf16[256,384]{1,0:T(8,128)(2,1)S(1)}, u32[]{:S(2)}, u32[]{:S(2)}) %collective-permute-start.9) | collective-permute-done | bytes 196640 | tf_op jit(solution)/shard_map/pre/ppermute | solution.py:28
  150.4 3.8 %collective-permute-start.15 = (bf16[32,16,1024]{2,1,0:T(8,128)(2,1)S(1)}, bf16[32,16,1024]{2,1,0:T(8,128)(2,1)}, u32[]{:S(2)}, u32[]{:S(2)}) collective-permute-start(bf16[32,16,1024]{2,1,0:T(8,128)(2,1)S(1)} %bitcast.67), channel_id=1, source_target_pairs={{0,8},{8,0},{1,9},{9,1},{2,10},{10,2},{3,11},{11,3},{4,12},{12,4},... | collective-permute-start | bytes 3145736 | tf_op jit(solution)/shard_map/pre/ppermute | solution.py:28
  154.3 1.0 select_bitcast_fusion.5
  155.3 1.0 broadcast_select_fusion.7
  156.4 0.1 maximum_convert_fusion
  156.5 0.8 fusion.9
  157.3 1.4 select_bitcast_fusion.1
  158.7 0.2 pad_maximum_fusion
  158.9 0.3 copy.34
  159.2 2.5 %multiply_reduce_fusion = (f32[]{:T(128)}, f32[1024,384]{1,0:T(8,128)S(1)}) fusion(bf16[256,384]{1,0:T(8,128)(2,1)S(1)} %get-tuple-element.38, bf16[256,384]{1,0:T(8,128)(2,1)S(1)} %get-tuple-element.37, bf16[256,384]{1,0:T(8,128)(2,1)S(1)} %get-tuple-element.36, bf16[256,384]{1,0:T(8,128)(2,1)S(1)} %get-tuple-element.35, ...), kind=kOutput, calls=%fused_computation.29 | convolution fusion | flops 817102848 | bytes 6029316 | tf_op jit(solution)/shard_map/ascent/dot_general | solution.py:63
  161.7 0.7 broadcast_in_dim.14
  162.4 16.8 %all_to_all.20 = f32[64,1,128]{2,1,0:T(1,128)S(1)} all-to-all(f32[64,1,128]{2,1,0:T(1,128)S(1)} %broadcast_in_dim.14), channel_id=1, replica_groups=mesh['yl'=4,'z'=8,'c'=2,'yh'=2,'x'=4] {'yl','z','c'}, dimensions={0} | all-to-all | bytes 65536 | tf_op jit(solution)/shard_map/ascent/all_to_all | solution.py:33
  179.2 0.7 slice_reduce_fusion.1
  180.6 2.9 %fusion.23 = bf16[1024,384]{1,0:T(8,128)(2,1)S(1)} fusion(f32[1024,384]{1,0:T(8,128)S(1)} %get-tuple-element.50, f32[]{:T(128)S(6)} %div.19, bf16[256,384]{1,0:T(8,128)(2,1)S(1)} %get-tuple-element.38, bf16[256,384]{1,0:T(8,128)(2,1)S(1)} %get-tuple-element.37, bf16[256,384]{1,0:T(8,128)(2,1)S(1)} %get-tuple-element.36, ...), kind=kLoop, calls=%fused_computation.28 | loop fusion | flops 11403264 | bytes 3932164 | tf_op jit(solution)/shard_map/sharp/convert_element_type | solution.py:191
  183.5 2.0 %fusion.49 = f32[768,384]{1,0:T(8,128)} fusion(bf16[1024,768]{1,0:T(8,128)(2,1)S(1)} %copy-done.5, bf16[1024,384]{1,0:T(8,128)(2,1)S(1)} %fusion.23), kind=kOutput, calls=%fused_computation.107 | convolution fusion | flops 603979776 | bytes 3538944 | tf_op jit(solution)/shard_map/sharp/dot_general | solution.py:63
  (55 shorter events, 0.3 us)
Async XLA Ops:
  0.0 16.0 %copy-start.19 = (bf16[128,384]{1,0:T(8,128)(2,1)S(1)}, bf16[128,384]{1,0:T(8,128)(2,1)}, u32[]{:S(2)}) copy-start(bf16[128,384]{1,0:T(8,128)(2,1)} %param.7) | copy-start | bytes 294916
  0.0 54.1 %copy-start.20 = (f32[768]{0:T(1024)S(1)}, f32[768]{0:T(1024)}, u32[]{:S(2)}) copy-start(f32[768]{0:T(1024)} %param.5) | copy-start | bytes 9220
  1.7 47.9 %all-to-all-start = ((bf16[32,16,768]{2,1,0:T(8,128)(2,1)}), bf16[32,16,768]{2,1,0:T(8,128)(2,1)S(1)}, u32[]{:S(2)}, u32[]{:S(2)}) async-start(bf16[32,16,768]{2,1,0:T(8,128)(2,1)} %broadcast_in_dim.10), calls=%async_computation | async-start | bytes 1572864 | tf_op jit(solution)/shard_map/token_gather/all_to_all | solution.py:33
  16.0 17.8 %collective-permute-start = (bf16[128,384]{1,0:T(8,128)(2,1)S(1)}, bf16[128,384]{1,0:T(8,128)(2,1)S(1)}, u32[]{:S(2)}, u32[]{:S(2)}) collective-permute-start(bf16[128,384]{1,0:T(8,128)(2,1)S(1)} %copy-done.19), channel_id=1, source_target_pairs={{0,4},{4,0},{1,5},{5,1},{2,6},{6,2},{3,7},{7,3},{8,12},{12,8},{9,1... | collective-permute-start | bytes 294920 | tf_op jit(solution)/shard_map/token_gather/ppermute | solution.py:28
  33.9 12.4 %copy-start.6 = (bf16[1,128,384]{2,1,0:T(8,128)(2,1)}, bf16[1,128,384]{2,1,0:T(8,128)(2,1)S(1)}, u32[]{:S(2)}) copy-start(bf16[1,128,384]{2,1,0:T(8,128)(2,1)S(1)} %get-tuple-element.43) | copy-start | bytes 294916
  33.9 12.4 %copy-start.8 = (bf16[1,128,384]{2,1,0:T(8,128)(2,1)}, bf16[1,128,384]{2,1,0:T(8,128)(2,1)S(1)}, u32[]{:S(2)}) copy-start(bf16[1,128,384]{2,1,0:T(8,128)(2,1)S(1)} %get-tuple-element.44) | copy-start | bytes 294916
  33.9 9.0 %collective-permute-start.3 = (bf16[2,128,384]{2,1,0:T(8,128)(2,1)S(1)}, bf16[2,128,384]{2,1,0:T(8,128)(2,1)S(1)}, u32[]{:S(2)}, u32[]{:S(2)}) collective-permute-start(bf16[2,128,384]{2,1,0:T(8,128)(2,1)S(1)} %pad_maximum_fusion.2), channel_id=1, source_target_pairs={{0,3},{1,2},{2,1},{3,0},{4,7},{5,6},{6,5},{7,4},{8,11},{9,10},{10,... | collective-permute-start | bytes 589832 | tf_op jit(solution)/shard_map/token_gather/ppermute | solution.py:28
  38.3 7.9 %collective-permute-start.2 = (bf16[2,128,384]{2,1,0:T(8,128)(2,1)S(1)}, bf16[2,128,384]{2,1,0:T(8,128)(2,1)S(1)}, u32[]{:S(2)}, u32[]{:S(2)}) collective-permute-start(bf16[2,128,384]{2,1,0:T(8,128)(2,1)S(1)} %pad_maximum_fusion.2), channel_id=1, source_target_pairs={{0,2},{1,3},{2,0},{3,1},{4,6},{5,7},{6,4},{7,5},{8,10},{9,11},{10,... | collective-permute-start | bytes 589832 | tf_op jit(solution)/shard_map/token_gather/ppermute | solution.py:28
  40.8 8.9 %collective-permute-start.1 = (bf16[2,128,384]{2,1,0:T(8,128)(2,1)S(1)}, bf16[2,128,384]{2,1,0:T(8,128)(2,1)}, u32[]{:S(2)}, u32[]{:S(2)}) collective-permute-start(bf16[2,128,384]{2,1,0:T(8,128)(2,1)S(1)} %pad_maximum_fusion.2), channel_id=1, source_target_pairs={{0,1},{1,0},{2,3},{3,2},{4,5},{5,4},{6,7},{7,6},{8,9},{9,8},{10,11... | collective-permute-start | bytes 589832 | tf_op jit(solution)/shard_map/token_gather/ppermute | solution.py:28
  42.9 3.3 %copy-start.14 = (bf16[2,128,384]{2,1,0:T(8,128)(2,1)}, bf16[2,128,384]{2,1,0:T(8,128)(2,1)S(1)}, u32[]{:S(2)}) copy-start(bf16[2,128,384]{2,1,0:T(8,128)(2,1)S(1)} %collective-permute-done.3) | copy-start | bytes 589828
  46.3 0.7 copy-start.16
  49.6 6.4 %collective-permute-start.4 = (bf16[32,16,768]{2,1,0:T(8,128)(2,1)S(1)}, bf16[32,16,768]{2,1,0:T(8,128)(2,1)S(1)}, u32[]{:S(2)}, u32[]{:S(2)}) collective-permute-start(bf16[32,16,768]{2,1,0:T(8,128)(2,1)S(1)} %all-to-all-done.mine), channel_id=1, source_target_pairs={{0,8},{8,0},{1,9},{9,1},{2,10},{10,2},{3,11},{11,3},{4,12},{12,4},... | collective-permute-start | bytes 2359304 | tf_op jit(solution)/shard_map/token_gather/ppermute | solution.py:28
  56.0 1.1 copy-start
  62.3 0.7 copy-start.1
  63.0 0.7 copy-start.2
  63.6 0.7 copy-start.3
  65.1 26.0 %all-to-all-start.1 = ((bf16[8,24,1024]{2,1,0:T(8,128)(2,1)}), bf16[8,24,1024]{2,1,0:T(8,128)(2,1)S(1)}, u32[]{:S(2)}, u32[]{:S(2)}) async-start(bf16[8,24,1024]{2,1,0:T(8,128)(2,1)} %broadcast_in_dim.12), calls=%async_computation.1 | async-start | bytes 786432 | tf_op jit(solution)/shard_map/sums_x/all_to_all | solution.py:33
  70.6 10.1 %collective-permute-start.5 = (bf16[256,384]{1,0:T(8,128)(2,1)}, bf16[256,384]{1,0:T(8,128)(2,1)S(1)}, u32[]{:S(2)}, u32[]{:S(2)}) collective-permute-start(bf16[256,384]{1,0:T(8,128)(2,1)} %copy-done.3), channel_id=1, source_target_pairs={{0,1},{1,0},{2,3},{3,2},{4,5},{5,4},{6,7},{7,6},{8,9},{9,8},{10,11... | collective-permute-start | bytes 589832 | tf_op jit(solution)/shard_map/sums_x/ppermute | solution.py:28
  74.0 12.9 %collective-permute-start.6 = (bf16[256,384]{1,0:T(8,128)(2,1)}, bf16[256,384]{1,0:T(8,128)(2,1)S(1)}, u32[]{:S(2)}, u32[]{:S(2)}) collective-permute-start(bf16[256,384]{1,0:T(8,128)(2,1)} %copy-done.2), channel_id=1, source_target_pairs={{0,2},{1,3},{2,0},{3,1},{4,6},{5,7},{6,4},{7,5},{8,10},{9,11},{10,... | collective-permute-start | bytes 589832 | tf_op jit(solution)/shard_map/sums_x/ppermute | solution.py:28
  78.3 12.8 %collective-permute-start.7 = (bf16[256,384]{1,0:T(8,128)(2,1)}, bf16[256,384]{1,0:T(8,128)(2,1)S(1)}, u32[]{:S(2)}, u32[]{:S(2)}) collective-permute-start(bf16[256,384]{1,0:T(8,128)(2,1)} %copy-done.1), channel_id=1, source_target_pairs={{0,3},{1,2},{2,1},{3,0},{4,7},{5,6},{6,5},{7,4},{8,11},{9,10},{10,... | collective-permute-start | bytes 589832 | tf_op jit(solution)/shard_map/sums_x/ppermute | solution.py:28
  86.9 29.4 %copy-start.10 = (bf16[256,384]{1,0:T(8,128)(2,1)}, bf16[256,384]{1,0:T(8,128)(2,1)S(1)}, u32[]{:S(2)}) copy-start(bf16[256,384]{1,0:T(8,128)(2,1)S(1)} %collective-permute-done.6) | copy-start | bytes 589828
  91.1 18.5 %copy-start.12 = (bf16[256,384]{1,0:T(8,128)(2,1)}, bf16[256,384]{1,0:T(8,128)(2,1)S(1)}, u32[]{:S(2)}) copy-start(bf16[256,384]{1,0:T(8,128)(2,1)S(1)} %collective-permute-done.7) | copy-start | bytes 589828
  91.2 0.9 copy-start.4
  92.9 12.2 %collective-permute-start.14 = (bf16[16,1024]{1,0:T(8,128)(2,1)S(1)}, bf16[16,1024]{1,0:T(8,128)(2,1)S(1)}, u32[]{:S(2)}, u32[]{:S(2)}) collective-permute-start(bf16[16,1024]{1,0:T(8,128)(2,1)S(1)} %fusion.28), channel_id=1, source_target_pairs={{0,128},{128,0},{256,384},{384,256},{1,129},{129,1},{257,385},{385... | collective-permute-start | bytes 98312 | tf_op jit(solution)/shard_map/gram/ppermute | solution.py:28
  94.8 10.2 %collective-permute-start.13 = (bf16[16,1024]{1,0:T(8,128)(2,1)S(1)}, bf16[16,1024]{1,0:T(8,128)(2,1)S(1)}, u32[]{:S(2)}, u32[]{:S(2)}) collective-permute-start(bf16[16,1024]{1,0:T(8,128)(2,1)S(1)} %fusion.28), channel_id=1, source_target_pairs={{0,256},{128,384},{256,0},{384,128},{1,257},{129,385},{257,1},{385... | collective-permute-start | bytes 98312 | tf_op jit(solution)/shard_map/gram/ppermute | solution.py:28
  102.0 6.5 %collective-permute-start.12 = (bf16[16,1024]{1,0:T(8,128)(2,1)S(1)}, bf16[16,1024]{1,0:T(8,128)(2,1)S(1)}, u32[]{:S(2)}, u32[]{:S(2)}) collective-permute-start(bf16[16,1024]{1,0:T(8,128)(2,1)S(1)} %fusion.28), channel_id=1, source_target_pairs={{0,384},{128,256},{256,128},{384,0},{1,385},{129,257},{257,129},{3... | collective-permute-start | bytes 98312 | tf_op jit(solution)/shard_map/gram/ppermute | solution.py:28
  109.6 40.8 %all-to-all-start.2 = ((bf16[8,4,16,1024]{3,2,1,0:T(8,128)(2,1)}), bf16[8,4,16,1024]{3,2,1,0:T(8,128)(2,1)S(1)}, u32[]{:S(2)}, u32[]{:S(2)}) async-start(bf16[8,4,16,1024]{3,2,1,0:T(8,128)(2,1)} %broadcast_in_dim.13), calls=%async_computation.2 | async-start | bytes 2097152 | tf_op jit(solution)/shard_map/gram/all_to_all | solution.py:33
  117.4 14.9 %collective-permute-start.8 = (bf16[256,384]{1,0:T(8,128)(2,1)S(1)}, bf16[256,384]{1,0:T(8,128)(2,1)S(1)}, u32[]{:S(2)}, u32[]{:S(2)}) collective-permute-start(bf16[256,384]{1,0:T(8,128)(2,1)S(1)} %fusion.35), channel_id=1, source_target_pairs={{0,4},{4,0},{1,5},{5,1},{2,6},{6,2},{3,7},{7,3},{8,12},{12,8},{9,1... | collective-permute-start | bytes 589832 | tf_op jit(solution)/shard_map/gram/ppermute | solution.py:28
  125.4 8.0 %copy-start.11 = (bf16[256,384]{1,0:T(8,128)(2,1)S(1)}, bf16[256,384]{1,0:T(8,128)(2,1)}, u32[]{:S(2)}) copy-start(bf16[256,384]{1,0:T(8,128)(2,1)} %copy-done.10) | copy-start | bytes 589828
  125.4 8.0 %copy-start.13 = (bf16[256,384]{1,0:T(8,128)(2,1)S(1)}, bf16[256,384]{1,0:T(8,128)(2,1)}, u32[]{:S(2)}) copy-start(bf16[256,384]{1,0:T(8,128)(2,1)} %copy-done.12) | copy-start | bytes 589828
  125.4 28.9 %copy-start.7 = (bf16[1,128,384]{2,1,0:T(8,128)(2,1)S(1)}, bf16[1,128,384]{2,1,0:T(8,128)(2,1)}, u32[]{:S(2)}) copy-start(bf16[1,128,384]{2,1,0:T(8,128)(2,1)} %copy-done.6) | copy-start | bytes 294916
  125.4 28.9 %copy-start.9 = (bf16[1,128,384]{2,1,0:T(8,128)(2,1)S(1)}, bf16[1,128,384]{2,1,0:T(8,128)(2,1)}, u32[]{:S(2)}) copy-start(bf16[1,128,384]{2,1,0:T(8,128)(2,1)} %copy-done.8) | copy-start | bytes 294916
  127.1 27.2 %copy-start.15 = (bf16[2,128,384]{2,1,0:T(8,128)(2,1)S(1)}, bf16[2,128,384]{2,1,0:T(8,128)(2,1)}, u32[]{:S(2)}) copy-start(bf16[2,128,384]{2,1,0:T(8,128)(2,1)} %copy-done.14) | copy-start | bytes 589828
  127.1 27.2 %copy-start.17 = (bf16[2,128,384]{2,1,0:T(8,128)(2,1)S(1)}, bf16[2,128,384]{2,1,0:T(8,128)(2,1)}, u32[]{:S(2)}) copy-start(bf16[2,128,384]{2,1,0:T(8,128)(2,1)} %copy-done.16) | copy-start | bytes 589828
  134.0 9.6 %collective-permute-start.11 = (bf16[256,384]{1,0:T(8,128)(2,1)S(1)}, bf16[256,384]{1,0:T(8,128)(2,1)S(1)}, u32[]{:S(2)}, u32[]{:S(2)}) collective-permute-start(bf16[256,384]{1,0:T(8,128)(2,1)S(1)} %fusion.26), channel_id=1, source_target_pairs={{0,1},{1,0},{2,3},{3,2},{4,5},{5,4},{6,7},{7,6},{8,9},{9,8},{10,11... | collective-permute-start | bytes 589832 | tf_op jit(solution)/shard_map/pre/ppermute | solution.py:28
  135.9 9.9 %collective-permute-start.10 = (bf16[256,384]{1,0:T(8,128)(2,1)S(1)}, bf16[256,384]{1,0:T(8,128)(2,1)S(1)}, u32[]{:S(2)}, u32[]{:S(2)}) collective-permute-start(bf16[256,384]{1,0:T(8,128)(2,1)S(1)} %fusion.26), channel_id=1, source_target_pairs={{0,2},{1,3},{2,0},{3,1},{4,6},{5,7},{6,4},{7,5},{8,10},{9,11},{10,... | collective-permute-start | bytes 589832 | tf_op jit(solution)/shard_map/pre/ppermute | solution.py:28
  139.3 11.1 %collective-permute-start.9 = (bf16[256,384]{1,0:T(8,128)(2,1)S(1)}, bf16[256,384]{1,0:T(8,128)(2,1)S(1)}, u32[]{:S(2)}, u32[]{:S(2)}) collective-permute-start(bf16[256,384]{1,0:T(8,128)(2,1)S(1)} %fusion.26), channel_id=1, source_target_pairs={{0,3},{1,2},{2,1},{3,0},{4,7},{5,6},{6,5},{7,4},{8,11},{9,10},{10,... | collective-permute-start | bytes 589832 | tf_op jit(solution)/shard_map/pre/ppermute | solution.py:28
  150.4 3.9 %copy-start.18 = (bf16[256,384]{1,0:T(8,128)(2,1)}, bf16[256,384]{1,0:T(8,128)(2,1)S(1)}, u32[]{:S(2)}) copy-start(bf16[256,384]{1,0:T(8,128)(2,1)S(1)} %collective-permute-done.9) | copy-start | bytes 589828
  150.4 6.9 %collective-permute-start.15 = (bf16[32,16,1024]{2,1,0:T(8,128)(2,1)S(1)}, bf16[32,16,1024]{2,1,0:T(8,128)(2,1)}, u32[]{:S(2)}, u32[]{:S(2)}) collective-permute-start(bf16[32,16,1024]{2,1,0:T(8,128)(2,1)S(1)} %bitcast.67), channel_id=1, source_target_pairs={{0,8},{8,0},{1,9},{9,1},{2,10},{10,2},{3,11},{11,3},{4,12},{12,4},... | collective-permute-start | bytes 3145736 | tf_op jit(solution)/shard_map/pre/ppermute | solution.py:28
  180.6 2.9 %copy-start.5 = (bf16[1024,768]{1,0:T(8,128)(2,1)S(1)}, bf16[1024,768]{1,0:T(8,128)(2,1)}, u32[]{:S(2)}) copy-start(bf16[1024,768]{1,0:T(8,128)(2,1)} %fusion.2) | copy-start | bytes 4718596

commit v7 on v5

v7 whole, which is shorter than its diff:
```python
import math

import jax
import jax.numpy as jnp
from jax import lax
from jax.experimental import pallas as pl
from jax.experimental.pallas import tpu as pltpu
from jax.sharding import Mesh
from jax.sharding import PartitionSpec as P

FF = 24576
D = 6144
TOKENS = 1024
DP = ("yl", "z", "c")
MP = ("yh", "x")
BF = jnp.bfloat16
F32 = jnp.float32


def gelu_slope(value):
    cdf = 0.5 * (1.0 + lax.erf(value * (1.0 / math.sqrt(2.0))))
    dens = jnp.exp(-0.5 * value * value) * (1.0 / math.sqrt(2.0 * math.pi))
    return cdf + value * dens


def swap(value, axis, bit):
    size = lax.axis_size(axis)
    return lax.ppermute(value, axis, [(i, i ^ bit) for i in range(size)])


def spread(value, axes, count):
    copies = jnp.broadcast_to(value[None], (count,) + value.shape)
    return lax.all_to_all(copies, axes, 0, 0, tiled=True)


def after(value, *others):
    return lax.optimization_barrier((value,) + others)[0]


def gather_x(value):
    return [value] + [swap(value, "x", b) for b in (1, 2, 3)]


def dot(left, right, dims, precision=None):
    return lax.dot_general(left, right, (dims, ((), ())), precision=precision, preferred_element_type=F32)


def split(value, count):
    out = []
    for _ in range(count):
        out.append(value.astype(BF).astype(F32))
        value = value - out[-1]
    return out


def local_kernel(at, mine, other, gain, w, joined, own, near, opposite, far, sent, high, part, out, sems):
    place, core, x = at[0], at[1], at[2]
    g = gain[...]
    width = g.shape[1]
    ones = jnp.ones((8, width), BF)
    gains = jnp.concatenate(split(g, 3) + [jnp.zeros((5, width), F32)], axis=0).astype(BF)
    local, css, lean = [], [], []
    for i in range(8):
        chips = pl.ds(4 * i, 4)
        joined[chips, core] = mine[chips]
        joined[chips, 1 - core] = other[chips]
        raw = joined[chips].reshape(128, width)
        value = raw.astype(F32)
        centred = value - jnp.sum(value, axis=1, keepdims=True) * (1.0 / width)
        full = centred * g
        first = full.astype(BF)
        second = (full - first.astype(F32)).astype(BF)
        high[pl.ds(128 * i, 128)] = first
        rows = dot(first, w[...], ((1,), (0,))) + dot(second, w[...], ((1,), (0,)))
        part[i // 2, pl.ds(128 * (i % 2), 128)] = rows
        square = centred * centred
        top = square.astype(BF)
        rest = (square - top.astype(F32)).astype(BF)
        across = ((1,), (1,))
        local.append(dot(ones, raw, across)[:1] * (1.0 / width))
        css.append((dot(ones, top, across) + dot(ones, rest, across))[:1])
        lean.append(jnp.sum(dot(gains, first, across), axis=0, keepdims=True))
    own[...] = part[x]
    copies = []
    for b, target in ((1, near), (2, opposite), (3, far)):
        out[b - 1] = part[x ^ b].astype(BF)
        copies.append(pltpu.make_async_copy(out.at[b - 1], target, sems.at[b - 1]))
        copies[-1].start()
    gram = dot(high[pl.ds(pl.multiple_of(place * 16, 16), 16)], high[...], ((1,), (1,)))
    local, css, lean = (jnp.concatenate(v, axis=1) for v in (local, css, lean))
    column = jnp.sum(dot(gains, w[...], ((1,), (0,))), axis=0, keepdims=True)
    power = jnp.broadcast_to(jnp.sum(g * g, axis=1, keepdims=True), (1, 128))
    extra = jnp.concatenate(split(column, 2) + split(power, 2), axis=1)
    rows = [gram] + split(local, 3) + split(css, 2) + split(lean, 2) + [extra]
    sent[...] = jnp.concatenate(rows, axis=0).astype(BF)
    for copy in copies:
        copy.wait()


def local_work(at, mine, other, gain, w):
    width, columns = w.shape
    block = jax.ShapeDtypeStruct((256, columns), BF)
    vmem = pl.BlockSpec(memory_space=pltpu.VMEM)
    return pl.pallas_call(
        local_kernel,
        out_shape=[
            jax.ShapeDtypeStruct((32, 2, 16, width), BF),
            jax.ShapeDtypeStruct((256, columns), F32),
            block,
            block,
            block,
            jax.ShapeDtypeStruct((24, TOKENS), BF),
        ],
        in_specs=[pl.BlockSpec(memory_space=pltpu.SMEM)] + [vmem] * 4,
        out_specs=[vmem] * 2 + [pl.BlockSpec(memory_space=pl.ANY)] * 3 + [vmem],
        scratch_shapes=[
            pltpu.VMEM((TOKENS, width), BF),
            pltpu.VMEM((4, 256, columns), F32),
            pltpu.VMEM((3, 256, columns), BF),
            pltpu.SemaphoreType.DMA((3,)),
        ],
        compiler_params=pltpu.CompilerParams(vmem_limit_bytes=40 << 20),
        cost_estimate=pl.CostEstimate(flops=2 * TOKENS * width * columns * 2, bytes_accessed=8 << 20, transcendentals=0),
        name="local_work",
    )(at, mine, other, gain, w)


def stats_kernel(at, got, own, one, two, three, cot, cot_other, rows, half, full, pair, scales, turned):
    place, x, low = at[0], at[2], at[3] == 0
    exact = lax.Precision.HIGHEST
    columns = own.shape[1]
    total = own[...] + one[...].astype(F32) + two[...].astype(F32) + three[...].astype(F32)
    half[...] = total.astype(BF)
    pair[at[3]] = cot[...]
    pair[1 - at[3]] = cot_other[...]
    gram = got[0, :16].astype(F32)
    for j in range(1, 8):
        gram = gram + got[j, :16].astype(F32)
    terms = [got[j, 16:24].astype(F32) for j in range(8)]
    local = jnp.concatenate([t[0:1] + t[1:2] + t[2:3] for t in terms], axis=0)
    css = jnp.concatenate([t[3:4] + t[4:5] for t in terms], axis=0)
    lean = jnp.concatenate([t[5:6] + t[6:7] for t in terms], axis=0)
    column = jnp.concatenate([t[7:8, :columns] + t[7:8, columns : 2 * columns] for t in terms], axis=0)
    power = jnp.concatenate([t[7:8, 2 * columns : 2 * columns + 1] + t[7:8, 2 * columns + 128 : 2 * columns + 129] for t in terms], axis=0)
    mean = jnp.sum(local, axis=0, keepdims=True) / 8
    apart = local - mean
    var = (jnp.sum(css, axis=0, keepdims=True) + (D // 8) * jnp.sum(apart * apart, axis=0, keepdims=True)) / D
    inv = lax.rsqrt(var + 1e-06)
    flat = jnp.concatenate([lean, apart, power * apart, apart, inv, mean, jnp.zeros((94, TOKENS), F32)], axis=0)
    turned[...] = flat.T
    mine = turned[pl.ds(pl.multiple_of(place * 16, 16), 16)]
    right = jnp.concatenate([apart, lean, apart], axis=0)
    gram = (gram + dot(mine[:, :24], right, ((1,), (0,)), exact)) * mine[:, 32:33] * inv
    rows[...] = gram.astype(BF)
    here = turned[pl.ds(pl.multiple_of(x * 256, 256), 256)]
    full[...] = total + dot(here[:, 24:32], column, ((1,), (0,)), exact)
    scales[...] = turned[...]


def stats_work(at, got, own, moved, cot, cot_other):
    columns = own.shape[1]
    vmem = pl.BlockSpec(memory_space=pltpu.VMEM)
    return pl.pallas_call(
        stats_kernel,
        out_shape=[
            jax.ShapeDtypeStruct((16, TOKENS), BF),
            jax.ShapeDtypeStruct((256, columns), BF),
            jax.ShapeDtypeStruct((256, columns), F32),
            jax.ShapeDtypeStruct((2, 128, columns), BF),
            jax.ShapeDtypeStruct((TOKENS, 128), F32),
        ],
        in_specs=[pl.BlockSpec(memory_space=pltpu.SMEM)] + [vmem] * 7,
        out_specs=[vmem] * 5,
        scratch_shapes=[pltpu.VMEM((TOKENS, 128), F32)],
        compiler_params=pltpu.CompilerParams(vmem_limit_bytes=40 << 20),
        cost_estimate=pl.CostEstimate(flops=10 << 20, bytes_accessed=3 << 20, transcendentals=0),
        name="stats_work",
    )(at, got, own, *moved, cot, cot_other)


def pre_kernel(at, full, moved, scales, one, two, three, out):
    inv = scales[pl.ds(pl.multiple_of(at[2] * 256, 256), 256)][:, 32:33]
    out[...] = ((full[...] + moved[...].astype(F32)) * inv).astype(BF)


def pre_work(at, full, moved, scales, cots):
    vmem = pl.BlockSpec(memory_space=pltpu.VMEM)
    return pl.pallas_call(
        pre_kernel,
        out_shape=jax.ShapeDtypeStruct(full.shape, BF),
        in_specs=[pl.BlockSpec(memory_space=pltpu.SMEM)] + [vmem] * 3 + [pl.BlockSpec(memory_space=pl.ANY)] * 3,
        out_specs=vmem,
        compiler_params=pltpu.CompilerParams(vmem_limit_bytes=40 << 20),
        cost_estimate=pl.CostEstimate(flops=1 << 20, bytes_accessed=1 << 20, transcendentals=0),
        name="pre_work",
    )(at, full, moved, scales, *cots)


def slope_of(cot, value):
    return (cot.astype(F32) * gelu_slope(value) * (1.0 / math.sqrt(TOKENS))).astype(BF)


def ascent_kernel(at, mine, other, p0, p1, p2, p3, c0, c1, c2, c3, along, pre, cot, squared, slope):
    core, x = at[1], at[2]
    columns = p0.shape[1]
    for b, (p, c) in enumerate(((p0, c0), (p1, c1), (p2, c2), (p3, c3))):
        q = x ^ b
        pre[pl.ds(pl.multiple_of(q * 256, 256), 256)] = p[...]
        cot[pl.ds(pl.multiple_of(q * 128, 128), 128)] = c[0]
        cot[pl.ds(pl.multiple_of(512 + q * 128, 128), 128)] = c[1]
    for i in range(8):
        rows = pl.ds(128 * i, 128)
        value = slope_of(cot[rows], pre[rows].astype(F32))
        slope[pl.ds(4 * i, 4)] = value.reshape(4, 2, 16, columns)
    total = jnp.zeros((1, 1), F32)
    for gram, c in ((mine, core), (other, 1 - core)):
        for i in range(2):
            chips = pl.ds(16 * i, 16)
            part = dot(gram[chips].reshape(256, TOKENS), slope[...].reshape(TOKENS, columns), ((1,), (0,)))
            along[chips, c] = part.reshape(16, 16, columns)
            weighed = part * slope[chips, c].reshape(256, columns).astype(F32)
            total = total + jnp.sum(jnp.sum(weighed, axis=0, keepdims=True), axis=1, keepdims=True)
    squared[...] = jnp.broadcast_to(total.reshape(1, 1, 1), squared.shape)


def ascent_work(at, mine, other, pres, cots):
    columns = pres[0].shape[1]
    vmem = pl.BlockSpec(memory_space=pltpu.VMEM)
    flat = jax.ShapeDtypeStruct((TOKENS, columns), BF)
    return pl.pallas_call(
        ascent_kernel,
        out_shape=[
            jax.ShapeDtypeStruct((32, 2, 16, columns), F32),
            flat,
            flat,
            jax.ShapeDtypeStruct((64, 1, 128), F32),
        ],
        in_specs=[pl.BlockSpec(memory_space=pltpu.SMEM)] + [vmem] * 10,
        out_specs=[vmem] * 4,
        scratch_shapes=[pltpu.VMEM((32, 2, 16, columns), BF)],
        compiler_params=pltpu.CompilerParams(vmem_limit_bytes=40 << 20),
        cost_estimate=pl.CostEstimate(flops=2 * TOKENS * TOKENS * columns, bytes_accessed=8 << 20, transcendentals=2 * TOKENS * columns),
        name="ascent_work",
    )(at, mine, other, *pres, *cots)


def per_device(tokens, norm_gain, w_up, cotangent):
    width, columns = w_up.shape
    places = (lax.axis_index(DP), lax.axis_index("c"), lax.axis_index("x"), lax.axis_index("yh"))
    at = jnp.stack(places).astype(jnp.int32)
    with jax.named_scope("token_gather"):
        mine = spread(tokens, ("yl", "z"), 32)
        other = swap(mine, "c", 1)
        cot_other = swap(after(cotangent, mine[0, 0, :128]), "yh", 1)
    with jax.named_scope("local_work"):
        joined, own, near, opposite, far, sent = local_work(at, mine, other, norm_gain[None], w_up)
    with jax.named_scope("sums_x"):
        got = spread(sent, MP, 8)
        moved = [swap(v, "x", b) for b, v in ((1, near), (2, opposite), (3, far))]
    with jax.named_scope("stats_work"):
        rows, half, full, pair, scales = stats_work(at, got, own, moved, cotangent, cot_other)
        normed = joined.reshape(TOKENS, width).astype(F32) - scales[:, 33:34]
        normed = (normed * scales[:, 32:33] * norm_gain[None, :]).astype(BF)
    with jax.named_scope("gram_gather"):
        gram = spread(rows, ("yl", "z"), 32)
        gram_other = swap(gram, "c", 1)
    with jax.named_scope("pre"):
        moved = swap(half, "yh", 1)
        cots = gather_x(pair)
        pres = gather_x(pre_work(at, full, moved, scales, cots[1:]))
    with jax.named_scope("ascent"):
        along, pre, cot, squared = ascent_work(at, gram, gram_other, pres, cots)
        squared = jnp.sum(lax.all_to_all(squared, DP, 0, 0, tiled=True)[:, 0, 0])
        size = jnp.sqrt(jnp.maximum(squared, 0.0)) + 1e-12
        radius = 0.5 * math.sqrt(FF)
    with jax.named_scope("sharp"):
        sharp = slope_of(cot, pre.astype(F32) + along.reshape(TOKENS, columns) * (radius / size))
        return dot(normed, sharp, ((0,), (0,)))


def solution(mesh):
    fine = Mesh(mesh.devices.reshape(4, 8, 2, 2, 4), DP + MP)
    placed = (P(DP, MP), P(MP), P(MP, DP), P(MP, DP))
    return jax.shard_map(
        per_device, mesh=fine, in_specs=placed, out_specs=P(MP, DP), check_vma=False
    )
```

time: 175 us -> 182 us (1.040)
  other arithmetic: 10.4 us -> 1.8 us
  starting transfers between devices: 58.3 us -> 66.3 us
  blocking collectives: 58.6 us -> 66.4 us
  matrix products: 9.85 us -> 2.25 us
  Pallas kernels: 5.22 us -> 11.1 us
  waiting for transfers between devices: 21.4 us -> 26.4 us
  local copies, waits for them, and re-layouts: 8.9 us -> 5.99 us
    all_to_all x0 -> x1, starting transfers between devices: none -> 9.08 us  [per_device(): squared = jnp.sum(lax.all_to_all(squared, DP, 0, 0, tiled=True)[:, 0, 0])]
    all_to_all x0 -> x1, waiting for transfers between devices: none -> 8.96 us  [per_device(): squared = jnp.sum(lax.all_to_all(squared, DP, 0, 0, tiled=True)[:, 0, 0])]
    all_to_all x2, blocking collectives: 58.6 us -> 66.4 us  [spread(): return lax.all_to_all(copies, axes, 0, 0, tiled=True)]
    dot_general x4 -> x1, matrix products: 9.85 us -> 2.25 us  [dot(): lax.dot_general(left, right, (dims, ((), ())), precision=precision, prefe...]
    all_to_all x2 -> x1, starting transfers between devices: 12.8 us -> 6.67 us  [spread(): return lax.all_to_all(copies, axes, 0, 0, tiled=True)]
    pallas_call x0 -> x3, Pallas kernels: none -> 5.44 us  [the longest x1 3.41 us: ascent_work(): pl.pallas_call(ascent_kernel, out_shape=[jax.ShapeDtypeStruct((32, 2, 16,...]
    ppermute x13, starting transfers between devices: 45.5 us -> 50.5 us  [swap(): return lax.ppermute(value, axis, [(i, i ^ bit) for i in range(size)])]
    ppermute x13, waiting for transfers between devices: 21.3 us -> 17.4 us  [swap(): return lax.ppermute(value, axis, [(i, i ^ bit) for i in range(size)])]
  transfers between devices with their start and end apart: 15 -> 15, of which waited for: 7 -> 8; matrix products, arithmetic and copies ran while one was open for 6% -> 0% of each run, Pallas kernels for 0% -> 0%
where the time goes in v7:
time: 182 us; the launch traced here: 181 us
  blocking collectives  66.4 us (36%)
  starting transfers between devices  66.3 us (36%)
  waiting for transfers between devices  26.4 us (15%)
  Pallas kernels  11.1 us (6%)
  local copies, waits for them, and re-layouts  5.99 us (3%)
  matrix products  2.25 us (1%)
    all_to_all x2, blocking collectives, spread(): return lax.all_to_all(copies, axes, 0, 0, tiled=True)  66.4 us
    ppermute x13, starting transfers between devices, swap(): return lax.ppermute(value, axis, [(i, i ^ bit) for i in range(size)])  50.5 us
    ppermute x13, waiting for transfers between devices, swap(): return lax.ppermute(value, axis, [(i, i ^ bit) for i in range(size)])  17.4 us
    all_to_all x1, starting transfers between devices, per_device(): squared = jnp.sum(lax.all_to_all(squared, DP, 0, 0, tiled=True)[:, 0, 0])  9.08 us
    all_to_all x1, waiting for transfers between devices, per_device(): squared = jnp.sum(lax.all_to_all(squared, DP, 0, 0, tiled=True)[:, 0, 0])  8.96 us
    all_to_all x1, starting transfers between devices, spread(): return lax.all_to_all(copies, axes, 0, 0, tiled=True)  6.67 us
    pallas_call x1, Pallas kernels, local_work(): pl.pallas_call(local_kernel, out_shape=[jax.ShapeDtypeStruct((32, 2, 16,...  5.69 us
  transfers between devices with their start and end apart: 15, of which 8 were waited for; matrix products, arithmetic and copies ran while one was open for 0% of the time, Pallas kernels for 0%

profile of v7, /device:TPU:1, one launch (start us, length us, event | category | flops | bytes accessed | tf_op | source)
XLA Modules:
  0.0 181.2 jit_solution(9348967846733073603)
XLA Ops:
  0.0 0.0 copy-start.6
  0.0 0.0 copy-start.3
  0.0 0.9 broadcast_in_dim.8
  0.9 34.5 %all_to_all.20.mine = bf16[32,16,768]{2,1,0:T(8,128)(2,1)S(1)} all-to-all(bf16[32,16,768]{2,1,0:T(8,128)(2,1)S(1)} %broadcast_in_dim.8), channel_id=1, replica_groups=mesh['yl'=4,'z'=8,'c'=2,'yh'=2,'x'=4] {'yl','z'}, dimensions={0} | all-to-all | bytes 1572864 | tf_op jit(solution)/shard_map/token_gather/all_to_all | solution.py:33
  35.4 4.2 %collective-permute-start = (bf16[32,16,768]{2,1,0:T(8,128)(2,1)S(1)}, bf16[32,16,768]{2,1,0:T(8,128)(2,1)S(1)}, u32[]{:S(2)}, u32[]{:S(2)}) collective-permute-start(bf16[32,16,768]{2,1,0:T(8,128)(2,1)S(1)} %all_to_all.20.mine), channel_id=1, source_target_pairs={{0,8},{8,0},{1,9},{9,1},{2,10},{10,2},{3,11},{11,3},{4,12},{12,4},... | collective-permute-start | bytes 2359304 | tf_op jit(solution)/shard_map/token_gather/ppermute | solution.py:28
  39.6 0.0 copy-done.6
  39.7 0.1 pad_add_fusion.at
  39.7 0.0 copy-start.2
  39.8 1.8 collective-permute-done.other
  41.5 0.0 copy-done.3
  41.5 5.7 %local_work.1 = (bf16[32,2,16,768]{3,2,1,0:T(8,128)(2,1)S(1)}, f32[256,384]{1,0:T(8,128)S(1)}, bf16[256,384]{1,0:T(8,128)(2,1)S(1)}, bf16[256,384]{1,0:T(8,128)(...) custom-call(s32[4]{0:T(128)S(1)} %pad_add_fusion.at, bf16[32,16,768]{2,1,0:T(8,128)(2,1)S(1)} %all_to_all.20.mine, ...), custom_call_target="tpu_custom_call" | custom-call | flops 1207959552 | bytes 8388608 | tf_op jit(solution)/shard_map/local_work/local_work/pallas_call | solution.py:104
  47.2 0.0 copy-start.4
  47.2 1.2 copy-done.4
  48.4 0.8 broadcast_in_dim.10
  49.2 6.7 %all-to-all-start.1 = ((bf16[8,24,1024]{2,1,0:T(8,128)(2,1)}), bf16[8,24,1024]{2,1,0:T(8,128)(2,1)S(1)}, u32[]{:S(2)}, u32[]{:S(2)}) async-start(bf16[8,24,1024]{2,1,0:T(8,128)(2,1)} %broadcast_in_dim.10), calls=%async_computation.1 | async-start | bytes 786432 | tf_op jit(solution)/shard_map/sums_x/all_to_all | solution.py:33
  55.9 3.4 %collective-permute-start.1 = (bf16[256,384]{1,0:T(8,128)(2,1)S(1)}, bf16[256,384]{1,0:T(8,128)(2,1)S(1)}, u32[]{:S(2)}, u32[]{:S(2)}) collective-permute-start(bf16[256,384]{1,0:T(8,128)(2,1)S(1)} %get-tuple-element.23), channel_id=1, source_target_pairs={{0,1},{1,0},{2,3},{3,2},{4,5},{5,4},{6,7},{7,6},{8,9},{9,8},{10,11... | collective-permute-start | bytes 589832 | tf_op jit(solution)/shard_map/sums_x/ppermute | solution.py:28
  59.2 4.3 %collective-permute-start.2 = (bf16[256,384]{1,0:T(8,128)(2,1)S(1)}, bf16[256,384]{1,0:T(8,128)(2,1)S(1)}, u32[]{:S(2)}, u32[]{:S(2)}) collective-permute-start(bf16[256,384]{1,0:T(8,128)(2,1)S(1)} %get-tuple-element.24), channel_id=1, source_target_pairs={{0,2},{1,3},{2,0},{3,1},{4,6},{5,7},{6,4},{7,5},{8,10},{9,11},{10,... | collective-permute-start | bytes 589832 | tf_op jit(solution)/shard_map/sums_x/ppermute | solution.py:28
  63.5 1.9 %collective-permute-start.3 = (bf16[256,384]{1,0:T(8,128)(2,1)S(1)}, bf16[256,384]{1,0:T(8,128)(2,1)S(1)}, u32[]{:S(2)}, u32[]{:S(2)}) collective-permute-start(bf16[256,384]{1,0:T(8,128)(2,1)S(1)} %get-tuple-element.25), channel_id=1, source_target_pairs={{0,3},{1,2},{2,1},{3,0},{4,7},{5,6},{6,5},{7,4},{8,11},{9,10},{10,... | collective-permute-start | bytes 589832 | tf_op jit(solution)/shard_map/sums_x/ppermute | solution.py:28
  65.5 0.0 copy-done.2
  65.5 7.3 %collective-permute-start.4 = (bf16[128,384]{1,0:T(8,128)(2,1)S(1)}, bf16[128,384]{1,0:T(8,128)(2,1)S(1)}, u32[]{:S(2)}, u32[]{:S(2)}) collective-permute-start(bf16[128,384]{1,0:T(8,128)(2,1)S(1)} %copy-done.2), channel_id=1, source_target_pairs={{0,4},{4,0},{1,5},{5,1},{2,6},{6,2},{3,7},{7,3},{8,12},{12,8},{9,1... | collective-permute-start | bytes 294920 | tf_op jit(solution)/shard_map/token_gather/ppermute | solution.py:28
  72.7 2.1 %collective-permute-done.4.cot_other = bf16[128,384]{1,0:T(8,128)(2,1)S(1)} collective-permute-done((bf16[128,384]{1,0:T(8,128)(2,1)S(1)}, bf16[128,384]{1,0:T(8,128)(2,1)S(1)}, u32[]{:S(2)}, u32[]{:S(2)}) %collective-permute-start.4) | collective-permute-done | bytes 98336 | tf_op jit(solution)/shard_map/token_gather/ppermute | solution.py:28
  74.8 0.0 collective-permute-done.1.one
  74.8 0.0 collective-permute-done.2.two
  74.8 1.3 collective-permute-done.3.three
  76.2 0.0 all-to-all-done.1.got
  76.2 1.4 stats_work.1
  77.6 0.1 broadcast_in_dim.11
  77.7 31.8 %all_to_all.21.mine = bf16[32,16,1024]{2,1,0:T(8,128)(2,1)S(1)} all-to-all(bf16[32,16,1024]{2,1,0:T(8,128)(2,1)S(1)} %broadcast_in_dim.11), channel_id=1, replica_groups=mesh['yl'=4,'z'=8,'c'=2,'yh'=2,'x'=4] {'yl','z'}, dimensions={0} | all-to-all | bytes 2097152 | tf_op jit(solution)/shard_map/gram_gather/all_to_all | solution.py:33
  109.5 4.5 %collective-permute-start.5 = (bf16[32,16,1024]{2,1,0:T(8,128)(2,1)S(1)}, bf16[32,16,1024]{2,1,0:T(8,128)(2,1)S(1)}, u32[]{:S(2)}, u32[]{:S(2)}) collective-permute-start(bf16[32,16,1024]{2,1,0:T(8,128)(2,1)S(1)} %all_to_all.21.mine), channel_id=1, source_target_pairs={{0,8},{8,0},{1,9},{9,1},{2,10},{10,2},{3,11},{11,3},{4,12},{12,4},... | collective-permute-start | bytes 3145736 | tf_op jit(solution)/shard_map/gram_gather/ppermute | solution.py:28
  114.0 7.0 %collective-permute-start.6 = (bf16[256,384]{1,0:T(8,128)(2,1)S(1)}, bf16[256,384]{1,0:T(8,128)(2,1)S(1)}, u32[]{:S(2)}, u32[]{:S(2)}) collective-permute-start(bf16[256,384]{1,0:T(8,128)(2,1)S(1)} %get-tuple-element.29), channel_id=1, source_target_pairs={{0,4},{4,0},{1,5},{5,1},{2,6},{6,2},{3,7},{7,3},{8,12},{12,8},{9,1... | collective-permute-start | bytes 589832 | tf_op jit(solution)/shard_map/pre/ppermute | solution.py:28
  121.0 2.6 %collective-permute-start.9 = (bf16[2,128,384]{2,1,0:T(8,128)(2,1)S(1)}, bf16[2,128,384]{2,1,0:T(8,128)(2,1)S(1)}, u32[]{:S(2)}, u32[]{:S(2)}) collective-permute-start(bf16[2,128,384]{2,1,0:T(8,128)(2,1)S(1)} %get-tuple-element.30.c0), channel_id=1, source_target_pairs={{0,3},{1,2},{2,1},{3,0},{4,7},{5,6},{6,5},{7,4},{8,11},{9,10},{10,... | collective-permute-start | bytes 589832 | tf_op jit(solution)/shard_map/pre/ppermute | solution.py:28
  123.6 1.9 %collective-permute-start.8 = (bf16[2,128,384]{2,1,0:T(8,128)(2,1)S(1)}, bf16[2,128,384]{2,1,0:T(8,128)(2,1)S(1)}, u32[]{:S(2)}, u32[]{:S(2)}) collective-permute-start(bf16[2,128,384]{2,1,0:T(8,128)(2,1)S(1)} %get-tuple-element.30.c0), channel_id=1, source_target_pairs={{0,2},{1,3},{2,0},{3,1},{4,6},{5,7},{6,4},{7,5},{8,10},{9,11},{10,... | collective-permute-start | bytes 589832 | tf_op jit(solution)/shard_map/pre/ppermute | solution.py:28
  125.5 4.5 %collective-permute-start.7 = (bf16[2,128,384]{2,1,0:T(8,128)(2,1)S(1)}, bf16[2,128,384]{2,1,0:T(8,128)(2,1)S(1)}, u32[]{:S(2)}, u32[]{:S(2)}) collective-permute-start(bf16[2,128,384]{2,1,0:T(8,128)(2,1)S(1)} %get-tuple-element.30.c0), channel_id=1, source_target_pairs={{0,1},{1,0},{2,3},{3,2},{4,5},{5,4},{6,7},{7,6},{8,9},{9,8},{10,11... | collective-permute-start | bytes 589832 | tf_op jit(solution)/shard_map/pre/ppermute | solution.py:28
  130.0 0.0 collective-permute-done.6.moved
  130.0 4.1 %collective-permute-done.9.three.c3 = bf16[2,128,384]{2,1,0:T(8,128)(2,1)S(1)} collective-permute-done((bf16[2,128,384]{2,1,0:T(8,128)(2,1)S(1)}, bf16[2,128,384]{2,1,0:T(8,128)(2,1)S(1)}, u32[]{:S(2)}, u32[]{:S(2)}) %collective-permute-start.9) | collective-permute-done | bytes 196640 | tf_op jit(solution)/shard_map/pre/ppermute | solution.py:28
  134.1 0.0 collective-permute-done.8.two.c2
  134.1 2.6 %collective-permute-done.7.one.c1 = bf16[2,128,384]{2,1,0:T(8,128)(2,1)S(1)} collective-permute-done((bf16[2,128,384]{2,1,0:T(8,128)(2,1)S(1)}, bf16[2,128,384]{2,1,0:T(8,128)(2,1)S(1)}, u32[]{:S(2)}, u32[]{:S(2)}) %collective-permute-start.7) | collective-permute-done | bytes 196640 | tf_op jit(solution)/shard_map/pre/ppermute | solution.py:28
  136.7 0.6 pre_work.1.p0
  137.3 2.7 %collective-permute-start.12 = (bf16[256,384]{1,0:T(8,128)(2,1)S(1)}, bf16[256,384]{1,0:T(8,128)(2,1)S(1)}, u32[]{:S(2)}, u32[]{:S(2)}) collective-permute-start(bf16[256,384]{1,0:T(8,128)(2,1)S(1)} %pre_work.1.p0), channel_id=1, source_target_pairs={{0,3},{1,2},{2,1},{3,0},{4,7},{5,6},{6,5},{7,4},{8,11},{9,10},{10,... | collective-permute-start | bytes 589832 | tf_op jit(solution)/shard_map/pre/ppermute | solution.py:28
  140.0 2.2 %collective-permute-start.11 = (bf16[256,384]{1,0:T(8,128)(2,1)S(1)}, bf16[256,384]{1,0:T(8,128)(2,1)S(1)}, u32[]{:S(2)}, u32[]{:S(2)}) collective-permute-start(bf16[256,384]{1,0:T(8,128)(2,1)S(1)} %pre_work.1.p0), channel_id=1, source_target_pairs={{0,2},{1,3},{2,0},{3,1},{4,6},{5,7},{6,4},{7,5},{8,10},{9,11},{10,... | collective-permute-start | bytes 589832 | tf_op jit(solution)/shard_map/pre/ppermute | solution.py:28
  142.2 4.1 %collective-permute-start.10 = (bf16[256,384]{1,0:T(8,128)(2,1)S(1)}, bf16[256,384]{1,0:T(8,128)(2,1)S(1)}, u32[]{:S(2)}, u32[]{:S(2)}) collective-permute-start(bf16[256,384]{1,0:T(8,128)(2,1)S(1)} %pre_work.1.p0), channel_id=1, source_target_pairs={{0,1},{1,0},{2,3},{3,2},{4,5},{5,4},{6,7},{7,6},{8,9},{9,8},{10,11... | collective-permute-start | bytes 589832 | tf_op jit(solution)/shard_map/pre/ppermute | solution.py:28
  146.4 0.0 collective-permute-done.12.p3
  146.4 1.7 collective-permute-done.11.p2
  148.1 3.9 %collective-permute-done.10.p1 = bf16[256,384]{1,0:T(8,128)(2,1)S(1)} collective-permute-done((bf16[256,384]{1,0:T(8,128)(2,1)S(1)}, bf16[256,384]{1,0:T(8,128)(2,1)S(1)}, u32[]{:S(2)}, u32[]{:S(2)}) %collective-permute-start.10) | collective-permute-done | bytes 196640 | tf_op jit(solution)/shard_map/pre/ppermute | solution.py:28
  151.9 0.0 collective-permute-done.5.other
  151.9 3.4 %ascent_work.1 = (f32[32,2,16,384]{3,2,1,0:T(8,128)S(1)}, bf16[1024,384]{1,0:T(8,128)(2,1)S(1)}, bf16[1024,384]{1,0:T(8,128)(2,1)S(1)}, f32[64,1,128]{2,1,0:T(1,128)}) custom-call(s32[4]{0:T(128)S(1)} %pad_add_fusion.at, bf16[32,16,1024]{2,1,0:T(8,128)(2,1)S(1)} %all_to_all.21.mine, bf16[32,16,1024]{2,1,0:T(8,128)(2,1)S(1)} %collective-permute-done.5.other, ...), custom_call_target="tpu_custom_call" | custom-call | flops 805306368 | bytes 8388608 | tf_op jit(solution)/shard_map/ascent/ascent_work/pallas_call | solution.py:230
  155.3 0.0 copy-start
  155.3 0.9 copy-done
  156.2 9.1 %all-to-all-start.3 = ((f32[64,1,128]{2,1,0:T(1,128)}), f32[64,1,128]{2,1,0:T(1,128)S(1)}, u32[]{:S(2)}, u32[]{:S(2)}) async-start(f32[64,1,128]{2,1,0:T(1,128)} %get-tuple-element.34), calls=%async_computation.3 | async-start | bytes 65536 | tf_op jit(solution)/shard_map/ascent/all_to_all | solution.py:273
  165.3 0.6 slice_reduce_fusion.1
  165.9 9.0 %all-to-all-done.3 = f32[64,1,128]{2,1,0:T(1,128)S(1)} async-done(((f32[64,1,128]{2,1,0:T(1,128)}), f32[64,1,128]{2,1,0:T(1,128)S(1)}, u32[]{:S(2)}, u32[]{:S(2)}) %all-to-all-start.3) | async-done | bytes 32800 | tf_op jit(solution)/shard_map/ascent/all_to_all | solution.py:273
  174.9 0.7 slice_reduce_fusion.2
  176.4 0.0 copy-start.1
  176.4 0.1 broadcast_multiply_fusion
  176.5 1.0 copy-done.1
  177.6 0.0 copy-start.5
  177.6 0.9 fusion.9
  178.4 0.5 copy-done.5
  179.0 2.2 %fusion.10 = f32[768,384]{1,0:T(8,128)} fusion(bf16[1024,384]{1,0:T(8,128)(2,1)S(1)} %fusion.9, bf16[1024,768]{1,0:T(8,128)(2,1)S(1)} %bitcast.11, f32[768]{0:T(1024)S(1)} %copy-done.6, f32[1024]{0:T(1024)S(1)} %get-tuple-element.36, f32[1024]{0:T(1024)S(1)} %get-tuple-element.35), kind=kOutput, calls=%fused_computation.12 | convolution fusion | flops 607911936 | bytes 3550208 | tf_op jit(solution)/shard_map/sharp/dot_general | solution.py:45
  (1 shorter events, 0.0 us)
Async XLA Ops:
  0.0 39.6 %copy-start.6 = (f32[768]{0:T(1024)S(1)}, f32[768]{0:T(1024)}, u32[]{:S(2)}) copy-start(f32[768]{0:T(1024)} %param.5) | copy-start | bytes 9220
  0.0 41.5 %copy-start.3 = (bf16[768,384]{1,0:T(8,128)(2,1)S(1)}, bf16[768,384]{1,0:T(8,128)(2,1)}, u32[]{:S(2)}) copy-start(bf16[768,384]{1,0:T(8,128)(2,1)} %w.1) | copy-start | bytes 1769476
  35.4 6.1 %collective-permute-start = (bf16[32,16,768]{2,1,0:T(8,128)(2,1)S(1)}, bf16[32,16,768]{2,1,0:T(8,128)(2,1)S(1)}, u32[]{:S(2)}, u32[]{:S(2)}) collective-permute-start(bf16[32,16,768]{2,1,0:T(8,128)(2,1)S(1)} %all_to_all.20.mine), channel_id=1, source_target_pairs={{0,8},{8,0},{1,9},{9,1},{2,10},{10,2},{3,11},{11,3},{4,12},{12,4},... | collective-permute-start | bytes 2359304 | tf_op jit(solution)/shard_map/token_gather/ppermute | solution.py:28
  39.7 25.7 %copy-start.2 = (bf16[128,384]{1,0:T(8,128)(2,1)S(1)}, bf16[128,384]{1,0:T(8,128)(2,1)}, u32[]{:S(2)}) copy-start(bf16[128,384]{1,0:T(8,128)(2,1)} %cot.1) | copy-start | bytes 294916
  47.2 1.2 copy-start.4
  49.2 27.0 %all-to-all-start.1 = ((bf16[8,24,1024]{2,1,0:T(8,128)(2,1)}), bf16[8,24,1024]{2,1,0:T(8,128)(2,1)S(1)}, u32[]{:S(2)}, u32[]{:S(2)}) async-start(bf16[8,24,1024]{2,1,0:T(8,128)(2,1)} %broadcast_in_dim.10), calls=%async_computation.1 | async-start | bytes 786432 | tf_op jit(solution)/shard_map/sums_x/all_to_all | solution.py:33
  55.9 19.0 %collective-permute-start.1 = (bf16[256,384]{1,0:T(8,128)(2,1)S(1)}, bf16[256,384]{1,0:T(8,128)(2,1)S(1)}, u32[]{:S(2)}, u32[]{:S(2)}) collective-permute-start(bf16[256,384]{1,0:T(8,128)(2,1)S(1)} %get-tuple-element.23), channel_id=1, source_target_pairs={{0,1},{1,0},{2,3},{3,2},{4,5},{5,4},{6,7},{7,6},{8,9},{9,8},{10,11... | collective-permute-start | bytes 589832 | tf_op jit(solution)/shard_map/sums_x/ppermute | solution.py:28
  59.2 15.6 %collective-permute-start.2 = (bf16[256,384]{1,0:T(8,128)(2,1)S(1)}, bf16[256,384]{1,0:T(8,128)(2,1)S(1)}, u32[]{:S(2)}, u32[]{:S(2)}) collective-permute-start(bf16[256,384]{1,0:T(8,128)(2,1)S(1)} %get-tuple-element.24), channel_id=1, source_target_pairs={{0,2},{1,3},{2,0},{3,1},{4,6},{5,7},{6,4},{7,5},{8,10},{9,11},{10,... | collective-permute-start | bytes 589832 | tf_op jit(solution)/shard_map/sums_x/ppermute | solution.py:28
  63.5 12.6 %collective-permute-start.3 = (bf16[256,384]{1,0:T(8,128)(2,1)S(1)}, bf16[256,384]{1,0:T(8,128)(2,1)S(1)}, u32[]{:S(2)}, u32[]{:S(2)}) collective-permute-start(bf16[256,384]{1,0:T(8,128)(2,1)S(1)} %get-tuple-element.25), channel_id=1, source_target_pairs={{0,3},{1,2},{2,1},{3,0},{4,7},{5,6},{6,5},{7,4},{8,11},{9,10},{10,... | collective-permute-start | bytes 589832 | tf_op jit(solution)/shard_map/sums_x/ppermute | solution.py:28
  65.5 9.4 %collective-permute-start.4 = (bf16[128,384]{1,0:T(8,128)(2,1)S(1)}, bf16[128,384]{1,0:T(8,128)(2,1)S(1)}, u32[]{:S(2)}, u32[]{:S(2)}) collective-permute-start(bf16[128,384]{1,0:T(8,128)(2,1)S(1)} %copy-done.2), channel_id=1, source_target_pairs={{0,4},{4,0},{1,5},{5,1},{2,6},{6,2},{3,7},{7,3},{8,12},{12,8},{9,1... | collective-permute-start | bytes 294920 | tf_op jit(solution)/shard_map/token_gather/ppermute | solution.py:28
  109.5 42.4 %collective-permute-start.5 = (bf16[32,16,1024]{2,1,0:T(8,128)(2,1)S(1)}, bf16[32,16,1024]{2,1,0:T(8,128)(2,1)S(1)}, u32[]{:S(2)}, u32[]{:S(2)}) collective-permute-start(bf16[32,16,1024]{2,1,0:T(8,128)(2,1)S(1)} %all_to_all.21.mine), channel_id=1, source_target_pairs={{0,8},{8,0},{1,9},{9,1},{2,10},{10,2},{3,11},{11,3},{4,12},{12,4},... | collective-permute-start | bytes 3145736 | tf_op jit(solution)/shard_map/gram_gather/ppermute | solution.py:28
  114.0 16.0 %collective-permute-start.6 = (bf16[256,384]{1,0:T(8,128)(2,1)S(1)}, bf16[256,384]{1,0:T(8,128)(2,1)S(1)}, u32[]{:S(2)}, u32[]{:S(2)}) collective-permute-start(bf16[256,384]{1,0:T(8,128)(2,1)S(1)} %get-tuple-element.29), channel_id=1, source_target_pairs={{0,4},{4,0},{1,5},{5,1},{2,6},{6,2},{3,7},{7,3},{8,12},{12,8},{9,1... | collective-permute-start | bytes 589832 | tf_op jit(solution)/shard_map/pre/ppermute | solution.py:28
  121.0 13.1 %collective-permute-start.9 = (bf16[2,128,384]{2,1,0:T(8,128)(2,1)S(1)}, bf16[2,128,384]{2,1,0:T(8,128)(2,1)S(1)}, u32[]{:S(2)}, u32[]{:S(2)}) collective-permute-start(bf16[2,128,384]{2,1,0:T(8,128)(2,1)S(1)} %get-tuple-element.30.c0), channel_id=1, source_target_pairs={{0,3},{1,2},{2,1},{3,0},{4,7},{5,6},{6,5},{7,4},{8,11},{9,10},{10,... | collective-permute-start | bytes 589832 | tf_op jit(solution)/shard_map/pre/ppermute | solution.py:28
  123.6 10.5 %collective-permute-start.8 = (bf16[2,128,384]{2,1,0:T(8,128)(2,1)S(1)}, bf16[2,128,384]{2,1,0:T(8,128)(2,1)S(1)}, u32[]{:S(2)}, u32[]{:S(2)}) collective-permute-start(bf16[2,128,384]{2,1,0:T(8,128)(2,1)S(1)} %get-tuple-element.30.c0), channel_id=1, source_target_pairs={{0,2},{1,3},{2,0},{3,1},{4,6},{5,7},{6,4},{7,5},{8,10},{9,11},{10,... | collective-permute-start | bytes 589832 | tf_op jit(solution)/shard_map/pre/ppermute | solution.py:28
  125.5 11.2 %collective-permute-start.7 = (bf16[2,128,384]{2,1,0:T(8,128)(2,1)S(1)}, bf16[2,128,384]{2,1,0:T(8,128)(2,1)S(1)}, u32[]{:S(2)}, u32[]{:S(2)}) collective-permute-start(bf16[2,128,384]{2,1,0:T(8,128)(2,1)S(1)} %get-tuple-element.30.c0), channel_id=1, source_target_pairs={{0,1},{1,0},{2,3},{3,2},{4,5},{5,4},{6,7},{7,6},{8,9},{9,8},{10,11... | collective-permute-start | bytes 589832 | tf_op jit(solution)/shard_map/pre/ppermute | solution.py:28
  137.3 9.0 %collective-permute-start.12 = (bf16[256,384]{1,0:T(8,128)(2,1)S(1)}, bf16[256,384]{1,0:T(8,128)(2,1)S(1)}, u32[]{:S(2)}, u32[]{:S(2)}) collective-permute-start(bf16[256,384]{1,0:T(8,128)(2,1)S(1)} %pre_work.1.p0), channel_id=1, source_target_pairs={{0,3},{1,2},{2,1},{3,0},{4,7},{5,6},{6,5},{7,4},{8,11},{9,10},{10,... | collective-permute-start | bytes 589832 | tf_op jit(solution)/shard_map/pre/ppermute | solution.py:28
  140.0 8.0 %collective-permute-start.11 = (bf16[256,384]{1,0:T(8,128)(2,1)S(1)}, bf16[256,384]{1,0:T(8,128)(2,1)S(1)}, u32[]{:S(2)}, u32[]{:S(2)}) collective-permute-start(bf16[256,384]{1,0:T(8,128)(2,1)S(1)} %pre_work.1.p0), channel_id=1, source_target_pairs={{0,2},{1,3},{2,0},{3,1},{4,6},{5,7},{6,4},{7,5},{8,10},{9,11},{10,... | collective-permute-start | bytes 589832 | tf_op jit(solution)/shard_map/pre/ppermute | solution.py:28
  142.2 9.7 %collective-permute-start.10 = (bf16[256,384]{1,0:T(8,128)(2,1)S(1)}, bf16[256,384]{1,0:T(8,128)(2,1)S(1)}, u32[]{:S(2)}, u32[]{:S(2)}) collective-permute-start(bf16[256,384]{1,0:T(8,128)(2,1)S(1)} %pre_work.1.p0), channel_id=1, source_target_pairs={{0,1},{1,0},{2,3},{3,2},{4,5},{5,4},{6,7},{7,6},{8,9},{9,8},{10,11... | collective-permute-start | bytes 589832 | tf_op jit(solution)/shard_map/pre/ppermute | solution.py:28
  155.3 0.9 copy-start
  156.2 18.7 %all-to-all-start.3 = ((f32[64,1,128]{2,1,0:T(1,128)}), f32[64,1,128]{2,1,0:T(1,128)S(1)}, u32[]{:S(2)}, u32[]{:S(2)}) async-start(f32[64,1,128]{2,1,0:T(1,128)} %get-tuple-element.34), calls=%async_computation.3 | async-start | bytes 65536 | tf_op jit(solution)/shard_map/ascent/all_to_all | solution.py:273
  176.4 1.1 copy-start.1
  177.6 1.4 copy-start.5

commit v8 on v7

--- a/solution.py
+++ b/solution.py
@@ -255,7 +255,7 @@
     with jax.named_scope("local_work"):
         joined, own, near, opposite, far, sent = local_work(at, mine, other, norm_gain[None], w_up)
     with jax.named_scope("sums_x"):
-        got = spread(sent, MP, 8)
+        got = spread(after(sent, cot_other[0, :128]), MP, 8)
         moved = [swap(v, "x", b) for b, v in ((1, near), (2, opposite), (3, far))]
     with jax.named_scope("stats_work"):
         rows, half, full, pair, scales = stats_work(at, got, own, moved, cotangent, cot_other)
@@ -263,11 +263,12 @@
         normed = (normed * scales[:, 32:33] * norm_gain[None, :]).astype(BF)
     with jax.named_scope("gram_gather"):
         gram = spread(rows, ("yl", "z"), 32)
-        gram_other = swap(gram, "c", 1)
     with jax.named_scope("pre"):
         moved = swap(half, "yh", 1)
         cots = gather_x(pair)
         pres = gather_x(pre_work(at, full, moved, scales, cots[1:]))
+        gram = after(gram, pres[1][0, :128])
+        gram_other = swap(gram, "c", 1)
     with jax.named_scope("ascent"):
         along, pre, cot, squared = ascent_work(at, gram, gram_other, pres, cots)
         squared = jnp.sum(lax.all_to_all(squared, DP, 0, 0, tiled=True)[:, 0, 0])

time: 182 us -> 182 us (level)
  no operation moved by 1% of the time
where the time goes in v8:
time: 182 us; the launch traced here: 181 us
  blocking collectives  66.4 us (36%)
  starting transfers between devices  66.3 us (36%)
  waiting for transfers between devices  26.4 us (15%)
  Pallas kernels  11.1 us (6%)
  local copies, waits for them, and re-layouts  5.99 us (3%)
  matrix products  2.25 us (1%)
    all_to_all x2, blocking collectives, spread(): return lax.all_to_all(copies, axes, 0, 0, tiled=True)  66.4 us
    ppermute x13, starting transfers between devices, swap(): return lax.ppermute(value, axis, [(i, i ^ bit) for i in range(size)])  50.5 us
    ppermute x13, waiting for transfers between devices, swap(): return lax.ppermute(value, axis, [(i, i ^ bit) for i in range(size)])  17.4 us
    all_to_all x1, starting transfers between devices, per_device(): squared = jnp.sum(lax.all_to_all(squared, DP, 0, 0, tiled=True)[:, 0, 0])  9.08 us
    all_to_all x1, waiting for transfers between devices, per_device(): squared = jnp.sum(lax.all_to_all(squared, DP, 0, 0, tiled=True)[:, 0, 0])  8.96 us
    all_to_all x1, starting transfers between devices, spread(): return lax.all_to_all(copies, axes, 0, 0, tiled=True)  6.67 us
    pallas_call x1, Pallas kernels, local_work(): pl.pallas_call(local_kernel, out_shape=[jax.ShapeDtypeStruct((32, 2, 16,...  5.69 us
  transfers between devices with their start and end apart: 15, of which 8 were waited for; matrix products, arithmetic and copies ran while one was open for 0% of the time, Pallas kernels for 0%

profile of v8, /device:TPU:1, one launch (start us, length us, event | category | flops | bytes accessed | tf_op | source)
XLA Modules:
  0.0 181.2 jit_solution(9348967846733073603)
XLA Ops:
  0.0 0.0 copy-start.6
  0.0 0.0 copy-start.3
  0.0 0.9 broadcast_in_dim.8
  0.9 34.5 %all_to_all.20.mine = bf16[32,16,768]{2,1,0:T(8,128)(2,1)S(1)} all-to-all(bf16[32,16,768]{2,1,0:T(8,128)(2,1)S(1)} %broadcast_in_dim.8), channel_id=1, replica_groups=mesh['yl'=4,'z'=8,'c'=2,'yh'=2,'x'=4] {'yl','z'}, dimensions={0} | all-to-all | bytes 1572864 | tf_op jit(solution)/shard_map/token_gather/all_to_all | solution.py:33
  35.4 4.2 %collective-permute-start = (bf16[32,16,768]{2,1,0:T(8,128)(2,1)S(1)}, bf16[32,16,768]{2,1,0:T(8,128)(2,1)S(1)}, u32[]{:S(2)}, u32[]{:S(2)}) collective-permute-start(bf16[32,16,768]{2,1,0:T(8,128)(2,1)S(1)} %all_to_all.20.mine), channel_id=1, source_target_pairs={{0,8},{8,0},{1,9},{9,1},{2,10},{10,2},{3,11},{11,3},{4,12},{12,4},... | collective-permute-start | bytes 2359304 | tf_op jit(solution)/shard_map/token_gather/ppermute | solution.py:28
  39.6 0.0 copy-done.6
  39.7 0.1 pad_add_fusion.at
  39.7 0.0 copy-start.2
  39.8 1.8 collective-permute-done.other
  41.5 0.0 copy-done.3
  41.5 5.7 %local_work.1 = (bf16[32,2,16,768]{3,2,1,0:T(8,128)(2,1)S(1)}, f32[256,384]{1,0:T(8,128)S(1)}, bf16[256,384]{1,0:T(8,128)(2,1)S(1)}, bf16[256,384]{1,0:T(8,128)(...) custom-call(s32[4]{0:T(128)S(1)} %pad_add_fusion.at, bf16[32,16,768]{2,1,0:T(8,128)(2,1)S(1)} %all_to_all.20.mine, ...), custom_call_target="tpu_custom_call" | custom-call | flops 1207959552 | bytes 8388608 | tf_op jit(solution)/shard_map/local_work/local_work/pallas_call | solution.py:104
  47.2 0.0 copy-start.4
  47.2 1.2 copy-done.4
  48.4 0.8 broadcast_in_dim.10
  49.2 6.7 %all-to-all-start.1 = ((bf16[8,24,1024]{2,1,0:T(8,128)(2,1)}), bf16[8,24,1024]{2,1,0:T(8,128)(2,1)S(1)}, u32[]{:S(2)}, u32[]{:S(2)}) async-start(bf16[8,24,1024]{2,1,0:T(8,128)(2,1)} %broadcast_in_dim.10), calls=%async_computation.1 | async-start | bytes 786432 | tf_op jit(solution)/shard_map/sums_x/all_to_all | solution.py:33
  55.9 3.4 %collective-permute-start.1 = (bf16[256,384]{1,0:T(8,128)(2,1)S(1)}, bf16[256,384]{1,0:T(8,128)(2,1)S(1)}, u32[]{:S(2)}, u32[]{:S(2)}) collective-permute-start(bf16[256,384]{1,0:T(8,128)(2,1)S(1)} %get-tuple-element.23), channel_id=1, source_target_pairs={{0,1},{1,0},{2,3},{3,2},{4,5},{5,4},{6,7},{7,6},{8,9},{9,8},{10,11... | collective-permute-start | bytes 589832 | tf_op jit(solution)/shard_map/sums_x/ppermute | solution.py:28
  59.2 4.3 %collective-permute-start.2 = (bf16[256,384]{1,0:T(8,128)(2,1)S(1)}, bf16[256,384]{1,0:T(8,128)(2,1)S(1)}, u32[]{:S(2)}, u32[]{:S(2)}) collective-permute-start(bf16[256,384]{1,0:T(8,128)(2,1)S(1)} %get-tuple-element.24), channel_id=1, source_target_pairs={{0,2},{1,3},{2,0},{3,1},{4,6},{5,7},{6,4},{7,5},{8,10},{9,11},{10,... | collective-permute-start | bytes 589832 | tf_op jit(solution)/shard_map/sums_x/ppermute | solution.py:28
  63.5 1.9 %collective-permute-start.3 = (bf16[256,384]{1,0:T(8,128)(2,1)S(1)}, bf16[256,384]{1,0:T(8,128)(2,1)S(1)}, u32[]{:S(2)}, u32[]{:S(2)}) collective-permute-start(bf16[256,384]{1,0:T(8,128)(2,1)S(1)} %get-tuple-element.25), channel_id=1, source_target_pairs={{0,3},{1,2},{2,1},{3,0},{4,7},{5,6},{6,5},{7,4},{8,11},{9,10},{10,... | collective-permute-start | bytes 589832 | tf_op jit(solution)/shard_map/sums_x/ppermute | solution.py:28
  65.5 0.0 copy-done.2
  65.5 7.3 %collective-permute-start.4 = (bf16[128,384]{1,0:T(8,128)(2,1)S(1)}, bf16[128,384]{1,0:T(8,128)(2,1)S(1)}, u32[]{:S(2)}, u32[]{:S(2)}) collective-permute-start(bf16[128,384]{1,0:T(8,128)(2,1)S(1)} %copy-done.2), channel_id=1, source_target_pairs={{0,4},{4,0},{1,5},{5,1},{2,6},{6,2},{3,7},{7,3},{8,12},{12,8},{9,1... | collective-permute-start | bytes 294920 | tf_op jit(solution)/shard_map/token_gather/ppermute | solution.py:28
  72.7 2.1 %collective-permute-done.4.cot_other = bf16[128,384]{1,0:T(8,128)(2,1)S(1)} collective-permute-done((bf16[128,384]{1,0:T(8,128)(2,1)S(1)}, bf16[128,384]{1,0:T(8,128)(2,1)S(1)}, u32[]{:S(2)}, u32[]{:S(2)}) %collective-permute-start.4) | collective-permute-done | bytes 98336 | tf_op jit(solution)/shard_map/token_gather/ppermute | solution.py:28
  74.8 0.0 collective-permute-done.1.one
  74.8 0.0 collective-permute-done.2.two
  74.8 1.3 collective-permute-done.3.three
  76.2 0.0 all-to-all-done.1.got
  76.2 1.4 stats_work.1
  77.6 0.1 broadcast_in_dim.11
  77.7 31.8 %all_to_all.21.mine = bf16[32,16,1024]{2,1,0:T(8,128)(2,1)S(1)} all-to-all(bf16[32,16,1024]{2,1,0:T(8,128)(2,1)S(1)} %broadcast_in_dim.11), channel_id=1, replica_groups=mesh['yl'=4,'z'=8,'c'=2,'yh'=2,'x'=4] {'yl','z'}, dimensions={0} | all-to-all | bytes 2097152 | tf_op jit(solution)/shard_map/gram_gather/all_to_all | solution.py:33
  109.5 4.5 %collective-permute-start.5 = (bf16[32,16,1024]{2,1,0:T(8,128)(2,1)S(1)}, bf16[32,16,1024]{2,1,0:T(8,128)(2,1)S(1)}, u32[]{:S(2)}, u32[]{:S(2)}) collective-permute-start(bf16[32,16,1024]{2,1,0:T(8,128)(2,1)S(1)} %all_to_all.21.mine), channel_id=1, source_target_pairs={{0,8},{8,0},{1,9},{9,1},{2,10},{10,2},{3,11},{11,3},{4,12},{12,4},... | collective-permute-start | bytes 3145736 | tf_op jit(solution)/shard_map/pre/ppermute | solution.py:28
  114.0 7.0 %collective-permute-start.6 = (bf16[256,384]{1,0:T(8,128)(2,1)S(1)}, bf16[256,384]{1,0:T(8,128)(2,1)S(1)}, u32[]{:S(2)}, u32[]{:S(2)}) collective-permute-start(bf16[256,384]{1,0:T(8,128)(2,1)S(1)} %get-tuple-element.29), channel_id=1, source_target_pairs={{0,4},{4,0},{1,5},{5,1},{2,6},{6,2},{3,7},{7,3},{8,12},{12,8},{9,1... | collective-permute-start | bytes 589832 | tf_op jit(solution)/shard_map/pre/ppermute | solution.py:28
  121.0 2.6 %collective-permute-start.9 = (bf16[2,128,384]{2,1,0:T(8,128)(2,1)S(1)}, bf16[2,128,384]{2,1,0:T(8,128)(2,1)S(1)}, u32[]{:S(2)}, u32[]{:S(2)}) collective-permute-start(bf16[2,128,384]{2,1,0:T(8,128)(2,1)S(1)} %get-tuple-element.30.c0), channel_id=1, source_target_pairs={{0,3},{1,2},{2,1},{3,0},{4,7},{5,6},{6,5},{7,4},{8,11},{9,10},{10,... | collective-permute-start | bytes 589832 | tf_op jit(solution)/shard_map/pre/ppermute | solution.py:28
  123.6 1.9 %collective-permute-start.8 = (bf16[2,128,384]{2,1,0:T(8,128)(2,1)S(1)}, bf16[2,128,384]{2,1,0:T(8,128)(2,1)S(1)}, u32[]{:S(2)}, u32[]{:S(2)}) collective-permute-start(bf16[2,128,384]{2,1,0:T(8,128)(2,1)S(1)} %get-tuple-element.30.c0), channel_id=1, source_target_pairs={{0,2},{1,3},{2,0},{3,1},{4,6},{5,7},{6,4},{7,5},{8,10},{9,11},{10,... | collective-permute-start | bytes 589832 | tf_op jit(solution)/shard_map/pre/ppermute | solution.py:28
  125.5 4.5 %collective-permute-start.7 = (bf16[2,128,384]{2,1,0:T(8,128)(2,1)S(1)}, bf16[2,128,384]{2,1,0:T(8,128)(2,1)S(1)}, u32[]{:S(2)}, u32[]{:S(2)}) collective-permute-start(bf16[2,128,384]{2,1,0:T(8,128)(2,1)S(1)} %get-tuple-element.30.c0), channel_id=1, source_target_pairs={{0,1},{1,0},{2,3},{3,2},{4,5},{5,4},{6,7},{7,6},{8,9},{9,8},{10,11... | collective-permute-start | bytes 589832 | tf_op jit(solution)/shard_map/pre/ppermute | solution.py:28
  130.0 0.0 collective-permute-done.6.moved
  130.0 4.1 %collective-permute-done.9.three.c3 = bf16[2,128,384]{2,1,0:T(8,128)(2,1)S(1)} collective-permute-done((bf16[2,128,384]{2,1,0:T(8,128)(2,1)S(1)}, bf16[2,128,384]{2,1,0:T(8,128)(2,1)S(1)}, u32[]{:S(2)}, u32[]{:S(2)}) %collective-permute-start.9) | collective-permute-done | bytes 196640 | tf_op jit(solution)/shard_map/pre/ppermute | solution.py:28
  134.1 0.0 collective-permute-done.8.two.c2
  134.1 2.6 %collective-permute-done.7.one.c1 = bf16[2,128,384]{2,1,0:T(8,128)(2,1)S(1)} collective-permute-done((bf16[2,128,384]{2,1,0:T(8,128)(2,1)S(1)}, bf16[2,128,384]{2,1,0:T(8,128)(2,1)S(1)}, u32[]{:S(2)}, u32[]{:S(2)}) %collective-permute-start.7) | collective-permute-done | bytes 196640 | tf_op jit(solution)/shard_map/pre/ppermute | solution.py:28
  136.7 0.6 pre_work.1.p0
  137.3 2.7 %collective-permute-start.12 = (bf16[256,384]{1,0:T(8,128)(2,1)S(1)}, bf16[256,384]{1,0:T(8,128)(2,1)S(1)}, u32[]{:S(2)}, u32[]{:S(2)}) collective-permute-start(bf16[256,384]{1,0:T(8,128)(2,1)S(1)} %pre_work.1.p0), channel_id=1, source_target_pairs={{0,3},{1,2},{2,1},{3,0},{4,7},{5,6},{6,5},{7,4},{8,11},{9,10},{10,... | collective-permute-start | bytes 589832 | tf_op jit(solution)/shard_map/pre/ppermute | solution.py:28
  140.0 2.2 %collective-permute-start.11 = (bf16[256,384]{1,0:T(8,128)(2,1)S(1)}, bf16[256,384]{1,0:T(8,128)(2,1)S(1)}, u32[]{:S(2)}, u32[]{:S(2)}) collective-permute-start(bf16[256,384]{1,0:T(8,128)(2,1)S(1)} %pre_work.1.p0), channel_id=1, source_target_pairs={{0,2},{1,3},{2,0},{3,1},{4,6},{5,7},{6,4},{7,5},{8,10},{9,11},{10,... | collective-permute-start | bytes 589832 | tf_op jit(solution)/shard_map/pre/ppermute | solution.py:28
  142.2 4.1 %collective-permute-start.10 = (bf16[256,384]{1,0:T(8,128)(2,1)S(1)}, bf16[256,384]{1,0:T(8,128)(2,1)S(1)}, u32[]{:S(2)}, u32[]{:S(2)}) collective-permute-start(bf16[256,384]{1,0:T(8,128)(2,1)S(1)} %pre_work.1.p0), channel_id=1, source_target_pairs={{0,1},{1,0},{2,3},{3,2},{4,5},{5,4},{6,7},{7,6},{8,9},{9,8},{10,11... | collective-permute-start | bytes 589832 | tf_op jit(solution)/shard_map/pre/ppermute | solution.py:28
  146.4 0.0 collective-permute-done.12.p3
  146.4 1.7 collective-permute-done.11.p2
  148.1 3.9 %collective-permute-done.10.p1 = bf16[256,384]{1,0:T(8,128)(2,1)S(1)} collective-permute-done((bf16[256,384]{1,0:T(8,128)(2,1)S(1)}, bf16[256,384]{1,0:T(8,128)(2,1)S(1)}, u32[]{:S(2)}, u32[]{:S(2)}) %collective-permute-start.10) | collective-permute-done | bytes 196640 | tf_op jit(solution)/shard_map/pre/ppermute | solution.py:28
  151.9 0.0 collective-permute-done.5.other
  151.9 3.4 %ascent_work.1 = (f32[32,2,16,384]{3,2,1,0:T(8,128)S(1)}, bf16[1024,384]{1,0:T(8,128)(2,1)S(1)}, bf16[1024,384]{1,0:T(8,128)(2,1)S(1)}, f32[64,1,128]{2,1,0:T(1,128)}) custom-call(s32[4]{0:T(128)S(1)} %pad_add_fusion.at, bf16[32,16,1024]{2,1,0:T(8,128)(2,1)S(1)} %all_to_all.21.mine, bf16[32,16,1024]{2,1,0:T(8,128)(2,1)S(1)} %collective-permute-done.5.other, ...), custom_call_target="tpu_custom_call" | custom-call | flops 805306368 | bytes 8388608 | tf_op jit(solution)/shard_map/ascent/ascent_work/pallas_call | solution.py:230
  155.3 0.0 copy-start
  155.3 0.9 copy-done
  156.2 9.1 %all-to-all-start.3 = ((f32[64,1,128]{2,1,0:T(1,128)}), f32[64,1,128]{2,1,0:T(1,128)S(1)}, u32[]{:S(2)}, u32[]{:S(2)}) async-start(f32[64,1,128]{2,1,0:T(1,128)} %get-tuple-element.34), calls=%async_computation.3 | async-start | bytes 65536 | tf_op jit(solution)/shard_map/ascent/all_to_all | solution.py:274
  165.3 0.6 slice_reduce_fusion.1
  165.9 9.0 %all-to-all-done.3 = f32[64,1,128]{2,1,0:T(1,128)S(1)} async-done(((f32[64,1,128]{2,1,0:T(1,128)}), f32[64,1,128]{2,1,0:T(1,128)S(1)}, u32[]{:S(2)}, u32[]{:S(2)}) %all-to-all-start.3) | async-done | bytes 32800 | tf_op jit(solution)/shard_map/ascent/all_to_all | solution.py:274
  174.9 0.7 slice_reduce_fusion.2
  176.4 0.0 copy-start.1
  176.4 0.1 broadcast_multiply_fusion
  176.5 1.0 copy-done.1
  177.6 0.0 copy-start.5
  177.6 0.9 fusion.9
  178.4 0.5 copy-done.5
  179.0 2.2 %fusion.10 = f32[768,384]{1,0:T(8,128)} fusion(bf16[1024,384]{1,0:T(8,128)(2,1)S(1)} %fusion.9, bf16[1024,768]{1,0:T(8,128)(2,1)S(1)} %bitcast.11, f32[768]{0:T(1024)S(1)} %copy-done.6, f32[1024]{0:T(1024)S(1)} %get-tuple-element.36, f32[1024]{0:T(1024)S(1)} %get-tuple-element.35), kind=kOutput, calls=%fused_computation.12 | convolution fusion | flops 607911936 | bytes 3550208 | tf_op jit(solution)/shard_map/sharp/dot_general | solution.py:45
  (1 shorter events, 0.0 us)
Async XLA Ops:
  0.0 39.6 %copy-start.6 = (f32[768]{0:T(1024)S(1)}, f32[768]{0:T(1024)}, u32[]{:S(2)}) copy-start(f32[768]{0:T(1024)} %param.5) | copy-start | bytes 9220
  0.0 41.5 %copy-start.3 = (bf16[768,384]{1,0:T(8,128)(2,1)S(1)}, bf16[768,384]{1,0:T(8,128)(2,1)}, u32[]{:S(2)}) copy-start(bf16[768,384]{1,0:T(8,128)(2,1)} %w.1) | copy-start | bytes 1769476
  35.4 6.1 %collective-permute-start = (bf16[32,16,768]{2,1,0:T(8,128)(2,1)S(1)}, bf16[32,16,768]{2,1,0:T(8,128)(2,1)S(1)}, u32[]{:S(2)}, u32[]{:S(2)}) collective-permute-start(bf16[32,16,768]{2,1,0:T(8,128)(2,1)S(1)} %all_to_all.20.mine), channel_id=1, source_target_pairs={{0,8},{8,0},{1,9},{9,1},{2,10},{10,2},{3,11},{11,3},{4,12},{12,4},... | collective-permute-start | bytes 2359304 | tf_op jit(solution)/shard_map/token_gather/ppermute | solution.py:28
  39.7 25.7 %copy-start.2 = (bf16[128,384]{1,0:T(8,128)(2,1)S(1)}, bf16[128,384]{1,0:T(8,128)(2,1)}, u32[]{:S(2)}) copy-start(bf16[128,384]{1,0:T(8,128)(2,1)} %cot.1) | copy-start | bytes 294916
  47.2 1.2 copy-start.4
  49.2 27.0 %all-to-all-start.1 = ((bf16[8,24,1024]{2,1,0:T(8,128)(2,1)}), bf16[8,24,1024]{2,1,0:T(8,128)(2,1)S(1)}, u32[]{:S(2)}, u32[]{:S(2)}) async-start(bf16[8,24,1024]{2,1,0:T(8,128)(2,1)} %broadcast_in_dim.10), calls=%async_computation.1 | async-start | bytes 786432 | tf_op jit(solution)/shard_map/sums_x/all_to_all | solution.py:33
  55.9 19.0 %collective-permute-start.1 = (bf16[256,384]{1,0:T(8,128)(2,1)S(1)}, bf16[256,384]{1,0:T(8,128)(2,1)S(1)}, u32[]{:S(2)}, u32[]{:S(2)}) collective-permute-start(bf16[256,384]{1,0:T(8,128)(2,1)S(1)} %get-tuple-element.23), channel_id=1, source_target_pairs={{0,1},{1,0},{2,3},{3,2},{4,5},{5,4},{6,7},{7,6},{8,9},{9,8},{10,11... | collective-permute-start | bytes 589832 | tf_op jit(solution)/shard_map/sums_x/ppermute | solution.py:28
  59.2 15.6 %collective-permute-start.2 = (bf16[256,384]{1,0:T(8,128)(2,1)S(1)}, bf16[256,384]{1,0:T(8,128)(2,1)S(1)}, u32[]{:S(2)}, u32[]{:S(2)}) collective-permute-start(bf16[256,384]{1,0:T(8,128)(2,1)S(1)} %get-tuple-element.24), channel_id=1, source_target_pairs={{0,2},{1,3},{2,0},{3,1},{4,6},{5,7},{6,4},{7,5},{8,10},{9,11},{10,... | collective-permute-start | bytes 589832 | tf_op jit(solution)/shard_map/sums_x/ppermute | solution.py:28
  63.5 12.6 %collective-permute-start.3 = (bf16[256,384]{1,0:T(8,128)(2,1)S(1)}, bf16[256,384]{1,0:T(8,128)(2,1)S(1)}, u32[]{:S(2)}, u32[]{:S(2)}) collective-permute-start(bf16[256,384]{1,0:T(8,128)(2,1)S(1)} %get-tuple-element.25), channel_id=1, source_target_pairs={{0,3},{1,2},{2,1},{3,0},{4,7},{5,6},{6,5},{7,4},{8,11},{9,10},{10,... | collective-permute-start | bytes 589832 | tf_op jit(solution)/shard_map/sums_x/ppermute | solution.py:28
  65.5 9.4 %collective-permute-start.4 = (bf16[128,384]{1,0:T(8,128)(2,1)S(1)}, bf16[128,384]{1,0:T(8,128)(2,1)S(1)}, u32[]{:S(2)}, u32[]{:S(2)}) collective-permute-start(bf16[128,384]{1,0:T(8,128)(2,1)S(1)} %copy-done.2), channel_id=1, source_target_pairs={{0,4},{4,0},{1,5},{5,1},{2,6},{6,2},{3,7},{7,3},{8,12},{12,8},{9,1... | collective-permute-start | bytes 294920 | tf_op jit(solution)/shard_map/token_gather/ppermute | solution.py:28
  109.5 42.4 %collective-permute-start.5 = (bf16[32,16,1024]{2,1,0:T(8,128)(2,1)S(1)}, bf16[32,16,1024]{2,1,0:T(8,128)(2,1)S(1)}, u32[]{:S(2)}, u32[]{:S(2)}) collective-permute-start(bf16[32,16,1024]{2,1,0:T(8,128)(2,1)S(1)} %all_to_all.21.mine), channel_id=1, source_target_pairs={{0,8},{8,0},{1,9},{9,1},{2,10},{10,2},{3,11},{11,3},{4,12},{12,4},... | collective-permute-start | bytes 3145736 | tf_op jit(solution)/shard_map/pre/ppermute | solution.py:28
  114.0 16.0 %collective-permute-start.6 = (bf16[256,384]{1,0:T(8,128)(2,1)S(1)}, bf16[256,384]{1,0:T(8,128)(2,1)S(1)}, u32[]{:S(2)}, u32[]{:S(2)}) collective-permute-start(bf16[256,384]{1,0:T(8,128)(2,1)S(1)} %get-tuple-element.29), channel_id=1, source_target_pairs={{0,4},{4,0},{1,5},{5,1},{2,6},{6,2},{3,7},{7,3},{8,12},{12,8},{9,1... | collective-permute-start | bytes 589832 | tf_op jit(solution)/shard_map/pre/ppermute | solution.py:28
  121.0 13.1 %collective-permute-start.9 = (bf16[2,128,384]{2,1,0:T(8,128)(2,1)S(1)}, bf16[2,128,384]{2,1,0:T(8,128)(2,1)S(1)}, u32[]{:S(2)}, u32[]{:S(2)}) collective-permute-start(bf16[2,128,384]{2,1,0:T(8,128)(2,1)S(1)} %get-tuple-element.30.c0), channel_id=1, source_target_pairs={{0,3},{1,2},{2,1},{3,0},{4,7},{5,6},{6,5},{7,4},{8,11},{9,10},{10,... | collective-permute-start | bytes 589832 | tf_op jit(solution)/shard_map/pre/ppermute | solution.py:28
  123.6 10.5 %collective-permute-start.8 = (bf16[2,128,384]{2,1,0:T(8,128)(2,1)S(1)}, bf16[2,128,384]{2,1,0:T(8,128)(2,1)S(1)}, u32[]{:S(2)}, u32[]{:S(2)}) collective-permute-start(bf16[2,128,384]{2,1,0:T(8,128)(2,1)S(1)} %get-tuple-element.30.c0), channel_id=1, source_target_pairs={{0,2},{1,3},{2,0},{3,1},{4,6},{5,7},{6,4},{7,5},{8,10},{9,11},{10,... | collective-permute-start | bytes 589832 | tf_op jit(solution)/shard_map/pre/ppermute | solution.py:28
  125.5 11.2 %collective-permute-start.7 = (bf16[2,128,384]{2,1,0:T(8,128)(2,1)S(1)}, bf16[2,128,384]{2,1,0:T(8,128)(2,1)S(1)}, u32[]{:S(2)}, u32[]{:S(2)}) collective-permute-start(bf16[2,128,384]{2,1,0:T(8,128)(2,1)S(1)} %get-tuple-element.30.c0), channel_id=1, source_target_pairs={{0,1},{1,0},{2,3},{3,2},{4,5},{5,4},{6,7},{7,6},{8,9},{9,8},{10,11... | collective-permute-start | bytes 589832 | tf_op jit(solution)/shard_map/pre/ppermute | solution.py:28
  137.3 9.0 %collective-permute-start.12 = (bf16[256,384]{1,0:T(8,128)(2,1)S(1)}, bf16[256,384]{1,0:T(8,128)(2,1)S(1)}, u32[]{:S(2)}, u32[]{:S(2)}) collective-permute-start(bf16[256,384]{1,0:T(8,128)(2,1)S(1)} %pre_work.1.p0), channel_id=1, source_target_pairs={{0,3},{1,2},{2,1},{3,0},{4,7},{5,6},{6,5},{7,4},{8,11},{9,10},{10,... | collective-permute-start | bytes 589832 | tf_op jit(solution)/shard_map/pre/ppermute | solution.py:28
  140.0 8.0 %collective-permute-start.11 = (bf16[256,384]{1,0:T(8,128)(2,1)S(1)}, bf16[256,384]{1,0:T(8,128)(2,1)S(1)}, u32[]{:S(2)}, u32[]{:S(2)}) collective-permute-start(bf16[256,384]{1,0:T(8,128)(2,1)S(1)} %pre_work.1.p0), channel_id=1, source_target_pairs={{0,2},{1,3},{2,0},{3,1},{4,6},{5,7},{6,4},{7,5},{8,10},{9,11},{10,... | collective-permute-start | bytes 589832 | tf_op jit(solution)/shard_map/pre/ppermute | solution.py:28
  142.2 9.7 %collective-permute-start.10 = (bf16[256,384]{1,0:T(8,128)(2,1)S(1)}, bf16[256,384]{1,0:T(8,128)(2,1)S(1)}, u32[]{:S(2)}, u32[]{:S(2)}) collective-permute-start(bf16[256,384]{1,0:T(8,128)(2,1)S(1)} %pre_work.1.p0), channel_id=1, source_target_pairs={{0,1},{1,0},{2,3},{3,2},{4,5},{5,4},{6,7},{7,6},{8,9},{9,8},{10,11... | collective-permute-start | bytes 589832 | tf_op jit(solution)/shard_map/pre/ppermute | solution.py:28
  155.3 0.9 copy-start
  156.2 18.7 %all-to-all-start.3 = ((f32[64,1,128]{2,1,0:T(1,128)}), f32[64,1,128]{2,1,0:T(1,128)S(1)}, u32[]{:S(2)}, u32[]{:S(2)}) async-start(f32[64,1,128]{2,1,0:T(1,128)} %get-tuple-element.34), calls=%async_computation.3 | async-start | bytes 65536 | tf_op jit(solution)/shard_map/ascent/all_to_all | solution.py:274
  176.4 1.1 copy-start.1
  177.6 1.4 copy-start.5

commit v9 on v7

--- a/solution.py
+++ b/solution.py
@@ -31,10 +31,6 @@
 def spread(value, axes, count):
     copies = jnp.broadcast_to(value[None], (count,) + value.shape)
     return lax.all_to_all(copies, axes, 0, 0, tiled=True)
-
-
-def after(value, *others):
-    return lax.optimization_barrier((value,) + others)[0]
 
 
 def gather_x(value):
@@ -178,18 +174,19 @@
     )(at, got, own, *moved, cot, cot_other)
 
 
-def pre_kernel(at, full, moved, scales, one, two, three, out):
+def pre_kernel(at, full, moved, scales, one, two, three, out, mark):
     inv = scales[pl.ds(pl.multiple_of(at[2] * 256, 256), 256)][:, 32:33]
     out[...] = ((full[...] + moved[...].astype(F32)) * inv).astype(BF)
+    mark[...] = inv[:8]
 
 
 def pre_work(at, full, moved, scales, cots):
     vmem = pl.BlockSpec(memory_space=pltpu.VMEM)
     return pl.pallas_call(
         pre_kernel,
-        out_shape=jax.ShapeDtypeStruct(full.shape, BF),
+        out_shape=[jax.ShapeDtypeStruct(full.shape, BF), jax.ShapeDtypeStruct((8, 1), F32)],
         in_specs=[pl.BlockSpec(memory_space=pltpu.SMEM)] + [vmem] * 3 + [pl.BlockSpec(memory_space=pl.ANY)] * 3,
-        out_specs=vmem,
+        out_specs=[vmem] * 2,
         compiler_params=pltpu.CompilerParams(vmem_limit_bytes=40 << 20),
         cost_estimate=pl.CostEstimate(flops=1 << 20, bytes_accessed=1 << 20, transcendentals=0),
         name="pre_work",
@@ -200,7 +197,7 @@
     return (cot.astype(F32) * gelu_slope(value) * (1.0 / math.sqrt(TOKENS))).astype(BF)
 
 
-def ascent_kernel(at, mine, other, p0, p1, p2, p3, c0, c1, c2, c3, along, pre, cot, squared, slope):
+def ascent_kernel(at, mine, other, p0, p1, p2, p3, c0, c1, c2, c3, mark, along, pre_out, cot_out, squared, slope, pre, cot, sems):
     core, x = at[1], at[2]
     columns = p0.shape[1]
     for b, (p, c) in enumerate(((p0, c0), (p1, c1), (p2, c2), (p3, c3))):
@@ -208,6 +205,9 @@
         pre[pl.ds(pl.multiple_of(q * 256, 256), 256)] = p[...]
         cot[pl.ds(pl.multiple_of(q * 128, 128), 128)] = c[0]
         cot[pl.ds(pl.multiple_of(512 + q * 128, 128), 128)] = c[1]
+    copies = [pltpu.make_async_copy(pre, pre_out, sems.at[0]), pltpu.make_async_copy(cot, cot_out, sems.at[1])]
+    for copy in copies:
+        copy.start()
     for i in range(8):
         rows = pl.ds(128 * i, 128)
         value = slope_of(cot[rows], pre[rows].astype(F32))
@@ -221,11 +221,14 @@
             weighed = part * slope[chips, c].reshape(256, columns).astype(F32)
             total = total + jnp.sum(jnp.sum(weighed, axis=0, keepdims=True), axis=1, keepdims=True)
     squared[...] = jnp.broadcast_to(total.reshape(1, 1, 1), squared.shape)
-
-
-def ascent_work(at, mine, other, pres, cots):
+    for copy in copies:
+        copy.wait()
+
+
+def ascent_work(at, mine, other, pres, cots, mark):
     columns = pres[0].shape[1]
     vmem = pl.BlockSpec(memory_space=pltpu.VMEM)
+    anywhere = pl.BlockSpec(memory_space=pl.ANY)
     flat = jax.ShapeDtypeStruct((TOKENS, columns), BF)
     return pl.pallas_call(
         ascent_kernel,
@@ -235,13 +238,18 @@
             flat,
             jax.ShapeDtypeStruct((64, 1, 128), F32),
         ],
-        in_specs=[pl.BlockSpec(memory_space=pltpu.SMEM)] + [vmem] * 10,
-        out_specs=[vmem] * 4,
-        scratch_shapes=[pltpu.VMEM((32, 2, 16, columns), BF)],
+        in_specs=[pl.BlockSpec(memory_space=pltpu.SMEM)] + [vmem] * 10 + [anywhere],
+        out_specs=[vmem, anywhere, anywhere, vmem],
+        scratch_shapes=[
+            pltpu.VMEM((32, 2, 16, columns), BF),
+            pltpu.VMEM((TOKENS, columns), BF),
+            pltpu.VMEM((TOKENS, columns), BF),
+            pltpu.SemaphoreType.DMA((2,)),
+        ],
         compiler_params=pltpu.CompilerParams(vmem_limit_bytes=40 << 20),
         cost_estimate=pl.CostEstimate(flops=2 * TOKENS * TOKENS * columns, bytes_accessed=8 << 20, transcendentals=2 * TOKENS * columns),
         name="ascent_work",
-    )(at, mine, other, *pres, *cots)
+    )(at, mine, other, *pres, *cots, mark)
 
 
 def per_device(tokens, norm_gain, w_up, cotangent):
@@ -250,11 +258,13 @@
     at = jnp.stack(places).astype(jnp.int32)
     with jax.named_scope("token_gather"):
         mine = spread(tokens, ("yl", "z"), 32)
+        mine, late = lax.optimization_barrier((mine, cotangent))
         other = swap(mine, "c", 1)
-        cot_other = swap(after(cotangent, mine[0, 0, :128]), "yh", 1)
+        cot_other = swap(late, "yh", 1)
     with jax.named_scope("local_work"):
         joined, own, near, opposite, far, sent = local_work(at, mine, other, norm_gain[None], w_up)
     with jax.named_scope("sums_x"):
+        sent, cot_other = lax.optimization_barrier((sent, cot_other))
         got = spread(sent, MP, 8)
         moved = [swap(v, "x", b) for b, v in ((1, near), (2, opposite), (3, far))]
     with jax.named_scope("stats_work"):
@@ -263,13 +273,15 @@
         normed = (normed * scales[:, 32:33] * norm_gain[None, :]).astype(BF)
     with jax.named_scope("gram_gather"):
         gram = spread(rows, ("yl", "z"), 32)
-        gram_other = swap(gram, "c", 1)
     with jax.named_scope("pre"):
         moved = swap(half, "yh", 1)
         cots = gather_x(pair)
-        pres = gather_x(pre_work(at, full, moved, scales, cots[1:]))
+        pre, mark = pre_work(at, full, moved, scales, cots[1:])
+        gram, mark = lax.optimization_barrier((gram, mark))
+        pres = gather_x(pre)
+        gram_other = swap(gram, "c", 1)
     with jax.named_scope("ascent"):
-        along, pre, cot, squared = ascent_work(at, gram, gram_other, pres, cots)
+        along, pre, cot, squared = ascent_work(at, gram, gram_other, pres, cots, mark)
         squared = jnp.sum(lax.all_to_all(squared, DP, 0, 0, tiled=True)[:, 0, 0])
         size = jnp.sqrt(jnp.maximum(squared, 0.0)) + 1e-12
         radius = 0.5 * math.sqrt(FF)

time: 182 us -> 176 us (0.967)
  blocking collectives: 66.4 us -> 34.5 us
  waiting for transfers between devices: 26.4 us -> 43.2 us
  local copies, waits for them, and re-layouts: 5.99 us -> 12.9 us
  starting transfers between devices: 66.3 us -> 69.2 us
    all_to_all x2 -> x1, blocking collectives: 66.4 us -> 34.5 us  [spread(): return lax.all_to_all(copies, axes, 0, 0, tiled=True)]
    ppermute x13, waiting for transfers between devices: 17.4 us -> 27.7 us  [swap(): return lax.ppermute(value, axis, [(i, i ^ bit) for i in range(size)])]
    all_to_all x1 -> x2, starting transfers between devices: 6.67 us -> 14.2 us  [spread(): return lax.all_to_all(copies, axes, 0, 0, tiled=True)]
    all_to_all x1 -> x2, waiting for transfers between devices: 0.01 us -> 6.55 us  [spread(): return lax.all_to_all(copies, axes, 0, 0, tiled=True)]
    unnamed x14 -> x32, local copies, waits for them, and re-layouts: 3.6 us -> 9.48 us
    ppermute x13, starting transfers between devices: 50.5 us -> 47.6 us  [swap(): return lax.ppermute(value, axis, [(i, i ^ bit) for i in range(size)])]
  transfers between devices with their start and end apart: 15 -> 16, of which waited for: 8 -> 8; matrix products, arithmetic and copies ran while one was open for 0% -> 0% of each run, Pallas kernels for 0% -> 3%
where the time goes in v9:
time: 176 us; the launch traced here: 175 us
  starting transfers between devices  69.2 us (39%)
  waiting for transfers between devices  43.2 us (25%)
  blocking collectives  34.5 us (20%)
  local copies, waits for them, and re-layouts  12.9 us (7%)
  Pallas kernels  10.1 us (6%)
  matrix products  2.25 us (1%)
  other arithmetic  1.79 us (1%)
    ppermute x13, starting transfers between devices, swap(): return lax.ppermute(value, axis, [(i, i ^ bit) for i in range(size)])  47.6 us
    all_to_all x1, blocking collectives, spread(): return lax.all_to_all(copies, axes, 0, 0, tiled=True)  34.5 us
    ppermute x13, waiting for transfers between devices, swap(): return lax.ppermute(value, axis, [(i, i ^ bit) for i in range(size)])  27.7 us
    all_to_all x2, starting transfers between devices, spread(): return lax.all_to_all(copies, axes, 0, 0, tiled=True)  14.2 us
    unnamed x32, local copies, waits for them, and re-layouts  9.48 us
    all_to_all x1, waiting for transfers between devices, per_device(): squared = jnp.sum(lax.all_to_all(squared, DP, 0, 0, tiled=True)[:, 0, 0])  8.95 us
    all_to_all x1, starting transfers between devices, per_device(): squared = jnp.sum(lax.all_to_all(squared, DP, 0, 0, tiled=True)[:, 0, 0])  7.36 us
    all_to_all x2, waiting for transfers between devices, spread(): return lax.all_to_all(copies, axes, 0, 0, tiled=True)  6.55 us
  transfers between devices with their start and end apart: 16, of which 8 were waited for; matrix products, arithmetic and copies ran while one was open for 0% of the time, Pallas kernels for 3%

profile of v9, /device:TPU:1, one launch (start us, length us, event | category | flops | bytes accessed | tf_op | source)
XLA Modules:
  0.0 174.9 jit_solution(16346725560073912370)
XLA Ops:
  0.0 0.9 broadcast_in_dim.8
  0.9 34.5 %all_to_all.20.mine = bf16[32,16,768]{2,1,0:T(8,128)(2,1)S(1)} all-to-all(bf16[32,16,768]{2,1,0:T(8,128)(2,1)S(1)} %broadcast_in_dim.8), channel_id=1, replica_groups=mesh['yl'=4,'z'=8,'c'=2,'yh'=2,'x'=4] {'yl','z'}, dimensions={0} | all-to-all | bytes 1572864 | tf_op jit(solution)/shard_map/token_gather/all_to_all | solution.py:33
  35.4 4.2 %collective-permute-start = (bf16[32,16,768]{2,1,0:T(8,128)(2,1)S(1)}, bf16[32,16,768]{2,1,0:T(8,128)(2,1)S(1)}, u32[]{:S(2)}, u32[]{:S(2)}) collective-permute-start(bf16[32,16,768]{2,1,0:T(8,128)(2,1)S(1)} %all_to_all.20.mine), channel_id=1, source_target_pairs={{0,8},{8,0},{1,9},{9,1},{2,10},{10,2},{3,11},{11,3},{4,12},{12,4},... | collective-permute-start | bytes 2359304 | tf_op jit(solution)/shard_map/token_gather/ppermute | solution.py:28
  39.6 0.0 copy-done.15
  39.7 0.1 pad_add_fusion.at
  39.8 0.0 copy-done.10
  39.8 4.8 %collective-permute-start.1 = (bf16[128,384]{1,0:T(8,128)(2,1)S(1)}, bf16[128,384]{1,0:T(8,128)(2,1)S(1)}, u32[]{:S(2)}, u32[]{:S(2)}) collective-permute-start(bf16[128,384]{1,0:T(8,128)(2,1)S(1)} %copy-done.10), channel_id=1, source_target_pairs={{0,4},{4,0},{1,5},{5,1},{2,6},{6,2},{3,7},{7,3},{8,12},{12,8},{9,1... | collective-permute-start | bytes 294920 | tf_op jit(solution)/shard_map/token_gather/ppermute | solution.py:28
  44.6 0.0 collective-permute-done.other
  44.6 0.0 copy-done.12
  44.6 5.1 %local_work.1 = (bf16[32,2,16,768]{3,2,1,0:T(8,128)(2,1)S(1)}, f32[256,384]{1,0:T(8,128)S(1)}, bf16[256,384]{1,0:T(8,128)(2,1)}, bf16[256,384]{1,0:T(8,128)(2,1)...) custom-call(s32[4]{0:T(128)S(1)} %pad_add_fusion.at, bf16[32,16,768]{2,1,0:T(8,128)(2,1)S(1)} %all_to_all.20.mine, ...), custom_call_target="tpu_custom_call" | custom-call | flops 1207959552 | bytes 8388608 | tf_op jit(solution)/shard_map/local_work/local_work/pallas_call | solution.py:100
  49.8 1.2 copy-done.13
  51.0 0.0 collective-permute-done.1.cot_other
  51.0 0.8 broadcast_in_dim.10
  51.8 6.2 %all-to-all-start.1 = ((bf16[8,24,1024]{2,1,0:T(8,128)(2,1)}), bf16[8,24,1024]{2,1,0:T(8,128)(2,1)S(1)}, u32[]{:S(2)}, u32[]{:S(2)}) async-start(bf16[8,24,1024]{2,1,0:T(8,128)(2,1)} %broadcast_in_dim.10), calls=%async_computation.1 | async-start | bytes 786432 | tf_op jit(solution)/shard_map/sums_x/all_to_all | solution.py:33
  57.9 3.4 %collective-permute-start.2 = (bf16[256,384]{1,0:T(8,128)(2,1)}, bf16[256,384]{1,0:T(8,128)(2,1)S(1)}, u32[]{:S(2)}, u32[]{:S(2)}) collective-permute-start(bf16[256,384]{1,0:T(8,128)(2,1)} %get-tuple-element.34), channel_id=1, source_target_pairs={{0,1},{1,0},{2,3},{3,2},{4,5},{5,4},{6,7},{7,6},{8,9},{9,8},{10,11... | collective-permute-start | bytes 589832 | tf_op jit(solution)/shard_map/sums_x/ppermute | solution.py:28
  61.3 4.3 %collective-permute-start.3 = (bf16[256,384]{1,0:T(8,128)(2,1)}, bf16[256,384]{1,0:T(8,128)(2,1)S(1)}, u32[]{:S(2)}, u32[]{:S(2)}) collective-permute-start(bf16[256,384]{1,0:T(8,128)(2,1)} %get-tuple-element.35), channel_id=1, source_target_pairs={{0,2},{1,3},{2,0},{3,1},{4,6},{5,7},{6,4},{7,5},{8,10},{9,11},{10,... | collective-permute-start | bytes 589832 | tf_op jit(solution)/shard_map/sums_x/ppermute | solution.py:28
  65.6 1.9 %collective-permute-start.4 = (bf16[256,384]{1,0:T(8,128)(2,1)S(1)}, bf16[256,384]{1,0:T(8,128)(2,1)S(1)}, u32[]{:S(2)}, u32[]{:S(2)}) collective-permute-start(bf16[256,384]{1,0:T(8,128)(2,1)S(1)} %get-tuple-element.36), channel_id=1, source_target_pairs={{0,3},{1,2},{2,1},{3,0},{4,7},{5,6},{6,5},{7,4},{8,11},{9,10},{10,... | collective-permute-start | bytes 589832 | tf_op jit(solution)/shard_map/sums_x/ppermute | solution.py:28
  67.5 0.5 collective-permute-done.2.one
  68.0 6.2 %collective-permute-done.3.two = bf16[256,384]{1,0:T(8,128)(2,1)S(1)} collective-permute-done((bf16[256,384]{1,0:T(8,128)(2,1)}, bf16[256,384]{1,0:T(8,128)(2,1)S(1)}, u32[]{:S(2)}, u32[]{:S(2)}) %collective-permute-start.3) | collective-permute-done | bytes 196640 | tf_op jit(solution)/shard_map/sums_x/ppermute | solution.py:28
  74.2 4.0 %collective-permute-done.4.three = bf16[256,384]{1,0:T(8,128)(2,1)S(1)} collective-permute-done((bf16[256,384]{1,0:T(8,128)(2,1)S(1)}, bf16[256,384]{1,0:T(8,128)(2,1)S(1)}, u32[]{:S(2)}, u32[]{:S(2)}) %collective-permute-start.4) | collective-permute-done | bytes 196640 | tf_op jit(solution)/shard_map/sums_x/ppermute | solution.py:28
  78.2 0.0 all-to-all-done.1.got
  78.2 1.4 stats_work.1
  79.6 1.1 broadcast_in_dim.11
  80.7 8.1 %all-to-all-start.2 = ((bf16[32,16,1024]{2,1,0:T(8,128)(2,1)}), bf16[32,16,1024]{2,1,0:T(8,128)(2,1)S(1)}, u32[]{:S(2)}, u32[]{:S(2)}) async-start(bf16[32,16,1024]{2,1,0:T(8,128)(2,1)} %broadcast_in_dim.11), calls=%async_computation.2 | async-start | bytes 2097152 | tf_op jit(solution)/shard_map/gram_gather/all_to_all | solution.py:33
  88.8 6.0 %collective-permute-start.5 = (bf16[256,384]{1,0:T(8,128)(2,1)S(1)}, bf16[256,384]{1,0:T(8,128)(2,1)S(1)}, u32[]{:S(2)}, u32[]{:S(2)}) collective-permute-start(bf16[256,384]{1,0:T(8,128)(2,1)S(1)} %get-tuple-element.41), channel_id=1, source_target_pairs={{0,4},{4,0},{1,5},{5,1},{2,6},{6,2},{3,7},{7,3},{8,12},{12,8},{9,1... | collective-permute-start | bytes 589832 | tf_op jit(solution)/shard_map/pre/ppermute | solution.py:28
  94.8 2.5 %collective-permute-start.8 = (bf16[2,128,384]{2,1,0:T(8,128)(2,1)S(1)}, bf16[2,128,384]{2,1,0:T(8,128)(2,1)S(1)}, u32[]{:S(2)}, u32[]{:S(2)}) collective-permute-start(bf16[2,128,384]{2,1,0:T(8,128)(2,1)S(1)} %get-tuple-element.42.c0), channel_id=1, source_target_pairs={{0,3},{1,2},{2,1},{3,0},{4,7},{5,6},{6,5},{7,4},{8,11},{9,10},{10,... | collective-permute-start | bytes 589832 | tf_op jit(solution)/shard_map/pre/ppermute | solution.py:28
  97.3 1.9 %collective-permute-start.7 = (bf16[2,128,384]{2,1,0:T(8,128)(2,1)S(1)}, bf16[2,128,384]{2,1,0:T(8,128)(2,1)S(1)}, u32[]{:S(2)}, u32[]{:S(2)}) collective-permute-start(bf16[2,128,384]{2,1,0:T(8,128)(2,1)S(1)} %get-tuple-element.42.c0), channel_id=1, source_target_pairs={{0,2},{1,3},{2,0},{3,1},{4,6},{5,7},{6,4},{7,5},{8,10},{9,11},{10,... | collective-permute-start | bytes 589832 | tf_op jit(solution)/shard_map/pre/ppermute | solution.py:28
  99.3 4.6 %collective-permute-start.6 = (bf16[2,128,384]{2,1,0:T(8,128)(2,1)S(1)}, bf16[2,128,384]{2,1,0:T(8,128)(2,1)S(1)}, u32[]{:S(2)}, u32[]{:S(2)}) collective-permute-start(bf16[2,128,384]{2,1,0:T(8,128)(2,1)S(1)} %get-tuple-element.42.c0), channel_id=1, source_target_pairs={{0,1},{1,0},{2,3},{3,2},{4,5},{5,4},{6,7},{7,6},{8,9},{9,8},{10,11... | collective-permute-start | bytes 589832 | tf_op jit(solution)/shard_map/pre/ppermute | solution.py:28
  103.9 10.6 %collective-permute-done.5.moved = bf16[256,384]{1,0:T(8,128)(2,1)S(1)} collective-permute-done((bf16[256,384]{1,0:T(8,128)(2,1)S(1)}, bf16[256,384]{1,0:T(8,128)(2,1)S(1)}, u32[]{:S(2)}, u32[]{:S(2)}) %collective-permute-start.5) | collective-permute-done | bytes 196640 | tf_op jit(solution)/shard_map/pre/ppermute | solution.py:28
  114.5 0.0 collective-permute-done.8.three.c3
  114.5 0.0 collective-permute-done.7.two.c2
  114.5 0.0 collective-permute-done.6.one.c1
  114.5 0.7 pre_work.1
  115.2 0.7 copy-done
  115.8 6.5 %all-to-all-done.2.mine = bf16[32,16,1024]{2,1,0:T(8,128)(2,1)S(1)} async-done(((bf16[32,16,1024]{2,1,0:T(8,128)(2,1)}), bf16[32,16,1024]{2,1,0:T(8,128)(2,1)S(1)}, u32[]{:S(2)}, u32[]{:S(2)}) %all-to-all-start.2) | async-done | bytes 1048608 | tf_op jit(solution)/shard_map/gram_gather/all_to_all | solution.py:33
  122.4 4.9 %collective-permute-start.9 = (bf16[32,16,1024]{2,1,0:T(8,128)(2,1)S(1)}, bf16[32,16,1024]{2,1,0:T(8,128)(2,1)S(1)}, u32[]{:S(2)}, u32[]{:S(2)}) collective-permute-start(bf16[32,16,1024]{2,1,0:T(8,128)(2,1)S(1)} %all-to-all-done.2.mine), channel_id=1, source_target_pairs={{0,8},{8,0},{1,9},{9,1},{2,10},{10,2},{3,11},{11,3},{4,12},{12,4},... | collective-permute-start | bytes 3145736 | tf_op jit(solution)/shard_map/pre/ppermute | solution.py:28
  127.3 2.5 %collective-permute-start.12 = (bf16[256,384]{1,0:T(8,128)(2,1)S(1)}, bf16[256,384]{1,0:T(8,128)(2,1)S(1)}, u32[]{:S(2)}, u32[]{:S(2)}) collective-permute-start(bf16[256,384]{1,0:T(8,128)(2,1)S(1)} %get-tuple-element.45.p0), channel_id=1, source_target_pairs={{0,3},{1,2},{2,1},{3,0},{4,7},{5,6},{6,5},{7,4},{8,11},{9,10},{10,... | collective-permute-start | bytes 589832 | tf_op jit(solution)/shard_map/pre/ppermute | solution.py:28
  129.8 2.5 %collective-permute-start.11 = (bf16[256,384]{1,0:T(8,128)(2,1)S(1)}, bf16[256,384]{1,0:T(8,128)(2,1)S(1)}, u32[]{:S(2)}, u32[]{:S(2)}) collective-permute-start(bf16[256,384]{1,0:T(8,128)(2,1)S(1)} %get-tuple-element.45.p0), channel_id=1, source_target_pairs={{0,2},{1,3},{2,0},{3,1},{4,6},{5,7},{6,4},{7,5},{8,10},{9,11},{10,... | collective-permute-start | bytes 589832 | tf_op jit(solution)/shard_map/pre/ppermute | solution.py:28
  132.3 4.0 %collective-permute-start.10 = (bf16[256,384]{1,0:T(8,128)(2,1)S(1)}, bf16[256,384]{1,0:T(8,128)(2,1)S(1)}, u32[]{:S(2)}, u32[]{:S(2)}) collective-permute-start(bf16[256,384]{1,0:T(8,128)(2,1)S(1)} %get-tuple-element.45.p0), channel_id=1, source_target_pairs={{0,1},{1,0},{2,3},{3,2},{4,5},{5,4},{6,7},{7,6},{8,9},{9,8},{10,11... | collective-permute-start | bytes 589832 | tf_op jit(solution)/shard_map/pre/ppermute | solution.py:28
  136.3 0.0 copy-start.8
  136.3 0.7 copy-done.8
  137.0 4.2 %collective-permute-done.12.p3 = bf16[256,384]{1,0:T(8,128)(2,1)S(1)} collective-permute-done((bf16[256,384]{1,0:T(8,128)(2,1)S(1)}, bf16[256,384]{1,0:T(8,128)(2,1)S(1)}, u32[]{:S(2)}, u32[]{:S(2)}) %collective-permute-start.12) | collective-permute-done | bytes 196640 | tf_op jit(solution)/shard_map/pre/ppermute | solution.py:28
  141.2 0.0 collective-permute-done.11.p2
  141.2 2.2 %collective-permute-done.10.p1 = bf16[256,384]{1,0:T(8,128)(2,1)S(1)} collective-permute-done((bf16[256,384]{1,0:T(8,128)(2,1)S(1)}, bf16[256,384]{1,0:T(8,128)(2,1)S(1)}, u32[]{:S(2)}, u32[]{:S(2)}) %collective-permute-start.10) | collective-permute-done | bytes 196640 | tf_op jit(solution)/shard_map/pre/ppermute | solution.py:28
  143.3 0.0 collective-permute-done.9.other
  143.3 0.9 copy-done.1
  144.3 0.9 copy-done.7
  145.2 0.9 copy-done.9
  146.1 2.9 %ascent_work.1 = (f32[32,2,16,384]{3,2,1,0:T(8,128)S(1)}, bf16[1024,384]{1,0:T(8,128)(2,1)S(1)}, bf16[1024,384]{1,0:T(8,128)(2,1)S(1)}, f32[64,1,128]{2,1,0:T(1,128)S(1)}) custom-call(s32[4]{0:T(128)S(1)} %pad_add_fusion.at, bf16[32,16,1024]{2,1,0:T(8,128)(2,1)S(1)} %all-to-all-done.2.mine, bf16[32,16,1024]{2,1,0:T(8,128)(2,1)S(1)} %collective-permute-done.9.other, ...), custom_call_target="tpu_custom_call" | custom-call | flops 805306368 | bytes 8388608 | tf_op jit(solution)/shard_map/ascent/ascent_work/pallas_call | solution.py:233
  149.0 0.0 copy-start.2
  149.0 0.9 copy-done.2
  149.9 0.9 copy-done.4
  150.8 0.6 copy-done.11
  151.4 7.4 %all-to-all-start.3 = ((f32[64,1,128]{2,1,0:T(1,128)}), f32[64,1,128]{2,1,0:T(1,128)S(1)}, u32[]{:S(2)}, u32[]{:S(2)}) async-start(f32[64,1,128]{2,1,0:T(1,128)} %copy-done.11), calls=%async_computation.3 | async-start | bytes 65536 | tf_op jit(solution)/shard_map/ascent/all_to_all | solution.py:285
  158.8 0.6 slice_reduce_fusion.1
  159.4 9.0 %all-to-all-done.3 = f32[64,1,128]{2,1,0:T(1,128)S(1)} async-done(((f32[64,1,128]{2,1,0:T(1,128)}), f32[64,1,128]{2,1,0:T(1,128)S(1)}, u32[]{:S(2)}, u32[]{:S(2)}) %all-to-all-start.3) | async-done | bytes 32800 | tf_op jit(solution)/shard_map/ascent/all_to_all | solution.py:285
  168.4 0.7 slice_reduce_fusion.2
  169.9 0.0 copy-start.3
  169.9 0.1 broadcast_multiply_fusion
  170.0 1.0 copy-done.3
  171.0 0.2 copy-done.5
  171.2 0.9 fusion.9
  172.1 0.5 copy-done.14
  172.6 2.2 %fusion.10 = f32[768,384]{1,0:T(8,128)} fusion(bf16[1024,384]{1,0:T(8,128)(2,1)S(1)} %fusion.9, bf16[1024,768]{1,0:T(8,128)(2,1)S(1)} %bitcast.11, f32[768]{0:T(1024)S(1)} %copy-done.15, f32[1024]{0:T(1024)S(1)} %get-tuple-element.52, f32[1024]{0:T(1024)S(1)} %get-tuple-element.51), kind=kOutput, calls=%fused_computation.12 | convolution fusion | flops 607911936 | bytes 3550208 | tf_op jit(solution)/shard_map/sharp/dot_general | solution.py:41
  (15 shorter events, 0.0 us)
Async XLA Ops:
  0.0 39.8 %copy-start.10 = (bf16[128,384]{1,0:T(8,128)(2,1)S(1)}, bf16[128,384]{1,0:T(8,128)(2,1)}, u32[]{:S(2)}) copy-start(bf16[128,384]{1,0:T(8,128)(2,1)} %cot.1) | copy-start | bytes 294916
  0.0 39.6 %copy-start.15 = (f32[768]{0:T(1024)S(1)}, f32[768]{0:T(1024)}, u32[]{:S(2)}) copy-start(f32[768]{0:T(1024)} %param.5) | copy-start | bytes 9220
  0.0 44.6 %copy-start.12 = (bf16[768,384]{1,0:T(8,128)(2,1)S(1)}, bf16[768,384]{1,0:T(8,128)(2,1)}, u32[]{:S(2)}) copy-start(bf16[768,384]{1,0:T(8,128)(2,1)} %w.1) | copy-start | bytes 1769476
  35.4 9.2 %collective-permute-start = (bf16[32,16,768]{2,1,0:T(8,128)(2,1)S(1)}, bf16[32,16,768]{2,1,0:T(8,128)(2,1)S(1)}, u32[]{:S(2)}, u32[]{:S(2)}) collective-permute-start(bf16[32,16,768]{2,1,0:T(8,128)(2,1)S(1)} %all_to_all.20.mine), channel_id=1, source_target_pairs={{0,8},{8,0},{1,9},{9,1},{2,10},{10,2},{3,11},{11,3},{4,12},{12,4},... | collective-permute-start | bytes 2359304 | tf_op jit(solution)/shard_map/token_gather/ppermute | solution.py:28
  39.8 11.2 %collective-permute-start.1 = (bf16[128,384]{1,0:T(8,128)(2,1)S(1)}, bf16[128,384]{1,0:T(8,128)(2,1)S(1)}, u32[]{:S(2)}, u32[]{:S(2)}) collective-permute-start(bf16[128,384]{1,0:T(8,128)(2,1)S(1)} %copy-done.10), channel_id=1, source_target_pairs={{0,4},{4,0},{1,5},{5,1},{2,6},{6,2},{3,7},{7,3},{8,12},{12,8},{9,1... | collective-permute-start | bytes 294920 | tf_op jit(solution)/shard_map/token_gather/ppermute | solution.py:28
  49.8 1.2 copy-start.13
  51.8 26.5 %all-to-all-start.1 = ((bf16[8,24,1024]{2,1,0:T(8,128)(2,1)}), bf16[8,24,1024]{2,1,0:T(8,128)(2,1)S(1)}, u32[]{:S(2)}, u32[]{:S(2)}) async-start(bf16[8,24,1024]{2,1,0:T(8,128)(2,1)} %broadcast_in_dim.10), calls=%async_computation.1 | async-start | bytes 786432 | tf_op jit(solution)/shard_map/sums_x/all_to_all | solution.py:33
  57.9 10.1 %collective-permute-start.2 = (bf16[256,384]{1,0:T(8,128)(2,1)}, bf16[256,384]{1,0:T(8,128)(2,1)S(1)}, u32[]{:S(2)}, u32[]{:S(2)}) collective-permute-start(bf16[256,384]{1,0:T(8,128)(2,1)} %get-tuple-element.34), channel_id=1, source_target_pairs={{0,1},{1,0},{2,3},{3,2},{4,5},{5,4},{6,7},{7,6},{8,9},{9,8},{10,11... | collective-permute-start | bytes 589832 | tf_op jit(solution)/shard_map/sums_x/ppermute | solution.py:28
  61.3 12.9 %collective-permute-start.3 = (bf16[256,384]{1,0:T(8,128)(2,1)}, bf16[256,384]{1,0:T(8,128)(2,1)S(1)}, u32[]{:S(2)}, u32[]{:S(2)}) collective-permute-start(bf16[256,384]{1,0:T(8,128)(2,1)} %get-tuple-element.35), channel_id=1, source_target_pairs={{0,2},{1,3},{2,0},{3,1},{4,6},{5,7},{6,4},{7,5},{8,10},{9,11},{10,... | collective-permute-start | bytes 589832 | tf_op jit(solution)/shard_map/sums_x/ppermute | solution.py:28
  65.6 12.6 %collective-permute-start.4 = (bf16[256,384]{1,0:T(8,128)(2,1)S(1)}, bf16[256,384]{1,0:T(8,128)(2,1)S(1)}, u32[]{:S(2)}, u32[]{:S(2)}) collective-permute-start(bf16[256,384]{1,0:T(8,128)(2,1)S(1)} %get-tuple-element.36), channel_id=1, source_target_pairs={{0,3},{1,2},{2,1},{3,0},{4,7},{5,6},{6,5},{7,4},{8,11},{9,10},{10,... | collective-permute-start | bytes 589832 | tf_op jit(solution)/shard_map/sums_x/ppermute | solution.py:28
  79.6 19.6 %copy-start.6 = (bf16[2,128,384]{2,1,0:T(8,128)(2,1)}, bf16[2,128,384]{2,1,0:T(8,128)(2,1)S(1)}, u32[]{:S(2)}) copy-start(bf16[2,128,384]{2,1,0:T(8,128)(2,1)S(1)} %get-tuple-element.42.c0) | copy-start | bytes 589828
  80.7 41.7 %all-to-all-start.2 = ((bf16[32,16,1024]{2,1,0:T(8,128)(2,1)}), bf16[32,16,1024]{2,1,0:T(8,128)(2,1)S(1)}, u32[]{:S(2)}, u32[]{:S(2)}) async-start(bf16[32,16,1024]{2,1,0:T(8,128)(2,1)} %broadcast_in_dim.11), calls=%async_computation.2 | async-start | bytes 2097152 | tf_op jit(solution)/shard_map/gram_gather/all_to_all | solution.py:33
  88.8 25.7 %collective-permute-start.5 = (bf16[256,384]{1,0:T(8,128)(2,1)S(1)}, bf16[256,384]{1,0:T(8,128)(2,1)S(1)}, u32[]{:S(2)}, u32[]{:S(2)}) collective-permute-start(bf16[256,384]{1,0:T(8,128)(2,1)S(1)} %get-tuple-element.41), channel_id=1, source_target_pairs={{0,4},{4,0},{1,5},{5,1},{2,6},{6,2},{3,7},{7,3},{8,12},{12,8},{9,1... | collective-permute-start | bytes 589832 | tf_op jit(solution)/shard_map/pre/ppermute | solution.py:28
  94.8 19.7 %collective-permute-start.8 = (bf16[2,128,384]{2,1,0:T(8,128)(2,1)S(1)}, bf16[2,128,384]{2,1,0:T(8,128)(2,1)S(1)}, u32[]{:S(2)}, u32[]{:S(2)}) collective-permute-start(bf16[2,128,384]{2,1,0:T(8,128)(2,1)S(1)} %get-tuple-element.42.c0), channel_id=1, source_target_pairs={{0,3},{1,2},{2,1},{3,0},{4,7},{5,6},{6,5},{7,4},{8,11},{9,10},{10,... | collective-permute-start | bytes 589832 | tf_op jit(solution)/shard_map/pre/ppermute | solution.py:28
  97.3 17.2 %collective-permute-start.7 = (bf16[2,128,384]{2,1,0:T(8,128)(2,1)S(1)}, bf16[2,128,384]{2,1,0:T(8,128)(2,1)S(1)}, u32[]{:S(2)}, u32[]{:S(2)}) collective-permute-start(bf16[2,128,384]{2,1,0:T(8,128)(2,1)S(1)} %get-tuple-element.42.c0), channel_id=1, source_target_pairs={{0,2},{1,3},{2,0},{3,1},{4,6},{5,7},{6,4},{7,5},{8,10},{9,11},{10,... | collective-permute-start | bytes 589832 | tf_op jit(solution)/shard_map/pre/ppermute | solution.py:28
  99.3 15.2 %collective-permute-start.6 = (bf16[2,128,384]{2,1,0:T(8,128)(2,1)S(1)}, bf16[2,128,384]{2,1,0:T(8,128)(2,1)S(1)}, u32[]{:S(2)}, u32[]{:S(2)}) collective-permute-start(bf16[2,128,384]{2,1,0:T(8,128)(2,1)S(1)} %get-tuple-element.42.c0), channel_id=1, source_target_pairs={{0,1},{1,0},{2,3},{3,2},{4,5},{5,4},{6,7},{7,6},{8,9},{9,8},{10,11... | collective-permute-start | bytes 589832 | tf_op jit(solution)/shard_map/pre/ppermute | solution.py:28
  115.2 0.7 copy-start
  122.4 21.0 %collective-permute-start.9 = (bf16[32,16,1024]{2,1,0:T(8,128)(2,1)S(1)}, bf16[32,16,1024]{2,1,0:T(8,128)(2,1)S(1)}, u32[]{:S(2)}, u32[]{:S(2)}) collective-permute-start(bf16[32,16,1024]{2,1,0:T(8,128)(2,1)S(1)} %all-to-all-done.2.mine), channel_id=1, source_target_pairs={{0,8},{8,0},{1,9},{9,1},{2,10},{10,2},{3,11},{11,3},{4,12},{12,4},... | collective-permute-start | bytes 3145736 | tf_op jit(solution)/shard_map/pre/ppermute | solution.py:28
  127.3 13.8 %collective-permute-start.12 = (bf16[256,384]{1,0:T(8,128)(2,1)S(1)}, bf16[256,384]{1,0:T(8,128)(2,1)S(1)}, u32[]{:S(2)}, u32[]{:S(2)}) collective-permute-start(bf16[256,384]{1,0:T(8,128)(2,1)S(1)} %get-tuple-element.45.p0), channel_id=1, source_target_pairs={{0,3},{1,2},{2,1},{3,0},{4,7},{5,6},{6,5},{7,4},{8,11},{9,10},{10,... | collective-permute-start | bytes 589832 | tf_op jit(solution)/shard_map/pre/ppermute | solution.py:28
  129.8 11.3 %collective-permute-start.11 = (bf16[256,384]{1,0:T(8,128)(2,1)S(1)}, bf16[256,384]{1,0:T(8,128)(2,1)S(1)}, u32[]{:S(2)}, u32[]{:S(2)}) collective-permute-start(bf16[256,384]{1,0:T(8,128)(2,1)S(1)} %get-tuple-element.45.p0), channel_id=1, source_target_pairs={{0,2},{1,3},{2,0},{3,1},{4,6},{5,7},{6,4},{7,5},{8,10},{9,11},{10,... | collective-permute-start | bytes 589832 | tf_op jit(solution)/shard_map/pre/ppermute | solution.py:28
  132.3 11.0 %collective-permute-start.10 = (bf16[256,384]{1,0:T(8,128)(2,1)S(1)}, bf16[256,384]{1,0:T(8,128)(2,1)S(1)}, u32[]{:S(2)}, u32[]{:S(2)}) collective-permute-start(bf16[256,384]{1,0:T(8,128)(2,1)S(1)} %get-tuple-element.45.p0), channel_id=1, source_target_pairs={{0,1},{1,0},{2,3},{3,2},{4,5},{5,4},{6,7},{7,6},{8,9},{9,8},{10,11... | collective-permute-start | bytes 589832 | tf_op jit(solution)/shard_map/pre/ppermute | solution.py:28
  136.3 0.7 copy-start.8
  143.3 0.9 copy-start.1
  144.3 0.9 copy-start.7
  145.2 0.9 copy-start.9
  149.0 0.9 copy-start.2
  149.9 0.9 copy-start.4
  150.8 0.6 copy-start.11
  151.4 17.0 %all-to-all-start.3 = ((f32[64,1,128]{2,1,0:T(1,128)}), f32[64,1,128]{2,1,0:T(1,128)S(1)}, u32[]{:S(2)}, u32[]{:S(2)}) async-start(f32[64,1,128]{2,1,0:T(1,128)} %copy-done.11), calls=%async_computation.3 | async-start | bytes 65536 | tf_op jit(solution)/shard_map/ascent/all_to_all | solution.py:285
  169.9 1.1 copy-start.3
  169.9 1.4 copy-start.5
  171.2 1.4 copy-start.14

commit v10 on v8

v10 whole, which is shorter than its diff:
```python
import math

import jax
import jax.numpy as jnp
from jax import lax
from jax.experimental import pallas as pl
from jax.experimental.pallas import tpu as pltpu
from jax.sharding import Mesh
from jax.sharding import PartitionSpec as P

FF = 24576
D = 6144
TOKENS = 1024
DP = ("yl", "z", "c")
MP = ("yh", "x")
BF = jnp.bfloat16
F32 = jnp.float32


def gelu_slope(value):
    cdf = 0.5 * (1.0 + lax.erf(value * (1.0 / math.sqrt(2.0))))
    dens = jnp.exp(-0.5 * value * value) * (1.0 / math.sqrt(2.0 * math.pi))
    return cdf + value * dens


def swap(value, axis, bit):
    size = lax.axis_size(axis)
    return lax.ppermute(value, axis, [(i, i ^ bit) for i in range(size)])


def spread(value, axes, count):
    copies = jnp.broadcast_to(value[None], (count,) + value.shape)
    return lax.all_to_all(copies, axes, 0, 0, tiled=True)


def gather_x(value):
    return [value] + [swap(value, "x", b) for b in (1, 2, 3)]


def dot(left, right, dims, precision=None):
    return lax.dot_general(left, right, (dims, ((), ())), precision=precision, preferred_element_type=F32)


def split(value, count):
    out = []
    for _ in range(count):
        out.append(value.astype(BF).astype(F32))
        value = value - out[-1]
    return out


def local_kernel(at, mine, other, gain, w, joined, own, near, opposite, far, sent, high, part, out, sems):
    place, core, x = at[0], at[1], at[2]
    g = gain[...]
    width = g.shape[1]
    ones = jnp.ones((8, width), BF)
    gains = jnp.concatenate(split(g, 3) + [jnp.zeros((5, width), F32)], axis=0).astype(BF)
    local, css, lean = [], [], []
    for i in range(8):
        chips = pl.ds(4 * i, 4)
        joined[chips, core] = mine[chips]
        joined[chips, 1 - core] = other[chips]
        raw = joined[chips].reshape(128, width)
        value = raw.astype(F32)
        centred = value - jnp.sum(value, axis=1, keepdims=True) * (1.0 / width)
        full = centred * g
        first = full.astype(BF)
        second = (full - first.astype(F32)).astype(BF)
        high[pl.ds(128 * i, 128)] = first
        rows = dot(first, w[...], ((1,), (0,))) + dot(second, w[...], ((1,), (0,)))
        part[i % 4, pl.ds(128 * (i // 4), 128)] = rows
        square = centred * centred
        top = square.astype(BF)
        rest = (square - top.astype(F32)).astype(BF)
        across = ((1,), (1,))
        local.append(dot(ones, raw, across)[:1] * (1.0 / width))
        css.append((dot(ones, top, across) + dot(ones, rest, across))[:1])
        lean.append(jnp.sum(dot(gains, first, across), axis=0, keepdims=True))
    own[...] = part[x]
    copies = []
    for b, target in ((1, near), (2, opposite), (3, far)):
        out[b - 1] = part[x ^ b].astype(BF)
        copies.append(pltpu.make_async_copy(out.at[b - 1], target, sems.at[b - 1]))
        copies[-1].start()
    gram = dot(high[pl.ds(pl.multiple_of(place * 16, 16), 16)], high[...], ((1,), (1,)))
    local, css, lean = (jnp.concatenate(v, axis=1) for v in (local, css, lean))
    column = jnp.sum(dot(gains, w[...], ((1,), (0,))), axis=0, keepdims=True)
    power = jnp.broadcast_to(jnp.sum(g * g, axis=1, keepdims=True), (1, 128))
    extra = jnp.concatenate(split(column, 2) + split(power, 2), axis=1)
    stats = jnp.concatenate(split(local, 3) + split(css, 2) + split(lean, 2) + [extra], axis=0)
    stats = [stats[:, 256 * q : 256 * q + 256] for q in range(4)]
    for j in range(8):
        q = 128 * (j % 4)
        block = jnp.concatenate([gram[:, q : q + 128], gram[:, 512 + q : 640 + q]], axis=1)
        sent[j] = jnp.concatenate([block] + stats, axis=0).astype(BF)
    for copy in copies:
        copy.wait()


def local_work(at, mine, other, gain, w):
    width, columns = w.shape
    block = jax.ShapeDtypeStruct((256, columns), BF)
    vmem = pl.BlockSpec(memory_space=pltpu.VMEM)
    return pl.pallas_call(
        local_kernel,
        out_shape=[
            jax.ShapeDtypeStruct((32, 2, 16, width), BF),
            jax.ShapeDtypeStruct((256, columns), F32),
            block,
            block,
            block,
            jax.ShapeDtypeStruct((8, 48, 256), BF),
        ],
        in_specs=[pl.BlockSpec(memory_space=pltpu.SMEM)] + [vmem] * 4,
        out_specs=[vmem] * 2 + [pl.BlockSpec(memory_space=pl.ANY)] * 3 + [vmem],
        scratch_shapes=[
            pltpu.VMEM((TOKENS, width), BF),
            pltpu.VMEM((4, 256, columns), F32),
            pltpu.VMEM((3, 256, columns), BF),
            pltpu.SemaphoreType.DMA((3,)),
        ],
        compiler_params=pltpu.CompilerParams(vmem_limit_bytes=40 << 20),
        cost_estimate=pl.CostEstimate(flops=2 * TOKENS * width * columns * 2, bytes_accessed=8 << 20, transcendentals=0),
        name="local_work",
    )(at, mine, other, gain, w)


def own_rows(ref, x):
    first = ref[pl.ds(pl.multiple_of(x * 128, 128), 128)]
    second = ref[pl.ds(pl.multiple_of(512 + x * 128, 128), 128)]
    return jnp.concatenate([first, second], axis=0)


def stats_kernel(at, got, own, one, two, three, cot, cot_other, rows, half, full, pair, scales, turned, wide):
    place, x = at[0], at[2]
    exact = lax.Precision.HIGHEST
    columns = own.shape[1]
    total = own[...] + one[...].astype(F32) + two[...].astype(F32) + three[...].astype(F32)
    half[...] = total.astype(BF)
    pair[at[3]] = cot[...]
    pair[1 - at[3]] = cot_other[...]
    gram = got[0, :16].astype(F32)
    for j in range(1, 8):
        gram = gram + got[j, :16].astype(F32)
    terms = [got[j, 16:].astype(F32) for j in range(8)]
    terms = [jnp.concatenate([t[8 * q : 8 * q + 8] for q in range(4)], axis=1) for t in terms]
    local = jnp.concatenate([t[0:1] + t[1:2] + t[2:3] for t in terms], axis=0)
    css = jnp.concatenate([t[3:4] + t[4:5] for t in terms], axis=0)
    lean = jnp.concatenate([t[5:6] + t[6:7] for t in terms], axis=0)
    column = jnp.concatenate([t[7:8, :columns] + t[7:8, columns : 2 * columns] for t in terms], axis=0)
    power = jnp.concatenate([t[7:8, 2 * columns : 2 * columns + 1] + t[7:8, 2 * columns + 128 : 2 * columns + 129] for t in terms], axis=0)
    mean = jnp.sum(local, axis=0, keepdims=True) / 8
    apart = local - mean
    var = (jnp.sum(css, axis=0, keepdims=True) + (D // 8) * jnp.sum(apart * apart, axis=0, keepdims=True)) / D
    inv = lax.rsqrt(var + 1e-06)
    flat = jnp.concatenate([lean, apart, power * apart, apart, inv, mean, jnp.zeros((94, TOKENS), F32)], axis=0)
    turned[...] = flat.T
    wide[...] = jnp.concatenate([apart, lean, apart, inv, jnp.zeros((7, TOKENS), F32)], axis=0)
    first = wide[:, pl.ds(pl.multiple_of(x * 128, 128), 128)]
    second = wide[:, pl.ds(pl.multiple_of(512 + x * 128, 128), 128)]
    right = jnp.concatenate([first, second], axis=1)
    mine = turned[pl.ds(pl.multiple_of(place * 16, 16), 16)]
    gram = (gram + dot(mine[:, :24], right[:24], ((1,), (0,)), exact)) * mine[:, 32:33] * right[24:25]
    rows[...] = gram.astype(BF)
    full[...] = total + dot(own_rows(turned, x)[:, 24:32], column, ((1,), (0,)), exact)
    scales[...] = turned[...]


def stats_work(at, got, own, moved, cot, cot_other):
    columns = own.shape[1]
    vmem = pl.BlockSpec(memory_space=pltpu.VMEM)
    return pl.pallas_call(
        stats_kernel,
        out_shape=[
            jax.ShapeDtypeStruct((16, 256), BF),
            jax.ShapeDtypeStruct((256, columns), BF),
            jax.ShapeDtypeStruct((256, columns), F32),
            jax.ShapeDtypeStruct((2, 128, columns), BF),
            jax.ShapeDtypeStruct((TOKENS, 128), F32),
        ],
        in_specs=[pl.BlockSpec(memory_space=pltpu.SMEM)] + [vmem] * 7,
        out_specs=[vmem] * 5,
        scratch_shapes=[pltpu.VMEM((TOKENS, 128), F32), pltpu.VMEM((32, TOKENS), F32)],
        compiler_params=pltpu.CompilerParams(vmem_limit_bytes=40 << 20),
        cost_estimate=pl.CostEstimate(flops=10 << 20, bytes_accessed=3 << 20, transcendentals=0),
        name="stats_work",
    )(at, got, own, *moved, cot, cot_other)


def slope_of(cot, value):
    return (cot.astype(F32) * gelu_slope(value) * (1.0 / math.sqrt(TOKENS))).astype(BF)


def slope_kernel(at, full, moved, scales, pair, pre, slope, mark):
    inv = own_rows(scales, at[2])[:, 32:33]
    value = (full[...] + moved[...].astype(F32)) * inv
    pre[...] = value
    slope[...] = slope_of(pair[...].reshape(value.shape), value)
    mark[...] = inv[:8]


def slope_work(at, full, moved, scales, pair):
    vmem = pl.BlockSpec(memory_space=pltpu.VMEM)
    return pl.pallas_call(
        slope_kernel,
        out_shape=[
            jax.ShapeDtypeStruct(full.shape, F32),
            jax.ShapeDtypeStruct(full.shape, BF),
            jax.ShapeDtypeStruct((8, 1), F32),
        ],
        in_specs=[pl.BlockSpec(memory_space=pltpu.SMEM)] + [vmem] * 4,
        out_specs=[vmem] * 3,
        compiler_params=pltpu.CompilerParams(vmem_limit_bytes=40 << 20),
        cost_estimate=pl.CostEstimate(flops=4 << 20, bytes_accessed=1 << 20, transcendentals=1 << 18),
        name="slope_work",
    )(at, full, moved, scales, pair)


def in_order(x, blocks, ordered):
    for b, block in enumerate(blocks):
        q = x ^ b
        shape = (4, 2, 16, block.shape[1])
        ordered[pl.ds(4 * q, 4)] = block[:128].reshape(shape)
        ordered[pl.ds(16 + 4 * q, 4)] = block[128:].reshape(shape)


def ascent_kernel(at, mine, other, s0, s1, s2, s3, mark, along, squared, ordered):
    core = at[1]
    columns = s0.shape[1]
    in_order(at[2], (s0, s1, s2, s3), ordered)
    half = TOKENS // 2
    part = dot(mine[...].reshape(half, 256), ordered[:, core].reshape(half, columns), ((0,), (0,)))
    part = part + dot(other[...].reshape(half, 256), ordered[:, 1 - core].reshape(half, columns), ((0,), (0,)))
    along[...] = part
    total = jnp.sum(jnp.sum(part * s0[...].astype(F32), axis=0, keepdims=True), axis=1, keepdims=True)
    squared[...] = jnp.broadcast_to(total.reshape(1, 1, 1), squared.shape)


def ascent_work(at, mine, other, slopes, mark):
    columns = slopes[0].shape[1]
    vmem = pl.BlockSpec(memory_space=pltpu.VMEM)
    return pl.pallas_call(
        ascent_kernel,
        out_shape=[jax.ShapeDtypeStruct((256, columns), F32), jax.ShapeDtypeStruct((256, 1, 128), F32)],
        in_specs=[pl.BlockSpec(memory_space=pltpu.SMEM)] + [vmem] * 6 + [pl.BlockSpec(memory_space=pl.ANY)],
        out_specs=[vmem] * 2,
        scratch_shapes=[pltpu.VMEM((32, 2, 16, columns), BF)],
        compiler_params=pltpu.CompilerParams(vmem_limit_bytes=40 << 20),
        cost_estimate=pl.CostEstimate(flops=2 * TOKENS * 256 * columns, bytes_accessed=2 << 20, transcendentals=0),
        name="ascent_work",
    )(at, mine, other, *slopes, mark)


def result_kernel(at, turned, s0, s1, s2, s3, out, ordered):
    in_order(at[2], (s0, s1, s2, s3), ordered)
    out[...] = dot(turned[...], ordered[...].reshape(TOKENS, out.shape[1]), ((1,), (0,)))


def result_work(at, turned, slopes):
    columns = slopes[0].shape[1]
    vmem = pl.BlockSpec(memory_space=pltpu.VMEM)
    return pl.pallas_call(
        result_kernel,
        out_shape=jax.ShapeDtypeStruct((turned.shape[0], columns), F32),
        in_specs=[pl.BlockSpec(memory_space=pltpu.SMEM)] + [vmem] * 5,
        out_specs=vmem,
        scratch_shapes=[pltpu.VMEM((32, 2, 16, columns), BF)],
        compiler_params=pltpu.CompilerParams(vmem_limit_bytes=40 << 20),
        cost_estimate=pl.CostEstimate(flops=2 * TOKENS * 768 * columns, bytes_accessed=4 << 20, transcendentals=0),
        name="result_work",
    )(at, turned, *slopes)


def per_device(tokens, norm_gain, w_up, cotangent):
    width = w_up.shape[0]
    places = (lax.axis_index(DP), lax.axis_index("c"), lax.axis_index("x"), lax.axis_index("yh"))
    at = jnp.stack(places).astype(jnp.int32)
    with jax.named_scope("token_gather"):
        mine = spread(tokens, ("yl", "z"), 32)
        mine, late = lax.optimization_barrier((mine, cotangent))
        other = swap(mine, "c", 1)
        cot_other = swap(late, "yh", 1)
    with jax.named_scope("local_work"):
        joined, own, near, opposite, far, sent = local_work(at, mine, other, norm_gain[None], w_up)
    with jax.named_scope("sums_x"):
        sent, cot_other = lax.optimization_barrier((sent, cot_other))
        got = lax.all_to_all(sent, MP, 0, 0, tiled=True)
        moved = [swap(v, "x", b) for b, v in ((1, near), (2, opposite), (3, far))]
    with jax.named_scope("stats_work"):
        rows, half, full, pair, scales = stats_work(at, got, own, moved, cotangent, cot_other)
        normed = joined.reshape(TOKENS, width).astype(F32) - scales[:, 33:34]
        turned = (normed * scales[:, 32:33] * norm_gain[None, :]).astype(BF).T
    with jax.named_scope("gram_gather"):
        gram = spread(rows, ("yl", "z"), 32)
    with jax.named_scope("slope"):
        moved = swap(half, "yh", 1)
        pre, slope, mark = slope_work(at, full, moved, scales, pair)
        gram, mark = lax.optimization_barrier((gram, mark))
        gram_other = swap(gram, "c", 1)
        slopes = gather_x(slope)
    with jax.named_scope("ascent"):
        along, squared = ascent_work(at, gram, gram_other, slopes, mark)
        squared = jnp.sum(lax.all_to_all(squared, DP + ("x",), 0, 0, tiled=True)[:, 0, 0])
        size = jnp.sqrt(jnp.maximum(squared, 0.0)) + 1e-12
        radius = 0.5 * math.sqrt(FF)
    with jax.named_scope("sharp"):
        sharp = slope_of(pair.reshape(pre.shape), pre + along * (radius / size))
        return result_work(at, turned, gather_x(sharp))


def solution(mesh):
    fine = Mesh(mesh.devices.reshape(4, 8, 2, 2, 4), DP + MP)
    placed = (P(DP, MP), P(MP), P(MP, DP), P(MP, DP))
    return jax.shard_map(
        per_device, mesh=fine, in_specs=placed, out_specs=P(MP, DP), check_vma=False
    )
```

time: 182 us -> 181 us (level)
  blocking collectives: 66.4 us -> 34.7 us
  starting transfers between devices: 66.3 us -> 76.1 us
  local copies, waits for them, and re-layouts: 5.99 us -> 15.5 us
  waiting for transfers between devices: 26.4 us -> 35.4 us
  other arithmetic: 1.8 us -> 5.44 us
  matrix products: 2.25 us -> 0 us
    all_to_all x2 -> x1, blocking collectives: 66.4 us -> 34.7 us  [spread(): return lax.all_to_all(copies, axes, 0, 0, tiled=True)]
    all_to_all x1 -> x2, starting transfers between devices: 9.08 us -> 23.8 us  [the longest x1 17.7 us: per_device(): lax.all_to_all(squared, DP + ('x',), 0, 0, tiled=True)[:, 0, 0]]
    ppermute x13, waiting for transfers between devices: 17.4 us -> 28.5 us  [swap(): return lax.ppermute(value, axis, [(i, i ^ bit) for i in range(size)])]
    unnamed x14 -> x26, local copies, waits for them, and re-layouts: 3.6 us -> 9.1 us
    ppermute x13, starting transfers between devices: 50.5 us -> 46.6 us  [swap(): return lax.ppermute(value, axis, [(i, i ^ bit) for i in range(size)])]
    convert_element_type x0 -> x1, local copies, waits for them, and re-layouts: none -> 3.57 us  [per_device(): normed = joined.reshape(TOKENS, width).astype(F32) - scales[:, 33:34]]
    transpose x0 -> x1, other arithmetic: none -> 2.28 us  [per_device(): turned = (normed * scales[:, 32:33] * norm_gain[None, :]).astype(BF).T]
    dot_general x1 -> x0, matrix products: 2.25 us -> none  [dot(): lax.dot_general(left, right, (dims, ((), ())), precision=precision, prefe...]
  transfers between devices with their start and end apart: 15 -> 16, of which waited for: 8 -> 7; matrix products, arithmetic and copies ran while one was open for 0% -> 5% of each run, Pallas kernels for 0% -> 4%
where the time goes in v10:
time: 181 us; the launch traced here: 180 us
  starting transfers between devices  76.1 us (42%)
  waiting for transfers between devices  35.4 us (20%)
  blocking collectives  34.7 us (19%)
  local copies, waits for them, and re-layouts  15.5 us (9%)
  Pallas kernels  12.1 us (7%)
  other arithmetic  5.44 us (3%)
    ppermute x13, starting transfers between devices, swap(): return lax.ppermute(value, axis, [(i, i ^ bit) for i in range(size)])  46.6 us
    all_to_all x1, blocking collectives, spread(): return lax.all_to_all(copies, axes, 0, 0, tiled=True)  34.7 us
    ppermute x13, waiting for transfers between devices, swap(): return lax.ppermute(value, axis, [(i, i ^ bit) for i in range(size)])  28.5 us
    all_to_all x1, starting transfers between devices, per_device(): lax.all_to_all(squared, DP + ('x',), 0, 0, tiled=True)[:, 0, 0]  17.7 us
    unnamed x26, local copies, waits for them, and re-layouts  9.1 us
    all_to_all x1, waiting for transfers between devices, per_device(): lax.all_to_all(squared, DP + ('x',), 0, 0, tiled=True)[:, 0, 0]  6.89 us
    all_to_all x1, starting transfers between devices, per_device(): got = lax.all_to_all(sent, MP, 0, 0, tiled=True)  6.18 us
    pallas_call x1, Pallas kernels, local_work(): pl.pallas_call(local_kernel, out_shape=[jax.ShapeDtypeStruct((32, 2, 16,...  6.11 us
  transfers between devices with their start and end apart: 16, of which 7 were waited for; matrix products, arithmetic and copies ran while one was open for 5% of the time, Pallas kernels for 4%

profile of v10, /device:TPU:1, one launch (start us, length us, event | category | flops | bytes accessed | tf_op | source)
XLA Modules:
  0.0 180.2 jit_solution(1512866767290051377)
XLA Ops:
  0.0 0.8 broadcast_in_dim.6
  0.8 0.0 copy-start.5
  0.8 34.7 %all_to_all.20.mine = bf16[32,16,768]{2,1,0:T(8,128)(2,1)S(1)} all-to-all(bf16[32,16,768]{2,1,0:T(8,128)(2,1)S(1)} %broadcast_in_dim.6), channel_id=1, replica_groups=mesh['yl'=4,'z'=8,'c'=2,'yh'=2,'x'=4] {'yl','z'}, dimensions={0} | all-to-all | bytes 1572864 | tf_op jit(solution)/shard_map/token_gather/all_to_all | solution.py:33
  35.5 4.2 %collective-permute-start = (bf16[32,16,768]{2,1,0:T(8,128)(2,1)S(1)}, bf16[32,16,768]{2,1,0:T(8,128)(2,1)S(1)}, u32[]{:S(2)}, u32[]{:S(2)}) collective-permute-start(bf16[32,16,768]{2,1,0:T(8,128)(2,1)S(1)} %all_to_all.20.mine), channel_id=1, source_target_pairs={{0,8},{8,0},{1,9},{9,1},{2,10},{10,2},{3,11},{11,3},{4,12},{12,4},... | collective-permute-start | bytes 2359304 | tf_op jit(solution)/shard_map/token_gather/ppermute | solution.py:28
  39.7 0.7 broadcast_in_dim.7.gain
  40.4 0.1 pad_add_fusion.at
  40.5 4.8 %collective-permute-start.1 = (bf16[128,384]{1,0:T(8,128)(2,1)}, bf16[128,384]{1,0:T(8,128)(2,1)S(1)}, u32[]{:S(2)}, u32[]{:S(2)}) collective-permute-start(bf16[128,384]{1,0:T(8,128)(2,1)} %cot.1), channel_id=1, source_target_pairs={{0,4},{4,0},{1,5},{5,1},{2,6},{6,2},{3,7},{7,3},{8,12},{12,8},{9,1... | collective-permute-start | bytes 294920 | tf_op jit(solution)/shard_map/token_gather/ppermute | solution.py:28
  45.3 0.0 collective-permute-done.other
  45.3 0.0 copy-start.6
  45.3 0.9 copy-done.6
  46.2 1.1 copy-done.7
  47.3 1.1 copy-done.8
  48.4 6.1 %local_work.1 = (bf16[32,2,16,768]{3,2,1,0:T(8,128)(2,1)S(1)}, f32[256,384]{1,0:T(8,128)S(1)}, bf16[256,384]{1,0:T(8,128)(2,1)}, bf16[256,384]{1,0:T(8,128)(2,1)...) custom-call(s32[4]{0:T(128)S(1)} %pad_add_fusion.at, bf16[32,16,768]{2,1,0:T(8,128)(2,1)S(1)} %all_to_all.20.mine, ...), custom_call_target="tpu_custom_call" | custom-call | flops 1207959552 | bytes 8388608 | tf_op jit(solution)/shard_map/local_work/local_work/pallas_call | solution.py:104
  54.5 0.7 copy-done.9
  55.2 0.7 copy-done.10
  55.9 0.0 collective-permute-done.1.cot_other
  55.9 6.2 %all-to-all-start.1 = ((bf16[8,48,256]{2,1,0:T(8,128)(2,1)}), bf16[8,48,256]{2,1,0:T(8,128)(2,1)S(1)}, u32[]{:S(2)}, u32[]{:S(2)}) async-start(bf16[8,48,256]{2,1,0:T(8,128)(2,1)} %get-tuple-element.31), calls=%async_computation.1 | async-start | bytes 393216 | tf_op jit(solution)/shard_map/sums_x/all_to_all | solution.py:287
  62.1 3.4 %collective-permute-start.2 = (bf16[256,384]{1,0:T(8,128)(2,1)}, bf16[256,384]{1,0:T(8,128)(2,1)S(1)}, u32[]{:S(2)}, u32[]{:S(2)}) collective-permute-start(bf16[256,384]{1,0:T(8,128)(2,1)} %get-tuple-element.33), channel_id=1, source_target_pairs={{0,1},{1,0},{2,3},{3,2},{4,5},{5,4},{6,7},{7,6},{8,9},{9,8},{10,11... | collective-permute-start | bytes 589832 | tf_op jit(solution)/shard_map/sums_x/ppermute | solution.py:28
  65.4 4.3 %collective-permute-start.3 = (bf16[256,384]{1,0:T(8,128)(2,1)}, bf16[256,384]{1,0:T(8,128)(2,1)S(1)}, u32[]{:S(2)}, u32[]{:S(2)}) collective-permute-start(bf16[256,384]{1,0:T(8,128)(2,1)} %copy-done.10), channel_id=1, source_target_pairs={{0,2},{1,3},{2,0},{3,1},{4,6},{5,7},{6,4},{7,5},{8,10},{9,11},{10,... | collective-permute-start | bytes 589832 | tf_op jit(solution)/shard_map/sums_x/ppermute | solution.py:28
  69.7 1.9 %collective-permute-start.4 = (bf16[256,384]{1,0:T(8,128)(2,1)}, bf16[256,384]{1,0:T(8,128)(2,1)S(1)}, u32[]{:S(2)}, u32[]{:S(2)}) collective-permute-start(bf16[256,384]{1,0:T(8,128)(2,1)} %copy-done.9), channel_id=1, source_target_pairs={{0,3},{1,2},{2,1},{3,0},{4,7},{5,6},{6,5},{7,4},{8,11},{9,10},{10,... | collective-permute-start | bytes 589832 | tf_op jit(solution)/shard_map/sums_x/ppermute | solution.py:28
  71.7 0.0 collective-permute-done.2.one
  71.7 5.8 %collective-permute-done.3.two = bf16[256,384]{1,0:T(8,128)(2,1)S(1)} collective-permute-done((bf16[256,384]{1,0:T(8,128)(2,1)}, bf16[256,384]{1,0:T(8,128)(2,1)S(1)}, u32[]{:S(2)}, u32[]{:S(2)}) %collective-permute-start.3) | collective-permute-done | bytes 196640 | tf_op jit(solution)/shard_map/sums_x/ppermute | solution.py:28
  77.4 5.3 %collective-permute-done.4.three = bf16[256,384]{1,0:T(8,128)(2,1)S(1)} collective-permute-done((bf16[256,384]{1,0:T(8,128)(2,1)}, bf16[256,384]{1,0:T(8,128)(2,1)S(1)}, u32[]{:S(2)}, u32[]{:S(2)}) %collective-permute-start.4) | collective-permute-done | bytes 196640 | tf_op jit(solution)/shard_map/sums_x/ppermute | solution.py:28
  82.7 0.7 copy-done.2
  83.4 0.0 all-to-all-done.1.got
  83.4 0.0 copy-done.5
  83.4 0.9 copy-done.3
  84.4 1.4 stats_work.1
  85.8 0.0 copy-start
  85.8 0.7 copy-done
  86.5 0.7 copy-done.11
  87.2 0.7 broadcast_in_dim.8
  87.9 5.6 %all-to-all-start.2 = ((bf16[32,16,256]{2,1,0:T(8,128)(2,1)}), bf16[32,16,256]{2,1,0:T(8,128)(2,1)S(1)}, u32[]{:S(2)}, u32[]{:S(2)}) async-start(bf16[32,16,256]{2,1,0:T(8,128)(2,1)} %broadcast_in_dim.8), calls=%async_computation.2 | async-start | bytes 524288 | tf_op jit(solution)/shard_map/gram_gather/all_to_all | solution.py:33
  93.6 6.4 %collective-permute-start.5 = (bf16[256,384]{1,0:T(8,128)(2,1)}, bf16[256,384]{1,0:T(8,128)(2,1)S(1)}, u32[]{:S(2)}, u32[]{:S(2)}) collective-permute-start(bf16[256,384]{1,0:T(8,128)(2,1)} %copy-done.11), channel_id=1, source_target_pairs={{0,4},{4,0},{1,5},{5,1},{2,6},{6,2},{3,7},{7,3},{8,12},{12,8},{9,1... | collective-permute-start | bytes 589832 | tf_op jit(solution)/shard_map/slope/ppermute | solution.py:28
  99.9 6.8 %collective-permute-done.5.moved = bf16[256,384]{1,0:T(8,128)(2,1)S(1)} collective-permute-done((bf16[256,384]{1,0:T(8,128)(2,1)}, bf16[256,384]{1,0:T(8,128)(2,1)S(1)}, u32[]{:S(2)}, u32[]{:S(2)}) %collective-permute-start.5) | collective-permute-done | bytes 196640 | tf_op jit(solution)/shard_map/slope/ppermute | solution.py:28
  106.7 1.0 copy-done.1
  107.7 0.8 slope_work.1
  108.6 0.0 all-to-all-done.2.mine
  108.6 3.7 %collective-permute-start.6 = (bf16[32,16,256]{2,1,0:T(8,128)(2,1)S(1)}, bf16[32,16,256]{2,1,0:T(8,128)(2,1)S(1)}, u32[]{:S(2)}, u32[]{:S(2)}) collective-permute-start(bf16[32,16,256]{2,1,0:T(8,128)(2,1)S(1)} %all-to-all-done.2.mine), channel_id=1, source_target_pairs={{0,8},{8,0},{1,9},{9,1},{2,10},{10,2},{3,11},{11,3},{4,12},{12,4},... | collective-permute-start | bytes 786440 | tf_op jit(solution)/shard_map/slope/ppermute | solution.py:28
  112.3 2.2 %collective-permute-start.9 = (bf16[256,384]{1,0:T(8,128)(2,1)S(1)}, bf16[256,384]{1,0:T(8,128)(2,1)S(1)}, u32[]{:S(2)}, u32[]{:S(2)}) collective-permute-start(bf16[256,384]{1,0:T(8,128)(2,1)S(1)} %get-tuple-element.45.s0), channel_id=1, source_target_pairs={{0,3},{1,2},{2,1},{3,0},{4,7},{5,6},{6,5},{7,4},{8,11},{9,10},{10,... | collective-permute-start | bytes 589832 | tf_op jit(solution)/shard_map/slope/ppermute | solution.py:28
  114.5 2.8 %collective-permute-start.8 = (bf16[256,384]{1,0:T(8,128)(2,1)S(1)}, bf16[256,384]{1,0:T(8,128)(2,1)S(1)}, u32[]{:S(2)}, u32[]{:S(2)}) collective-permute-start(bf16[256,384]{1,0:T(8,128)(2,1)S(1)} %get-tuple-element.45.s0), channel_id=1, source_target_pairs={{0,2},{1,3},{2,0},{3,1},{4,6},{5,7},{6,4},{7,5},{8,10},{9,11},{10,... | collective-permute-start | bytes 589832 | tf_op jit(solution)/shard_map/slope/ppermute | solution.py:28
  117.3 3.9 %collective-permute-start.7 = (bf16[256,384]{1,0:T(8,128)(2,1)S(1)}, bf16[256,384]{1,0:T(8,128)(2,1)S(1)}, u32[]{:S(2)}, u32[]{:S(2)}) collective-permute-start(bf16[256,384]{1,0:T(8,128)(2,1)S(1)} %get-tuple-element.45.s0), channel_id=1, source_target_pairs={{0,1},{1,0},{2,3},{3,2},{4,5},{5,4},{6,7},{7,6},{8,9},{9,8},{10,11... | collective-permute-start | bytes 589832 | tf_op jit(solution)/shard_map/slope/ppermute | solution.py:28
  121.3 4.8 %collective-permute-done.9.s3 = bf16[256,384]{1,0:T(8,128)(2,1)S(1)} collective-permute-done((bf16[256,384]{1,0:T(8,128)(2,1)S(1)}, bf16[256,384]{1,0:T(8,128)(2,1)S(1)}, u32[]{:S(2)}, u32[]{:S(2)}) %collective-permute-start.9) | collective-permute-done | bytes 196640 | tf_op jit(solution)/shard_map/slope/ppermute | solution.py:28
  126.1 0.0 collective-permute-done.8.s2
  126.1 2.2 %collective-permute-done.7.s1 = bf16[256,384]{1,0:T(8,128)(2,1)S(1)} collective-permute-done((bf16[256,384]{1,0:T(8,128)(2,1)S(1)}, bf16[256,384]{1,0:T(8,128)(2,1)S(1)}, u32[]{:S(2)}, u32[]{:S(2)}) %collective-permute-start.7) | collective-permute-done | bytes 196640 | tf_op jit(solution)/shard_map/slope/ppermute | solution.py:28
  128.3 0.0 collective-permute-done.6.other
  128.3 1.2 ascent_work.1
  129.5 0.0 copy-start.4
  129.5 0.6 copy-done.4
  130.1 17.7 %all-to-all-start.3 = ((f32[256,1,128]{2,1,0:T(1,128)}), f32[256,1,128]{2,1,0:T(1,128)S(1)}, u32[]{:S(2)}, u32[]{:S(2)}) async-start(f32[256,1,128]{2,1,0:T(1,128)} %copy-done.4), calls=%async_computation.3 | async-start | bytes 262144 | tf_op jit(solution)/shard_map/ascent/all_to_all | solution.py:303
  147.8 2.0 %bitcast_convert_fusion = f32[1024,768]{1,0:T(8,128)} fusion(bf16[32,2,16,768]{3,2,1,0:T(8,128)(2,1)S(1)} %get-tuple-element.28), kind=kLoop, calls=%fused_computation.2 | loop fusion | flops 786432 | bytes 4718592 | tf_op jit(solution)/shard_map/stats_work/convert_element_type | solution.py:291
  149.8 3.6 %copy.6 = f32[1024,768]{0,1:T(8,128)} copy(f32[1024,768]{1,0:T(8,128)} %bitcast_convert_fusion) | data formatting | bytes 6291456 | tf_op jit(solution)/shard_map/stats_work/convert_element_type | solution.py:291
  153.4 0.6 slice_reduce_fusion.1
  154.0 6.9 %all-to-all-done.3 = f32[256,1,128]{2,1,0:T(1,128)S(1)} async-done(((f32[256,1,128]{2,1,0:T(1,128)}), f32[256,1,128]{2,1,0:T(1,128)S(1)}, u32[]{:S(2)}, u32[]{:S(2)}) %all-to-all-start.3) | async-done | bytes 131104 | tf_op jit(solution)/shard_map/ascent/all_to_all | solution.py:303
  160.9 0.9 slice_reduce_fusion.2
  162.5 0.2 fusion.7.s0
  162.7 2.5 %collective-permute-start.12 = (bf16[256,384]{1,0:T(8,128)(2,1)S(1)}, bf16[256,384]{1,0:T(8,128)(2,1)S(1)}, u32[]{:S(2)}, u32[]{:S(2)}) collective-permute-start(bf16[256,384]{1,0:T(8,128)(2,1)S(1)} %fusion.7.s0), channel_id=1, source_target_pairs={{0,3},{1,2},{2,1},{3,0},{4,7},{5,6},{6,5},{7,4},{8,11},{9,10},{10,... | collective-permute-start | bytes 589832 | tf_op jit(solution)/shard_map/sharp/ppermute | solution.py:28
  165.2 3.3 %collective-permute-start.11 = (bf16[256,384]{1,0:T(8,128)(2,1)S(1)}, bf16[256,384]{1,0:T(8,128)(2,1)S(1)}, u32[]{:S(2)}, u32[]{:S(2)}) collective-permute-start(bf16[256,384]{1,0:T(8,128)(2,1)S(1)} %fusion.7.s0), channel_id=1, source_target_pairs={{0,2},{1,3},{2,0},{3,1},{4,6},{5,7},{6,4},{7,5},{8,10},{9,11},{10,... | collective-permute-start | bytes 589832 | tf_op jit(solution)/shard_map/sharp/ppermute | solution.py:28
  168.5 3.2 %collective-permute-start.10 = (bf16[256,384]{1,0:T(8,128)(2,1)S(1)}, bf16[256,384]{1,0:T(8,128)(2,1)S(1)}, u32[]{:S(2)}, u32[]{:S(2)}) collective-permute-start(bf16[256,384]{1,0:T(8,128)(2,1)S(1)} %fusion.7.s0), channel_id=1, source_target_pairs={{0,1},{1,0},{2,3},{3,2},{4,5},{5,4},{6,7},{7,6},{8,9},{9,8},{10,11... | collective-permute-start | bytes 589832 | tf_op jit(solution)/shard_map/sharp/ppermute | solution.py:28
  171.7 2.3 %fusion.turned = bf16[768,1024]{1,0:T(8,128)(2,1)S(1)} fusion(f32[1024,768]{0,1:T(8,128)} %copy.6, f32[768]{0:T(1024)S(1)} %copy-done.12, f32[1024]{0:T(1024)S(1)} %get-tuple-element.50, f32[1024]{0:T(1024)S(1)} %get-tuple-element.49), kind=kLoop, calls=%fused_computation.1 | loop fusion | flops 3145728 | bytes 4729856 | tf_op jit(solution)/shard_map/stats_work/transpose | solution.py:292
  174.0 0.0 collective-permute-done.12.s3
  174.0 0.0 collective-permute-done.11.s2
  174.0 3.6 %collective-permute-done.10.s1 = bf16[256,384]{1,0:T(8,128)(2,1)S(1)} collective-permute-done((bf16[256,384]{1,0:T(8,128)(2,1)S(1)}, bf16[256,384]{1,0:T(8,128)(2,1)S(1)}, u32[]{:S(2)}, u32[]{:S(2)}) %collective-permute-start.10) | collective-permute-done | bytes 196640 | tf_op jit(solution)/shard_map/sharp/ppermute | solution.py:28
  177.6 2.6 %result_work.1 = f32[768,384]{1,0:T(8,128)} custom-call(s32[4]{0:T(128)S(1)} %pad_add_fusion.at, bf16[768,1024]{1,0:T(8,128)(2,1)S(1)} %fusion.turned, bf16[256,384]{1,0:T(8,128)(2,1)S(1)} %fusion.7.s0, bf16[256,384]{1,0:T(8,128)(2,1)S(1)} %collective-permute-done.10.s1, bf16[256,384]{1,0:T(8,128)(2,1)S(1)} %collective-permute-done.11.s2, ...), custom_call_target="tpu_custom_call" | custom-call | flops 603979776 | bytes 4194304 | tf_op jit(solution)/shard_map/sharp/result_work/pallas_call | solution.py:262
  (10 shorter events, 0.0 us)
Async XLA Ops:
  0.8 82.6 %copy-start.5 = (bf16[128,384]{1,0:T(8,128)(2,1)S(1)}, bf16[128,384]{1,0:T(8,128)(2,1)}, u32[]{:S(2)}) copy-start(bf16[128,384]{1,0:T(8,128)(2,1)} %cot.1) | copy-start | bytes 294916
  35.5 9.8 %collective-permute-start = (bf16[32,16,768]{2,1,0:T(8,128)(2,1)S(1)}, bf16[32,16,768]{2,1,0:T(8,128)(2,1)S(1)}, u32[]{:S(2)}, u32[]{:S(2)}) collective-permute-start(bf16[32,16,768]{2,1,0:T(8,128)(2,1)S(1)} %all_to_all.20.mine), channel_id=1, source_target_pairs={{0,8},{8,0},{1,9},{9,1},{2,10},{10,2},{3,11},{11,3},{4,12},{12,4},... | collective-permute-start | bytes 2359304 | tf_op jit(solution)/shard_map/token_gather/ppermute | solution.py:28
  40.5 15.4 %collective-permute-start.1 = (bf16[128,384]{1,0:T(8,128)(2,1)}, bf16[128,384]{1,0:T(8,128)(2,1)S(1)}, u32[]{:S(2)}, u32[]{:S(2)}) collective-permute-start(bf16[128,384]{1,0:T(8,128)(2,1)} %cot.1), channel_id=1, source_target_pairs={{0,4},{4,0},{1,5},{5,1},{2,6},{6,2},{3,7},{7,3},{8,12},{12,8},{9,1... | collective-permute-start | bytes 294920 | tf_op jit(solution)/shard_map/token_gather/ppermute | solution.py:28
  45.3 0.9 copy-start.6
  46.2 1.1 copy-start.7
  47.3 1.1 copy-start.8
  54.5 0.7 copy-start.9
  55.2 0.7 copy-start.10
  55.9 27.5 %all-to-all-start.1 = ((bf16[8,48,256]{2,1,0:T(8,128)(2,1)}), bf16[8,48,256]{2,1,0:T(8,128)(2,1)S(1)}, u32[]{:S(2)}, u32[]{:S(2)}) async-start(bf16[8,48,256]{2,1,0:T(8,128)(2,1)} %get-tuple-element.31), calls=%async_computation.1 | async-start | bytes 393216 | tf_op jit(solution)/shard_map/sums_x/all_to_all | solution.py:287
  62.1 9.6 %collective-permute-start.2 = (bf16[256,384]{1,0:T(8,128)(2,1)}, bf16[256,384]{1,0:T(8,128)(2,1)S(1)}, u32[]{:S(2)}, u32[]{:S(2)}) collective-permute-start(bf16[256,384]{1,0:T(8,128)(2,1)} %get-tuple-element.33), channel_id=1, source_target_pairs={{0,1},{1,0},{2,3},{3,2},{4,5},{5,4},{6,7},{7,6},{8,9},{9,8},{10,11... | collective-permute-start | bytes 589832 | tf_op jit(solution)/shard_map/sums_x/ppermute | solution.py:28
  65.4 12.0 %collective-permute-start.3 = (bf16[256,384]{1,0:T(8,128)(2,1)}, bf16[256,384]{1,0:T(8,128)(2,1)S(1)}, u32[]{:S(2)}, u32[]{:S(2)}) collective-permute-start(bf16[256,384]{1,0:T(8,128)(2,1)} %copy-done.10), channel_id=1, source_target_pairs={{0,2},{1,3},{2,0},{3,1},{4,6},{5,7},{6,4},{7,5},{8,10},{9,11},{10,... | collective-permute-start | bytes 589832 | tf_op jit(solution)/shard_map/sums_x/ppermute | solution.py:28
  69.7 13.0 %collective-permute-start.4 = (bf16[256,384]{1,0:T(8,128)(2,1)}, bf16[256,384]{1,0:T(8,128)(2,1)S(1)}, u32[]{:S(2)}, u32[]{:S(2)}) collective-permute-start(bf16[256,384]{1,0:T(8,128)(2,1)} %copy-done.9), channel_id=1, source_target_pairs={{0,3},{1,2},{2,1},{3,0},{4,7},{5,6},{6,5},{7,4},{8,11},{9,10},{10,... | collective-permute-start | bytes 589832 | tf_op jit(solution)/shard_map/sums_x/ppermute | solution.py:28
  82.7 0.7 copy-start.2
  83.4 0.9 copy-start.3
  85.8 0.7 copy-start
  86.5 0.7 copy-start.11
  87.9 20.6 %all-to-all-start.2 = ((bf16[32,16,256]{2,1,0:T(8,128)(2,1)}), bf16[32,16,256]{2,1,0:T(8,128)(2,1)S(1)}, u32[]{:S(2)}, u32[]{:S(2)}) async-start(bf16[32,16,256]{2,1,0:T(8,128)(2,1)} %broadcast_in_dim.8), calls=%async_computation.2 | async-start | bytes 524288 | tf_op jit(solution)/shard_map/gram_gather/all_to_all | solution.py:33
  93.6 13.2 %collective-permute-start.5 = (bf16[256,384]{1,0:T(8,128)(2,1)}, bf16[256,384]{1,0:T(8,128)(2,1)S(1)}, u32[]{:S(2)}, u32[]{:S(2)}) collective-permute-start(bf16[256,384]{1,0:T(8,128)(2,1)} %copy-done.11), channel_id=1, source_target_pairs={{0,4},{4,0},{1,5},{5,1},{2,6},{6,2},{3,7},{7,3},{8,12},{12,8},{9,1... | collective-permute-start | bytes 589832 | tf_op jit(solution)/shard_map/slope/ppermute | solution.py:28
  106.7 1.0 copy-start.1
  108.6 19.7 %collective-permute-start.6 = (bf16[32,16,256]{2,1,0:T(8,128)(2,1)S(1)}, bf16[32,16,256]{2,1,0:T(8,128)(2,1)S(1)}, u32[]{:S(2)}, u32[]{:S(2)}) collective-permute-start(bf16[32,16,256]{2,1,0:T(8,128)(2,1)S(1)} %all-to-all-done.2.mine), channel_id=1, source_target_pairs={{0,8},{8,0},{1,9},{9,1},{2,10},{10,2},{3,11},{11,3},{4,12},{12,4},... | collective-permute-start | bytes 786440 | tf_op jit(solution)/shard_map/slope/ppermute | solution.py:28
  112.3 13.8 %collective-permute-start.9 = (bf16[256,384]{1,0:T(8,128)(2,1)S(1)}, bf16[256,384]{1,0:T(8,128)(2,1)S(1)}, u32[]{:S(2)}, u32[]{:S(2)}) collective-permute-start(bf16[256,384]{1,0:T(8,128)(2,1)S(1)} %get-tuple-element.45.s0), channel_id=1, source_target_pairs={{0,3},{1,2},{2,1},{3,0},{4,7},{5,6},{6,5},{7,4},{8,11},{9,10},{10,... | collective-permute-start | bytes 589832 | tf_op jit(solution)/shard_map/slope/ppermute | solution.py:28
  114.5 11.6 %collective-permute-start.8 = (bf16[256,384]{1,0:T(8,128)(2,1)S(1)}, bf16[256,384]{1,0:T(8,128)(2,1)S(1)}, u32[]{:S(2)}, u32[]{:S(2)}) collective-permute-start(bf16[256,384]{1,0:T(8,128)(2,1)S(1)} %get-tuple-element.45.s0), channel_id=1, source_target_pairs={{0,2},{1,3},{2,0},{3,1},{4,6},{5,7},{6,4},{7,5},{8,10},{9,11},{10,... | collective-permute-start | bytes 589832 | tf_op jit(solution)/shard_map/slope/ppermute | solution.py:28
  117.3 11.0 %collective-permute-start.7 = (bf16[256,384]{1,0:T(8,128)(2,1)S(1)}, bf16[256,384]{1,0:T(8,128)(2,1)S(1)}, u32[]{:S(2)}, u32[]{:S(2)}) collective-permute-start(bf16[256,384]{1,0:T(8,128)(2,1)S(1)} %get-tuple-element.45.s0), channel_id=1, source_target_pairs={{0,1},{1,0},{2,3},{3,2},{4,5},{5,4},{6,7},{7,6},{8,9},{9,8},{10,11... | collective-permute-start | bytes 589832 | tf_op jit(solution)/shard_map/slope/ppermute | solution.py:28
  129.5 0.7 copy-start.4
  130.1 30.7 %all-to-all-start.3 = ((f32[256,1,128]{2,1,0:T(1,128)}), f32[256,1,128]{2,1,0:T(1,128)S(1)}, u32[]{:S(2)}, u32[]{:S(2)}) async-start(f32[256,1,128]{2,1,0:T(1,128)} %copy-done.4), calls=%async_computation.3 | async-start | bytes 262144 | tf_op jit(solution)/shard_map/ascent/all_to_all | solution.py:303
  149.8 22.0 %copy-start.12 = (f32[768]{0:T(1024)S(1)}, f32[768]{0:T(1024)}, u32[]{:S(2)}) copy-start(f32[768]{0:T(1024)} %param.5) | copy-start | bytes 9220
  162.7 11.3 %collective-permute-start.12 = (bf16[256,384]{1,0:T(8,128)(2,1)S(1)}, bf16[256,384]{1,0:T(8,128)(2,1)S(1)}, u32[]{:S(2)}, u32[]{:S(2)}) collective-permute-start(bf16[256,384]{1,0:T(8,128)(2,1)S(1)} %fusion.7.s0), channel_id=1, source_target_pairs={{0,3},{1,2},{2,1},{3,0},{4,7},{5,6},{6,5},{7,4},{8,11},{9,10},{10,... | collective-permute-start | bytes 589832 | tf_op jit(solution)/shard_map/sharp/ppermute | solution.py:28
  165.2 8.8 %collective-permute-start.11 = (bf16[256,384]{1,0:T(8,128)(2,1)S(1)}, bf16[256,384]{1,0:T(8,128)(2,1)S(1)}, u32[]{:S(2)}, u32[]{:S(2)}) collective-permute-start(bf16[256,384]{1,0:T(8,128)(2,1)S(1)} %fusion.7.s0), channel_id=1, source_target_pairs={{0,2},{1,3},{2,0},{3,1},{4,6},{5,7},{6,4},{7,5},{8,10},{9,11},{10,... | collective-permute-start | bytes 589832 | tf_op jit(solution)/shard_map/sharp/ppermute | solution.py:28
  168.5 9.1 %collective-permute-start.10 = (bf16[256,384]{1,0:T(8,128)(2,1)S(1)}, bf16[256,384]{1,0:T(8,128)(2,1)S(1)}, u32[]{:S(2)}, u32[]{:S(2)}) collective-permute-start(bf16[256,384]{1,0:T(8,128)(2,1)S(1)} %fusion.7.s0), channel_id=1, source_target_pairs={{0,1},{1,0},{2,3},{3,2},{4,5},{5,4},{6,7},{7,6},{8,9},{9,8},{10,11... | collective-permute-start | bytes 589832 | tf_op jit(solution)/shard_map/sharp/ppermute | solution.py:28

commit v11 on v10

--- a/solution.py
+++ b/solution.py
@@ -49,8 +49,22 @@
     return out
 
 
-def local_kernel(at, mine, other, gain, w, joined, own, near, opposite, far, sent, high, part, out, sems):
+def fetch(sources, targets, sems):
+    copies = [pltpu.make_async_copy(s, t, sems.at[i]) for i, (s, t) in enumerate(zip(sources, targets))]
+    for copy in copies:
+        copy.start()
+    return copies
+
+
+HBM = pl.BlockSpec(memory_space=pltpu.HBM)
+
+
+def local_kernel(at, mine, other, gain, w_far, joined, own, near, opposite, far, sent, high, part, out, w, sems, in_sems):
     place, core, x = at[0], at[1], at[2]
+    halves = [pl.ds(16 * i, 16) for i in range(2)]
+    sources = [v.at[h] for h in halves for v in (mine, other)]
+    targets = [joined.at[h, c] for h in halves for c in (core, 1 - core)]
+    arrivals = fetch(sources[:2] + [w_far] + sources[2:], targets[:2] + [w] + targets[2:], in_sems)
     g = gain[...]
     width = g.shape[1]
     ones = jnp.ones((8, width), BF)
@@ -58,8 +72,8 @@
     local, css, lean = [], [], []
     for i in range(8):
         chips = pl.ds(4 * i, 4)
-        joined[chips, core] = mine[chips]
-        joined[chips, 1 - core] = other[chips]
+        for copy in {0: arrivals[:3], 4: arrivals[3:]}.get(i, []):
+            copy.wait()
         raw = joined[chips].reshape(128, width)
         value = raw.astype(F32)
         centred = value - jnp.sum(value, axis=1, keepdims=True) * (1.0 / width)
@@ -111,13 +125,15 @@
             block,
             jax.ShapeDtypeStruct((8, 48, 256), BF),
         ],
-        in_specs=[pl.BlockSpec(memory_space=pltpu.SMEM)] + [vmem] * 4,
-        out_specs=[vmem] * 2 + [pl.BlockSpec(memory_space=pl.ANY)] * 3 + [vmem],
+        in_specs=[pl.BlockSpec(memory_space=pltpu.SMEM), HBM, HBM, vmem, HBM],
+        out_specs=[vmem] * 2 + [HBM] * 3 + [vmem],
         scratch_shapes=[
             pltpu.VMEM((TOKENS, width), BF),
             pltpu.VMEM((4, 256, columns), F32),
             pltpu.VMEM((3, 256, columns), BF),
+            pltpu.VMEM((width, columns), BF),
             pltpu.SemaphoreType.DMA((3,)),
+            pltpu.SemaphoreType.DMA((5,)),
         ],
         compiler_params=pltpu.CompilerParams(vmem_limit_bytes=40 << 20),
         cost_estimate=pl.CostEstimate(flops=2 * TOKENS * width * columns * 2, bytes_accessed=8 << 20, transcendentals=0),
@@ -131,12 +147,19 @@
     return jnp.concatenate([first, second], axis=0)
 
 
-def stats_kernel(at, got, own, one, two, three, cot, cot_other, rows, half, full, pair, scales, turned, wide):
+def stats_kernel(
+    at, got_far, own, one_far, two_far, three_far, cot, cot_other_far, rows, half_far, full_far, pair, scales,
+    turned, wide, got, one, two, three, cot_other, half, full, sems,
+):
     place, x = at[0], at[2]
     exact = lax.Precision.HIGHEST
     columns = own.shape[1]
+    sources = (one_far, two_far, three_far, got_far, cot_other_far)
+    for copy in fetch(sources, (one, two, three, got, cot_other), sems):
+        copy.wait()
     total = own[...] + one[...].astype(F32) + two[...].astype(F32) + three[...].astype(F32)
     half[...] = total.astype(BF)
+    away = fetch((half,), (half_far,), sems.at[pl.ds(5, 1)])
     pair[at[3]] = cot[...]
     pair[1 - at[3]] = cot_other[...]
     gram = got[0, :16].astype(F32)
@@ -163,7 +186,10 @@
     gram = (gram + dot(mine[:, :24], right[:24], ((1,), (0,)), exact)) * mine[:, 32:33] * right[24:25]
     rows[...] = gram.astype(BF)
     full[...] = total + dot(own_rows(turned, x)[:, 24:32], column, ((1,), (0,)), exact)
+    away += fetch((full,), (full_far,), sems.at[pl.ds(6, 1)])
     scales[...] = turned[...]
+    for copy in away:
+        copy.wait()
 
 
 def stats_work(at, got, own, moved, cot, cot_other):
@@ -178,9 +204,20 @@
             jax.ShapeDtypeStruct((2, 128, columns), BF),
             jax.ShapeDtypeStruct((TOKENS, 128), F32),
         ],
-        in_specs=[pl.BlockSpec(memory_space=pltpu.SMEM)] + [vmem] * 7,
-        out_specs=[vmem] * 5,
-        scratch_shapes=[pltpu.VMEM((TOKENS, 128), F32), pltpu.VMEM((32, TOKENS), F32)],
+        in_specs=[pl.BlockSpec(memory_space=pltpu.SMEM), HBM, vmem, HBM, HBM, HBM, vmem, HBM],
+        out_specs=[vmem, HBM, HBM, vmem, vmem],
+        scratch_shapes=[
+            pltpu.VMEM((TOKENS, 128), F32),
+            pltpu.VMEM((32, TOKENS), F32),
+            pltpu.VMEM(got.shape, BF),
+            pltpu.VMEM((256, columns), BF),
+            pltpu.VMEM((256, columns), BF),
+            pltpu.VMEM((256, columns), BF),
+            pltpu.VMEM((128, columns), BF),
+            pltpu.VMEM((256, columns), BF),
+            pltpu.VMEM((256, columns), F32),
+            pltpu.SemaphoreType.DMA((7,)),
+        ],
         compiler_params=pltpu.CompilerParams(vmem_limit_bytes=40 << 20),
         cost_estimate=pl.CostEstimate(flops=10 << 20, bytes_accessed=3 << 20, transcendentals=0),
         name="stats_work",
@@ -191,15 +228,18 @@
     return (cot.astype(F32) * gelu_slope(value) * (1.0 / math.sqrt(TOKENS))).astype(BF)
 
 
-def slope_kernel(at, full, moved, scales, pair, pre, slope, mark):
+def slope_kernel(at, full_far, moved_far, scales, pair, turned, pre, slope_far, mark, full, moved, slope, sems):
+    for copy in fetch((full_far, moved_far), (full, moved), sems):
+        copy.wait()
     inv = own_rows(scales, at[2])[:, 32:33]
     value = (full[...] + moved[...].astype(F32)) * inv
     pre[...] = value
     slope[...] = slope_of(pair[...].reshape(value.shape), value)
     mark[...] = inv[:8]
-
-
-def slope_work(at, full, moved, scales, pair):
+    fetch((slope,), (slope_far,), sems.at[pl.ds(2, 1)])[0].wait()
+
+
+def slope_work(at, full, moved, scales, pair, turned):
     vmem = pl.BlockSpec(memory_space=pltpu.VMEM)
     return pl.pallas_call(
         slope_kernel,
@@ -208,12 +248,41 @@
             jax.ShapeDtypeStruct(full.shape, BF),
             jax.ShapeDtypeStruct((8, 1), F32),
         ],
-        in_specs=[pl.BlockSpec(memory_space=pltpu.SMEM)] + [vmem] * 4,
-        out_specs=[vmem] * 3,
+        in_specs=[pl.BlockSpec(memory_space=pltpu.SMEM), HBM, HBM, vmem, vmem, HBM],
+        out_specs=[vmem, HBM, vmem],
+        scratch_shapes=[
+            pltpu.VMEM(full.shape, F32),
+            pltpu.VMEM(full.shape, BF),
+            pltpu.VMEM(full.shape, BF),
+            pltpu.SemaphoreType.DMA((3,)),
+        ],
         compiler_params=pltpu.CompilerParams(vmem_limit_bytes=40 << 20),
         cost_estimate=pl.CostEstimate(flops=4 << 20, bytes_accessed=1 << 20, transcendentals=1 << 18),
         name="slope_work",
-    )(at, full, moved, scales, pair)
+    )(at, full, moved, scales, pair, turned)
+
+
+def norm_kernel(joined, scales, gain, turned):
+    width = gain.shape[1]
+    for i in range(8):
+        rows = pl.ds(128 * i, 128)
+        value = joined[pl.ds(4 * i, 4)].reshape(128, width).astype(F32) - scales[rows, 33:34]
+        value = value * scales[rows, 32:33] * gain[...]
+        turned[:, rows] = value.T.astype(BF)
+
+
+def norm_work(joined, scales, gain):
+    width = gain.shape[1]
+    vmem = pl.BlockSpec(memory_space=pltpu.VMEM)
+    return pl.pallas_call(
+        norm_kernel,
+        out_shape=jax.ShapeDtypeStruct((width, TOKENS), BF),
+        in_specs=[vmem] * 3,
+        out_specs=vmem,
+        compiler_params=pltpu.CompilerParams(vmem_limit_bytes=40 << 20),
+        cost_estimate=pl.CostEstimate(flops=4 << 20, bytes_accessed=4 << 20, transcendentals=0),
+        name="norm_work",
+    )(joined, scales, gain)
 
 
 def in_order(x, blocks, ordered):
@@ -233,7 +302,7 @@
     part = part + dot(other[...].reshape(half, 256), ordered[:, 1 - core].reshape(half, columns), ((0,), (0,)))
     along[...] = part
     total = jnp.sum(jnp.sum(part * s0[...].astype(F32), axis=0, keepdims=True), axis=1, keepdims=True)
-    squared[...] = jnp.broadcast_to(total.reshape(1, 1, 1), squared.shape)
+    squared[...] = jnp.broadcast_to(total, squared.shape)
 
 
 def ascent_work(at, mine, other, slopes, mark):
@@ -241,7 +310,7 @@
     vmem = pl.BlockSpec(memory_space=pltpu.VMEM)
     return pl.pallas_call(
         ascent_kernel,
-        out_shape=[jax.ShapeDtypeStruct((256, columns), F32), jax.ShapeDtypeStruct((256, 1, 128), F32)],
+        out_shape=[jax.ShapeDtypeStruct((256, columns), F32), jax.ShapeDtypeStruct((8, 128), F32)],
         in_specs=[pl.BlockSpec(memory_space=pltpu.SMEM)] + [vmem] * 6 + [pl.BlockSpec(memory_space=pl.ANY)],
         out_specs=[vmem] * 2,
         scratch_shapes=[pltpu.VMEM((32, 2, 16, columns), BF)],
@@ -288,19 +357,19 @@
         moved = [swap(v, "x", b) for b, v in ((1, near), (2, opposite), (3, far))]
     with jax.named_scope("stats_work"):
         rows, half, full, pair, scales = stats_work(at, got, own, moved, cotangent, cot_other)
-        normed = joined.reshape(TOKENS, width).astype(F32) - scales[:, 33:34]
-        turned = (normed * scales[:, 32:33] * norm_gain[None, :]).astype(BF).T
+        turned = norm_work(joined, scales, norm_gain[None])
     with jax.named_scope("gram_gather"):
         gram = spread(rows, ("yl", "z"), 32)
     with jax.named_scope("slope"):
         moved = swap(half, "yh", 1)
-        pre, slope, mark = slope_work(at, full, moved, scales, pair)
+        pre, slope, mark = slope_work(at, full, moved, scales, pair, turned)
         gram, mark = lax.optimization_barrier((gram, mark))
         gram_other = swap(gram, "c", 1)
         slopes = gather_x(slope)
     with jax.named_scope("ascent"):
         along, squared = ascent_work(at, gram, gram_other, slopes, mark)
-        squared = jnp.sum(lax.all_to_all(squared, DP + ("x",), 0, 0, tiled=True)[:, 0, 0])
+        squared = sum(gather_x(squared))[:1]
+        squared = jnp.sum(spread(squared, DP, 64)[:, 0, 0])
         size = jnp.sqrt(jnp.maximum(squared, 0.0)) + 1e-12
         radius = 0.5 * math.sqrt(FF)
     with jax.named_scope("sharp"):

time: 181 us -> 182 us (level)
  blocking collectives: 34.7 us -> 60.3 us
  local copies, waits for them, and re-layouts: 15.5 us -> 4.2 us
  starting transfers between devices: 76.1 us -> 67.9 us
  waiting for transfers between devices: 35.4 us -> 29.7 us
  other arithmetic: 5.44 us -> 1 us
  Pallas kernels: 12.1 us -> 16.2 us
    all_to_all x1 -> x2, blocking collectives: 34.7 us -> 60.3 us  [spread(): return lax.all_to_all(copies, axes, 0, 0, tiled=True)]
    all_to_all x1 -> x0, starting transfers between devices: 17.7 us -> none  [per_device(): lax.all_to_all(squared, DP + ('x',), 0, 0, tiled=True)[:, 0, 0]]
    ppermute x13 -> x16, starting transfers between devices: 46.6 us -> 56 us  [swap(): return lax.ppermute(value, axis, [(i, i ^ bit) for i in range(size)])]
    all_to_all x1 -> x0, waiting for transfers between devices: 6.89 us -> none  [per_device(): lax.all_to_all(squared, DP + ('x',), 0, 0, tiled=True)[:, 0, 0]]
    unnamed x26 -> x10, local copies, waits for them, and re-layouts: 9.1 us -> 2.59 us
    convert_element_type x1 -> x0, local copies, waits for them, and re-layouts: 3.57 us -> none  [per_device(): normed = joined.reshape(TOKENS, width).astype(F32) - scales[:, 33:34]]
    transpose x1 -> x0, other arithmetic: 2.28 us -> none  [per_device(): turned = (normed * scales[:, 32:33] * norm_gain[None, :]).astype(BF).T]
    convert_element_type x1 -> x0, other arithmetic: 1.97 us -> none  [per_device(): normed = joined.reshape(TOKENS, width).astype(F32) - scales[:, 33:34]]
  transfers between devices with their start and end apart: 16 -> 18, of which waited for: 7 -> 8; matrix products, arithmetic and copies ran while one was open for 5% -> 0% of each run, Pallas kernels for 4% -> 5%
where the time goes in v11:
time: 182 us; the launch traced here: 180 us
  starting transfers between devices  67.9 us (37%)
  blocking collectives  60.3 us (33%)
  waiting for transfers between devices  29.7 us (16%)
  Pallas kernels  16.2 us (9%)
  local copies, waits for them, and re-layouts  4.2 us (2%)
    all_to_all x2, blocking collectives, spread(): return lax.all_to_all(copies, axes, 0, 0, tiled=True)  60.3 us
    ppermute x16, starting transfers between devices, swap(): return lax.ppermute(value, axis, [(i, i ^ bit) for i in range(size)])  56 us
    ppermute x16, waiting for transfers between devices, swap(): return lax.ppermute(value, axis, [(i, i ^ bit) for i in range(size)])  29.7 us
    pallas_call x1, Pallas kernels, local_work(): pl.pallas_call(local_kernel, out_shape=[jax.ShapeDtypeStruct((32, 2, 16,...  6.84 us
    all_to_all x1, starting transfers between devices, per_device(): got = lax.all_to_all(sent, MP, 0, 0, tiled=True)  6.18 us
    all_to_all x1, starting transfers between devices, spread(): return lax.all_to_all(copies, axes, 0, 0, tiled=True)  5.65 us
  transfers between devices with their start and end apart: 18, of which 8 were waited for; matrix products, arithmetic and copies ran while one was open for 0% of the time, Pallas kernels for 5%

profile of v11, /device:TPU:1, one launch (start us, length us, event | category | flops | bytes accessed | tf_op | source)
XLA Modules:
  0.0 180.3 jit_solution(10641597521425880186)
XLA Ops:
  0.0 0.0 copy-start.2
  0.0 0.0 copy-start.4
  0.0 0.0 copy-start.3
  0.0 0.9 broadcast_in_dim.10
  0.9 34.5 %all_to_all.20.mine = bf16[32,16,768]{2,1,0:T(8,128)(2,1)S(1)} all-to-all(bf16[32,16,768]{2,1,0:T(8,128)(2,1)S(1)} %broadcast_in_dim.10), channel_id=1, replica_groups=mesh['yl'=4,'z'=8,'c'=2,'yh'=2,'x'=4] {'yl','z'}, dimensions={0} | all-to-all | bytes 1572864 | tf_op jit(solution)/shard_map/token_gather/all_to_all | solution.py:33
  35.4 4.2 %collective-permute-start = (bf16[32,16,768]{2,1,0:T(8,128)(2,1)S(1)}, bf16[32,16,768]{2,1,0:T(8,128)(2,1)S(1)}, u32[]{:S(2)}, u32[]{:S(2)}) collective-permute-start(bf16[32,16,768]{2,1,0:T(8,128)(2,1)S(1)} %all_to_all.20.mine), channel_id=1, source_target_pairs={{0,8},{8,0},{1,9},{9,1},{2,10},{10,2},{3,11},{11,3},{4,12},{12,4},... | collective-permute-start | bytes 2359304 | tf_op jit(solution)/shard_map/token_gather/ppermute | solution.py:28
  39.6 0.0 copy-done.4
  39.7 0.1 pad_add_fusion.at
  39.8 0.0 copy-done.2
  39.8 4.8 %collective-permute-start.1 = (bf16[128,384]{1,0:T(8,128)(2,1)S(1)}, bf16[128,384]{1,0:T(8,128)(2,1)S(1)}, u32[]{:S(2)}, u32[]{:S(2)}) collective-permute-start(bf16[128,384]{1,0:T(8,128)(2,1)S(1)} %copy-done.2), channel_id=1, source_target_pairs={{0,4},{4,0},{1,5},{5,1},{2,6},{6,2},{3,7},{7,3},{8,12},{12,8},{9,1... | collective-permute-start | bytes 294920 | tf_op jit(solution)/shard_map/token_gather/ppermute | solution.py:28
  44.6 0.0 collective-permute-done.other
  44.6 0.0 copy-done.3
  44.6 6.8 %local_work.1 = (bf16[32,2,16,768]{3,2,1,0:T(8,128)(2,1)S(1)}, f32[256,384]{1,0:T(8,128)S(1)}, bf16[256,384]{1,0:T(8,128)(2,1)S(1)}, bf16[256,384]{1,0:T(8,128)(...) custom-call(s32[4]{0:T(128)S(1)} %pad_add_fusion.at, bf16[32,16,768]{2,1,0:T(8,128)(2,1)S(1)} %all_to_all.20.mine, ...), custom_call_target="tpu_custom_call" | custom-call | flops 1207959552 | bytes 8388608 | tf_op jit(solution)/shard_map/local_work/local_work/pallas_call | solution.py:118
  51.5 0.0 copy-start
  51.5 1.2 copy-done
  52.7 0.0 collective-permute-done.1.cot_other_far
  52.7 6.2 %all-to-all-start.1 = ((bf16[8,48,256]{2,1,0:T(8,128)(2,1)}), bf16[8,48,256]{2,1,0:T(8,128)(2,1)S(1)}, u32[]{:S(2)}, u32[]{:S(2)}) async-start(bf16[8,48,256]{2,1,0:T(8,128)(2,1)} %get-tuple-element.31), calls=%async_computation.1 | async-start | bytes 393216 | tf_op jit(solution)/shard_map/sums_x/all_to_all | solution.py:356
  58.8 3.4 %collective-permute-start.2 = (bf16[256,384]{1,0:T(8,128)(2,1)S(1)}, bf16[256,384]{1,0:T(8,128)(2,1)S(1)}, u32[]{:S(2)}, u32[]{:S(2)}) collective-permute-start(bf16[256,384]{1,0:T(8,128)(2,1)S(1)} %get-tuple-element.33), channel_id=1, source_target_pairs={{0,1},{1,0},{2,3},{3,2},{4,5},{5,4},{6,7},{7,6},{8,9},{9,8},{10,11... | collective-permute-start | bytes 589832 | tf_op jit(solution)/shard_map/sums_x/ppermute | solution.py:28
  62.2 4.3 %collective-permute-start.3 = (bf16[256,384]{1,0:T(8,128)(2,1)S(1)}, bf16[256,384]{1,0:T(8,128)(2,1)S(1)}, u32[]{:S(2)}, u32[]{:S(2)}) collective-permute-start(bf16[256,384]{1,0:T(8,128)(2,1)S(1)} %get-tuple-element.34), channel_id=1, source_target_pairs={{0,2},{1,3},{2,0},{3,1},{4,6},{5,7},{6,4},{7,5},{8,10},{9,11},{10,... | collective-permute-start | bytes 589832 | tf_op jit(solution)/shard_map/sums_x/ppermute | solution.py:28
  66.5 1.9 %collective-permute-start.4 = (bf16[256,384]{1,0:T(8,128)(2,1)S(1)}, bf16[256,384]{1,0:T(8,128)(2,1)S(1)}, u32[]{:S(2)}, u32[]{:S(2)}) collective-permute-start(bf16[256,384]{1,0:T(8,128)(2,1)S(1)} %get-tuple-element.35), channel_id=1, source_target_pairs={{0,3},{1,2},{2,1},{3,0},{4,7},{5,6},{6,5},{7,4},{8,11},{9,10},{10,... | collective-permute-start | bytes 589832 | tf_op jit(solution)/shard_map/sums_x/ppermute | solution.py:28
  68.4 0.0 collective-permute-done.2.one_far
  68.5 5.5 %collective-permute-done.3.two_far = bf16[256,384]{1,0:T(8,128)(2,1)S(1)} collective-permute-done((bf16[256,384]{1,0:T(8,128)(2,1)S(1)}, bf16[256,384]{1,0:T(8,128)(2,1)S(1)}, u32[]{:S(2)}, u32[]{:S(2)}) %collective-permute-start.3) | collective-permute-done | bytes 196640 | tf_op jit(solution)/shard_map/sums_x/ppermute | solution.py:28
  74.0 5.3 %collective-permute-done.4.three_far = bf16[256,384]{1,0:T(8,128)(2,1)S(1)} collective-permute-done((bf16[256,384]{1,0:T(8,128)(2,1)S(1)}, bf16[256,384]{1,0:T(8,128)(2,1)S(1)}, u32[]{:S(2)}, u32[]{:S(2)}) %collective-permute-start.4) | collective-permute-done | bytes 196640 | tf_op jit(solution)/shard_map/sums_x/ppermute | solution.py:28
  79.3 0.0 all-to-all-done.1.got_far
  79.3 3.1 %stats_work.1 = (bf16[16,256]{1,0:T(8,128)(2,1)S(1)}, bf16[256,384]{1,0:T(8,128)(2,1)S(1)}, f32[256,384]{1,0:T(8,128)S(1)}, bf16[2,128,384]{2,1,0:T(8,128)(2,1)S(1)}, f32[1024,128]{1,0:T(8,128)S(1)}) custom-call(s32[4]{0:T(128)S(1)} %pad_add_fusion.at, bf16[8,48,256]{2,1,0:T(8,128)(2,1)S(1)} %all-to-all-done.1.got_far, ...), custom_call_target="tpu_custom_call" | custom-call | flops 10485760 | bytes 3145728 | tf_op jit(solution)/shard_map/stats_work/stats_work/pallas_call | solution.py:198
  82.4 0.7 broadcast_in_dim.12
  83.2 5.6 %all-to-all-start.2 = ((bf16[32,16,256]{2,1,0:T(8,128)(2,1)}), bf16[32,16,256]{2,1,0:T(8,128)(2,1)S(1)}, u32[]{:S(2)}, u32[]{:S(2)}) async-start(bf16[32,16,256]{2,1,0:T(8,128)(2,1)} %broadcast_in_dim.12), calls=%async_computation.2 | async-start | bytes 524288 | tf_op jit(solution)/shard_map/gram_gather/all_to_all | solution.py:33
  88.8 6.5 %collective-permute-start.5 = (bf16[256,384]{1,0:T(8,128)(2,1)S(1)}, bf16[256,384]{1,0:T(8,128)(2,1)S(1)}, u32[]{:S(2)}, u32[]{:S(2)}) collective-permute-start(bf16[256,384]{1,0:T(8,128)(2,1)S(1)} %get-tuple-element.40), channel_id=1, source_target_pairs={{0,4},{4,0},{1,5},{5,1},{2,6},{6,2},{3,7},{7,3},{8,12},{12,8},{9,1... | collective-permute-start | bytes 589832 | tf_op jit(solution)/shard_map/slope/ppermute | solution.py:28
  95.3 0.0 copy-start.1
  95.3 1.4 copy-done.1
  96.7 0.9 norm_work.1.turned
  97.6 4.5 %collective-permute-done.5.moved_far = bf16[256,384]{1,0:T(8,128)(2,1)S(1)} collective-permute-done((bf16[256,384]{1,0:T(8,128)(2,1)S(1)}, bf16[256,384]{1,0:T(8,128)(2,1)S(1)}, u32[]{:S(2)}, u32[]{:S(2)}) %collective-permute-start.5) | collective-permute-done | bytes 196640 | tf_op jit(solution)/shard_map/slope/ppermute | solution.py:28
  102.1 1.6 slope_work.1
  103.7 0.0 all-to-all-done.2.mine
  103.7 3.7 %collective-permute-start.6 = (bf16[32,16,256]{2,1,0:T(8,128)(2,1)S(1)}, bf16[32,16,256]{2,1,0:T(8,128)(2,1)S(1)}, u32[]{:S(2)}, u32[]{:S(2)}) collective-permute-start(bf16[32,16,256]{2,1,0:T(8,128)(2,1)S(1)} %all-to-all-done.2.mine), channel_id=1, source_target_pairs={{0,8},{8,0},{1,9},{9,1},{2,10},{10,2},{3,11},{11,3},{4,12},{12,4},... | collective-permute-start | bytes 786440 | tf_op jit(solution)/shard_map/slope/ppermute | solution.py:28
  107.4 2.0 %collective-permute-start.9 = (bf16[256,384]{1,0:T(8,128)(2,1)S(1)}, bf16[256,384]{1,0:T(8,128)(2,1)S(1)}, u32[]{:S(2)}, u32[]{:S(2)}) collective-permute-start(bf16[256,384]{1,0:T(8,128)(2,1)S(1)} %get-tuple-element.45.s0), channel_id=1, source_target_pairs={{0,3},{1,2},{2,1},{3,0},{4,7},{5,6},{6,5},{7,4},{8,11},{9,10},{10,... | collective-permute-start | bytes 589832 | tf_op jit(solution)/shard_map/slope/ppermute | solution.py:28
  109.4 3.0 %collective-permute-start.8 = (bf16[256,384]{1,0:T(8,128)(2,1)S(1)}, bf16[256,384]{1,0:T(8,128)(2,1)S(1)}, u32[]{:S(2)}, u32[]{:S(2)}) collective-permute-start(bf16[256,384]{1,0:T(8,128)(2,1)S(1)} %get-tuple-element.45.s0), channel_id=1, source_target_pairs={{0,2},{1,3},{2,0},{3,1},{4,6},{5,7},{6,4},{7,5},{8,10},{9,11},{10,... | collective-permute-start | bytes 589832 | tf_op jit(solution)/shard_map/slope/ppermute | solution.py:28
  112.4 4.0 %collective-permute-start.7 = (bf16[256,384]{1,0:T(8,128)(2,1)S(1)}, bf16[256,384]{1,0:T(8,128)(2,1)S(1)}, u32[]{:S(2)}, u32[]{:S(2)}) collective-permute-start(bf16[256,384]{1,0:T(8,128)(2,1)S(1)} %get-tuple-element.45.s0), channel_id=1, source_target_pairs={{0,1},{1,0},{2,3},{3,2},{4,5},{5,4},{6,7},{7,6},{8,9},{9,8},{10,11... | collective-permute-start | bytes 589832 | tf_op jit(solution)/shard_map/slope/ppermute | solution.py:28
  116.4 4.8 %collective-permute-done.9.s3 = bf16[256,384]{1,0:T(8,128)(2,1)S(1)} collective-permute-done((bf16[256,384]{1,0:T(8,128)(2,1)S(1)}, bf16[256,384]{1,0:T(8,128)(2,1)S(1)}, u32[]{:S(2)}, u32[]{:S(2)}) %collective-permute-start.9) | collective-permute-done | bytes 196640 | tf_op jit(solution)/shard_map/slope/ppermute | solution.py:28
  121.3 0.0 collective-permute-done.8.s2
  121.3 2.2 %collective-permute-done.7.s1 = bf16[256,384]{1,0:T(8,128)(2,1)S(1)} collective-permute-done((bf16[256,384]{1,0:T(8,128)(2,1)S(1)}, bf16[256,384]{1,0:T(8,128)(2,1)S(1)}, u32[]{:S(2)}, u32[]{:S(2)}) %collective-permute-start.7) | collective-permute-done | bytes 196640 | tf_op jit(solution)/shard_map/slope/ppermute | solution.py:28
  123.4 0.0 collective-permute-done.6.other
  123.4 1.1 ascent_work.1
  124.6 2.0 %collective-permute-start.12 = (f32[8,128]{1,0:T(8,128)S(1)}, f32[8,128]{1,0:T(8,128)S(1)}, u32[]{:S(2)}, u32[]{:S(2)}) collective-permute-start(f32[8,128]{1,0:T(8,128)S(1)} %get-tuple-element.48), channel_id=1, source_target_pairs={{0,3},{1,2},{2,1},{3,0},{4,7},{5,6},{6,5},{7,4},{8,11},{9,10},{10,... | collective-permute-start | bytes 12296 | tf_op jit(solution)/shard_map/ascent/ppermute | solution.py:28
  126.6 2.8 %collective-permute-start.11 = (f32[8,128]{1,0:T(8,128)S(1)}, f32[8,128]{1,0:T(8,128)S(1)}, u32[]{:S(2)}, u32[]{:S(2)}) collective-permute-start(f32[8,128]{1,0:T(8,128)S(1)} %get-tuple-element.48), channel_id=1, source_target_pairs={{0,2},{1,3},{2,0},{3,1},{4,6},{5,7},{6,4},{7,5},{8,10},{9,11},{10,... | collective-permute-start | bytes 12296 | tf_op jit(solution)/shard_map/ascent/ppermute | solution.py:28
  129.5 4.1 %collective-permute-start.10 = (f32[8,128]{1,0:T(8,128)S(1)}, f32[8,128]{1,0:T(8,128)S(1)}, u32[]{:S(2)}, u32[]{:S(2)}) collective-permute-start(f32[8,128]{1,0:T(8,128)S(1)} %get-tuple-element.48), channel_id=1, source_target_pairs={{0,1},{1,0},{2,3},{3,2},{4,5},{5,4},{6,7},{7,6},{8,9},{9,8},{10,11... | collective-permute-start | bytes 12296 | tf_op jit(solution)/shard_map/ascent/ppermute | solution.py:28
  133.6 0.0 collective-permute-done.12
  133.6 0.0 collective-permute-done.11
  133.6 1.0 collective-permute-done.10
  134.7 25.7 %all_to_all.21 = f32[64,1,128]{2,1,0:T(1,128)S(1)} all-to-all(f32[64,1,128]{2,1,0:T(1,128)S(1)} %broadcast_in_dim.28), channel_id=1, replica_groups=mesh['yl'=4,'z'=8,'c'=2,'yh'=2,'x'=4] {'yl','z','c'}, dimensions={0} | all-to-all | bytes 65536 | tf_op jit(solution)/shard_map/ascent/all_to_all | solution.py:33
  160.4 0.7 slice_reduce_fusion
  161.8 0.2 fusion.6.s0
  162.0 3.1 %collective-permute-start.15 = (bf16[256,384]{1,0:T(8,128)(2,1)S(1)}, bf16[256,384]{1,0:T(8,128)(2,1)S(1)}, u32[]{:S(2)}, u32[]{:S(2)}) collective-permute-start(bf16[256,384]{1,0:T(8,128)(2,1)S(1)} %fusion.6.s0), channel_id=1, source_target_pairs={{0,3},{1,2},{2,1},{3,0},{4,7},{5,6},{6,5},{7,4},{8,11},{9,10},{10,... | collective-permute-start | bytes 589832 | tf_op jit(solution)/shard_map/sharp/ppermute | solution.py:28
  165.1 4.3 %collective-permute-start.14 = (bf16[256,384]{1,0:T(8,128)(2,1)S(1)}, bf16[256,384]{1,0:T(8,128)(2,1)S(1)}, u32[]{:S(2)}, u32[]{:S(2)}) collective-permute-start(bf16[256,384]{1,0:T(8,128)(2,1)S(1)} %fusion.6.s0), channel_id=1, source_target_pairs={{0,2},{1,3},{2,0},{3,1},{4,6},{5,7},{6,4},{7,5},{8,10},{9,11},{10,... | collective-permute-start | bytes 589832 | tf_op jit(solution)/shard_map/sharp/ppermute | solution.py:28
  169.4 1.9 %collective-permute-start.13 = (bf16[256,384]{1,0:T(8,128)(2,1)S(1)}, bf16[256,384]{1,0:T(8,128)(2,1)S(1)}, u32[]{:S(2)}, u32[]{:S(2)}) collective-permute-start(bf16[256,384]{1,0:T(8,128)(2,1)S(1)} %fusion.6.s0), channel_id=1, source_target_pairs={{0,1},{1,0},{2,3},{3,2},{4,5},{5,4},{6,7},{7,6},{8,9},{9,8},{10,11... | collective-permute-start | bytes 589832 | tf_op jit(solution)/shard_map/sharp/ppermute | solution.py:28
  171.3 0.0 collective-permute-done.15.s3
  171.3 2.7 %collective-permute-done.14.s2 = bf16[256,384]{1,0:T(8,128)(2,1)S(1)} collective-permute-done((bf16[256,384]{1,0:T(8,128)(2,1)S(1)}, bf16[256,384]{1,0:T(8,128)(2,1)S(1)}, u32[]{:S(2)}, u32[]{:S(2)}) %collective-permute-start.14) | collective-permute-done | bytes 196640 | tf_op jit(solution)/shard_map/sharp/ppermute | solution.py:28
  174.0 3.6 %collective-permute-done.13.s1 = bf16[256,384]{1,0:T(8,128)(2,1)S(1)} collective-permute-done((bf16[256,384]{1,0:T(8,128)(2,1)S(1)}, bf16[256,384]{1,0:T(8,128)(2,1)S(1)}, u32[]{:S(2)}, u32[]{:S(2)}) %collective-permute-start.13) | collective-permute-done | bytes 196640 | tf_op jit(solution)/shard_map/sharp/ppermute | solution.py:28
  177.6 2.6 %result_work.1 = f32[768,384]{1,0:T(8,128)} custom-call(s32[4]{0:T(128)S(1)} %pad_add_fusion.at, bf16[768,1024]{1,0:T(8,128)(2,1)S(1)} %norm_work.1.turned, bf16[256,384]{1,0:T(8,128)(2,1)S(1)} %fusion.6.s0, bf16[256,384]{1,0:T(8,128)(2,1)S(1)} %collective-permute-done.13.s1, bf16[256,384]{1,0:T(8,128)(2,1)S(1)} %collective-permute-done.14.s2, ...), custom_call_target="tpu_custom_call" | custom-call | flops 603979776 | bytes 4194304 | tf_op jit(solution)/shard_map/sharp/result_work/pallas_call | solution.py:331
  (4 shorter events, 0.0 us)
Async XLA Ops:
  0.0 39.8 %copy-start.2 = (bf16[128,384]{1,0:T(8,128)(2,1)S(1)}, bf16[128,384]{1,0:T(8,128)(2,1)}, u32[]{:S(2)}) copy-start(bf16[128,384]{1,0:T(8,128)(2,1)} %cot.1) | copy-start | bytes 294916
  0.0 39.6 %copy-start.4 = (f32[768]{0:T(1024)S(1)}, f32[768]{0:T(1024)}, u32[]{:S(2)}) copy-start(f32[768]{0:T(1024)} %param.5) | copy-start | bytes 9220
  0.0 44.6 %copy-start.3 = (bf16[768,384]{1,0:T(8,128)(2,1)S(1)}, bf16[768,384]{1,0:T(8,128)(2,1)}, u32[]{:S(2)}) copy-start(bf16[768,384]{1,0:T(8,128)(2,1)} %w_far.1) | copy-start | bytes 1769476
  35.4 9.2 %collective-permute-start = (bf16[32,16,768]{2,1,0:T(8,128)(2,1)S(1)}, bf16[32,16,768]{2,1,0:T(8,128)(2,1)S(1)}, u32[]{:S(2)}, u32[]{:S(2)}) collective-permute-start(bf16[32,16,768]{2,1,0:T(8,128)(2,1)S(1)} %all_to_all.20.mine), channel_id=1, source_target_pairs={{0,8},{8,0},{1,9},{9,1},{2,10},{10,2},{3,11},{11,3},{4,12},{12,4},... | collective-permute-start | bytes 2359304 | tf_op jit(solution)/shard_map/token_gather/ppermute | solution.py:28
  39.8 12.9 %collective-permute-start.1 = (bf16[128,384]{1,0:T(8,128)(2,1)S(1)}, bf16[128,384]{1,0:T(8,128)(2,1)S(1)}, u32[]{:S(2)}, u32[]{:S(2)}) collective-permute-start(bf16[128,384]{1,0:T(8,128)(2,1)S(1)} %copy-done.2), channel_id=1, source_target_pairs={{0,4},{4,0},{1,5},{5,1},{2,6},{6,2},{3,7},{7,3},{8,12},{12,8},{9,1... | collective-permute-start | bytes 294920 | tf_op jit(solution)/shard_map/token_gather/ppermute | solution.py:28
  51.5 1.2 copy-start
  52.7 26.7 %all-to-all-start.1 = ((bf16[8,48,256]{2,1,0:T(8,128)(2,1)}), bf16[8,48,256]{2,1,0:T(8,128)(2,1)S(1)}, u32[]{:S(2)}, u32[]{:S(2)}) async-start(bf16[8,48,256]{2,1,0:T(8,128)(2,1)} %get-tuple-element.31), calls=%async_computation.1 | async-start | bytes 393216 | tf_op jit(solution)/shard_map/sums_x/all_to_all | solution.py:356
  58.8 9.6 %collective-permute-start.2 = (bf16[256,384]{1,0:T(8,128)(2,1)S(1)}, bf16[256,384]{1,0:T(8,128)(2,1)S(1)}, u32[]{:S(2)}, u32[]{:S(2)}) collective-permute-start(bf16[256,384]{1,0:T(8,128)(2,1)S(1)} %get-tuple-element.33), channel_id=1, source_target_pairs={{0,1},{1,0},{2,3},{3,2},{4,5},{5,4},{6,7},{7,6},{8,9},{9,8},{10,11... | collective-permute-start | bytes 589832 | tf_op jit(solution)/shard_map/sums_x/ppermute | solution.py:28
  62.2 11.8 %collective-permute-start.3 = (bf16[256,384]{1,0:T(8,128)(2,1)S(1)}, bf16[256,384]{1,0:T(8,128)(2,1)S(1)}, u32[]{:S(2)}, u32[]{:S(2)}) collective-permute-start(bf16[256,384]{1,0:T(8,128)(2,1)S(1)} %get-tuple-element.34), channel_id=1, source_target_pairs={{0,2},{1,3},{2,0},{3,1},{4,6},{5,7},{6,4},{7,5},{8,10},{9,11},{10,... | collective-permute-start | bytes 589832 | tf_op jit(solution)/shard_map/sums_x/ppermute | solution.py:28
  66.5 12.8 %collective-permute-start.4 = (bf16[256,384]{1,0:T(8,128)(2,1)S(1)}, bf16[256,384]{1,0:T(8,128)(2,1)S(1)}, u32[]{:S(2)}, u32[]{:S(2)}) collective-permute-start(bf16[256,384]{1,0:T(8,128)(2,1)S(1)} %get-tuple-element.35), channel_id=1, source_target_pairs={{0,3},{1,2},{2,1},{3,0},{4,7},{5,6},{6,5},{7,4},{8,11},{9,10},{10,... | collective-permute-start | bytes 589832 | tf_op jit(solution)/shard_map/sums_x/ppermute | solution.py:28
  83.2 20.5 %all-to-all-start.2 = ((bf16[32,16,256]{2,1,0:T(8,128)(2,1)}), bf16[32,16,256]{2,1,0:T(8,128)(2,1)S(1)}, u32[]{:S(2)}, u32[]{:S(2)}) async-start(bf16[32,16,256]{2,1,0:T(8,128)(2,1)} %broadcast_in_dim.12), calls=%async_computation.2 | async-start | bytes 524288 | tf_op jit(solution)/shard_map/gram_gather/all_to_all | solution.py:33
  88.8 13.3 %collective-permute-start.5 = (bf16[256,384]{1,0:T(8,128)(2,1)S(1)}, bf16[256,384]{1,0:T(8,128)(2,1)S(1)}, u32[]{:S(2)}, u32[]{:S(2)}) collective-permute-start(bf16[256,384]{1,0:T(8,128)(2,1)S(1)} %get-tuple-element.40), channel_id=1, source_target_pairs={{0,4},{4,0},{1,5},{5,1},{2,6},{6,2},{3,7},{7,3},{8,12},{12,8},{9,1... | collective-permute-start | bytes 589832 | tf_op jit(solution)/shard_map/slope/ppermute | solution.py:28
  95.3 1.4 copy-start.1
  103.7 19.7 %collective-permute-start.6 = (bf16[32,16,256]{2,1,0:T(8,128)(2,1)S(1)}, bf16[32,16,256]{2,1,0:T(8,128)(2,1)S(1)}, u32[]{:S(2)}, u32[]{:S(2)}) collective-permute-start(bf16[32,16,256]{2,1,0:T(8,128)(2,1)S(1)} %all-to-all-done.2.mine), channel_id=1, source_target_pairs={{0,8},{8,0},{1,9},{9,1},{2,10},{10,2},{3,11},{11,3},{4,12},{12,4},... | collective-permute-start | bytes 786440 | tf_op jit(solution)/shard_map/slope/ppermute | solution.py:28
  107.4 13.8 %collective-permute-start.9 = (bf16[256,384]{1,0:T(8,128)(2,1)S(1)}, bf16[256,384]{1,0:T(8,128)(2,1)S(1)}, u32[]{:S(2)}, u32[]{:S(2)}) collective-permute-start(bf16[256,384]{1,0:T(8,128)(2,1)S(1)} %get-tuple-element.45.s0), channel_id=1, source_target_pairs={{0,3},{1,2},{2,1},{3,0},{4,7},{5,6},{6,5},{7,4},{8,11},{9,10},{10,... | collective-permute-start | bytes 589832 | tf_op jit(solution)/shard_map/slope/ppermute | solution.py:28
  109.4 11.8 %collective-permute-start.8 = (bf16[256,384]{1,0:T(8,128)(2,1)S(1)}, bf16[256,384]{1,0:T(8,128)(2,1)S(1)}, u32[]{:S(2)}, u32[]{:S(2)}) collective-permute-start(bf16[256,384]{1,0:T(8,128)(2,1)S(1)} %get-tuple-element.45.s0), channel_id=1, source_target_pairs={{0,2},{1,3},{2,0},{3,1},{4,6},{5,7},{6,4},{7,5},{8,10},{9,11},{10,... | collective-permute-start | bytes 589832 | tf_op jit(solution)/shard_map/slope/ppermute | solution.py:28
  112.4 11.0 %collective-permute-start.7 = (bf16[256,384]{1,0:T(8,128)(2,1)S(1)}, bf16[256,384]{1,0:T(8,128)(2,1)S(1)}, u32[]{:S(2)}, u32[]{:S(2)}) collective-permute-start(bf16[256,384]{1,0:T(8,128)(2,1)S(1)} %get-tuple-element.45.s0), channel_id=1, source_target_pairs={{0,1},{1,0},{2,3},{3,2},{4,5},{5,4},{6,7},{7,6},{8,9},{9,8},{10,11... | collective-permute-start | bytes 589832 | tf_op jit(solution)/shard_map/slope/ppermute | solution.py:28
  124.6 9.0 %collective-permute-start.12 = (f32[8,128]{1,0:T(8,128)S(1)}, f32[8,128]{1,0:T(8,128)S(1)}, u32[]{:S(2)}, u32[]{:S(2)}) collective-permute-start(f32[8,128]{1,0:T(8,128)S(1)} %get-tuple-element.48), channel_id=1, source_target_pairs={{0,3},{1,2},{2,1},{3,0},{4,7},{5,6},{6,5},{7,4},{8,11},{9,10},{10,... | collective-permute-start | bytes 12296 | tf_op jit(solution)/shard_map/ascent/ppermute | solution.py:28
  126.6 7.0 %collective-permute-start.11 = (f32[8,128]{1,0:T(8,128)S(1)}, f32[8,128]{1,0:T(8,128)S(1)}, u32[]{:S(2)}, u32[]{:S(2)}) collective-permute-start(f32[8,128]{1,0:T(8,128)S(1)} %get-tuple-element.48), channel_id=1, source_target_pairs={{0,2},{1,3},{2,0},{3,1},{4,6},{5,7},{6,4},{7,5},{8,10},{9,11},{10,... | collective-permute-start | bytes 12296 | tf_op jit(solution)/shard_map/ascent/ppermute | solution.py:28
  129.5 5.2 %collective-permute-start.10 = (f32[8,128]{1,0:T(8,128)S(1)}, f32[8,128]{1,0:T(8,128)S(1)}, u32[]{:S(2)}, u32[]{:S(2)}) collective-permute-start(f32[8,128]{1,0:T(8,128)S(1)} %get-tuple-element.48), channel_id=1, source_target_pairs={{0,1},{1,0},{2,3},{3,2},{4,5},{5,4},{6,7},{7,6},{8,9},{9,8},{10,11... | collective-permute-start | bytes 12296 | tf_op jit(solution)/shard_map/ascent/ppermute | solution.py:28
  162.0 9.3 %collective-permute-start.15 = (bf16[256,384]{1,0:T(8,128)(2,1)S(1)}, bf16[256,384]{1,0:T(8,128)(2,1)S(1)}, u32[]{:S(2)}, u32[]{:S(2)}) collective-permute-start(bf16[256,384]{1,0:T(8,128)(2,1)S(1)} %fusion.6.s0), channel_id=1, source_target_pairs={{0,3},{1,2},{2,1},{3,0},{4,7},{5,6},{6,5},{7,4},{8,11},{9,10},{10,... | collective-permute-start | bytes 589832 | tf_op jit(solution)/shard_map/sharp/ppermute | solution.py:28
  165.1 8.9 %collective-permute-start.14 = (bf16[256,384]{1,0:T(8,128)(2,1)S(1)}, bf16[256,384]{1,0:T(8,128)(2,1)S(1)}, u32[]{:S(2)}, u32[]{:S(2)}) collective-permute-start(bf16[256,384]{1,0:T(8,128)(2,1)S(1)} %fusion.6.s0), channel_id=1, source_target_pairs={{0,2},{1,3},{2,0},{3,1},{4,6},{5,7},{6,4},{7,5},{8,10},{9,11},{10,... | collective-permute-start | bytes 589832 | tf_op jit(solution)/shard_map/sharp/ppermute | solution.py:28
  169.4 8.3 %collective-permute-start.13 = (bf16[256,384]{1,0:T(8,128)(2,1)S(1)}, bf16[256,384]{1,0:T(8,128)(2,1)S(1)}, u32[]{:S(2)}, u32[]{:S(2)}) collective-permute-start(bf16[256,384]{1,0:T(8,128)(2,1)S(1)} %fusion.6.s0), channel_id=1, source_target_pairs={{0,1},{1,0},{2,3},{3,2},{4,5},{5,4},{6,7},{7,6},{8,9},{9,8},{10,11... | collective-permute-start | bytes 589832 | tf_op jit(solution)/shard_map/sharp/ppermute | solution.py:28

commit v12 on v11

--- a/solution.py
+++ b/solution.py
@@ -106,7 +106,7 @@
     for j in range(8):
         q = 128 * (j % 4)
         block = jnp.concatenate([gram[:, q : q + 128], gram[:, 512 + q : 640 + q]], axis=1)
-        sent[j] = jnp.concatenate([block] + stats, axis=0).astype(BF)
+        sent[j] = jnp.concatenate(split(block, 2) + stats, axis=0).astype(BF)
     for copy in copies:
         copy.wait()
 
@@ -123,7 +123,7 @@
             block,
             block,
             block,
-            jax.ShapeDtypeStruct((8, 48, 256), BF),
+            jax.ShapeDtypeStruct((8, 64, 256), BF),
         ],
         in_specs=[pl.BlockSpec(memory_space=pltpu.SMEM), HBM, HBM, vmem, HBM],
         out_specs=[vmem] * 2 + [HBM] * 3 + [vmem],
@@ -162,10 +162,10 @@
     away = fetch((half,), (half_far,), sems.at[pl.ds(5, 1)])
     pair[at[3]] = cot[...]
     pair[1 - at[3]] = cot_other[...]
-    gram = got[0, :16].astype(F32)
-    for j in range(1, 8):
-        gram = gram + got[j, :16].astype(F32)
-    terms = [got[j, 16:].astype(F32) for j in range(8)]
+    gram = jnp.zeros((16, 256), F32)
+    for j in range(8):
+        gram = gram + (got[j, :16].astype(F32) + got[j, 16:32].astype(F32))
+    terms = [got[j, 32:].astype(F32) for j in range(8)]
     terms = [jnp.concatenate([t[8 * q : 8 * q + 8] for q in range(4)], axis=1) for t in terms]
     local = jnp.concatenate([t[0:1] + t[1:2] + t[2:3] for t in terms], axis=0)
     css = jnp.concatenate([t[3:4] + t[4:5] for t in terms], axis=0)
@@ -184,7 +184,8 @@
     right = jnp.concatenate([first, second], axis=1)
     mine = turned[pl.ds(pl.multiple_of(place * 16, 16), 16)]
     gram = (gram + dot(mine[:, :24], right[:24], ((1,), (0,)), exact)) * mine[:, 32:33] * right[24:25]
-    rows[...] = gram.astype(BF)
+    for i, term in enumerate(split(gram, 2)):
+        rows[i] = term.astype(BF)
     full[...] = total + dot(own_rows(turned, x)[:, 24:32], column, ((1,), (0,)), exact)
     away += fetch((full,), (full_far,), sems.at[pl.ds(6, 1)])
     scales[...] = turned[...]
@@ -198,7 +199,7 @@
     return pl.pallas_call(
         stats_kernel,
         out_shape=[
-            jax.ShapeDtypeStruct((16, 256), BF),
+            jax.ShapeDtypeStruct((2, 16, 256), BF),
             jax.ShapeDtypeStruct((256, columns), BF),
             jax.ShapeDtypeStruct((256, columns), F32),
             jax.ShapeDtypeStruct((2, 128, columns), BF),
@@ -228,28 +229,22 @@
     return (cot.astype(F32) * gelu_slope(value) * (1.0 / math.sqrt(TOKENS))).astype(BF)
 
 
-def slope_kernel(at, full_far, moved_far, scales, pair, turned, pre, slope_far, mark, full, moved, slope, sems):
+def pre_kernel(at, full_far, moved_far, scales, turned, one, two, three, out_far, mark, full, moved, out, sems):
     for copy in fetch((full_far, moved_far), (full, moved), sems):
         copy.wait()
     inv = own_rows(scales, at[2])[:, 32:33]
-    value = (full[...] + moved[...].astype(F32)) * inv
-    pre[...] = value
-    slope[...] = slope_of(pair[...].reshape(value.shape), value)
+    out[...] = ((full[...] + moved[...].astype(F32)) * inv).astype(BF)
     mark[...] = inv[:8]
-    fetch((slope,), (slope_far,), sems.at[pl.ds(2, 1)])[0].wait()
-
-
-def slope_work(at, full, moved, scales, pair, turned):
-    vmem = pl.BlockSpec(memory_space=pltpu.VMEM)
-    return pl.pallas_call(
-        slope_kernel,
-        out_shape=[
-            jax.ShapeDtypeStruct(full.shape, F32),
-            jax.ShapeDtypeStruct(full.shape, BF),
-            jax.ShapeDtypeStruct((8, 1), F32),
-        ],
-        in_specs=[pl.BlockSpec(memory_space=pltpu.SMEM), HBM, HBM, vmem, vmem, HBM],
-        out_specs=[vmem, HBM, vmem],
+    fetch((out,), (out_far,), sems.at[pl.ds(2, 1)])[0].wait()
+
+
+def pre_work(at, full, moved, scales, turned, cots):
+    vmem = pl.BlockSpec(memory_space=pltpu.VMEM)
+    return pl.pallas_call(
+        pre_kernel,
+        out_shape=[jax.ShapeDtypeStruct(full.shape, BF), jax.ShapeDtypeStruct((8, 1), F32)],
+        in_specs=[pl.BlockSpec(memory_space=pltpu.SMEM), HBM, HBM, vmem] + [HBM] * 4,
+        out_specs=[HBM, vmem],
         scratch_shapes=[
             pltpu.VMEM(full.shape, F32),
             pltpu.VMEM(full.shape, BF),
@@ -257,9 +252,9 @@
             pltpu.SemaphoreType.DMA((3,)),
         ],
         compiler_params=pltpu.CompilerParams(vmem_limit_bytes=40 << 20),
-        cost_estimate=pl.CostEstimate(flops=4 << 20, bytes_accessed=1 << 20, transcendentals=1 << 18),
-        name="slope_work",
-    )(at, full, moved, scales, pair, turned)
+        cost_estimate=pl.CostEstimate(flops=1 << 20, bytes_accessed=1 << 20, transcendentals=0),
+        name="pre_work",
+    )(at, full, moved, scales, turned, *cots)
 
 
 def norm_kernel(joined, scales, gain, turned):
@@ -285,59 +280,113 @@
     )(joined, scales, gain)
 
 
-def in_order(x, blocks, ordered):
-    for b, block in enumerate(blocks):
-        q = x ^ b
-        shape = (4, 2, 16, block.shape[1])
-        ordered[pl.ds(4 * q, 4)] = block[:128].reshape(shape)
-        ordered[pl.ds(16 + 4 * q, 4)] = block[128:].reshape(shape)
-
-
-def ascent_kernel(at, mine, other, s0, s1, s2, s3, mark, along, squared, ordered):
-    core = at[1]
-    columns = s0.shape[1]
-    in_order(at[2], (s0, s1, s2, s3), ordered)
+def put(q, block, ordered):
+    shape = (4, 2, 16, block.shape[1])
+    ordered[pl.ds(4 * q, 4)] = block[:128].reshape(shape)
+    ordered[pl.ds(16 + 4 * q, 4)] = block[128:].reshape(shape)
+
+
+def ascent_kernel(at, gram, gram_other, p0, p1, p2, p3, c0, c1, c2, c3, mark, slopes, along_far, ordered, pres, cots, along, sems):
+    core, x = at[1], at[2]
+    sources = (p0, c0, p1, c1, p2, c2, p3, c3)
+    targets = [v.at[b] for b in range(4) for v in (pres, cots)]
+    copies = fetch(sources, targets, sems)
+    columns = along.shape[1]
+    for b in range(4):
+        copies[2 * b].wait()
+        copies[2 * b + 1].wait()
+        slope = slope_of(cots[b].reshape(256, columns), pres[b].astype(F32))
+        slopes[b] = slope
+        put(x ^ b, slope, ordered)
     half = TOKENS // 2
-    part = dot(mine[...].reshape(half, 256), ordered[:, core].reshape(half, columns), ((0,), (0,)))
-    part = part + dot(other[...].reshape(half, 256), ordered[:, 1 - core].reshape(half, columns), ((0,), (0,)))
-    along[...] = part
-    total = jnp.sum(jnp.sum(part * s0[...].astype(F32), axis=0, keepdims=True), axis=1, keepdims=True)
-    squared[...] = jnp.broadcast_to(total, squared.shape)
-
-
-def ascent_work(at, mine, other, slopes, mark):
-    columns = slopes[0].shape[1]
+    part = jnp.zeros((256, columns), F32)
+    for source, c in ((gram, core), (gram_other, 1 - core)):
+        right = ordered[:, c].reshape(half, columns)
+        for i in range(2):
+            part = part + dot(source[:, i].reshape(half, 256), right, ((0,), (0,)))
+    along[...] = part.astype(BF)
+    fetch((along,), (along_far,), sems.at[pl.ds(8, 1)])[0].wait()
+
+
+def ascent_work(at, gram, gram_other, pres, cots, mark):
+    columns = pres[0].shape[1]
     vmem = pl.BlockSpec(memory_space=pltpu.VMEM)
     return pl.pallas_call(
         ascent_kernel,
-        out_shape=[jax.ShapeDtypeStruct((256, columns), F32), jax.ShapeDtypeStruct((8, 128), F32)],
-        in_specs=[pl.BlockSpec(memory_space=pltpu.SMEM)] + [vmem] * 6 + [pl.BlockSpec(memory_space=pl.ANY)],
-        out_specs=[vmem] * 2,
-        scratch_shapes=[pltpu.VMEM((32, 2, 16, columns), BF)],
-        compiler_params=pltpu.CompilerParams(vmem_limit_bytes=40 << 20),
-        cost_estimate=pl.CostEstimate(flops=2 * TOKENS * 256 * columns, bytes_accessed=2 << 20, transcendentals=0),
+        out_shape=[jax.ShapeDtypeStruct((4, 256, columns), BF), jax.ShapeDtypeStruct((256, columns), BF)],
+        in_specs=[pl.BlockSpec(memory_space=pltpu.SMEM), vmem, vmem] + [HBM] * 9,
+        out_specs=[vmem, HBM],
+        scratch_shapes=[
+            pltpu.VMEM((32, 2, 16, columns), BF),
+            pltpu.VMEM((4, 256, columns), BF),
+            pltpu.VMEM((4, 2, 128, columns), BF),
+            pltpu.VMEM((256, columns), BF),
+            pltpu.SemaphoreType.DMA((9,)),
+        ],
+        compiler_params=pltpu.CompilerParams(vmem_limit_bytes=40 << 20),
+        cost_estimate=pl.CostEstimate(flops=2 * TOKENS * 256 * columns, bytes_accessed=3 << 20, transcendentals=2 * TOKENS * columns),
         name="ascent_work",
-    )(at, mine, other, *slopes, mark)
-
-
-def result_kernel(at, turned, s0, s1, s2, s3, out, ordered):
-    in_order(at[2], (s0, s1, s2, s3), ordered)
-    out[...] = dot(turned[...], ordered[...].reshape(TOKENS, out.shape[1]), ((1,), (0,)))
-
-
-def result_work(at, turned, slopes):
-    columns = slopes[0].shape[1]
+    )(at, gram, gram_other, *pres, *cots, mark)
+
+
+def sum_kernel(slopes, a0, a1, a2, a3, squared, alongs, sems):
+    total = jnp.zeros((1, alongs.shape[2]), F32)
+    for b, copy in enumerate(fetch((a0, a1, a2, a3), [alongs.at[b] for b in range(4)], sems)):
+        copy.wait()
+        total = total + jnp.sum(alongs[b].astype(F32) * slopes[b].astype(F32), axis=0, keepdims=True)
+    total = jnp.sum(total, axis=1, keepdims=True)
+    squared[...] = jnp.broadcast_to(total.reshape(1, 1, 1), squared.shape)
+
+
+def sum_work(slopes, alongs):
+    vmem = pl.BlockSpec(memory_space=pltpu.VMEM)
+    return pl.pallas_call(
+        sum_kernel,
+        out_shape=jax.ShapeDtypeStruct((64, 1, 128), F32),
+        in_specs=[vmem] + [HBM] * 4,
+        out_specs=vmem,
+        scratch_shapes=[pltpu.VMEM(slopes.shape, BF), pltpu.SemaphoreType.DMA((4,))],
+        compiler_params=pltpu.CompilerParams(vmem_limit_bytes=40 << 20),
+        cost_estimate=pl.CostEstimate(flops=1 << 20, bytes_accessed=2 << 20, transcendentals=0),
+        name="sum_work",
+    )(slopes, *alongs)
+
+
+def result_kernel(at, got, turned, p0, p1, p2, p3, c0, c1, c2, c3, a0, a1, a2, a3, out, ordered, pres, cots, alongs, sems):
+    x = at[2]
+    sources = (p0, c0, a0, p1, c1, a1, p2, c2, a2, p3, c3, a3)
+    targets = [v.at[b] for b in range(4) for v in (pres, cots, alongs)]
+    copies = fetch(sources, targets, sems)
+    columns = out.shape[1]
+    squared = jnp.sum(got[...].reshape(64, 128), axis=0, keepdims=True)[:, :1]
+    step = 0.5 * math.sqrt(FF) / (jnp.sqrt(jnp.maximum(squared, 0.0)) + 1e-12)
+    for b in range(4):
+        for copy in copies[3 * b : 3 * b + 3]:
+            copy.wait()
+        value = pres[b].astype(F32) + alongs[b].astype(F32) * step
+        put(x ^ b, slope_of(cots[b].reshape(256, columns), value), ordered)
+    out[...] = dot(turned[...], ordered[...].reshape(TOKENS, columns), ((1,), (0,)))
+
+
+def result_work(at, got, turned, pres, cots, alongs):
+    columns = pres[0].shape[1]
     vmem = pl.BlockSpec(memory_space=pltpu.VMEM)
     return pl.pallas_call(
         result_kernel,
         out_shape=jax.ShapeDtypeStruct((turned.shape[0], columns), F32),
-        in_specs=[pl.BlockSpec(memory_space=pltpu.SMEM)] + [vmem] * 5,
+        in_specs=[pl.BlockSpec(memory_space=pltpu.SMEM), vmem, vmem] + [HBM] * 12,
         out_specs=vmem,
-        scratch_shapes=[pltpu.VMEM((32, 2, 16, columns), BF)],
-        compiler_params=pltpu.CompilerParams(vmem_limit_bytes=40 << 20),
-        cost_estimate=pl.CostEstimate(flops=2 * TOKENS * 768 * columns, bytes_accessed=4 << 20, transcendentals=0),
+        scratch_shapes=[
+            pltpu.VMEM((32, 2, 16, columns), BF),
+            pltpu.VMEM((4, 256, columns), BF),
+            pltpu.VMEM((4, 2, 128, columns), BF),
+            pltpu.VMEM((4, 256, columns), BF),
+            pltpu.SemaphoreType.DMA((12,)),
+        ],
+        compiler_params=pltpu.CompilerParams(vmem_limit_bytes=40 << 20),
+        cost_estimate=pl.CostEstimate(flops=2 * TOKENS * 768 * columns, bytes_accessed=4 << 20, transcendentals=2 * TOKENS * columns),
         name="result_work",
-    )(at, turned, *slopes)
+    )(at, got, turned, *pres, *cots, *alongs)
 
 
 def per_device(tokens, norm_gain, w_up, cotangent):
@@ -360,21 +409,20 @@
         turned = norm_work(joined, scales, norm_gain[None])
     with jax.named_scope("gram_gather"):
         gram = spread(rows, ("yl", "z"), 32)
-    with jax.named_scope("slope"):
+    with jax.named_scope("pre"):
         moved = swap(half, "yh", 1)
-        pre, slope, mark = slope_work(at, full, moved, scales, pair, turned)
+        cots = gather_x(pair)
+        pre, mark = pre_work(at, full, moved, scales, turned, cots[1:])
         gram, mark = lax.optimization_barrier((gram, mark))
         gram_other = swap(gram, "c", 1)
-        slopes = gather_x(slope)
+        pres = gather_x(pre)
     with jax.named_scope("ascent"):
-        along, squared = ascent_work(at, gram, gram_other, slopes, mark)
-        squared = sum(gather_x(squared))[:1]
-        squared = jnp.sum(spread(squared, DP, 64)[:, 0, 0])
-        size = jnp.sqrt(jnp.maximum(squared, 0.0)) + 1e-12
-        radius = 0.5 * math.sqrt(FF)
+        slopes, along = ascent_work(at, gram, gram_other, pres, cots, mark)
+        alongs = gather_x(along)
+        squared = sum_work(slopes, alongs)
+        squared = lax.all_to_all(squared, DP, 0, 0, tiled=True)
     with jax.named_scope("sharp"):
-        sharp = slope_of(pair.reshape(pre.shape), pre + along * (radius / size))
-        return result_work(at, turned, gather_x(sharp))
+        return result_work(at, squared, turned, pres, cots, alongs)
 
 
 def solution(mesh):

time: 182 us -> 185 us (1.016)
  Pallas kernels: 16.2 us -> 24.9 us
  blocking collectives: 60.3 us -> 56.3 us
  local copies, waits for them, and re-layouts: 4.2 us -> 6.65 us
  waiting for transfers between devices: 29.7 us -> 27.3 us
    all_to_all x2 -> x1, blocking collectives: 60.3 us -> 34.5 us  [spread(): return lax.all_to_all(copies, axes, 0, 0, tiled=True)]
    all_to_all x0 -> x1, blocking collectives: none -> 21.7 us  [per_device(): squared = lax.all_to_all(squared, DP, 0, 0, tiled=True)]
    pallas_call x3 -> x4, Pallas kernels: 5.81 us -> 10.3 us  [the longest x1 4.59 us: ascent_work(): pl.pallas_call(ascent_kernel, out_shape=[jax.ShapeDtypeStruct((4, 256, co...]
    pallas_call x1, Pallas kernels: 2.6 us -> 6.91 us  [result_work(): pl.pallas_call(result_kernel, out_shape=jax.ShapeDtypeStruct((turned.shap...]
    ppermute x16, waiting for transfers between devices: 29.7 us -> 27.3 us  [swap(): return lax.ppermute(value, axis, [(i, i ^ bit) for i in range(size)])]
    unnamed x10 -> x20, local copies, waits for them, and re-layouts: 2.59 us -> 4.93 us
where the time goes in v12:
time: 185 us; the launch traced here: 184 us
  starting transfers between devices  68.4 us (37%)
  blocking collectives  56.3 us (30%)
  waiting for transfers between devices  27.3 us (15%)
  Pallas kernels  24.9 us (13%)
  local copies, waits for them, and re-layouts  6.65 us (4%)
    ppermute x16, starting transfers between devices, swap(): return lax.ppermute(value, axis, [(i, i ^ bit) for i in range(size)])  56.6 us
    all_to_all x1, blocking collectives, spread(): return lax.all_to_all(copies, axes, 0, 0, tiled=True)  34.5 us
    ppermute x16, waiting for transfers between devices, swap(): return lax.ppermute(value, axis, [(i, i ^ bit) for i in range(size)])  27.3 us
    all_to_all x1, blocking collectives, per_device(): squared = lax.all_to_all(squared, DP, 0, 0, tiled=True)  21.7 us
    pallas_call x1, Pallas kernels, result_work(): pl.pallas_call(result_kernel, out_shape=jax.ShapeDtypeStruct((turned.shap...  6.91 us
    pallas_call x1, Pallas kernels, local_work(): pl.pallas_call(local_kernel, out_shape=[jax.ShapeDtypeStruct((32, 2, 16,...  6.84 us
    all_to_all x1, starting transfers between devices, per_device(): got = lax.all_to_all(sent, MP, 0, 0, tiled=True)  6.18 us
    all_to_all x1, starting transfers between devices, spread(): return lax.all_to_all(copies, axes, 0, 0, tiled=True)  5.67 us
  transfers between devices with their start and end apart: 18, of which 8 were waited for; matrix products, arithmetic and copies ran while one was open for 0% of the time, Pallas kernels for 5%

profile of v12, /device:TPU:1, one launch (start us, length us, event | category | flops | bytes accessed | tf_op | source)
XLA Modules:
  0.0 184.0 jit_solution(11868075558191866670)
XLA Ops:
  0.0 0.0 copy-start.7
  0.0 0.0 copy-start.9
  0.0 0.9 broadcast_in_dim.6
  0.9 34.5 %all_to_all.20.mine = bf16[32,16,768]{2,1,0:T(8,128)(2,1)S(1)} all-to-all(bf16[32,16,768]{2,1,0:T(8,128)(2,1)S(1)} %broadcast_in_dim.6), channel_id=1, replica_groups=mesh['yl'=4,'z'=8,'c'=2,'yh'=2,'x'=4] {'yl','z'}, dimensions={0} | all-to-all | bytes 1572864 | tf_op jit(solution)/shard_map/token_gather/all_to_all | solution.py:33
  35.4 4.2 %collective-permute-start = (bf16[32,16,768]{2,1,0:T(8,128)(2,1)S(1)}, bf16[32,16,768]{2,1,0:T(8,128)(2,1)S(1)}, u32[]{:S(2)}, u32[]{:S(2)}) collective-permute-start(bf16[32,16,768]{2,1,0:T(8,128)(2,1)S(1)} %all_to_all.20.mine), channel_id=1, source_target_pairs={{0,8},{8,0},{1,9},{9,1},{2,10},{10,2},{3,11},{11,3},{4,12},{12,4},... | collective-permute-start | bytes 2359304 | tf_op jit(solution)/shard_map/token_gather/ppermute | solution.py:28
  39.6 0.0 copy-done.9
  39.7 0.1 pad_add_fusion.at
  39.8 0.0 copy-done.7
  39.8 4.8 %collective-permute-start.1 = (bf16[128,384]{1,0:T(8,128)(2,1)S(1)}, bf16[128,384]{1,0:T(8,128)(2,1)S(1)}, u32[]{:S(2)}, u32[]{:S(2)}) collective-permute-start(bf16[128,384]{1,0:T(8,128)(2,1)S(1)} %copy-done.7), channel_id=1, source_target_pairs={{0,4},{4,0},{1,5},{5,1},{2,6},{6,2},{3,7},{7,3},{8,12},{12,8},{9,1... | collective-permute-start | bytes 294920 | tf_op jit(solution)/shard_map/token_gather/ppermute | solution.py:28
  44.6 0.0 collective-permute-done.other
  44.6 0.0 copy-done.8
  44.6 6.8 %local_work.1 = (bf16[32,2,16,768]{3,2,1,0:T(8,128)(2,1)S(1)}, f32[256,384]{1,0:T(8,128)S(1)}, bf16[256,384]{1,0:T(8,128)(2,1)S(1)}, bf16[256,384]{1,0:T(8,128)(...) custom-call(s32[4]{0:T(128)S(1)} %pad_add_fusion.at, bf16[32,16,768]{2,1,0:T(8,128)(2,1)S(1)} %all_to_all.20.mine, ...), custom_call_target="tpu_custom_call" | custom-call | flops 1207959552 | bytes 8388608 | tf_op jit(solution)/shard_map/local_work/local_work/pallas_call | solution.py:118
  51.5 0.0 copy-start
  51.5 1.2 copy-done
  52.7 0.0 collective-permute-done.1.cot_other_far
  52.7 6.2 %all-to-all-start.1 = ((bf16[8,64,256]{2,1,0:T(8,128)(2,1)}), bf16[8,64,256]{2,1,0:T(8,128)(2,1)S(1)}, u32[]{:S(2)}, u32[]{:S(2)}) async-start(bf16[8,64,256]{2,1,0:T(8,128)(2,1)} %get-tuple-element.29), calls=%async_computation.1 | async-start | bytes 524288 | tf_op jit(solution)/shard_map/sums_x/all_to_all | solution.py:405
  58.8 3.4 %collective-permute-start.2 = (bf16[256,384]{1,0:T(8,128)(2,1)S(1)}, bf16[256,384]{1,0:T(8,128)(2,1)S(1)}, u32[]{:S(2)}, u32[]{:S(2)}) collective-permute-start(bf16[256,384]{1,0:T(8,128)(2,1)S(1)} %get-tuple-element.31), channel_id=1, source_target_pairs={{0,1},{1,0},{2,3},{3,2},{4,5},{5,4},{6,7},{7,6},{8,9},{9,8},{10,11... | collective-permute-start | bytes 589832 | tf_op jit(solution)/shard_map/sums_x/ppermute | solution.py:28
  62.2 4.3 %collective-permute-start.3 = (bf16[256,384]{1,0:T(8,128)(2,1)S(1)}, bf16[256,384]{1,0:T(8,128)(2,1)S(1)}, u32[]{:S(2)}, u32[]{:S(2)}) collective-permute-start(bf16[256,384]{1,0:T(8,128)(2,1)S(1)} %get-tuple-element.32), channel_id=1, source_target_pairs={{0,2},{1,3},{2,0},{3,1},{4,6},{5,7},{6,4},{7,5},{8,10},{9,11},{10,... | collective-permute-start | bytes 589832 | tf_op jit(solution)/shard_map/sums_x/ppermute | solution.py:28
  66.5 1.9 %collective-permute-start.4 = (bf16[256,384]{1,0:T(8,128)(2,1)S(1)}, bf16[256,384]{1,0:T(8,128)(2,1)S(1)}, u32[]{:S(2)}, u32[]{:S(2)}) collective-permute-start(bf16[256,384]{1,0:T(8,128)(2,1)S(1)} %get-tuple-element.33), channel_id=1, source_target_pairs={{0,3},{1,2},{2,1},{3,0},{4,7},{5,6},{6,5},{7,4},{8,11},{9,10},{10,... | collective-permute-start | bytes 589832 | tf_op jit(solution)/shard_map/sums_x/ppermute | solution.py:28
  68.4 0.0 collective-permute-done.2.one_far
  68.5 5.9 %collective-permute-done.3.two_far = bf16[256,384]{1,0:T(8,128)(2,1)S(1)} collective-permute-done((bf16[256,384]{1,0:T(8,128)(2,1)S(1)}, bf16[256,384]{1,0:T(8,128)(2,1)S(1)}, u32[]{:S(2)}, u32[]{:S(2)}) %collective-permute-start.3) | collective-permute-done | bytes 196640 | tf_op jit(solution)/shard_map/sums_x/ppermute | solution.py:28
  74.3 5.0 %collective-permute-done.4.three_far = bf16[256,384]{1,0:T(8,128)(2,1)S(1)} collective-permute-done((bf16[256,384]{1,0:T(8,128)(2,1)S(1)}, bf16[256,384]{1,0:T(8,128)(2,1)S(1)}, u32[]{:S(2)}, u32[]{:S(2)}) %collective-permute-start.4) | collective-permute-done | bytes 196640 | tf_op jit(solution)/shard_map/sums_x/ppermute | solution.py:28
  79.3 0.0 all-to-all-done.1.got_far
  79.3 3.0 %stats_work.1 = (bf16[2,16,256]{2,1,0:T(8,128)(2,1)S(1)}, bf16[256,384]{1,0:T(8,128)(2,1)}, f32[256,384]{1,0:T(8,128)S(1)}, bf16[2,128,384]{2,1,0:T(8,128)(2,1)S(1)}, f32[1024,128]{1,0:T(8,128)S(1)}) custom-call(s32[4]{0:T(128)S(1)} %pad_add_fusion.at, bf16[8,64,256]{2,1,0:T(8,128)(2,1)S(1)} %all-to-all-done.1.got_far, ...), custom_call_target="tpu_custom_call" | custom-call | flops 10485760 | bytes 3145728 | tf_op jit(solution)/shard_map/stats_work/stats_work/pallas_call | solution.py:199
  82.3 0.0 copy-start.5
  82.3 0.7 copy-done.5
  83.1 0.9 broadcast_in_dim.8
  83.9 5.7 %all-to-all-start.2 = ((bf16[32,2,16,256]{3,2,1,0:T(8,128)(2,1)}), bf16[32,2,16,256]{3,2,1,0:T(8,128)(2,1)S(1)}, u32[]{:S(2)}, u32[]{:S(2)}) async-start(bf16[32,2,16,256]{3,2,1,0:T(8,128)(2,1)} %broadcast_in_dim.8), calls=%async_computation.2 | async-start | bytes 1048576 | tf_op jit(solution)/shard_map/gram_gather/all_to_all | solution.py:33
  89.6 6.7 %collective-permute-start.5 = (bf16[256,384]{1,0:T(8,128)(2,1)}, bf16[256,384]{1,0:T(8,128)(2,1)S(1)}, u32[]{:S(2)}, u32[]{:S(2)}) collective-permute-start(bf16[256,384]{1,0:T(8,128)(2,1)} %get-tuple-element.37), channel_id=1, source_target_pairs={{0,4},{4,0},{1,5},{5,1},{2,6},{6,2},{3,7},{7,3},{8,12},{12,8},{9,1... | collective-permute-start | bytes 589832 | tf_op jit(solution)/shard_map/pre/ppermute | solution.py:28
  96.3 2.4 %collective-permute-start.8 = (bf16[2,128,384]{2,1,0:T(8,128)(2,1)S(1)}, bf16[2,128,384]{2,1,0:T(8,128)(2,1)S(1)}, u32[]{:S(2)}, u32[]{:S(2)}) collective-permute-start(bf16[2,128,384]{2,1,0:T(8,128)(2,1)S(1)} %get-tuple-element.40.c0), channel_id=1, source_target_pairs={{0,3},{1,2},{2,1},{3,0},{4,7},{5,6},{6,5},{7,4},{8,11},{9,10},{10,... | collective-permute-start | bytes 589832 | tf_op jit(solution)/shard_map/pre/ppermute | solution.py:28
  98.7 2.8 %collective-permute-start.7 = (bf16[2,128,384]{2,1,0:T(8,128)(2,1)S(1)}, bf16[2,128,384]{2,1,0:T(8,128)(2,1)S(1)}, u32[]{:S(2)}, u32[]{:S(2)}) collective-permute-start(bf16[2,128,384]{2,1,0:T(8,128)(2,1)S(1)} %get-tuple-element.40.c0), channel_id=1, source_target_pairs={{0,2},{1,3},{2,0},{3,1},{4,6},{5,7},{6,4},{7,5},{8,10},{9,11},{10,... | collective-permute-start | bytes 589832 | tf_op jit(solution)/shard_map/pre/ppermute | solution.py:28
  101.5 3.8 %collective-permute-start.6 = (bf16[2,128,384]{2,1,0:T(8,128)(2,1)S(1)}, bf16[2,128,384]{2,1,0:T(8,128)(2,1)S(1)}, u32[]{:S(2)}, u32[]{:S(2)}) collective-permute-start(bf16[2,128,384]{2,1,0:T(8,128)(2,1)S(1)} %get-tuple-element.40.c0), channel_id=1, source_target_pairs={{0,1},{1,0},{2,3},{3,2},{4,5},{5,4},{6,7},{7,6},{8,9},{9,8},{10,11... | collective-permute-start | bytes 589832 | tf_op jit(solution)/shard_map/pre/ppermute | solution.py:28
  105.3 0.0 copy-start.1
  105.4 1.4 copy-done.1
  106.8 0.9 norm_work.1.turned
  107.7 2.9 %collective-permute-done.5.moved_far = bf16[256,384]{1,0:T(8,128)(2,1)S(1)} collective-permute-done((bf16[256,384]{1,0:T(8,128)(2,1)}, bf16[256,384]{1,0:T(8,128)(2,1)S(1)}, u32[]{:S(2)}, u32[]{:S(2)}) %collective-permute-start.5) | collective-permute-done | bytes 196640 | tf_op jit(solution)/shard_map/pre/ppermute | solution.py:28
  110.5 0.0 collective-permute-done.8.three.c3
  110.5 0.0 collective-permute-done.7.two.c2
  110.6 0.6 collective-permute-done.6.one.c1
  111.1 0.0 copy-done.6
  111.1 1.4 pre_work.1
  112.5 0.0 copy-start.2
  112.5 0.7 copy-done.2
  113.2 0.0 all-to-all-done.2.gram
  113.2 4.2 %collective-permute-start.9 = (bf16[32,2,16,256]{3,2,1,0:T(8,128)(2,1)S(1)}, bf16[32,2,16,256]{3,2,1,0:T(8,128)(2,1)S(1)}, u32[]{:S(2)}, u32[]{:S(2)}) collective-permute-start(bf16[32,2,16,256]{3,2,1,0:T(8,128)(2,1)S(1)} %all-to-all-done.2.gram), channel_id=1, source_target_pairs={{0,8},{8,0},{1,9},{9,1},{2,10},{10,2},{3,11},{11,3},{4,12},{12,4},... | collective-permute-start | bytes 1572872 | tf_op jit(solution)/shard_map/pre/ppermute | solution.py:28
  117.4 2.4 %collective-permute-start.12 = (bf16[256,384]{1,0:T(8,128)(2,1)}, bf16[256,384]{1,0:T(8,128)(2,1)S(1)}, u32[]{:S(2)}, u32[]{:S(2)}) collective-permute-start(bf16[256,384]{1,0:T(8,128)(2,1)} %copy-done.2), channel_id=1, source_target_pairs={{0,3},{1,2},{2,1},{3,0},{4,7},{5,6},{6,5},{7,4},{8,11},{9,10},{10,... | collective-permute-start | bytes 589832 | tf_op jit(solution)/shard_map/pre/ppermute | solution.py:28
  119.8 2.8 %collective-permute-start.11 = (bf16[256,384]{1,0:T(8,128)(2,1)}, bf16[256,384]{1,0:T(8,128)(2,1)S(1)}, u32[]{:S(2)}, u32[]{:S(2)}) collective-permute-start(bf16[256,384]{1,0:T(8,128)(2,1)} %copy-done.2), channel_id=1, source_target_pairs={{0,2},{1,3},{2,0},{3,1},{4,6},{5,7},{6,4},{7,5},{8,10},{9,11},{10,... | collective-permute-start | bytes 589832 | tf_op jit(solution)/shard_map/pre/ppermute | solution.py:28
  122.6 3.8 %collective-permute-start.10 = (bf16[256,384]{1,0:T(8,128)(2,1)}, bf16[256,384]{1,0:T(8,128)(2,1)S(1)}, u32[]{:S(2)}, u32[]{:S(2)}) collective-permute-start(bf16[256,384]{1,0:T(8,128)(2,1)} %copy-done.2), channel_id=1, source_target_pairs={{0,1},{1,0},{2,3},{3,2},{4,5},{5,4},{6,7},{7,6},{8,9},{9,8},{10,11... | collective-permute-start | bytes 589832 | tf_op jit(solution)/shard_map/pre/ppermute | solution.py:28
  126.4 5.0 %collective-permute-done.12.p3 = bf16[256,384]{1,0:T(8,128)(2,1)S(1)} collective-permute-done((bf16[256,384]{1,0:T(8,128)(2,1)}, bf16[256,384]{1,0:T(8,128)(2,1)S(1)}, u32[]{:S(2)}, u32[]{:S(2)}) %collective-permute-start.12) | collective-permute-done | bytes 196640 | tf_op jit(solution)/shard_map/pre/ppermute | solution.py:28
  131.5 0.0 collective-permute-done.11.p2
  131.5 2.2 %collective-permute-done.10.p1 = bf16[256,384]{1,0:T(8,128)(2,1)S(1)} collective-permute-done((bf16[256,384]{1,0:T(8,128)(2,1)}, bf16[256,384]{1,0:T(8,128)(2,1)S(1)}, u32[]{:S(2)}, u32[]{:S(2)}) %collective-permute-start.10) | collective-permute-done | bytes 196640 | tf_op jit(solution)/shard_map/pre/ppermute | solution.py:28
  133.7 0.0 collective-permute-done.9.gram_other
  133.7 0.9 copy-done.3
  134.6 4.6 %ascent_work.1 = (bf16[4,256,384]{2,1,0:T(8,128)(2,1)S(1)}, bf16[256,384]{1,0:T(8,128)(2,1)S(1)}) custom-call(s32[4]{0:T(128)S(1)} %pad_add_fusion.at, bf16[32,2,16,256]{3,2,1,0:T(8,128)(2,1)S(1)} %all-to-all-done.2.gram, bf16[32,2,16,256]{3,2,1,0:T(8,128)(2,1)S(1)} %collective-permute-done.9.gram_other, bf16[256,384]{1,0:T(8,128)(2,1)S(1)} %copy-done.3, ...), custom_call_target="tpu_custom_call" | custom-call | flops 201326592 | bytes 3145728 | tf_op jit(solution)/shard_map/ascent/ascent_work/pallas_call | solution.py:314
  139.2 2.4 %collective-permute-start.15 = (bf16[256,384]{1,0:T(8,128)(2,1)S(1)}, bf16[256,384]{1,0:T(8,128)(2,1)S(1)}, u32[]{:S(2)}, u32[]{:S(2)}) collective-permute-start(bf16[256,384]{1,0:T(8,128)(2,1)S(1)} %get-tuple-element.46.a0), channel_id=1, source_target_pairs={{0,3},{1,2},{2,1},{3,0},{4,7},{5,6},{6,5},{7,4},{8,11},{9,10},{10,... | collective-permute-start | bytes 589832 | tf_op jit(solution)/shard_map/ascent/ppermute | solution.py:28
  141.6 2.8 %collective-permute-start.14 = (bf16[256,384]{1,0:T(8,128)(2,1)S(1)}, bf16[256,384]{1,0:T(8,128)(2,1)S(1)}, u32[]{:S(2)}, u32[]{:S(2)}) collective-permute-start(bf16[256,384]{1,0:T(8,128)(2,1)S(1)} %get-tuple-element.46.a0), channel_id=1, source_target_pairs={{0,2},{1,3},{2,0},{3,1},{4,6},{5,7},{6,4},{7,5},{8,10},{9,11},{10,... | collective-permute-start | bytes 589832 | tf_op jit(solution)/shard_map/ascent/ppermute | solution.py:28
  144.5 3.7 %collective-permute-start.13 = (bf16[256,384]{1,0:T(8,128)(2,1)S(1)}, bf16[256,384]{1,0:T(8,128)(2,1)S(1)}, u32[]{:S(2)}, u32[]{:S(2)}) collective-permute-start(bf16[256,384]{1,0:T(8,128)(2,1)S(1)} %get-tuple-element.46.a0), channel_id=1, source_target_pairs={{0,1},{1,0},{2,3},{3,2},{4,5},{5,4},{6,7},{7,6},{8,9},{9,8},{10,11... | collective-permute-start | bytes 589832 | tf_op jit(solution)/shard_map/ascent/ppermute | solution.py:28
  148.2 0.0 collective-permute-done.15.a3
  148.2 1.9 %collective-permute-done.14.a2 = bf16[256,384]{1,0:T(8,128)(2,1)S(1)} collective-permute-done((bf16[256,384]{1,0:T(8,128)(2,1)S(1)}, bf16[256,384]{1,0:T(8,128)(2,1)S(1)}, u32[]{:S(2)}, u32[]{:S(2)}) %collective-permute-start.14) | collective-permute-done | bytes 196640 | tf_op jit(solution)/shard_map/ascent/ppermute | solution.py:28
  150.1 3.9 %collective-permute-done.13.a1 = bf16[256,384]{1,0:T(8,128)(2,1)S(1)} collective-permute-done((bf16[256,384]{1,0:T(8,128)(2,1)S(1)}, bf16[256,384]{1,0:T(8,128)(2,1)S(1)}, u32[]{:S(2)}, u32[]{:S(2)}) %collective-permute-start.13) | collective-permute-done | bytes 196640 | tf_op jit(solution)/shard_map/ascent/ppermute | solution.py:28
  154.0 1.3 sum_work.1
  155.3 21.7 %all_to_all.21.got = f32[64,1,128]{2,1,0:T(1,128)S(1)} all-to-all(f32[64,1,128]{2,1,0:T(1,128)S(1)} %sum_work.1), channel_id=1, replica_groups=mesh['yl'=4,'z'=8,'c'=2,'yh'=2,'x'=4] {'yl','z','c'}, dimensions={0} | all-to-all | bytes 65536 | tf_op jit(solution)/shard_map/ascent/all_to_all | solution.py:423
  177.0 0.0 copy-done.4
  177.0 6.9 %result_work.1 = f32[768,384]{1,0:T(8,128)} custom-call(s32[4]{0:T(128)S(1)} %pad_add_fusion.at, f32[64,1,128]{2,1,0:T(1,128)S(1)} %all_to_all.21.got, bf16[768,1024]{1,0:T(8,128)(2,1)S(1)} %norm_work.1.turned, bf16[256,384]{1,0:T(8,128)(2,1)S(1)} %copy-done.4, bf16[256,384]{1,0:T(8,128)(2,1)S(1)} %collective-permute-done.10.p1, ...), custom_call_target="tpu_custom_call" | custom-call | flops 603979776 | bytes 4194304 | tf_op jit(solution)/shard_map/sharp/result_work/pallas_call | solution.py:374
  (5 shorter events, 0.0 us)
Async XLA Ops:
  0.0 39.8 %copy-start.7 = (bf16[128,384]{1,0:T(8,128)(2,1)S(1)}, bf16[128,384]{1,0:T(8,128)(2,1)}, u32[]{:S(2)}) copy-start(bf16[128,384]{1,0:T(8,128)(2,1)} %cot.1) | copy-start | bytes 294916
  0.0 39.6 %copy-start.9 = (f32[768]{0:T(1024)S(1)}, f32[768]{0:T(1024)}, u32[]{:S(2)}) copy-start(f32[768]{0:T(1024)} %param.5) | copy-start | bytes 9220
  0.0 44.6 %copy-start.8 = (bf16[768,384]{1,0:T(8,128)(2,1)S(1)}, bf16[768,384]{1,0:T(8,128)(2,1)}, u32[]{:S(2)}) copy-start(bf16[768,384]{1,0:T(8,128)(2,1)} %w_far.1) | copy-start | bytes 1769476
  35.4 9.2 %collective-permute-start = (bf16[32,16,768]{2,1,0:T(8,128)(2,1)S(1)}, bf16[32,16,768]{2,1,0:T(8,128)(2,1)S(1)}, u32[]{:S(2)}, u32[]{:S(2)}) collective-permute-start(bf16[32,16,768]{2,1,0:T(8,128)(2,1)S(1)} %all_to_all.20.mine), channel_id=1, source_target_pairs={{0,8},{8,0},{1,9},{9,1},{2,10},{10,2},{3,11},{11,3},{4,12},{12,4},... | collective-permute-start | bytes 2359304 | tf_op jit(solution)/shard_map/token_gather/ppermute | solution.py:28
  39.8 12.9 %collective-permute-start.1 = (bf16[128,384]{1,0:T(8,128)(2,1)S(1)}, bf16[128,384]{1,0:T(8,128)(2,1)S(1)}, u32[]{:S(2)}, u32[]{:S(2)}) collective-permute-start(bf16[128,384]{1,0:T(8,128)(2,1)S(1)} %copy-done.7), channel_id=1, source_target_pairs={{0,4},{4,0},{1,5},{5,1},{2,6},{6,2},{3,7},{7,3},{8,12},{12,8},{9,1... | collective-permute-start | bytes 294920 | tf_op jit(solution)/shard_map/token_gather/ppermute | solution.py:28
  51.5 1.2 copy-start
  52.7 26.6 %all-to-all-start.1 = ((bf16[8,64,256]{2,1,0:T(8,128)(2,1)}), bf16[8,64,256]{2,1,0:T(8,128)(2,1)S(1)}, u32[]{:S(2)}, u32[]{:S(2)}) async-start(bf16[8,64,256]{2,1,0:T(8,128)(2,1)} %get-tuple-element.29), calls=%async_computation.1 | async-start | bytes 524288 | tf_op jit(solution)/shard_map/sums_x/all_to_all | solution.py:405
  58.8 9.6 %collective-permute-start.2 = (bf16[256,384]{1,0:T(8,128)(2,1)S(1)}, bf16[256,384]{1,0:T(8,128)(2,1)S(1)}, u32[]{:S(2)}, u32[]{:S(2)}) collective-permute-start(bf16[256,384]{1,0:T(8,128)(2,1)S(1)} %get-tuple-element.31), channel_id=1, source_target_pairs={{0,1},{1,0},{2,3},{3,2},{4,5},{5,4},{6,7},{7,6},{8,9},{9,8},{10,11... | collective-permute-start | bytes 589832 | tf_op jit(solution)/shard_map/sums_x/ppermute | solution.py:28
  62.2 12.1 %collective-permute-start.3 = (bf16[256,384]{1,0:T(8,128)(2,1)S(1)}, bf16[256,384]{1,0:T(8,128)(2,1)S(1)}, u32[]{:S(2)}, u32[]{:S(2)}) collective-permute-start(bf16[256,384]{1,0:T(8,128)(2,1)S(1)} %get-tuple-element.32), channel_id=1, source_target_pairs={{0,2},{1,3},{2,0},{3,1},{4,6},{5,7},{6,4},{7,5},{8,10},{9,11},{10,... | collective-permute-start | bytes 589832 | tf_op jit(solution)/shard_map/sums_x/ppermute | solution.py:28
  66.5 12.8 %collective-permute-start.4 = (bf16[256,384]{1,0:T(8,128)(2,1)S(1)}, bf16[256,384]{1,0:T(8,128)(2,1)S(1)}, u32[]{:S(2)}, u32[]{:S(2)}) collective-permute-start(bf16[256,384]{1,0:T(8,128)(2,1)S(1)} %get-tuple-element.33), channel_id=1, source_target_pairs={{0,3},{1,2},{2,1},{3,0},{4,7},{5,6},{6,5},{7,4},{8,11},{9,10},{10,... | collective-permute-start | bytes 589832 | tf_op jit(solution)/shard_map/sums_x/ppermute | solution.py:28
  82.3 0.8 copy-start.5
  83.9 29.3 %all-to-all-start.2 = ((bf16[32,2,16,256]{3,2,1,0:T(8,128)(2,1)}), bf16[32,2,16,256]{3,2,1,0:T(8,128)(2,1)S(1)}, u32[]{:S(2)}, u32[]{:S(2)}) async-start(bf16[32,2,16,256]{3,2,1,0:T(8,128)(2,1)} %broadcast_in_dim.8), calls=%async_computation.2 | async-start | bytes 1048576 | tf_op jit(solution)/shard_map/gram_gather/all_to_all | solution.py:33
  89.6 21.0 %collective-permute-start.5 = (bf16[256,384]{1,0:T(8,128)(2,1)}, bf16[256,384]{1,0:T(8,128)(2,1)S(1)}, u32[]{:S(2)}, u32[]{:S(2)}) collective-permute-start(bf16[256,384]{1,0:T(8,128)(2,1)} %get-tuple-element.37), channel_id=1, source_target_pairs={{0,4},{4,0},{1,5},{5,1},{2,6},{6,2},{3,7},{7,3},{8,12},{12,8},{9,1... | collective-permute-start | bytes 589832 | tf_op jit(solution)/shard_map/pre/ppermute | solution.py:28
  96.3 14.2 %collective-permute-start.8 = (bf16[2,128,384]{2,1,0:T(8,128)(2,1)S(1)}, bf16[2,128,384]{2,1,0:T(8,128)(2,1)S(1)}, u32[]{:S(2)}, u32[]{:S(2)}) collective-permute-start(bf16[2,128,384]{2,1,0:T(8,128)(2,1)S(1)} %get-tuple-element.40.c0), channel_id=1, source_target_pairs={{0,3},{1,2},{2,1},{3,0},{4,7},{5,6},{6,5},{7,4},{8,11},{9,10},{10,... | collective-permute-start | bytes 589832 | tf_op jit(solution)/shard_map/pre/ppermute | solution.py:28
  98.7 11.9 %collective-permute-start.7 = (bf16[2,128,384]{2,1,0:T(8,128)(2,1)S(1)}, bf16[2,128,384]{2,1,0:T(8,128)(2,1)S(1)}, u32[]{:S(2)}, u32[]{:S(2)}) collective-permute-start(bf16[2,128,384]{2,1,0:T(8,128)(2,1)S(1)} %get-tuple-element.40.c0), channel_id=1, source_target_pairs={{0,2},{1,3},{2,0},{3,1},{4,6},{5,7},{6,4},{7,5},{8,10},{9,11},{10,... | collective-permute-start | bytes 589832 | tf_op jit(solution)/shard_map/pre/ppermute | solution.py:28
  101.5 9.6 %collective-permute-start.6 = (bf16[2,128,384]{2,1,0:T(8,128)(2,1)S(1)}, bf16[2,128,384]{2,1,0:T(8,128)(2,1)S(1)}, u32[]{:S(2)}, u32[]{:S(2)}) collective-permute-start(bf16[2,128,384]{2,1,0:T(8,128)(2,1)S(1)} %get-tuple-element.40.c0), channel_id=1, source_target_pairs={{0,1},{1,0},{2,3},{3,2},{4,5},{5,4},{6,7},{7,6},{8,9},{9,8},{10,11... | collective-permute-start | bytes 589832 | tf_op jit(solution)/shard_map/pre/ppermute | solution.py:28
  105.3 1.4 copy-start.1
  106.8 4.4 %copy-start.6 = (f32[256,384]{1,0:T(8,128)S(1)}, f32[256,384]{1,0:T(8,128)}, u32[]{:S(2)}) copy-start(f32[256,384]{1,0:T(8,128)} %copy-done.5) | copy-start | bytes 1179652
  112.5 0.7 copy-start.2
  113.2 20.5 %collective-permute-start.9 = (bf16[32,2,16,256]{3,2,1,0:T(8,128)(2,1)S(1)}, bf16[32,2,16,256]{3,2,1,0:T(8,128)(2,1)S(1)}, u32[]{:S(2)}, u32[]{:S(2)}) collective-permute-start(bf16[32,2,16,256]{3,2,1,0:T(8,128)(2,1)S(1)} %all-to-all-done.2.gram), channel_id=1, source_target_pairs={{0,8},{8,0},{1,9},{9,1},{2,10},{10,2},{3,11},{11,3},{4,12},{12,4},... | collective-permute-start | bytes 1572872 | tf_op jit(solution)/shard_map/pre/ppermute | solution.py:28
  117.4 14.0 %collective-permute-start.12 = (bf16[256,384]{1,0:T(8,128)(2,1)}, bf16[256,384]{1,0:T(8,128)(2,1)S(1)}, u32[]{:S(2)}, u32[]{:S(2)}) collective-permute-start(bf16[256,384]{1,0:T(8,128)(2,1)} %copy-done.2), channel_id=1, source_target_pairs={{0,3},{1,2},{2,1},{3,0},{4,7},{5,6},{6,5},{7,4},{8,11},{9,10},{10,... | collective-permute-start | bytes 589832 | tf_op jit(solution)/shard_map/pre/ppermute | solution.py:28
  119.8 11.6 %collective-permute-start.11 = (bf16[256,384]{1,0:T(8,128)(2,1)}, bf16[256,384]{1,0:T(8,128)(2,1)S(1)}, u32[]{:S(2)}, u32[]{:S(2)}) collective-permute-start(bf16[256,384]{1,0:T(8,128)(2,1)} %copy-done.2), channel_id=1, source_target_pairs={{0,2},{1,3},{2,0},{3,1},{4,6},{5,7},{6,4},{7,5},{8,10},{9,11},{10,... | collective-permute-start | bytes 589832 | tf_op jit(solution)/shard_map/pre/ppermute | solution.py:28
  122.6 11.1 %collective-permute-start.10 = (bf16[256,384]{1,0:T(8,128)(2,1)}, bf16[256,384]{1,0:T(8,128)(2,1)S(1)}, u32[]{:S(2)}, u32[]{:S(2)}) collective-permute-start(bf16[256,384]{1,0:T(8,128)(2,1)} %copy-done.2), channel_id=1, source_target_pairs={{0,1},{1,0},{2,3},{3,2},{4,5},{5,4},{6,7},{7,6},{8,9},{9,8},{10,11... | collective-permute-start | bytes 589832 | tf_op jit(solution)/shard_map/pre/ppermute | solution.py:28
  133.7 0.9 copy-start.3
  134.6 42.5 %copy-start.4 = (bf16[256,384]{1,0:T(8,128)(2,1)S(1)}, bf16[256,384]{1,0:T(8,128)(2,1)}, u32[]{:S(2)}) copy-start(bf16[256,384]{1,0:T(8,128)(2,1)} %copy-done.2) | copy-start | bytes 589828
  139.2 9.0 %collective-permute-start.15 = (bf16[256,384]{1,0:T(8,128)(2,1)S(1)}, bf16[256,384]{1,0:T(8,128)(2,1)S(1)}, u32[]{:S(2)}, u32[]{:S(2)}) collective-permute-start(bf16[256,384]{1,0:T(8,128)(2,1)S(1)} %get-tuple-element.46.a0), channel_id=1, source_target_pairs={{0,3},{1,2},{2,1},{3,0},{4,7},{5,6},{6,5},{7,4},{8,11},{9,10},{10,... | collective-permute-start | bytes 589832 | tf_op jit(solution)/shard_map/ascent/ppermute | solution.py:28
  141.6 8.5 %collective-permute-start.14 = (bf16[256,384]{1,0:T(8,128)(2,1)S(1)}, bf16[256,384]{1,0:T(8,128)(2,1)S(1)}, u32[]{:S(2)}, u32[]{:S(2)}) collective-permute-start(bf16[256,384]{1,0:T(8,128)(2,1)S(1)} %get-tuple-element.46.a0), channel_id=1, source_target_pairs={{0,2},{1,3},{2,0},{3,1},{4,6},{5,7},{6,4},{7,5},{8,10},{9,11},{10,... | collective-permute-start | bytes 589832 | tf_op jit(solution)/shard_map/ascent/ppermute | solution.py:28
  144.5 9.5 %collective-permute-start.13 = (bf16[256,384]{1,0:T(8,128)(2,1)S(1)}, bf16[256,384]{1,0:T(8,128)(2,1)S(1)}, u32[]{:S(2)}, u32[]{:S(2)}) collective-permute-start(bf16[256,384]{1,0:T(8,128)(2,1)S(1)} %get-tuple-element.46.a0), channel_id=1, source_target_pairs={{0,1},{1,0},{2,3},{3,2},{4,5},{5,4},{6,7},{7,6},{8,9},{9,8},{10,11... | collective-permute-start | bytes 589832 | tf_op jit(solution)/shard_map/ascent/ppermute | solution.py:28

commit v13 on v9

--- a/solution.py
+++ b/solution.py
@@ -87,7 +87,7 @@
     column = jnp.sum(dot(gains, w[...], ((1,), (0,))), axis=0, keepdims=True)
     power = jnp.broadcast_to(jnp.sum(g * g, axis=1, keepdims=True), (1, 128))
     extra = jnp.concatenate(split(column, 2) + split(power, 2), axis=1)
-    rows = [gram] + split(local, 3) + split(css, 2) + split(lean, 2) + [extra]
+    rows = split(gram, 2) + split(local, 3) + split(css, 2) + split(lean, 2) + [extra]
     sent[...] = jnp.concatenate(rows, axis=0).astype(BF)
     for copy in copies:
         copy.wait()
@@ -105,7 +105,7 @@
             block,
             block,
             block,
-            jax.ShapeDtypeStruct((24, TOKENS), BF),
+            jax.ShapeDtypeStruct((40, TOKENS), BF),
         ],
         in_specs=[pl.BlockSpec(memory_space=pltpu.SMEM)] + [vmem] * 4,
         out_specs=[vmem] * 2 + [pl.BlockSpec(memory_space=pl.ANY)] * 3 + [vmem],
@@ -129,10 +129,10 @@
     half[...] = total.astype(BF)
     pair[at[3]] = cot[...]
     pair[1 - at[3]] = cot_other[...]
-    gram = got[0, :16].astype(F32)
-    for j in range(1, 8):
-        gram = gram + got[j, :16].astype(F32)
-    terms = [got[j, 16:24].astype(F32) for j in range(8)]
+    gram = jnp.zeros((16, TOKENS), F32)
+    for j in range(8):
+        gram = gram + (got[j, :16].astype(F32) + got[j, 16:32].astype(F32))
+    terms = [got[j, 32:40].astype(F32) for j in range(8)]
     local = jnp.concatenate([t[0:1] + t[1:2] + t[2:3] for t in terms], axis=0)
     css = jnp.concatenate([t[3:4] + t[4:5] for t in terms], axis=0)
     lean = jnp.concatenate([t[5:6] + t[6:7] for t in terms], axis=0)

time: 176 us -> 179 us (1.017)
    ppermute x13, waiting for transfers between devices: 27.7 us -> 30 us  [swap(): return lax.ppermute(value, axis, [(i, i ^ bit) for i in range(size)])]
    unnamed x32 -> x36, local copies, waits for them, and re-layouts: 9.48 us -> 10.2 us
where the time goes in v13:
time: 179 us; the launch traced here: 178 us
  starting transfers between devices  70 us (39%)
  waiting for transfers between devices  44.4 us (25%)
  blocking collectives  34.5 us (19%)
  local copies, waits for them, and re-layouts  13.7 us (8%)
  Pallas kernels  10.1 us (6%)
  matrix products  2.24 us (1%)
    ppermute x13, starting transfers between devices, swap(): return lax.ppermute(value, axis, [(i, i ^ bit) for i in range(size)])  48.5 us
    all_to_all x1, blocking collectives, spread(): return lax.all_to_all(copies, axes, 0, 0, tiled=True)  34.5 us
    ppermute x13, waiting for transfers between devices, swap(): return lax.ppermute(value, axis, [(i, i ^ bit) for i in range(size)])  30 us
    all_to_all x2, starting transfers between devices, spread(): return lax.all_to_all(copies, axes, 0, 0, tiled=True)  13.6 us
    unnamed x36, local copies, waits for them, and re-layouts  10.2 us
    all_to_all x1, waiting for transfers between devices, per_device(): squared = jnp.sum(lax.all_to_all(squared, DP, 0, 0, tiled=True)[:, 0, 0])  8.97 us
    all_to_all x1, starting transfers between devices, per_device(): squared = jnp.sum(lax.all_to_all(squared, DP, 0, 0, tiled=True)[:, 0, 0])  7.92 us
    all_to_all x2, waiting for transfers between devices, spread(): return lax.all_to_all(copies, axes, 0, 0, tiled=True)  5.48 us
  transfers between devices with their start and end apart: 16, of which 8 were waited for; matrix products, arithmetic and copies ran while one was open for 0% of the time, Pallas kernels for 3%

profile of v13, /device:TPU:1, one launch (start us, length us, event | category | flops | bytes accessed | tf_op | source)
XLA Modules:
  0.0 177.7 jit_solution(15271692306308593829)
XLA Ops:
  0.0 0.9 broadcast_in_dim.8
  0.9 34.5 %all_to_all.20.mine = bf16[32,16,768]{2,1,0:T(8,128)(2,1)S(1)} all-to-all(bf16[32,16,768]{2,1,0:T(8,128)(2,1)S(1)} %broadcast_in_dim.8), channel_id=1, replica_groups=mesh['yl'=4,'z'=8,'c'=2,'yh'=2,'x'=4] {'yl','z'}, dimensions={0} | all-to-all | bytes 1572864 | tf_op jit(solution)/shard_map/token_gather/all_to_all | solution.py:33
  35.4 4.2 %collective-permute-start = (bf16[32,16,768]{2,1,0:T(8,128)(2,1)S(1)}, bf16[32,16,768]{2,1,0:T(8,128)(2,1)S(1)}, u32[]{:S(2)}, u32[]{:S(2)}) collective-permute-start(bf16[32,16,768]{2,1,0:T(8,128)(2,1)S(1)} %all_to_all.20.mine), channel_id=1, source_target_pairs={{0,8},{8,0},{1,9},{9,1},{2,10},{10,2},{3,11},{11,3},{4,12},{12,4},... | collective-permute-start | bytes 2359304 | tf_op jit(solution)/shard_map/token_gather/ppermute | solution.py:28
  39.6 0.0 copy-done.17
  39.7 0.1 pad_add_fusion.at
  39.8 4.8 %collective-permute-start.1 = (bf16[128,384]{1,0:T(8,128)(2,1)S(1)}, bf16[128,384]{1,0:T(8,128)(2,1)S(1)}, u32[]{:S(2)}, u32[]{:S(2)}) collective-permute-start(bf16[128,384]{1,0:T(8,128)(2,1)S(1)} %copy-done.10), channel_id=1, source_target_pairs={{0,4},{4,0},{1,5},{5,1},{2,6},{6,2},{3,7},{7,3},{8,12},{12,8},{9,1... | collective-permute-start | bytes 294920 | tf_op jit(solution)/shard_map/token_gather/ppermute | solution.py:28
  44.6 0.0 collective-permute-done.other
  44.6 5.1 %local_work.1 = (bf16[32,2,16,768]{3,2,1,0:T(8,128)(2,1)S(1)}, f32[256,384]{1,0:T(8,128)S(1)}, bf16[256,384]{1,0:T(8,128)(2,1)}, bf16[256,384]{1,0:T(8,128)(2,1)...) custom-call(s32[4]{0:T(128)S(1)} %pad_add_fusion.at, bf16[32,16,768]{2,1,0:T(8,128)(2,1)S(1)} %all_to_all.20.mine, ...), custom_call_target="tpu_custom_call" | custom-call | flops 1207959552 | bytes 8388608 | tf_op jit(solution)/shard_map/local_work/local_work/pallas_call | solution.py:100
  49.8 0.7 copy-done.13
  50.5 1.2 copy-done.15
  51.6 0.0 collective-permute-done.1.cot_other
  51.6 0.9 broadcast_in_dim.10
  52.6 6.2 %all-to-all-start.1 = ((bf16[8,40,1024]{2,1,0:T(8,128)(2,1)}), bf16[8,40,1024]{2,1,0:T(8,128)(2,1)S(1)}, u32[]{:S(2)}, u32[]{:S(2)}) async-start(bf16[8,40,1024]{2,1,0:T(8,128)(2,1)} %broadcast_in_dim.10), calls=%async_computation.1 | async-start | bytes 1310720 | tf_op jit(solution)/shard_map/sums_x/all_to_all | solution.py:33
  58.7 3.4 %collective-permute-start.2 = (bf16[256,384]{1,0:T(8,128)(2,1)}, bf16[256,384]{1,0:T(8,128)(2,1)S(1)}, u32[]{:S(2)}, u32[]{:S(2)}) collective-permute-start(bf16[256,384]{1,0:T(8,128)(2,1)} %get-tuple-element.34), channel_id=1, source_target_pairs={{0,1},{1,0},{2,3},{3,2},{4,5},{5,4},{6,7},{7,6},{8,9},{9,8},{10,11... | collective-permute-start | bytes 589832 | tf_op jit(solution)/shard_map/sums_x/ppermute | solution.py:28
  62.1 4.3 %collective-permute-start.3 = (bf16[256,384]{1,0:T(8,128)(2,1)}, bf16[256,384]{1,0:T(8,128)(2,1)S(1)}, u32[]{:S(2)}, u32[]{:S(2)}) collective-permute-start(bf16[256,384]{1,0:T(8,128)(2,1)} %get-tuple-element.35), channel_id=1, source_target_pairs={{0,2},{1,3},{2,0},{3,1},{4,6},{5,7},{6,4},{7,5},{8,10},{9,11},{10,... | collective-permute-start | bytes 589832 | tf_op jit(solution)/shard_map/sums_x/ppermute | solution.py:28
  66.4 1.9 %collective-permute-start.4 = (bf16[256,384]{1,0:T(8,128)(2,1)S(1)}, bf16[256,384]{1,0:T(8,128)(2,1)S(1)}, u32[]{:S(2)}, u32[]{:S(2)}) collective-permute-start(bf16[256,384]{1,0:T(8,128)(2,1)S(1)} %copy-done.14), channel_id=1, source_target_pairs={{0,3},{1,2},{2,1},{3,0},{4,7},{5,6},{6,5},{7,4},{8,11},{9,10},{10,... | collective-permute-start | bytes 589832 | tf_op jit(solution)/shard_map/sums_x/ppermute | solution.py:28
  68.3 3.5 %collective-permute-done.2.one = bf16[256,384]{1,0:T(8,128)(2,1)S(1)} collective-permute-done((bf16[256,384]{1,0:T(8,128)(2,1)}, bf16[256,384]{1,0:T(8,128)(2,1)S(1)}, u32[]{:S(2)}, u32[]{:S(2)}) %collective-permute-start.2) | collective-permute-done | bytes 196640 | tf_op jit(solution)/shard_map/sums_x/ppermute | solution.py:28
  71.8 6.1 %collective-permute-done.3.two = bf16[256,384]{1,0:T(8,128)(2,1)S(1)} collective-permute-done((bf16[256,384]{1,0:T(8,128)(2,1)}, bf16[256,384]{1,0:T(8,128)(2,1)S(1)}, u32[]{:S(2)}, u32[]{:S(2)}) %collective-permute-start.3) | collective-permute-done | bytes 196640 | tf_op jit(solution)/shard_map/sums_x/ppermute | solution.py:28
  77.9 3.2 %collective-permute-done.4.three = bf16[256,384]{1,0:T(8,128)(2,1)S(1)} collective-permute-done((bf16[256,384]{1,0:T(8,128)(2,1)S(1)}, bf16[256,384]{1,0:T(8,128)(2,1)S(1)}, u32[]{:S(2)}, u32[]{:S(2)}) %collective-permute-start.4) | collective-permute-done | bytes 196640 | tf_op jit(solution)/shard_map/sums_x/ppermute | solution.py:28
  81.1 0.0 all-to-all-done.1.got
  81.1 1.4 stats_work.1
  82.5 0.0 copy-start.6
  82.6 1.1 broadcast_in_dim.11
  83.7 7.4 %all-to-all-start.2 = ((bf16[32,16,1024]{2,1,0:T(8,128)(2,1)}), bf16[32,16,1024]{2,1,0:T(8,128)(2,1)S(1)}, u32[]{:S(2)}, u32[]{:S(2)}) async-start(bf16[32,16,1024]{2,1,0:T(8,128)(2,1)} %broadcast_in_dim.11), calls=%async_computation.2 | async-start | bytes 2097152 | tf_op jit(solution)/shard_map/gram_gather/all_to_all | solution.py:33
  91.1 6.9 %collective-permute-start.5 = (bf16[256,384]{1,0:T(8,128)(2,1)S(1)}, bf16[256,384]{1,0:T(8,128)(2,1)S(1)}, u32[]{:S(2)}, u32[]{:S(2)}) collective-permute-start(bf16[256,384]{1,0:T(8,128)(2,1)S(1)} %get-tuple-element.41), channel_id=1, source_target_pairs={{0,4},{4,0},{1,5},{5,1},{2,6},{6,2},{3,7},{7,3},{8,12},{12,8},{9,1... | collective-permute-start | bytes 589832 | tf_op jit(solution)/shard_map/pre/ppermute | solution.py:28
  98.0 1.9 %collective-permute-start.8 = (bf16[2,128,384]{2,1,0:T(8,128)(2,1)S(1)}, bf16[2,128,384]{2,1,0:T(8,128)(2,1)S(1)}, u32[]{:S(2)}, u32[]{:S(2)}) collective-permute-start(bf16[2,128,384]{2,1,0:T(8,128)(2,1)S(1)} %get-tuple-element.42.c0), channel_id=1, source_target_pairs={{0,3},{1,2},{2,1},{3,0},{4,7},{5,6},{6,5},{7,4},{8,11},{9,10},{10,... | collective-permute-start | bytes 589832 | tf_op jit(solution)/shard_map/pre/ppermute | solution.py:28
  99.9 2.2 %collective-permute-start.7 = (bf16[2,128,384]{2,1,0:T(8,128)(2,1)S(1)}, bf16[2,128,384]{2,1,0:T(8,128)(2,1)S(1)}, u32[]{:S(2)}, u32[]{:S(2)}) collective-permute-start(bf16[2,128,384]{2,1,0:T(8,128)(2,1)S(1)} %get-tuple-element.42.c0), channel_id=1, source_target_pairs={{0,2},{1,3},{2,0},{3,1},{4,6},{5,7},{6,4},{7,5},{8,10},{9,11},{10,... | collective-permute-start | bytes 589832 | tf_op jit(solution)/shard_map/pre/ppermute | solution.py:28
  102.2 4.8 %collective-permute-start.6 = (bf16[2,128,384]{2,1,0:T(8,128)(2,1)S(1)}, bf16[2,128,384]{2,1,0:T(8,128)(2,1)S(1)}, u32[]{:S(2)}, u32[]{:S(2)}) collective-permute-start(bf16[2,128,384]{2,1,0:T(8,128)(2,1)S(1)} %get-tuple-element.42.c0), channel_id=1, source_target_pairs={{0,1},{1,0},{2,3},{3,2},{4,5},{5,4},{6,7},{7,6},{8,9},{9,8},{10,11... | collective-permute-start | bytes 589832 | tf_op jit(solution)/shard_map/pre/ppermute | solution.py:28
  107.0 10.8 %collective-permute-done.5.moved = bf16[256,384]{1,0:T(8,128)(2,1)S(1)} collective-permute-done((bf16[256,384]{1,0:T(8,128)(2,1)S(1)}, bf16[256,384]{1,0:T(8,128)(2,1)S(1)}, u32[]{:S(2)}, u32[]{:S(2)}) %collective-permute-start.5) | collective-permute-done | bytes 196640 | tf_op jit(solution)/shard_map/pre/ppermute | solution.py:28
  117.8 0.0 collective-permute-done.8.three.c3
  117.8 0.0 collective-permute-done.7.two.c2
  117.8 0.0 collective-permute-done.6.one.c1
  117.8 0.7 pre_work.1
  118.5 0.7 copy-done
  119.2 5.5 %all-to-all-done.2.mine = bf16[32,16,1024]{2,1,0:T(8,128)(2,1)S(1)} async-done(((bf16[32,16,1024]{2,1,0:T(8,128)(2,1)}), bf16[32,16,1024]{2,1,0:T(8,128)(2,1)S(1)}, u32[]{:S(2)}, u32[]{:S(2)}) %all-to-all-start.2) | async-done | bytes 1048608 | tf_op jit(solution)/shard_map/gram_gather/all_to_all | solution.py:33
  124.7 4.9 %collective-permute-start.9 = (bf16[32,16,1024]{2,1,0:T(8,128)(2,1)S(1)}, bf16[32,16,1024]{2,1,0:T(8,128)(2,1)S(1)}, u32[]{:S(2)}, u32[]{:S(2)}) collective-permute-start(bf16[32,16,1024]{2,1,0:T(8,128)(2,1)S(1)} %all-to-all-done.2.mine), channel_id=1, source_target_pairs={{0,8},{8,0},{1,9},{9,1},{2,10},{10,2},{3,11},{11,3},{4,12},{12,4},... | collective-permute-start | bytes 3145736 | tf_op jit(solution)/shard_map/pre/ppermute | solution.py:28
  129.6 1.9 %collective-permute-start.12 = (bf16[256,384]{1,0:T(8,128)(2,1)S(1)}, bf16[256,384]{1,0:T(8,128)(2,1)S(1)}, u32[]{:S(2)}, u32[]{:S(2)}) collective-permute-start(bf16[256,384]{1,0:T(8,128)(2,1)S(1)} %get-tuple-element.45.p0), channel_id=1, source_target_pairs={{0,3},{1,2},{2,1},{3,0},{4,7},{5,6},{6,5},{7,4},{8,11},{9,10},{10,... | collective-permute-start | bytes 589832 | tf_op jit(solution)/shard_map/pre/ppermute | solution.py:28
  131.5 2.7 %collective-permute-start.11 = (bf16[256,384]{1,0:T(8,128)(2,1)S(1)}, bf16[256,384]{1,0:T(8,128)(2,1)S(1)}, u32[]{:S(2)}, u32[]{:S(2)}) collective-permute-start(bf16[256,384]{1,0:T(8,128)(2,1)S(1)} %get-tuple-element.45.p0), channel_id=1, source_target_pairs={{0,2},{1,3},{2,0},{3,1},{4,6},{5,7},{6,4},{7,5},{8,10},{9,11},{10,... | collective-permute-start | bytes 589832 | tf_op jit(solution)/shard_map/pre/ppermute | solution.py:28
  134.3 4.3 %collective-permute-start.10 = (bf16[256,384]{1,0:T(8,128)(2,1)S(1)}, bf16[256,384]{1,0:T(8,128)(2,1)S(1)}, u32[]{:S(2)}, u32[]{:S(2)}) collective-permute-start(bf16[256,384]{1,0:T(8,128)(2,1)S(1)} %get-tuple-element.45.p0), channel_id=1, source_target_pairs={{0,1},{1,0},{2,3},{3,2},{4,5},{5,4},{6,7},{7,6},{8,9},{9,8},{10,11... | collective-permute-start | bytes 589832 | tf_op jit(solution)/shard_map/pre/ppermute | solution.py:28
  138.6 0.0 copy-start.8
  138.6 0.7 copy-done.8
  139.3 4.2 %collective-permute-done.12.p3 = bf16[256,384]{1,0:T(8,128)(2,1)S(1)} collective-permute-done((bf16[256,384]{1,0:T(8,128)(2,1)S(1)}, bf16[256,384]{1,0:T(8,128)(2,1)S(1)}, u32[]{:S(2)}, u32[]{:S(2)}) %collective-permute-start.12) | collective-permute-done | bytes 196640 | tf_op jit(solution)/shard_map/pre/ppermute | solution.py:28
  143.4 0.0 collective-permute-done.11.p2
  143.4 2.2 %collective-permute-done.10.p1 = bf16[256,384]{1,0:T(8,128)(2,1)S(1)} collective-permute-done((bf16[256,384]{1,0:T(8,128)(2,1)S(1)}, bf16[256,384]{1,0:T(8,128)(2,1)S(1)}, u32[]{:S(2)}, u32[]{:S(2)}) %collective-permute-start.10) | collective-permute-done | bytes 196640 | tf_op jit(solution)/shard_map/pre/ppermute | solution.py:28
  145.6 0.0 collective-permute-done.9.other
  145.6 0.9 copy-done.1
  146.5 0.9 copy-done.7
  147.5 0.9 copy-done.9
  148.4 2.9 %ascent_work.1 = (f32[32,2,16,384]{3,2,1,0:T(8,128)S(1)}, bf16[1024,384]{1,0:T(8,128)(2,1)S(1)}, bf16[1024,384]{1,0:T(8,128)(2,1)S(1)}, f32[64,1,128]{2,1,0:T(1,128)S(1)}) custom-call(s32[4]{0:T(128)S(1)} %pad_add_fusion.at, bf16[32,16,1024]{2,1,0:T(8,128)(2,1)S(1)} %all-to-all-done.2.mine, bf16[32,16,1024]{2,1,0:T(8,128)(2,1)S(1)} %collective-permute-done.9.other, ...), custom_call_target="tpu_custom_call" | custom-call | flops 805306368 | bytes 8388608 | tf_op jit(solution)/shard_map/ascent/ascent_work/pallas_call | solution.py:233
  151.3 0.0 copy-start.2
  151.3 0.9 copy-done.2
  152.2 0.9 copy-done.4
  153.1 0.6 copy-done.11
  153.7 7.9 %all-to-all-start.3 = ((f32[64,1,128]{2,1,0:T(1,128)}), f32[64,1,128]{2,1,0:T(1,128)S(1)}, u32[]{:S(2)}, u32[]{:S(2)}) async-start(f32[64,1,128]{2,1,0:T(1,128)} %copy-done.11), calls=%async_computation.3 | async-start | bytes 65536 | tf_op jit(solution)/shard_map/ascent/all_to_all | solution.py:285
  161.6 0.6 slice_reduce_fusion.1
  162.2 9.0 %all-to-all-done.3 = f32[64,1,128]{2,1,0:T(1,128)S(1)} async-done(((f32[64,1,128]{2,1,0:T(1,128)}), f32[64,1,128]{2,1,0:T(1,128)S(1)}, u32[]{:S(2)}, u32[]{:S(2)}) %all-to-all-start.3) | async-done | bytes 32800 | tf_op jit(solution)/shard_map/ascent/all_to_all | solution.py:285
  171.2 0.7 slice_reduce_fusion.2
  172.6 0.0 copy-start.3
  172.7 0.1 broadcast_multiply_fusion
  172.8 1.0 copy-done.3
  173.8 0.2 copy-done.5
  174.0 0.9 fusion.9
  174.9 0.5 copy-done.16
  175.4 2.2 %fusion.10 = f32[768,384]{1,0:T(8,128)} fusion(bf16[1024,384]{1,0:T(8,128)(2,1)S(1)} %fusion.9, bf16[1024,768]{1,0:T(8,128)(2,1)S(1)} %bitcast.11, f32[768]{0:T(1024)S(1)} %copy-done.17, f32[1024]{0:T(1024)S(1)} %get-tuple-element.52, f32[1024]{0:T(1024)S(1)} %get-tuple-element.51), kind=kOutput, calls=%fused_computation.12 | convolution fusion | flops 607911936 | bytes 3550208 | tf_op jit(solution)/shard_map/sharp/dot_general | solution.py:41
  (19 shorter events, 0.0 us)
Async XLA Ops:
  0.0 39.8 %copy-start.10 = (bf16[128,384]{1,0:T(8,128)(2,1)S(1)}, bf16[128,384]{1,0:T(8,128)(2,1)}, u32[]{:S(2)}) copy-start(bf16[128,384]{1,0:T(8,128)(2,1)} %cot.1) | copy-start | bytes 294916
  0.0 39.6 %copy-start.17 = (f32[768]{0:T(1024)S(1)}, f32[768]{0:T(1024)}, u32[]{:S(2)}) copy-start(f32[768]{0:T(1024)} %param.5) | copy-start | bytes 9220
  0.0 44.6 %copy-start.12 = (bf16[768,384]{1,0:T(8,128)(2,1)S(1)}, bf16[768,384]{1,0:T(8,128)(2,1)}, u32[]{:S(2)}) copy-start(bf16[768,384]{1,0:T(8,128)(2,1)} %w.1) | copy-start | bytes 1769476
  35.4 9.2 %collective-permute-start = (bf16[32,16,768]{2,1,0:T(8,128)(2,1)S(1)}, bf16[32,16,768]{2,1,0:T(8,128)(2,1)S(1)}, u32[]{:S(2)}, u32[]{:S(2)}) collective-permute-start(bf16[32,16,768]{2,1,0:T(8,128)(2,1)S(1)} %all_to_all.20.mine), channel_id=1, source_target_pairs={{0,8},{8,0},{1,9},{9,1},{2,10},{10,2},{3,11},{11,3},{4,12},{12,4},... | collective-permute-start | bytes 2359304 | tf_op jit(solution)/shard_map/token_gather/ppermute | solution.py:28
  39.8 11.9 %collective-permute-start.1 = (bf16[128,384]{1,0:T(8,128)(2,1)S(1)}, bf16[128,384]{1,0:T(8,128)(2,1)S(1)}, u32[]{:S(2)}, u32[]{:S(2)}) collective-permute-start(bf16[128,384]{1,0:T(8,128)(2,1)S(1)} %copy-done.10), channel_id=1, source_target_pairs={{0,4},{4,0},{1,5},{5,1},{2,6},{6,2},{3,7},{7,3},{8,12},{12,8},{9,1... | collective-permute-start | bytes 294920 | tf_op jit(solution)/shard_map/token_gather/ppermute | solution.py:28
  49.8 0.7 copy-start.13
  50.5 1.2 copy-start.15
  51.6 14.8 %copy-start.14 = (bf16[256,384]{1,0:T(8,128)(2,1)S(1)}, bf16[256,384]{1,0:T(8,128)(2,1)}, u32[]{:S(2)}) copy-start(bf16[256,384]{1,0:T(8,128)(2,1)} %copy-done.13) | copy-start | bytes 589828
  52.6 28.6 %all-to-all-start.1 = ((bf16[8,40,1024]{2,1,0:T(8,128)(2,1)}), bf16[8,40,1024]{2,1,0:T(8,128)(2,1)S(1)}, u32[]{:S(2)}, u32[]{:S(2)}) async-start(bf16[8,40,1024]{2,1,0:T(8,128)(2,1)} %broadcast_in_dim.10), calls=%async_computation.1 | async-start | bytes 1310720 | tf_op jit(solution)/shard_map/sums_x/all_to_all | solution.py:33
  58.7 13.1 %collective-permute-start.2 = (bf16[256,384]{1,0:T(8,128)(2,1)}, bf16[256,384]{1,0:T(8,128)(2,1)S(1)}, u32[]{:S(2)}, u32[]{:S(2)}) collective-permute-start(bf16[256,384]{1,0:T(8,128)(2,1)} %get-tuple-element.34), channel_id=1, source_target_pairs={{0,1},{1,0},{2,3},{3,2},{4,5},{5,4},{6,7},{7,6},{8,9},{9,8},{10,11... | collective-permute-start | bytes 589832 | tf_op jit(solution)/shard_map/sums_x/ppermute | solution.py:28
  62.1 15.8 %collective-permute-start.3 = (bf16[256,384]{1,0:T(8,128)(2,1)}, bf16[256,384]{1,0:T(8,128)(2,1)S(1)}, u32[]{:S(2)}, u32[]{:S(2)}) collective-permute-start(bf16[256,384]{1,0:T(8,128)(2,1)} %get-tuple-element.35), channel_id=1, source_target_pairs={{0,2},{1,3},{2,0},{3,1},{4,6},{5,7},{6,4},{7,5},{8,10},{9,11},{10,... | collective-permute-start | bytes 589832 | tf_op jit(solution)/shard_map/sums_x/ppermute | solution.py:28
  66.4 14.7 %collective-permute-start.4 = (bf16[256,384]{1,0:T(8,128)(2,1)S(1)}, bf16[256,384]{1,0:T(8,128)(2,1)S(1)}, u32[]{:S(2)}, u32[]{:S(2)}) collective-permute-start(bf16[256,384]{1,0:T(8,128)(2,1)S(1)} %copy-done.14), channel_id=1, source_target_pairs={{0,3},{1,2},{2,1},{3,0},{4,7},{5,6},{6,5},{7,4},{8,11},{9,10},{10,... | collective-permute-start | bytes 589832 | tf_op jit(solution)/shard_map/sums_x/ppermute | solution.py:28
  82.5 19.6 %copy-start.6 = (bf16[2,128,384]{2,1,0:T(8,128)(2,1)}, bf16[2,128,384]{2,1,0:T(8,128)(2,1)S(1)}, u32[]{:S(2)}) copy-start(bf16[2,128,384]{2,1,0:T(8,128)(2,1)S(1)} %get-tuple-element.42.c0) | copy-start | bytes 589828
  83.7 41.0 %all-to-all-start.2 = ((bf16[32,16,1024]{2,1,0:T(8,128)(2,1)}), bf16[32,16,1024]{2,1,0:T(8,128)(2,1)S(1)}, u32[]{:S(2)}, u32[]{:S(2)}) async-start(bf16[32,16,1024]{2,1,0:T(8,128)(2,1)} %broadcast_in_dim.11), calls=%async_computation.2 | async-start | bytes 2097152 | tf_op jit(solution)/shard_map/gram_gather/all_to_all | solution.py:33
  91.1 26.8 %collective-permute-start.5 = (bf16[256,384]{1,0:T(8,128)(2,1)S(1)}, bf16[256,384]{1,0:T(8,128)(2,1)S(1)}, u32[]{:S(2)}, u32[]{:S(2)}) collective-permute-start(bf16[256,384]{1,0:T(8,128)(2,1)S(1)} %get-tuple-element.41), channel_id=1, source_target_pairs={{0,4},{4,0},{1,5},{5,1},{2,6},{6,2},{3,7},{7,3},{8,12},{12,8},{9,1... | collective-permute-start | bytes 589832 | tf_op jit(solution)/shard_map/pre/ppermute | solution.py:28
  98.0 19.8 %collective-permute-start.8 = (bf16[2,128,384]{2,1,0:T(8,128)(2,1)S(1)}, bf16[2,128,384]{2,1,0:T(8,128)(2,1)S(1)}, u32[]{:S(2)}, u32[]{:S(2)}) collective-permute-start(bf16[2,128,384]{2,1,0:T(8,128)(2,1)S(1)} %get-tuple-element.42.c0), channel_id=1, source_target_pairs={{0,3},{1,2},{2,1},{3,0},{4,7},{5,6},{6,5},{7,4},{8,11},{9,10},{10,... | collective-permute-start | bytes 589832 | tf_op jit(solution)/shard_map/pre/ppermute | solution.py:28
  99.9 17.9 %collective-permute-start.7 = (bf16[2,128,384]{2,1,0:T(8,128)(2,1)S(1)}, bf16[2,128,384]{2,1,0:T(8,128)(2,1)S(1)}, u32[]{:S(2)}, u32[]{:S(2)}) collective-permute-start(bf16[2,128,384]{2,1,0:T(8,128)(2,1)S(1)} %get-tuple-element.42.c0), channel_id=1, source_target_pairs={{0,2},{1,3},{2,0},{3,1},{4,6},{5,7},{6,4},{7,5},{8,10},{9,11},{10,... | collective-permute-start | bytes 589832 | tf_op jit(solution)/shard_map/pre/ppermute | solution.py:28
  102.2 15.7 %collective-permute-start.6 = (bf16[2,128,384]{2,1,0:T(8,128)(2,1)S(1)}, bf16[2,128,384]{2,1,0:T(8,128)(2,1)S(1)}, u32[]{:S(2)}, u32[]{:S(2)}) collective-permute-start(bf16[2,128,384]{2,1,0:T(8,128)(2,1)S(1)} %get-tuple-element.42.c0), channel_id=1, source_target_pairs={{0,1},{1,0},{2,3},{3,2},{4,5},{5,4},{6,7},{7,6},{8,9},{9,8},{10,11... | collective-permute-start | bytes 589832 | tf_op jit(solution)/shard_map/pre/ppermute | solution.py:28
  118.5 0.7 copy-start
  124.7 20.9 %collective-permute-start.9 = (bf16[32,16,1024]{2,1,0:T(8,128)(2,1)S(1)}, bf16[32,16,1024]{2,1,0:T(8,128)(2,1)S(1)}, u32[]{:S(2)}, u32[]{:S(2)}) collective-permute-start(bf16[32,16,1024]{2,1,0:T(8,128)(2,1)S(1)} %all-to-all-done.2.mine), channel_id=1, source_target_pairs={{0,8},{8,0},{1,9},{9,1},{2,10},{10,2},{3,11},{11,3},{4,12},{12,4},... | collective-permute-start | bytes 3145736 | tf_op jit(solution)/shard_map/pre/ppermute | solution.py:28
  129.6 13.8 %collective-permute-start.12 = (bf16[256,384]{1,0:T(8,128)(2,1)S(1)}, bf16[256,384]{1,0:T(8,128)(2,1)S(1)}, u32[]{:S(2)}, u32[]{:S(2)}) collective-permute-start(bf16[256,384]{1,0:T(8,128)(2,1)S(1)} %get-tuple-element.45.p0), channel_id=1, source_target_pairs={{0,3},{1,2},{2,1},{3,0},{4,7},{5,6},{6,5},{7,4},{8,11},{9,10},{10,... | collective-permute-start | bytes 589832 | tf_op jit(solution)/shard_map/pre/ppermute | solution.py:28
  131.5 11.9 %collective-permute-start.11 = (bf16[256,384]{1,0:T(8,128)(2,1)S(1)}, bf16[256,384]{1,0:T(8,128)(2,1)S(1)}, u32[]{:S(2)}, u32[]{:S(2)}) collective-permute-start(bf16[256,384]{1,0:T(8,128)(2,1)S(1)} %get-tuple-element.45.p0), channel_id=1, source_target_pairs={{0,2},{1,3},{2,0},{3,1},{4,6},{5,7},{6,4},{7,5},{8,10},{9,11},{10,... | collective-permute-start | bytes 589832 | tf_op jit(solution)/shard_map/pre/ppermute | solution.py:28
  134.3 11.3 %collective-permute-start.10 = (bf16[256,384]{1,0:T(8,128)(2,1)S(1)}, bf16[256,384]{1,0:T(8,128)(2,1)S(1)}, u32[]{:S(2)}, u32[]{:S(2)}) collective-permute-start(bf16[256,384]{1,0:T(8,128)(2,1)S(1)} %get-tuple-element.45.p0), channel_id=1, source_target_pairs={{0,1},{1,0},{2,3},{3,2},{4,5},{5,4},{6,7},{7,6},{8,9},{9,8},{10,11... | collective-permute-start | bytes 589832 | tf_op jit(solution)/shard_map/pre/ppermute | solution.py:28
  138.6 0.7 copy-start.8
  145.6 0.9 copy-start.1
  146.5 0.9 copy-start.7
  147.5 0.9 copy-start.9
  151.3 0.9 copy-start.2
  152.2 0.9 copy-start.4
  153.1 0.6 copy-start.11
  153.7 17.5 %all-to-all-start.3 = ((f32[64,1,128]{2,1,0:T(1,128)}), f32[64,1,128]{2,1,0:T(1,128)S(1)}, u32[]{:S(2)}, u32[]{:S(2)}) async-start(f32[64,1,128]{2,1,0:T(1,128)} %copy-done.11), calls=%async_computation.3 | async-start | bytes 65536 | tf_op jit(solution)/shard_map/ascent/all_to_all | solution.py:285
  172.6 1.1 copy-start.3
  172.6 1.4 copy-start.5
  174.0 1.4 copy-start.16

commit v14 on v13

--- a/solution.py
+++ b/solution.py
@@ -200,11 +200,19 @@
 def ascent_kernel(at, mine, other, p0, p1, p2, p3, c0, c1, c2, c3, mark, along, pre_out, cot_out, squared, slope, pre, cot, sems):
     core, x = at[1], at[2]
     columns = p0.shape[1]
+    arrivals = []
     for b, (p, c) in enumerate(((p0, c0), (p1, c1), (p2, c2), (p3, c3))):
         q = x ^ b
-        pre[pl.ds(pl.multiple_of(q * 256, 256), 256)] = p[...]
-        cot[pl.ds(pl.multiple_of(q * 128, 128), 128)] = c[0]
-        cot[pl.ds(pl.multiple_of(512 + q * 128, 128), 128)] = c[1]
+        places = (
+            (p, pre.at[pl.ds(pl.multiple_of(q * 256, 256), 256)]),
+            (c.at[0], cot.at[pl.ds(pl.multiple_of(q * 128, 128), 128)]),
+            (c.at[1], cot.at[pl.ds(pl.multiple_of(512 + q * 128, 128), 128)]),
+        )
+        for i, (source, target) in enumerate(places):
+            arrivals.append(pltpu.make_async_copy(source, target, sems.at[2 + 3 * b + i]))
+            arrivals[-1].start()
+    for copy in arrivals:
+        copy.wait()
     copies = [pltpu.make_async_copy(pre, pre_out, sems.at[0]), pltpu.make_async_copy(cot, cot_out, sems.at[1])]
     for copy in copies:
         copy.start()
@@ -229,6 +237,7 @@
     columns = pres[0].shape[1]
     vmem = pl.BlockSpec(memory_space=pltpu.VMEM)
     anywhere = pl.BlockSpec(memory_space=pl.ANY)
+    far = pl.BlockSpec(memory_space=pltpu.HBM)
     flat = jax.ShapeDtypeStruct((TOKENS, columns), BF)
     return pl.pallas_call(
         ascent_kernel,
@@ -238,13 +247,13 @@
             flat,
             jax.ShapeDtypeStruct((64, 1, 128), F32),
         ],
-        in_specs=[pl.BlockSpec(memory_space=pltpu.SMEM)] + [vmem] * 10 + [anywhere],
-        out_specs=[vmem, anywhere, anywhere, vmem],
+        in_specs=[pl.BlockSpec(memory_space=pltpu.SMEM)] + [vmem] * 2 + [far] * 8 + [anywhere],
+        out_specs=[vmem, far, far, vmem],
         scratch_shapes=[
             pltpu.VMEM((32, 2, 16, columns), BF),
             pltpu.VMEM((TOKENS, columns), BF),
             pltpu.VMEM((TOKENS, columns), BF),
-            pltpu.SemaphoreType.DMA((2,)),
+            pltpu.SemaphoreType.DMA((14,)),
         ],
         compiler_params=pltpu.CompilerParams(vmem_limit_bytes=40 << 20),
         cost_estimate=pl.CostEstimate(flops=2 * TOKENS * TOKENS * columns, bytes_accessed=8 << 20, transcendentals=2 * TOKENS * columns),

time: 179 us -> 181 us (1.011)
  Pallas kernels: 10.1 us -> 12.1 us
    pallas_call x1, Pallas kernels: 2.88 us -> 4.91 us  [ascent_work(): pl.pallas_call(ascent_kernel, out_shape=[jax.ShapeDtypeStruct((32, 2, 16,...]
where the time goes in v14:
time: 181 us; the launch traced here: 180 us
  starting transfers between devices  70 us (39%)
  waiting for transfers between devices  44.4 us (25%)
  blocking collectives  34.5 us (19%)
  local copies, waits for them, and re-layouts  13.7 us (8%)
  Pallas kernels  12.1 us (7%)
  matrix products  2.25 us (1%)
    ppermute x13, starting transfers between devices, swap(): return lax.ppermute(value, axis, [(i, i ^ bit) for i in range(size)])  48.5 us
    all_to_all x1, blocking collectives, spread(): return lax.all_to_all(copies, axes, 0, 0, tiled=True)  34.5 us
    ppermute x13, waiting for transfers between devices, swap(): return lax.ppermute(value, axis, [(i, i ^ bit) for i in range(size)])  30 us
    all_to_all x2, starting transfers between devices, spread(): return lax.all_to_all(copies, axes, 0, 0, tiled=True)  13.6 us
    unnamed x36, local copies, waits for them, and re-layouts  10.2 us
    all_to_all x1, waiting for transfers between devices, per_device(): squared = jnp.sum(lax.all_to_all(squared, DP, 0, 0, tiled=True)[:, 0, 0])  8.97 us
    all_to_all x1, starting transfers between devices, per_device(): squared = jnp.sum(lax.all_to_all(squared, DP, 0, 0, tiled=True)[:, 0, 0])  7.92 us
    all_to_all x2, waiting for transfers between devices, spread(): return lax.all_to_all(copies, axes, 0, 0, tiled=True)  5.48 us
  transfers between devices with their start and end apart: 16, of which 8 were waited for; matrix products, arithmetic and copies ran while one was open for 0% of the time, Pallas kernels for 3%

profile of v14, /device:TPU:1, one launch (start us, length us, event | category | flops | bytes accessed | tf_op | source)
XLA Modules:
  0.0 179.7 jit_solution(10864089845385844853)
XLA Ops:
  0.0 0.9 broadcast_in_dim.8
  0.9 34.5 %all_to_all.20.mine = bf16[32,16,768]{2,1,0:T(8,128)(2,1)S(1)} all-to-all(bf16[32,16,768]{2,1,0:T(8,128)(2,1)S(1)} %broadcast_in_dim.8), channel_id=1, replica_groups=mesh['yl'=4,'z'=8,'c'=2,'yh'=2,'x'=4] {'yl','z'}, dimensions={0} | all-to-all | bytes 1572864 | tf_op jit(solution)/shard_map/token_gather/all_to_all | solution.py:33
  35.4 4.2 %collective-permute-start = (bf16[32,16,768]{2,1,0:T(8,128)(2,1)S(1)}, bf16[32,16,768]{2,1,0:T(8,128)(2,1)S(1)}, u32[]{:S(2)}, u32[]{:S(2)}) collective-permute-start(bf16[32,16,768]{2,1,0:T(8,128)(2,1)S(1)} %all_to_all.20.mine), channel_id=1, source_target_pairs={{0,8},{8,0},{1,9},{9,1},{2,10},{10,2},{3,11},{11,3},{4,12},{12,4},... | collective-permute-start | bytes 2359304 | tf_op jit(solution)/shard_map/token_gather/ppermute | solution.py:28
  39.7 0.1 pad_add_fusion.at
  39.8 0.0 copy-done.10
  39.8 4.8 %collective-permute-start.1 = (bf16[128,384]{1,0:T(8,128)(2,1)S(1)}, bf16[128,384]{1,0:T(8,128)(2,1)S(1)}, u32[]{:S(2)}, u32[]{:S(2)}) collective-permute-start(bf16[128,384]{1,0:T(8,128)(2,1)S(1)} %copy-done.10), channel_id=1, source_target_pairs={{0,4},{4,0},{1,5},{5,1},{2,6},{6,2},{3,7},{7,3},{8,12},{12,8},{9,1... | collective-permute-start | bytes 294920 | tf_op jit(solution)/shard_map/token_gather/ppermute | solution.py:28
  44.6 0.0 collective-permute-done.other
  44.6 0.0 copy-done.12
  44.6 5.1 %local_work.1 = (bf16[32,2,16,768]{3,2,1,0:T(8,128)(2,1)S(1)}, f32[256,384]{1,0:T(8,128)S(1)}, bf16[256,384]{1,0:T(8,128)(2,1)}, bf16[256,384]{1,0:T(8,128)(2,1)...) custom-call(s32[4]{0:T(128)S(1)} %pad_add_fusion.at, bf16[32,16,768]{2,1,0:T(8,128)(2,1)S(1)} %all_to_all.20.mine, ...), custom_call_target="tpu_custom_call" | custom-call | flops 1207959552 | bytes 8388608 | tf_op jit(solution)/shard_map/local_work/local_work/pallas_call | solution.py:100
  49.8 0.7 copy-done.13
  50.5 1.2 copy-done.15
  51.6 0.0 collective-permute-done.1.cot_other
  51.6 0.9 broadcast_in_dim.10
  52.6 6.2 %all-to-all-start.1 = ((bf16[8,40,1024]{2,1,0:T(8,128)(2,1)}), bf16[8,40,1024]{2,1,0:T(8,128)(2,1)S(1)}, u32[]{:S(2)}, u32[]{:S(2)}) async-start(bf16[8,40,1024]{2,1,0:T(8,128)(2,1)} %broadcast_in_dim.10), calls=%async_computation.1 | async-start | bytes 1310720 | tf_op jit(solution)/shard_map/sums_x/all_to_all | solution.py:33
  58.7 3.4 %collective-permute-start.2 = (bf16[256,384]{1,0:T(8,128)(2,1)}, bf16[256,384]{1,0:T(8,128)(2,1)S(1)}, u32[]{:S(2)}, u32[]{:S(2)}) collective-permute-start(bf16[256,384]{1,0:T(8,128)(2,1)} %get-tuple-element.34), channel_id=1, source_target_pairs={{0,1},{1,0},{2,3},{3,2},{4,5},{5,4},{6,7},{7,6},{8,9},{9,8},{10,11... | collective-permute-start | bytes 589832 | tf_op jit(solution)/shard_map/sums_x/ppermute | solution.py:28
  62.1 4.3 %collective-permute-start.3 = (bf16[256,384]{1,0:T(8,128)(2,1)}, bf16[256,384]{1,0:T(8,128)(2,1)S(1)}, u32[]{:S(2)}, u32[]{:S(2)}) collective-permute-start(bf16[256,384]{1,0:T(8,128)(2,1)} %get-tuple-element.35), channel_id=1, source_target_pairs={{0,2},{1,3},{2,0},{3,1},{4,6},{5,7},{6,4},{7,5},{8,10},{9,11},{10,... | collective-permute-start | bytes 589832 | tf_op jit(solution)/shard_map/sums_x/ppermute | solution.py:28
  66.4 1.9 %collective-permute-start.4 = (bf16[256,384]{1,0:T(8,128)(2,1)S(1)}, bf16[256,384]{1,0:T(8,128)(2,1)S(1)}, u32[]{:S(2)}, u32[]{:S(2)}) collective-permute-start(bf16[256,384]{1,0:T(8,128)(2,1)S(1)} %copy-done.14), channel_id=1, source_target_pairs={{0,3},{1,2},{2,1},{3,0},{4,7},{5,6},{6,5},{7,4},{8,11},{9,10},{10,... | collective-permute-start | bytes 589832 | tf_op jit(solution)/shard_map/sums_x/ppermute | solution.py:28
  68.3 3.5 %collective-permute-done.2.one = bf16[256,384]{1,0:T(8,128)(2,1)S(1)} collective-permute-done((bf16[256,384]{1,0:T(8,128)(2,1)}, bf16[256,384]{1,0:T(8,128)(2,1)S(1)}, u32[]{:S(2)}, u32[]{:S(2)}) %collective-permute-start.2) | collective-permute-done | bytes 196640 | tf_op jit(solution)/shard_map/sums_x/ppermute | solution.py:28
  71.8 6.1 %collective-permute-done.3.two = bf16[256,384]{1,0:T(8,128)(2,1)S(1)} collective-permute-done((bf16[256,384]{1,0:T(8,128)(2,1)}, bf16[256,384]{1,0:T(8,128)(2,1)S(1)}, u32[]{:S(2)}, u32[]{:S(2)}) %collective-permute-start.3) | collective-permute-done | bytes 196640 | tf_op jit(solution)/shard_map/sums_x/ppermute | solution.py:28
  77.9 3.2 %collective-permute-done.4.three = bf16[256,384]{1,0:T(8,128)(2,1)S(1)} collective-permute-done((bf16[256,384]{1,0:T(8,128)(2,1)S(1)}, bf16[256,384]{1,0:T(8,128)(2,1)S(1)}, u32[]{:S(2)}, u32[]{:S(2)}) %collective-permute-start.4) | collective-permute-done | bytes 196640 | tf_op jit(solution)/shard_map/sums_x/ppermute | solution.py:28
  81.1 0.0 all-to-all-done.1.got
  81.1 1.4 stats_work.1
  82.6 1.1 broadcast_in_dim.11
  83.7 7.4 %all-to-all-start.2 = ((bf16[32,16,1024]{2,1,0:T(8,128)(2,1)}), bf16[32,16,1024]{2,1,0:T(8,128)(2,1)S(1)}, u32[]{:S(2)}, u32[]{:S(2)}) async-start(bf16[32,16,1024]{2,1,0:T(8,128)(2,1)} %broadcast_in_dim.11), calls=%async_computation.2 | async-start | bytes 2097152 | tf_op jit(solution)/shard_map/gram_gather/all_to_all | solution.py:33
  91.1 6.9 %collective-permute-start.5 = (bf16[256,384]{1,0:T(8,128)(2,1)S(1)}, bf16[256,384]{1,0:T(8,128)(2,1)S(1)}, u32[]{:S(2)}, u32[]{:S(2)}) collective-permute-start(bf16[256,384]{1,0:T(8,128)(2,1)S(1)} %get-tuple-element.41), channel_id=1, source_target_pairs={{0,4},{4,0},{1,5},{5,1},{2,6},{6,2},{3,7},{7,3},{8,12},{12,8},{9,1... | collective-permute-start | bytes 589832 | tf_op jit(solution)/shard_map/pre/ppermute | solution.py:28
  98.0 1.9 %collective-permute-start.8 = (bf16[2,128,384]{2,1,0:T(8,128)(2,1)S(1)}, bf16[2,128,384]{2,1,0:T(8,128)(2,1)S(1)}, u32[]{:S(2)}, u32[]{:S(2)}) collective-permute-start(bf16[2,128,384]{2,1,0:T(8,128)(2,1)S(1)} %get-tuple-element.42.c0), channel_id=1, source_target_pairs={{0,3},{1,2},{2,1},{3,0},{4,7},{5,6},{6,5},{7,4},{8,11},{9,10},{10,... | collective-permute-start | bytes 589832 | tf_op jit(solution)/shard_map/pre/ppermute | solution.py:28
  99.9 2.2 %collective-permute-start.7 = (bf16[2,128,384]{2,1,0:T(8,128)(2,1)S(1)}, bf16[2,128,384]{2,1,0:T(8,128)(2,1)S(1)}, u32[]{:S(2)}, u32[]{:S(2)}) collective-permute-start(bf16[2,128,384]{2,1,0:T(8,128)(2,1)S(1)} %get-tuple-element.42.c0), channel_id=1, source_target_pairs={{0,2},{1,3},{2,0},{3,1},{4,6},{5,7},{6,4},{7,5},{8,10},{9,11},{10,... | collective-permute-start | bytes 589832 | tf_op jit(solution)/shard_map/pre/ppermute | solution.py:28
  102.2 4.8 %collective-permute-start.6 = (bf16[2,128,384]{2,1,0:T(8,128)(2,1)S(1)}, bf16[2,128,384]{2,1,0:T(8,128)(2,1)S(1)}, u32[]{:S(2)}, u32[]{:S(2)}) collective-permute-start(bf16[2,128,384]{2,1,0:T(8,128)(2,1)S(1)} %get-tuple-element.42.c0), channel_id=1, source_target_pairs={{0,1},{1,0},{2,3},{3,2},{4,5},{5,4},{6,7},{7,6},{8,9},{9,8},{10,11... | collective-permute-start | bytes 589832 | tf_op jit(solution)/shard_map/pre/ppermute | solution.py:28
  107.0 10.8 %collective-permute-done.5.moved = bf16[256,384]{1,0:T(8,128)(2,1)S(1)} collective-permute-done((bf16[256,384]{1,0:T(8,128)(2,1)S(1)}, bf16[256,384]{1,0:T(8,128)(2,1)S(1)}, u32[]{:S(2)}, u32[]{:S(2)}) %collective-permute-start.5) | collective-permute-done | bytes 196640 | tf_op jit(solution)/shard_map/pre/ppermute | solution.py:28
  117.8 0.0 collective-permute-done.8.three.c3
  117.8 0.0 collective-permute-done.7.two.c2
  117.8 0.0 collective-permute-done.6.one.c1
  117.8 0.7 pre_work.1
  118.5 0.7 copy-done
  119.2 5.5 %all-to-all-done.2.mine = bf16[32,16,1024]{2,1,0:T(8,128)(2,1)S(1)} async-done(((bf16[32,16,1024]{2,1,0:T(8,128)(2,1)}), bf16[32,16,1024]{2,1,0:T(8,128)(2,1)S(1)}, u32[]{:S(2)}, u32[]{:S(2)}) %all-to-all-start.2) | async-done | bytes 1048608 | tf_op jit(solution)/shard_map/gram_gather/all_to_all | solution.py:33
  124.7 4.9 %collective-permute-start.9 = (bf16[32,16,1024]{2,1,0:T(8,128)(2,1)S(1)}, bf16[32,16,1024]{2,1,0:T(8,128)(2,1)S(1)}, u32[]{:S(2)}, u32[]{:S(2)}) collective-permute-start(bf16[32,16,1024]{2,1,0:T(8,128)(2,1)S(1)} %all-to-all-done.2.mine), channel_id=1, source_target_pairs={{0,8},{8,0},{1,9},{9,1},{2,10},{10,2},{3,11},{11,3},{4,12},{12,4},... | collective-permute-start | bytes 3145736 | tf_op jit(solution)/shard_map/pre/ppermute | solution.py:28
  129.6 1.9 %collective-permute-start.12 = (bf16[256,384]{1,0:T(8,128)(2,1)S(1)}, bf16[256,384]{1,0:T(8,128)(2,1)S(1)}, u32[]{:S(2)}, u32[]{:S(2)}) collective-permute-start(bf16[256,384]{1,0:T(8,128)(2,1)S(1)} %get-tuple-element.45.p0), channel_id=1, source_target_pairs={{0,3},{1,2},{2,1},{3,0},{4,7},{5,6},{6,5},{7,4},{8,11},{9,10},{10,... | collective-permute-start | bytes 589832 | tf_op jit(solution)/shard_map/pre/ppermute | solution.py:28
  131.5 2.7 %collective-permute-start.11 = (bf16[256,384]{1,0:T(8,128)(2,1)S(1)}, bf16[256,384]{1,0:T(8,128)(2,1)S(1)}, u32[]{:S(2)}, u32[]{:S(2)}) collective-permute-start(bf16[256,384]{1,0:T(8,128)(2,1)S(1)} %get-tuple-element.45.p0), channel_id=1, source_target_pairs={{0,2},{1,3},{2,0},{3,1},{4,6},{5,7},{6,4},{7,5},{8,10},{9,11},{10,... | collective-permute-start | bytes 589832 | tf_op jit(solution)/shard_map/pre/ppermute | solution.py:28
  134.3 4.3 %collective-permute-start.10 = (bf16[256,384]{1,0:T(8,128)(2,1)S(1)}, bf16[256,384]{1,0:T(8,128)(2,1)S(1)}, u32[]{:S(2)}, u32[]{:S(2)}) collective-permute-start(bf16[256,384]{1,0:T(8,128)(2,1)S(1)} %get-tuple-element.45.p0), channel_id=1, source_target_pairs={{0,1},{1,0},{2,3},{3,2},{4,5},{5,4},{6,7},{7,6},{8,9},{9,8},{10,11... | collective-permute-start | bytes 589832 | tf_op jit(solution)/shard_map/pre/ppermute | solution.py:28
  138.6 0.0 copy-start.8
  138.6 0.7 copy-done.8
  139.3 4.2 %collective-permute-done.12.p3 = bf16[256,384]{1,0:T(8,128)(2,1)S(1)} collective-permute-done((bf16[256,384]{1,0:T(8,128)(2,1)S(1)}, bf16[256,384]{1,0:T(8,128)(2,1)S(1)}, u32[]{:S(2)}, u32[]{:S(2)}) %collective-permute-start.12) | collective-permute-done | bytes 196640 | tf_op jit(solution)/shard_map/pre/ppermute | solution.py:28
  143.4 0.0 collective-permute-done.11.p2
  143.4 2.2 %collective-permute-done.10.p1 = bf16[256,384]{1,0:T(8,128)(2,1)S(1)} collective-permute-done((bf16[256,384]{1,0:T(8,128)(2,1)S(1)}, bf16[256,384]{1,0:T(8,128)(2,1)S(1)}, u32[]{:S(2)}, u32[]{:S(2)}) %collective-permute-start.10) | collective-permute-done | bytes 196640 | tf_op jit(solution)/shard_map/pre/ppermute | solution.py:28
  145.6 0.0 collective-permute-done.9.other
  145.6 0.9 copy-done.1
  146.5 0.9 copy-done.7
  147.5 0.9 copy-done.9
  148.4 4.9 %ascent_work.1 = (f32[32,2,16,384]{3,2,1,0:T(8,128)S(1)}, bf16[1024,384]{1,0:T(8,128)(2,1)S(1)}, bf16[1024,384]{1,0:T(8,128)(2,1)S(1)}, f32[64,1,128]{2,1,0:T(1,128)S(1)}) custom-call(s32[4]{0:T(128)S(1)} %pad_add_fusion.at, bf16[32,16,1024]{2,1,0:T(8,128)(2,1)S(1)} %all-to-all-done.2.mine, bf16[32,16,1024]{2,1,0:T(8,128)(2,1)S(1)} %collective-permute-done.9.other, ...), custom_call_target="tpu_custom_call" | custom-call | flops 805306368 | bytes 8388608 | tf_op jit(solution)/shard_map/ascent/ascent_work/pallas_call | solution.py:242
  153.3 0.0 copy-start.2
  153.3 0.9 copy-done.2
  154.2 0.9 copy-done.4
  155.1 0.6 copy-done.11
  155.7 7.9 %all-to-all-start.3 = ((f32[64,1,128]{2,1,0:T(1,128)}), f32[64,1,128]{2,1,0:T(1,128)S(1)}, u32[]{:S(2)}, u32[]{:S(2)}) async-start(f32[64,1,128]{2,1,0:T(1,128)} %copy-done.11), calls=%async_computation.3 | async-start | bytes 65536 | tf_op jit(solution)/shard_map/ascent/all_to_all | solution.py:294
  163.6 0.6 slice_reduce_fusion.1
  164.3 9.0 %all-to-all-done.3 = f32[64,1,128]{2,1,0:T(1,128)S(1)} async-done(((f32[64,1,128]{2,1,0:T(1,128)}), f32[64,1,128]{2,1,0:T(1,128)S(1)}, u32[]{:S(2)}, u32[]{:S(2)}) %all-to-all-start.3) | async-done | bytes 32800 | tf_op jit(solution)/shard_map/ascent/all_to_all | solution.py:294
  173.2 0.7 slice_reduce_fusion.2
  174.7 0.0 copy-start.3
  174.7 0.1 broadcast_multiply_fusion
  174.8 1.0 copy-done.3
  175.8 0.2 copy-done.5
  176.0 0.9 fusion.9
  176.9 0.5 copy-done.16
  177.4 2.2 %fusion.10 = f32[768,384]{1,0:T(8,128)} fusion(bf16[1024,384]{1,0:T(8,128)(2,1)S(1)} %fusion.9, bf16[1024,768]{1,0:T(8,128)(2,1)S(1)} %bitcast.11, f32[768]{0:T(1024)S(1)} %copy-done.17, f32[1024]{0:T(1024)S(1)} %get-tuple-element.52, f32[1024]{0:T(1024)S(1)} %get-tuple-element.51), kind=kOutput, calls=%fused_computation.12 | convolution fusion | flops 607911936 | bytes 3550208 | tf_op jit(solution)/shard_map/sharp/dot_general | solution.py:41
  (19 shorter events, 0.0 us)
Async XLA Ops:
  0.0 39.8 %copy-start.10 = (bf16[128,384]{1,0:T(8,128)(2,1)S(1)}, bf16[128,384]{1,0:T(8,128)(2,1)}, u32[]{:S(2)}) copy-start(bf16[128,384]{1,0:T(8,128)(2,1)} %cot.1) | copy-start | bytes 294916
  0.0 39.6 %copy-start.17 = (f32[768]{0:T(1024)S(1)}, f32[768]{0:T(1024)}, u32[]{:S(2)}) copy-start(f32[768]{0:T(1024)} %param.5) | copy-start | bytes 9220
  0.0 44.6 %copy-start.12 = (bf16[768,384]{1,0:T(8,128)(2,1)S(1)}, bf16[768,384]{1,0:T(8,128)(2,1)}, u32[]{:S(2)}) copy-start(bf16[768,384]{1,0:T(8,128)(2,1)} %w.1) | copy-start | bytes 1769476
  35.4 9.2 %collective-permute-start = (bf16[32,16,768]{2,1,0:T(8,128)(2,1)S(1)}, bf16[32,16,768]{2,1,0:T(8,128)(2,1)S(1)}, u32[]{:S(2)}, u32[]{:S(2)}) collective-permute-start(bf16[32,16,768]{2,1,0:T(8,128)(2,1)S(1)} %all_to_all.20.mine), channel_id=1, source_target_pairs={{0,8},{8,0},{1,9},{9,1},{2,10},{10,2},{3,11},{11,3},{4,12},{12,4},... | collective-permute-start | bytes 2359304 | tf_op jit(solution)/shard_map/token_gather/ppermute | solution.py:28
  39.8 11.9 %collective-permute-start.1 = (bf16[128,384]{1,0:T(8,128)(2,1)S(1)}, bf16[128,384]{1,0:T(8,128)(2,1)S(1)}, u32[]{:S(2)}, u32[]{:S(2)}) collective-permute-start(bf16[128,384]{1,0:T(8,128)(2,1)S(1)} %copy-done.10), channel_id=1, source_target_pairs={{0,4},{4,0},{1,5},{5,1},{2,6},{6,2},{3,7},{7,3},{8,12},{12,8},{9,1... | collective-permute-start | bytes 294920 | tf_op jit(solution)/shard_map/token_gather/ppermute | solution.py:28
  49.8 0.7 copy-start.13
  50.5 1.2 copy-start.15
  51.6 14.8 %copy-start.14 = (bf16[256,384]{1,0:T(8,128)(2,1)S(1)}, bf16[256,384]{1,0:T(8,128)(2,1)}, u32[]{:S(2)}) copy-start(bf16[256,384]{1,0:T(8,128)(2,1)} %copy-done.13) | copy-start | bytes 589828
  52.6 28.6 %all-to-all-start.1 = ((bf16[8,40,1024]{2,1,0:T(8,128)(2,1)}), bf16[8,40,1024]{2,1,0:T(8,128)(2,1)S(1)}, u32[]{:S(2)}, u32[]{:S(2)}) async-start(bf16[8,40,1024]{2,1,0:T(8,128)(2,1)} %broadcast_in_dim.10), calls=%async_computation.1 | async-start | bytes 1310720 | tf_op jit(solution)/shard_map/sums_x/all_to_all | solution.py:33
  58.7 13.1 %collective-permute-start.2 = (bf16[256,384]{1,0:T(8,128)(2,1)}, bf16[256,384]{1,0:T(8,128)(2,1)S(1)}, u32[]{:S(2)}, u32[]{:S(2)}) collective-permute-start(bf16[256,384]{1,0:T(8,128)(2,1)} %get-tuple-element.34), channel_id=1, source_target_pairs={{0,1},{1,0},{2,3},{3,2},{4,5},{5,4},{6,7},{7,6},{8,9},{9,8},{10,11... | collective-permute-start | bytes 589832 | tf_op jit(solution)/shard_map/sums_x/ppermute | solution.py:28
  62.1 15.8 %collective-permute-start.3 = (bf16[256,384]{1,0:T(8,128)(2,1)}, bf16[256,384]{1,0:T(8,128)(2,1)S(1)}, u32[]{:S(2)}, u32[]{:S(2)}) collective-permute-start(bf16[256,384]{1,0:T(8,128)(2,1)} %get-tuple-element.35), channel_id=1, source_target_pairs={{0,2},{1,3},{2,0},{3,1},{4,6},{5,7},{6,4},{7,5},{8,10},{9,11},{10,... | collective-permute-start | bytes 589832 | tf_op jit(solution)/shard_map/sums_x/ppermute | solution.py:28
  66.4 14.7 %collective-permute-start.4 = (bf16[256,384]{1,0:T(8,128)(2,1)S(1)}, bf16[256,384]{1,0:T(8,128)(2,1)S(1)}, u32[]{:S(2)}, u32[]{:S(2)}) collective-permute-start(bf16[256,384]{1,0:T(8,128)(2,1)S(1)} %copy-done.14), channel_id=1, source_target_pairs={{0,3},{1,2},{2,1},{3,0},{4,7},{5,6},{6,5},{7,4},{8,11},{9,10},{10,... | collective-permute-start | bytes 589832 | tf_op jit(solution)/shard_map/sums_x/ppermute | solution.py:28
  82.5 19.6 %copy-start.6 = (bf16[2,128,384]{2,1,0:T(8,128)(2,1)}, bf16[2,128,384]{2,1,0:T(8,128)(2,1)S(1)}, u32[]{:S(2)}) copy-start(bf16[2,128,384]{2,1,0:T(8,128)(2,1)S(1)} %get-tuple-element.42.c0) | copy-start | bytes 589828
  83.7 41.0 %all-to-all-start.2 = ((bf16[32,16,1024]{2,1,0:T(8,128)(2,1)}), bf16[32,16,1024]{2,1,0:T(8,128)(2,1)S(1)}, u32[]{:S(2)}, u32[]{:S(2)}) async-start(bf16[32,16,1024]{2,1,0:T(8,128)(2,1)} %broadcast_in_dim.11), calls=%async_computation.2 | async-start | bytes 2097152 | tf_op jit(solution)/shard_map/gram_gather/all_to_all | solution.py:33
  91.1 26.8 %collective-permute-start.5 = (bf16[256,384]{1,0:T(8,128)(2,1)S(1)}, bf16[256,384]{1,0:T(8,128)(2,1)S(1)}, u32[]{:S(2)}, u32[]{:S(2)}) collective-permute-start(bf16[256,384]{1,0:T(8,128)(2,1)S(1)} %get-tuple-element.41), channel_id=1, source_target_pairs={{0,4},{4,0},{1,5},{5,1},{2,6},{6,2},{3,7},{7,3},{8,12},{12,8},{9,1... | collective-permute-start | bytes 589832 | tf_op jit(solution)/shard_map/pre/ppermute | solution.py:28
  98.0 19.8 %collective-permute-start.8 = (bf16[2,128,384]{2,1,0:T(8,128)(2,1)S(1)}, bf16[2,128,384]{2,1,0:T(8,128)(2,1)S(1)}, u32[]{:S(2)}, u32[]{:S(2)}) collective-permute-start(bf16[2,128,384]{2,1,0:T(8,128)(2,1)S(1)} %get-tuple-element.42.c0), channel_id=1, source_target_pairs={{0,3},{1,2},{2,1},{3,0},{4,7},{5,6},{6,5},{7,4},{8,11},{9,10},{10,... | collective-permute-start | bytes 589832 | tf_op jit(solution)/shard_map/pre/ppermute | solution.py:28
  99.9 17.9 %collective-permute-start.7 = (bf16[2,128,384]{2,1,0:T(8,128)(2,1)S(1)}, bf16[2,128,384]{2,1,0:T(8,128)(2,1)S(1)}, u32[]{:S(2)}, u32[]{:S(2)}) collective-permute-start(bf16[2,128,384]{2,1,0:T(8,128)(2,1)S(1)} %get-tuple-element.42.c0), channel_id=1, source_target_pairs={{0,2},{1,3},{2,0},{3,1},{4,6},{5,7},{6,4},{7,5},{8,10},{9,11},{10,... | collective-permute-start | bytes 589832 | tf_op jit(solution)/shard_map/pre/ppermute | solution.py:28
  102.2 15.7 %collective-permute-start.6 = (bf16[2,128,384]{2,1,0:T(8,128)(2,1)S(1)}, bf16[2,128,384]{2,1,0:T(8,128)(2,1)S(1)}, u32[]{:S(2)}, u32[]{:S(2)}) collective-permute-start(bf16[2,128,384]{2,1,0:T(8,128)(2,1)S(1)} %get-tuple-element.42.c0), channel_id=1, source_target_pairs={{0,1},{1,0},{2,3},{3,2},{4,5},{5,4},{6,7},{7,6},{8,9},{9,8},{10,11... | collective-permute-start | bytes 589832 | tf_op jit(solution)/shard_map/pre/ppermute | solution.py:28
  118.5 0.7 copy-start
  124.7 20.9 %collective-permute-start.9 = (bf16[32,16,1024]{2,1,0:T(8,128)(2,1)S(1)}, bf16[32,16,1024]{2,1,0:T(8,128)(2,1)S(1)}, u32[]{:S(2)}, u32[]{:S(2)}) collective-permute-start(bf16[32,16,1024]{2,1,0:T(8,128)(2,1)S(1)} %all-to-all-done.2.mine), channel_id=1, source_target_pairs={{0,8},{8,0},{1,9},{9,1},{2,10},{10,2},{3,11},{11,3},{4,12},{12,4},... | collective-permute-start | bytes 3145736 | tf_op jit(solution)/shard_map/pre/ppermute | solution.py:28
  129.6 13.8 %collective-permute-start.12 = (bf16[256,384]{1,0:T(8,128)(2,1)S(1)}, bf16[256,384]{1,0:T(8,128)(2,1)S(1)}, u32[]{:S(2)}, u32[]{:S(2)}) collective-permute-start(bf16[256,384]{1,0:T(8,128)(2,1)S(1)} %get-tuple-element.45.p0), channel_id=1, source_target_pairs={{0,3},{1,2},{2,1},{3,0},{4,7},{5,6},{6,5},{7,4},{8,11},{9,10},{10,... | collective-permute-start | bytes 589832 | tf_op jit(solution)/shard_map/pre/ppermute | solution.py:28
  131.5 11.9 %collective-permute-start.11 = (bf16[256,384]{1,0:T(8,128)(2,1)S(1)}, bf16[256,384]{1,0:T(8,128)(2,1)S(1)}, u32[]{:S(2)}, u32[]{:S(2)}) collective-permute-start(bf16[256,384]{1,0:T(8,128)(2,1)S(1)} %get-tuple-element.45.p0), channel_id=1, source_target_pairs={{0,2},{1,3},{2,0},{3,1},{4,6},{5,7},{6,4},{7,5},{8,10},{9,11},{10,... | collective-permute-start | bytes 589832 | tf_op jit(solution)/shard_map/pre/ppermute | solution.py:28
  134.3 11.3 %collective-permute-start.10 = (bf16[256,384]{1,0:T(8,128)(2,1)S(1)}, bf16[256,384]{1,0:T(8,128)(2,1)S(1)}, u32[]{:S(2)}, u32[]{:S(2)}) collective-permute-start(bf16[256,384]{1,0:T(8,128)(2,1)S(1)} %get-tuple-element.45.p0), channel_id=1, source_target_pairs={{0,1},{1,0},{2,3},{3,2},{4,5},{5,4},{6,7},{7,6},{8,9},{9,8},{10,11... | collective-permute-start | bytes 589832 | tf_op jit(solution)/shard_map/pre/ppermute | solution.py:28
  138.6 0.7 copy-start.8
  145.6 0.9 copy-start.1
  146.5 0.9 copy-start.7
  147.5 0.9 copy-start.9
  153.3 0.9 copy-start.2
  154.2 0.9 copy-start.4
  155.1 0.6 copy-start.11
  155.7 17.5 %all-to-all-start.3 = ((f32[64,1,128]{2,1,0:T(1,128)}), f32[64,1,128]{2,1,0:T(1,128)S(1)}, u32[]{:S(2)}, u32[]{:S(2)}) async-start(f32[64,1,128]{2,1,0:T(1,128)} %copy-done.11), calls=%async_computation.3 | async-start | bytes 65536 | tf_op jit(solution)/shard_map/ascent/all_to_all | solution.py:294
  174.7 1.1 copy-start.3
  174.7 1.4 copy-start.5
  176.0 1.4 copy-start.16
